TPU v7x, 32 devices: a whole 2x2x4 slice. The times are simulated.
32 devices in a mesh: dp: 4 (over y, x), mp: 8 (over z, core).
Axes of the slice: x: 2, y: 2, z: 4, core: 2. Of those that a mesh axis runs over, the one named last changes fastest.
Arguments:
- tokens: bfloat16 [8192, 2304], P(('dp', 'mp')), may hold values from -6 to 6
- ada_ffn: float32 [8, 2, 2304], P('dp'), may hold values from -4 to 4
- ffn_gate: float32 [8, 2304], P('dp'), may hold values from 0.5 to 1.5
- up_weight: bfloat16 [2304, 9216], P(None, 'mp'), may hold values from -0.125 to 0.125
- up_bias: float32 [9216], P('mp'), may hold values from -6 to 6
- down_weight: bfloat16 [9216, 2304], P('mp'), may hold values from -0.125 to 0.125
- down_bias: float32 [2304], replicated, may hold values from -6 to 6
- ada_head: float32 [8, 2, 2304], P('dp'), may hold values from -4 to 4
- head_weight: bfloat16 [2304, 4096], P(None, 'mp'), may hold values from -0.125 to 0.125
- head_bias: float32 [4096], P('mp'), may hold values from -6 to 6
- gumbel_noise: float32 [4, 1024, 4096], P('dp', None, 'mp'), as said below
- codebook: bfloat16 [4096, 32], P('mp'), may hold values from -16 to 16
- phi_weight: float32 [32, 32, 3, 3], replicated, may hold values from -0.375 to 0.375
- phi_bias: float32 [32], replicated, may hold values from -6 to 6
- f_hat: float32 [4, 32, 1024], P('dp', None, 'mp'), may hold values from -6 to 6
Outputs:
- block_out: bfloat16 [8192, 2304], P(('dp', 'mp'))
- f_hat_out: float32 [4, 32, 1024], P('dp', None, 'mp')
Inputs may be any that keep to these rules, and one draw needn't show every extreme that they name: `gumbel_noise`: noise added to the guided logits.
All inputs are finite; a program needn't handle non-finite values.
Results may differ from a plain program's by a relative error of at most 0.024.
Values may be sent and summed in bfloat16 or wider, within the bound.
No kernel may reach another device: no remote copies, remote signals or barrier semaphores. Data moves between devices by JAX's collectives and lax.ppermute only.
A program may use at most 256 MiB of HBM per device.

v0:
```python
import functools

import jax
import jax.numpy as jnp
from jax import lax
from jax.experimental import pallas as pl
from jax.experimental.pallas import tpu as pltpu
from jax.sharding import PartitionSpec as P

SIDE = 32
NEW = 1024
GUIDE = 1.5
CHUNKS = 2
FLOWS = 4
HEAD_FLOWS = 2


def norm_rows(values):
    row_mean = jnp.mean(values, axis=-1, keepdims=True)
    centred = values - row_mean
    spread = jnp.mean(centred * centred, axis=-1, keepdims=True)
    return centred * lax.rsqrt(spread + 1e-06)


def modulate(values, ada):
    return norm_rows(values.astype(jnp.float32)) * (1.0 + ada[1]) + ada[0]


def permute_devices(value, dp, mp, target):
    pairs = []
    for d in range(dp):
        for m in range(mp):
            to = target(d, m)
            if to is not None:
                pairs.append((d * mp + m, to[0] * mp + to[1]))
    return lax.ppermute(value, ("dp", "mp"), pairs)


def general_body(
    tokens,
    ada_ffn,
    ffn_gate,
    up_weight,
    up_bias,
    down_weight,
    down_bias,
    ada_head,
    head_weight,
    head_bias,
    gumbel_noise,
    codebook,
    phi_weight,
    phi_bias,
    f_hat,
):
    rows, width = tokens.shape
    dp, mp = lax.axis_size("dp"), lax.axis_size("mp")
    d_index, m_index = lax.axis_index("dp"), lax.axis_index("mp")
    images = ada_ffn.shape[0]
    pairs = f_hat.shape[0]
    channels = f_hat.shape[1]
    vocab = head_weight.shape[1]
    own_image = (m_index * rows) // NEW
    ada_own = lax.dynamic_index_in_dim(ada_ffn, own_image, 0, keepdims=False)
    gate_own = lax.dynamic_index_in_dim(ffn_gate, own_image, 0, keepdims=False)
    head_own = lax.dynamic_index_in_dim(ada_head, own_image, 0, keepdims=False)
    half_dp, half_mp = dp // 2, mp // 2
    upper = d_index // half_dp

    def swap(d, m):
        return ((d + half_dp) % dp, m)

    def cross(d, m):
        if d // half_dp == m // half_mp:
            return None
        return ((d + half_dp) % dp, (m + half_mp) % mp)

    stays = upper == m_index // half_mp
    head_twin = permute_devices(head_own, dp, mp, swap)
    head_cond = jnp.where(upper == 0, head_own, head_twin)
    head_uncond = jnp.where(upper == 0, head_twin, head_own)

    step = rows // FLOWS
    normed = modulate(tokens, ada_own).astype(jnp.bfloat16)
    outs = []
    for c in range(FLOWS):
        part = lax.slice_in_dim(normed, c * step, (c + 1) * step, axis=0)
        gathered = lax.all_gather(part, "mp", axis=0, tiled=True)
        hidden = jax.nn.gelu(
            jnp.dot(gathered, up_weight, preferred_element_type=jnp.float32) + up_bias,
            approximate=True,
        ).astype(jnp.bfloat16)
        partial = jnp.dot(hidden, down_weight, preferred_element_type=jnp.float32).astype(jnp.bfloat16)
        summed = lax.psum_scatter(partial, "mp", scatter_dimension=0, tiled=True).astype(jnp.float32)
        own = lax.slice_in_dim(tokens, c * step, (c + 1) * step, axis=0).astype(jnp.float32)
        outs.append((own + gate_own * (summed + down_bias)).astype(jnp.bfloat16))
    block_out = jnp.concatenate(outs, axis=0)

    group = FLOWS // HEAD_FLOWS
    half = rows // HEAD_FLOWS // 2
    noise = gumbel_noise.reshape(pairs, NEW // rows, HEAD_FLOWS, 2, half, vocab)
    peaks, totals, codes = [], [], []
    for c in range(HEAD_FLOWS):
        part = jnp.concatenate(outs[c * group : (c + 1) * group], axis=0)
        first, second = part[:half], part[half:]
        kept = jnp.where(upper == 0, first, second)
        sent = jnp.where(upper == 0, second, first)
        came = permute_devices(sent, dp, mp, swap)
        cond = jnp.where(upper == 0, kept, came)
        uncond = jnp.where(upper == 0, came, kept)
        mixed = (
            (1.0 + GUIDE) * modulate(cond, head_cond) - GUIDE * modulate(uncond, head_uncond)
        ).astype(jnp.bfloat16)
        crossed = permute_devices(mixed, dp, mp, cross)
        mixed = jnp.where(stays, mixed, crossed)
        gathered = lax.all_gather(mixed, "mp", axis=0, tiled=True)
        logits = jnp.dot(gathered, head_weight, preferred_element_type=jnp.float32) + head_bias
        logits = logits.reshape(2, half_mp, half, vocab)
        order = jnp.transpose(logits, (1, 0, 2, 3)).reshape(pairs, NEW // rows, 2, half, vocab)
        scores = order + noise[:, :, c]
        peak = jnp.max(scores, axis=-1)
        weights = jnp.exp(scores - peak[..., None]).astype(jnp.bfloat16)
        totals.append(jnp.sum(weights.astype(jnp.float32), axis=-1))
        codes.append(jnp.dot(weights, codebook, preferred_element_type=jnp.float32))
        peaks.append(peak)
    stack = lambda parts: jnp.stack(parts, axis=2)
    peak = stack(peaks).reshape(pairs, 1, NEW)
    total = stack(totals).reshape(pairs, 1, NEW)
    code = stack(codes).reshape(pairs, NEW, channels).transpose(0, 2, 1)
    stats = jnp.concatenate([code, total, peak], axis=1)

    cells = f_hat.shape[2]
    band = cells // SIDE
    padded = jnp.pad(stats, ((0, 0), (0, 0), (SIDE, SIDE)))
    windows = jnp.stack(
        [padded[:, :, m * cells : m * cells + cells + 2 * SIDE] for m in range(mp)], axis=0
    )
    parts = lax.all_to_all(windows, "mp", 0, 0, tiled=True)
    top = jnp.max(parts[:, :, channels + 1], axis=0)
    factor = jnp.exp(parts[:, :, channels + 1] - top[None])[:, :, None]
    sums = jnp.sum(parts[:, :, : channels + 1] * factor, axis=0)
    cell_index = m_index * cells - SIDE + jnp.arange(cells + 2 * SIDE)
    inside = (cell_index >= 0) & (cell_index < NEW)
    soft = jnp.where(inside, sums[:, :channels] / jnp.where(inside, sums[:, channels:], 1.0), 0.0)
    code_map = soft.reshape(pairs, channels, band + 2, SIDE)
    wide = jnp.pad(code_map, ((0, 0), (0, 0), (0, 0), (1, 1)))
    taps = jnp.stack(
        [wide[:, :, i : i + band, j : j + SIDE] for i in range(3) for j in range(3)], axis=2
    ).reshape(pairs, channels * 9, cells)
    conv = jnp.einsum(
        "ok,pkn->pon",
        phi_weight.reshape(channels, channels * 9),
        taps,
        precision=lax.Precision.HIGHEST,
        preferred_element_type=jnp.float32,
    ) + phi_bias[None, :, None]
    f_hat_out = f_hat + 0.5 * soft[:, :, SIDE : SIDE + cells] + 0.5 * conv
    return (block_out, f_hat_out)


SCALARS = pl.BlockSpec(memory_space=pltpu.SMEM)
ON_CHIP = pl.BlockSpec(memory_space=pltpu.VMEM)
VMEM_LIMIT = 16 * 1024 * 1024


def call(kernel, args, outs, scalars=0, scratch=()):
    return pl.pallas_call(
        kernel,
        out_shape=outs,
        in_specs=[SCALARS] * scalars + [ON_CHIP] * (len(args) - scalars),
        out_specs=[ON_CHIP] * len(outs),
        scratch_shapes=scratch,
        compiler_params=pltpu.CompilerParams(vmem_limit_bytes=VMEM_LIMIT),
        cost_estimate=pl.CostEstimate(flops=0, bytes_accessed=0, transcendentals=0),
    )(*args)


def shape_of(shape, kind=jnp.bfloat16):
    return jax.ShapeDtypeStruct(shape, kind)


def after(value, *others):
    return lax.optimization_barrier((value, *others))[0]


def modulated(ref, ada_ref):
    return norm_rows(ref[...].astype(jnp.float32)) * (1.0 + ada_ref[1:2, :]) + ada_ref[0:1, :]


def norm_kernel(tokens_ref, ada_ref, out_ref):
    out_ref[...] = modulated(tokens_ref, ada_ref).astype(jnp.bfloat16)


def norm_part(tokens, ada):
    return call(norm_kernel, (tokens, ada), [shape_of(tokens.shape)])[0]


def ffn_kernel(groups, tile, where_ref, *refs):
    count = sum(groups)
    parts = refs[:count]
    up_refs, down_refs = refs[count : count + 2], refs[count + 2 : count + 4]
    bias_ref = refs[count + 4]
    outs = refs[count + 5 : count + 5 + len(groups)]
    x_ref, hidden_ref = refs[count + 5 + len(groups) :]
    panel, width = down_refs[0].shape
    step = outs[0].shape[0]
    place = 0
    for g, size in enumerate(groups):
        if size == 1:
            value = parts[place][...]
        else:
            value = jnp.where(where_ref[0] == 1, parts[place][...], parts[place + 1][...])
        x_ref[g * step : (g + 1) * step, :] = value
        place += size
    for begin in range(0, 2 * panel, tile):
        end = begin + tile
        if end <= panel:
            weight = up_refs[0][:, begin:end]
        elif begin >= panel:
            weight = up_refs[1][:, begin - panel : end - panel]
        else:
            weight = jnp.concatenate([up_refs[0][:, begin:], up_refs[1][:, : end - panel]], axis=1)
        v = jnp.dot(x_ref[...], weight, preferred_element_type=jnp.float32) + bias_ref[:, begin:end]
        hidden_ref[:, begin:end] = jax.nn.gelu(v, approximate=True).astype(jnp.bfloat16)
    for begin in range(0, width, tile):
        cols = slice(begin, begin + tile)
        weight = jnp.concatenate([down_refs[0][:, cols], down_refs[1][:, cols]], axis=0)
        result = jnp.dot(hidden_ref[...], weight, preferred_element_type=jnp.float32)
        for g in range(len(groups)):
            outs[g][:, cols] = result[g * step : (g + 1) * step].astype(jnp.bfloat16)


def ffn(where, slots, ups, downs, bias):
    groups = tuple(len(slot) for slot in slots)
    parts = [part for slot in slots for part in slot]
    rows, width = parts[0].shape
    panel = ups[0].shape[1]
    total = rows * len(slots)
    return call(
        functools.partial(ffn_kernel, groups, 256),
        (where, *parts, *ups, *downs, bias),
        [shape_of((rows, width))] * len(slots),
        scalars=1,
        scratch=[
            pltpu.VMEM((total, width), jnp.bfloat16),
            pltpu.VMEM((total, 2 * panel), jnp.bfloat16),
        ],
    )


def add_kernel(where_ref, a_ref, b_ref, out_ref):
    b = jnp.where(where_ref[0] == 1, b_ref[...].astype(jnp.float32), 0.0)
    out_ref[...] = (a_ref[...].astype(jnp.float32) + b).astype(jnp.bfloat16)


def add_mid(where, a, b):
    return call(add_kernel, (where, a, b), [shape_of(a.shape)], scalars=1)[0]


def out_kernel(where_ref, own_ref, near_ref, mid_ref, tokens_ref, gate_ref, bias_ref, out_ref, kept_ref, sent_ref):
    from_mid = jnp.where(where_ref[0] == 1, mid_ref[...].astype(jnp.float32), 0.0)
    summed = own_ref[...].astype(jnp.float32) + near_ref[...].astype(jnp.float32) + from_mid
    value = tokens_ref[...].astype(jnp.float32) + gate_ref[...] * (summed + bias_ref[...])
    value = value.astype(jnp.bfloat16)
    out_ref[...] = value
    half = value.shape[0] // 2
    lower = where_ref[1] == 0
    kept_ref[...] = jnp.where(lower, value[:half], value[half:])
    sent_ref[...] = jnp.where(lower, value[half:], value[:half])


def block_rows(where, own, near, mid, tokens, gate, bias):
    rows, width = own.shape
    return call(
        out_kernel,
        (where, own, near, mid, tokens, gate, bias),
        [shape_of((rows, width)), shape_of((rows // 2, width)), shape_of((rows // 2, width))],
        scalars=1,
    )


def mix_kernel(where_ref, kept_ref, came_ref, ada_ref, twin_ref, out_ref):
    kept, came = modulated(kept_ref, ada_ref), modulated(came_ref, twin_ref)
    lower = where_ref[1] == 0
    share = jnp.where(lower, 1.0 + GUIDE, -GUIDE)
    other = jnp.where(lower, -GUIDE, 1.0 + GUIDE)
    out_ref[...] = (share * kept + other * came).astype(jnp.bfloat16)


def mix_twins(where, kept, came, ada, twin):
    return call(mix_kernel, (where, kept, came, ada, twin), [shape_of(kept.shape)], scalars=1)[0]


def head_kernel(
    chunk, where_ref, own_ref, near_ref, far_a, far_b, last_a, last_b, weight_a, weight_b, bias_ref, code_ref,
    noise_own, noise_core, noise_twin, noise_both, stats_ref, x_ref
):
    step = own_ref.shape[0]
    panel = weight_a.shape[1]
    mid = where_ref[0] == 1
    x_ref[0:step, :] = own_ref[...]
    x_ref[step : 2 * step, :] = near_ref[...]
    x_ref[2 * step : 3 * step, :] = jnp.where(mid, far_a[...], far_b[...])
    x_ref[3 * step : 4 * step, :] = jnp.where(mid, last_a[...], last_b[...])
    x = x_ref[...]
    odd = where_ref[2]
    even = 1 - odd
    same = where_ref[3] == 1
    scores = []
    for which, weight, ours, theirs in ((0, weight_a, noise_own, noise_twin), (1, weight_b, noise_core, noise_both)):
        picked = []
        for first in (True, False):
            for block in (odd, even):
                a, b = ours[block, chunk], theirs[block, chunk]
                picked.append(jnp.where(same, a, b) if first else jnp.where(same, b, a))
        logits = jnp.dot(x, weight[...], preferred_element_type=jnp.float32)
        scores.append(
            logits + bias_ref[:, which * panel : (which + 1) * panel] + jnp.concatenate(picked, axis=0)
        )
    peak = jnp.max(jnp.maximum(scores[0], scores[1]), axis=1, keepdims=True)
    sums = 0.0
    total = 0.0
    for which in range(2):
        weights = jnp.exp(scores[which] - peak).astype(jnp.bfloat16)
        total = total + jnp.sum(weights.astype(jnp.float32), axis=1, keepdims=True)
        codes = code_ref[which * panel : (which + 1) * panel, :].astype(jnp.bfloat16)
        sums = sums + jnp.dot(weights, codes, preferred_element_type=jnp.float32)
    channels = code_ref.shape[1]
    pad = jnp.zeros((4 * step, 128 - channels), jnp.float32)
    table = jnp.concatenate([sums, pad], axis=1)
    lane = lax.broadcasted_iota(jnp.int32, table.shape, 1)
    table = jnp.where(lane == channels, total, table)
    table = jnp.where(lane == channels + 1, peak, table)
    stats_ref[...] = jnp.transpose(table)[: stats_ref.shape[0], :]


def head_stats(chunk, where, slots, weights, bias, codes, noises):
    step, width = slots[0].shape
    panel = weights[0].shape[1]
    height = -(-(codes.shape[1] + 2) // 8) * 8
    return call(
        functools.partial(head_kernel, chunk),
        (where, *slots, *weights, bias, codes, *noises),
        [shape_of((height, 4 * step), jnp.float32)],
        scalars=1,
        scratch=[pltpu.VMEM((4 * step, width), jnp.bfloat16)],
    )[0]


def soft_kernel(channels, *refs):
    parts, out_ref = refs[:-1], refs[-1]
    tops = [part[channels + 1 : channels + 2, :] for part in parts]
    top = functools.reduce(jnp.maximum, tops)
    code = 0.0
    total = 0.0
    for part, peak in zip(parts, tops):
        factor = jnp.exp(peak - top)
        code = code + part[0:channels, :] * factor
        total = total + part[channels : channels + 1, :] * factor
    out_ref[...] = code / total


def soft_codes(parts, channels):
    return call(
        functools.partial(soft_kernel, channels),
        tuple(parts),
        [shape_of((channels, parts[0].shape[1]), jnp.float32)],
    )[0]


def line_body(
    tokens,
    ada_ffn,
    ffn_gate,
    up_weight,
    up_bias,
    down_weight,
    down_bias,
    ada_head,
    head_weight,
    head_bias,
    gumbel_noise,
    codebook,
    phi_weight,
    phi_bias,
    f_hat,
):
    rows, width = tokens.shape
    dp, mp = lax.axis_size("dp"), lax.axis_size("mp")
    d_index, m_index = lax.axis_index("dp"), lax.axis_index("mp")
    channels = f_hat.shape[1]
    half_dp = dp // 2
    upper = d_index // half_dp
    z_index, core = m_index // 2, m_index % 2
    where = jnp.stack(
        [(z_index == 1) | (z_index == 2), upper, z_index % 2, z_index // 2 == upper]
    ).astype(jnp.int32)

    def along_z(value, target):
        def to(d, m):
            z = target(m // 2)
            return None if z is None else (d, 2 * z + m % 2)

        return permute_devices(value, dp, mp, to)

    def near(value):
        return along_z(value, lambda z: z ^ 1)

    def middle(value):
        return along_z(value, lambda z: 3 - z if z in (1, 2) else z)

    def outward(value):
        return along_z(value, lambda z: {1: 0, 2: 3}.get(z))

    def inward(value):
        return along_z(value, lambda z: {0: 1, 3: 2}.get(z))

    def swap_cores(value):
        return permute_devices(value, dp, mp, lambda d, m: (d, m ^ 1))

    def swap_twins(value):
        return permute_devices(value, dp, mp, lambda d, m: ((d + half_dp) % dp, m))

    def swap_both(value):
        return permute_devices(value, dp, mp, lambda d, m: ((d + half_dp) % dp, m ^ 1))

    own_image = (m_index * rows) // NEW
    ada_own = lax.dynamic_index_in_dim(ada_ffn, own_image, 0, keepdims=False)
    gate_own = lax.dynamic_index_in_dim(ffn_gate, own_image, 0, keepdims=True)
    head_own = lax.dynamic_index_in_dim(ada_head, own_image, 0, keepdims=False)

    ups, downs = (up_weight, swap_cores(up_weight)), (down_weight, swap_cores(down_weight))
    small = jnp.concatenate([up_bias, head_bias, codebook.astype(jnp.float32).reshape(-1)])
    small_other = swap_cores(small)
    head_twin = swap_twins(head_own)
    hid, voc = up_bias.shape[0], head_bias.shape[0]
    bias_up = jnp.concatenate([up_bias, small_other[:hid]])[None]
    bias_head = jnp.concatenate([head_bias, small_other[hid : hid + voc]])[None]
    codes = jnp.concatenate(
        [codebook.astype(jnp.float32), small_other[hid + voc :].reshape(codebook.shape)], axis=0
    )

    half = rows // CHUNKS // 2
    noise = gumbel_noise.reshape(2, 2, CHUNKS, 2, half, voc)

    def noise_for(to_core, to_upper):
        picked = lax.dynamic_slice(
            noise, (0, to_core, 0, to_upper, 0, 0), (2, 1, CHUNKS, 1, half, voc)
        )
        return picked.reshape(2, CHUNKS, half, voc)

    step = rows // CHUNKS
    rows_a, rows_b = tokens[:step], tokens[step:]
    own_a = norm_part(rows_a, ada_own)
    near_a, mid_a = near(own_a), middle(own_a)
    own_b = norm_part(rows_b, ada_own)
    far_mid_a, far_end_a = middle(near_a), outward(mid_a)
    near_b = near(after(own_b, near_a))
    noises = (
        noise_for(core, upper),
        swap_cores(after(noise_for(1 - core, upper), mid_a)),
        swap_twins(after(noise_for(core, 1 - upper), mid_a)),
        swap_both(after(noise_for(1 - core, 1 - upper), mid_a)),
    )
    sum_own_a, sum_near_a = ffn(where, [[own_a], [near_a]], ups, downs, bias_up)
    head_other = swap_cores(after(head_weight, ups[1], downs[1]))
    far_a = (after(far_mid_a, sum_near_a), far_end_a)
    last_end_a = outward(far_a[0])
    mid_b = middle(after(own_b, far_a[0]))
    (sum_far_a,) = ffn(where, [far_a], ups, downs, bias_up)
    came_far_a = inward(sum_far_a)
    near_b, mid_b = after(near_b, sum_far_a), after(mid_b, sum_far_a)
    far_mid_b, far_end_b = middle(near_b), outward(mid_b)
    (sum_last_a,) = ffn(where, [(mid_a, after(last_end_a, sum_far_a))], ups, downs, bias_up)
    came_last_a = inward(sum_last_a)
    sum_own_b, sum_near_b = ffn(where, [[after(own_b, sum_last_a, came_far_a, *noises)], [near_b]], ups, downs, bias_up)
    far_b = (after(far_mid_b, sum_near_b), far_end_b)
    last_end_b = outward(far_b[0])
    both_last_a = add_mid(where, after(sum_last_a, far_b[0]), came_far_a)
    went_last_a = middle(both_last_a)
    (sum_far_b,) = ffn(where, [(after(far_b[0], both_last_a), far_b[1])], ups, downs, bias_up)
    came_far_b = inward(sum_far_b)
    both_far_a = add_mid(where, after(sum_far_a, sum_far_b), came_last_a)
    went_far_a = middle(both_far_a)
    (sum_last_b,) = ffn(where, [(after(mid_b, went_last_a, both_far_a), after(last_end_b, sum_far_b))], ups, downs, bias_up)
    came_last_b = inward(sum_last_b)
    came_near_a = near(add_mid(where, sum_near_a, went_far_a))
    went_last_b = middle(add_mid(where, sum_last_b, came_far_b))
    went_far_b = middle(add_mid(where, sum_far_b, came_last_b))

    def finish(own, came_near, went_last, part):
        return block_rows(where, own, came_near, went_last, part, gate_own, down_bias[None])

    def gather(own):
        from_near, from_mid = near(own), middle(own)
        far_mid, far_end = middle(from_near), outward(from_mid)
        return own, from_near, far_mid, far_end, from_mid, outward(far_mid)

    out_a, kept_a, sent_a = finish(sum_own_a, came_near_a, went_last_a, rows_a)
    came_a = swap_twins(sent_a)
    mixed_a = mix_twins(where, kept_a, came_a, head_own, head_twin)
    came_near_b = near(add_mid(where, sum_near_b, went_far_b))
    slots_a = gather(mixed_a)
    out_b, kept_b, sent_b = finish(sum_own_b, came_near_b, went_last_b, rows_b)
    came_b = swap_twins(sent_b)
    mixed_b = mix_twins(where, kept_b, came_b, head_own, head_twin)
    slots_b = gather(mixed_b)
    heads = (head_weight, head_other)
    stats = [
        head_stats(0, where, slots_a, heads, bias_head, codes, noises),
        head_stats(1, where, slots_b, heads, bias_head, codes, noises),
    ]
    block_out = jnp.concatenate([out_a, out_b], axis=0)

    slots = [
        jnp.concatenate([part[:, r * half : (r + 1) * half] for part in stats], axis=1) for r in range(4)
    ]
    parts = [slots[0]] + [along_z(slots[r], lambda z, r=r: z ^ r) for r in (1, 2, 3)]
    soft = soft_codes(parts, channels)

    def to_cells(d, m, core_of):
        y, x = d // half_dp, d % half_dp
        z, c = m // 2, m % 2
        return ((z // 2) * half_dp + x, 2 * (2 * (z % 2) + c) + core_of(y))

    def to_halo(d, m):
        y, x = d // half_dp, d % half_dp
        z, c = m // 2, m % 2
        block = 2 * (z % 2) + c + (1 if y == 1 else -1)
        if block < 0 or block > 3:
            return None
        return ((z // 2) * half_dp + x, 2 * block + (0 if y == 1 else 1))

    first = permute_devices(soft, dp, mp, lambda d, m: to_cells(d, m, lambda y: y))
    second = permute_devices(soft, dp, mp, lambda d, m: to_cells(d, m, lambda y: 1 - y))
    halo = permute_devices(soft, dp, mp, to_halo)
    lower, higher = jnp.where(core == 0, first, second), jnp.where(core == 0, second, first)
    window = jnp.where(
        core == 0,
        jnp.concatenate([halo[:, -SIDE:], lower[:, :half], higher[:, :half], lower[:, half : half + SIDE]], axis=1),
        jnp.concatenate([higher[:, half - SIDE : half], lower[:, half:], higher[:, half:], halo[:, :SIDE]], axis=1),
    )
    cells = f_hat.shape[2]
    band = cells // SIDE
    code_map = window.reshape(channels, band + 2, SIDE)
    wide = jnp.pad(code_map, ((0, 0), (0, 0), (1, 1)))
    taps = jnp.stack(
        [wide[:, i : i + band, j : j + SIDE] for i in range(3) for j in range(3)], axis=1
    ).reshape(channels * 9, cells)
    conv = jnp.dot(
        phi_weight.reshape(channels, channels * 9),
        taps,
        precision=lax.Precision.HIGHEST,
        preferred_element_type=jnp.float32,
    ) + phi_bias[:, None]
    f_hat_out = f_hat + (0.5 * window[:, SIDE : SIDE + cells] + 0.5 * conv)[None]
    return (block_out, f_hat_out)


def solution(mesh):
    in_specs = (
        P(("dp", "mp"), None),
        P("dp", None, None),
        P("dp", None),
        P(None, "mp"),
        P("mp"),
        P("mp", None),
        P(),
        P("dp", None, None),
        P(None, "mp"),
        P("mp"),
        P("dp", None, "mp"),
        P("mp", None),
        P(),
        P(),
        P("dp", None, "mp"),
    )
    out_specs = (P(("dp", "mp"), None), P("dp", None, "mp"))
    line = mesh.shape["dp"] == 4 and mesh.shape["mp"] == 8
    body = line_body if line else general_body
    return jax.shard_map(body, mesh=mesh, in_specs=in_specs, out_specs=out_specs, check_vma=False)
```

profile of v0, /device:TPU:13, one launch (start us, length us, event | category | flops | bytes accessed | tf_op | source)
XLA Modules:
  0.0 266.6 jit_solution(12830588782534744264)
XLA Ops:
  3.5 4.3 %collective-permute-start.5 = (bf16[128,2304]{1,0:T(8,128)(2,1)S(1)}, bf16[128,2304]{1,0:T(8,128)(2,1)S(1)}, u32[]{:S(2)}, u32[]{:S(2)}) collective-permute-start(bf16[128,2304]{1,0:T(8,128)(2,1)S(1)} %shard_map.158.refs_0_), channel_id=1, source_target_pairs={{0,0},{1,1},{2,4},{3,5},{4,2},{5,3},{6,6},{7,7},{8,8},{9,9},{10,12... | collective-permute-start | bytes 1769480 | tf_op jit(solution)/shard_map/ppermute | solution.py:36
  7.8 9.8 %collective-permute-done.refs_1_ = bf16[128,2304]{1,0:T(8,128)(2,1)S(1)} collective-permute-done((bf16[128,2304]{1,0:T(8,128)(2,1)S(1)}, bf16[128,2304]{1,0:T(8,128)(2,1)S(1)}, u32[]{:S(2)}, u32[]{:S(2)}) %collective-permute-start) | collective-permute-done | bytes 589856 | tf_op jit(solution)/shard_map/ppermute | solution.py:36
  17.6 3.2 %collective-permute-start.4 = (bf16[128,2304]{1,0:T(8,128)(2,1)S(1)}, bf16[128,2304]{1,0:T(8,128)(2,1)}, u32[]{:S(2)}, u32[]{:S(2)}) collective-permute-start(bf16[128,2304]{1,0:T(8,128)(2,1)S(1)} %collective-permute-done.refs_1_), channel_id=1, source_target_pairs={{0,0},{1,1},{2,4},{3,5},{4,2},{5,3},{6,6},{7,7},{8,8},{9,9},{10,12... | collective-permute-start | bytes 1769480 | tf_op jit(solution)/shard_map/ppermute | solution.py:36
  21.8 1.7 collective-permute-start.3
  25.6 3.4 %collective-permute-start.6 = (bf16[128,2304]{1,0:T(8,128)(2,1)S(1)}, bf16[128,2304]{1,0:T(8,128)(2,1)S(1)}, u32[]{:S(2)}, u32[]{:S(2)}) collective-permute-start(bf16[128,2304]{1,0:T(8,128)(2,1)S(1)} %collective-permute-done.5.refs_0_), channel_id=1, source_target_pairs={{2,0},{3,1},{4,6},{5,7},{10,8},{11,9},{12,14},{13,15},{18,16},{19,... | collective-permute-start | bytes 1769480 | tf_op jit(solution)/shard_map/ppermute | solution.py:36
  29.0 2.5 copy-done.2
  31.5 2.5 copy-done.4
  34.0 10.3 %shard_map.159 = (bf16[128,2304]{1,0:T(8,128)(2,1)S(1)}, bf16[128,2304]{1,0:T(8,128)(2,1)S(1)}) custom-call(s32[4]{0:T(128)S(1)} %pad_add_fusion.where_ref, bf16[128,2304]{1,0:T(8,128)(2,1)S(1)} %shard_map.158.refs_0_, bf16[128,2304]{1,0:T(8,128)(2,1)S(1)} %collective-permute-done.refs_1_, bf16[2304,1152]{1,0:T(8,128)(2,1)S(1)} %copy-done.2, ...), custom_call_target="tpu_custom_call" | custom-call | tf_op jit(solution)/shard_map/pallas_call | solution.py:167
  47.6 3.4 %collective-permute-done.6.refs_1_ = bf16[128,2304]{1,0:T(8,128)(2,1)S(1)} collective-permute-done((bf16[128,2304]{1,0:T(8,128)(2,1)S(1)}, bf16[128,2304]{1,0:T(8,128)(2,1)S(1)}, u32[]{:S(2)}, u32[]{:S(2)}) %collective-permute-start.6) | collective-permute-done | bytes 589856 | tf_op jit(solution)/shard_map/ppermute | solution.py:36
  50.9 7.5 %shard_map.160.a_ref = bf16[128,2304]{1,0:T(8,128)(2,1)S(1)} custom-call(s32[4]{0:T(128)S(1)} %pad_add_fusion.where_ref, bf16[128,2304]{1,0:T(8,128)(2,1)} %collective-permute-done.4.refs_0_, bf16[128,2304]{1,0:T(8,128)(2,1)S(1)} %collective-permute-done.6.refs_1_, bf16[2304,1152]{1,0:T(8,128)(2,1)S(1)} %copy-done.3, ...), custom_call_target="tpu_custom_call" | custom-call | tf_op jit(solution)/shard_map/pallas_call | solution.py:167
  59.7 2.2 collective-permute-start.14
  61.9 3.3 %collective-permute-start.8 = (bf16[128,2304]{1,0:T(8,128)(2,1)S(1)}, bf16[128,2304]{1,0:T(8,128)(2,1)S(1)}, u32[]{:S(2)}, u32[]{:S(2)}) collective-permute-start(bf16[128,2304]{1,0:T(8,128)(2,1)S(1)} %collective-permute-done.7.refs_1_), channel_id=1, source_target_pairs={{0,0},{1,1},{2,4},{3,5},{4,2},{5,3},{6,6},{7,7},{8,8},{9,9},{10,12... | collective-permute-start | bytes 1769480 | tf_op jit(solution)/shard_map/ppermute | solution.py:36
  66.3 3.2 %collective-permute-start.13 = (f32[2,2,64,512]{3,2,1,0:T(8,128)S(1)}, f32[2,2,64,512]{3,2,1,0:T(8,128)S(1)}, u32[]{:S(2)}, u32[]{:S(2)}) collective-permute-start(f32[2,2,64,512]{3,2,1,0:T(8,128)S(1)} %get-tuple-element.37), channel_id=1, source_target_pairs={{0,17},{1,16},{2,19},{3,18},{4,21},{5,20},{6,23},{7,22},{8,25},{9,... | collective-permute-start | bytes 1572872 | tf_op jit(solution)/shard_map/ppermute | solution.py:36
  69.5 7.3 %shard_map.162.a_ref = bf16[128,2304]{1,0:T(8,128)(2,1)S(1)} custom-call(s32[4]{0:T(128)S(1)} %pad_add_fusion.where_ref, bf16[128,2304]{1,0:T(8,128)(2,1)S(1)} %copy-done.18, bf16[128,2304]{1,0:T(8,128)(2,1)S(1)} %collective-permute-done.9.refs_1_, bf16[2304,1152]{1,0:T(8,128)(2,1)S(1)} %copy-done.3, bf16[2304,1152]{1,0:T(8,128)(2,1)} %collective-permute-done.1.refs_3_, ...), custom_call_target="tpu_custom_call" | custom-call | tf_op jit(solution)/shard_map/pallas_call | solution.py:167
  79.8 11.5 %collective-permute-done.13.noise_both = f32[2,2,64,512]{3,2,1,0:T(8,128)S(1)} collective-permute-done((f32[2,2,64,512]{3,2,1,0:T(8,128)S(1)}, f32[2,2,64,512]{3,2,1,0:T(8,128)S(1)}, u32[]{:S(2)}, u32[]{:S(2)}) %collective-permute-start.13) | collective-permute-done | bytes 524320 | tf_op jit(solution)/shard_map/ppermute | solution.py:36
  93.4 10.2 %shard_map.163 = (bf16[128,2304]{1,0:T(8,128)(2,1)S(1)}, bf16[128,2304]{1,0:T(8,128)(2,1)S(1)}) custom-call(s32[4]{0:T(128)S(1)} %pad_add_fusion.where_ref, bf16[128,2304]{1,0:T(8,128)(2,1)S(1)} %shard_map.161.refs_0_, bf16[128,2304]{1,0:T(8,128)(2,1)S(1)} %collective-permute-done.7.refs_1_, bf16[2304,1152]{1,0:T(8,128)(2,1)S(1)} %copy-done.3, ...), custom_call_target="tpu_custom_call" | custom-call | tf_op jit(solution)/shard_map/pallas_call | solution.py:167
  104.4 2.2 collective-permute-start.19
  108.1 7.3 %shard_map.165.a_ref = bf16[128,2304]{1,0:T(8,128)(2,1)S(1)} custom-call(s32[4]{0:T(128)S(1)} %pad_add_fusion.where_ref, bf16[128,2304]{1,0:T(8,128)(2,1)S(1)} %collective-permute-done.8.refs_0_, bf16[128,2304]{1,0:T(8,128)(2,1)S(1)} %collective-permute-done.15.refs_1_, bf16[2304,1152]{1,0:T(8,128)(2,1)S(1)} %copy-done.3, ...), custom_call_target="tpu_custom_call" | custom-call | tf_op jit(solution)/shard_map/pallas_call | solution.py:167
  116.2 4.0 %collective-permute-done.19.mid_ref = bf16[128,2304]{1,0:T(8,128)(2,1)S(1)} collective-permute-done((bf16[128,2304]{1,0:T(8,128)(2,1)S(1)}, bf16[128,2304]{1,0:T(8,128)(2,1)S(1)}, u32[]{:S(2)}, u32[]{:S(2)}) %collective-permute-start.19) | collective-permute-done | bytes 589856 | tf_op jit(solution)/shard_map/ppermute | solution.py:36
  120.2 7.3 %shard_map.169.a_ref = bf16[128,2304]{1,0:T(8,128)(2,1)S(1)} custom-call(s32[4]{0:T(128)S(1)} %pad_add_fusion.where_ref, bf16[128,2304]{1,0:T(8,128)(2,1)S(1)} %collective-permute-done.14.refs_0_, bf16[128,2304]{1,0:T(8,128)(2,1)S(1)} %collective-permute-done.20.refs_1_, bf16[2304,1152]{1,0:T(8,128)(2,1)S(1)} %copy-done.3, ...), custom_call_target="tpu_custom_call" | custom-call | tf_op jit(solution)/shard_map/pallas_call | solution.py:167
  128.8 2.8 %collective-permute-start.17 = (bf16[128,2304]{1,0:T(8,128)(2,1)S(1)}, bf16[128,2304]{1,0:T(8,128)(2,1)S(1)}, u32[]{:S(2)}, u32[]{:S(2)}) collective-permute-start(bf16[128,2304]{1,0:T(8,128)(2,1)S(1)} %shard_map.166), channel_id=1, source_target_pairs={{0,0},{1,1},{2,4},{3,5},{4,2},{5,3},{6,6},{7,7},{8,8},{9,9},{10,12... | collective-permute-start | bytes 1769480 | tf_op jit(solution)/shard_map/ppermute | solution.py:36
  132.9 11.9 %collective-permute-done.21.b_ref = bf16[128,2304]{1,0:T(8,128)(2,1)S(1)} collective-permute-done((bf16[128,2304]{1,0:T(8,128)(2,1)S(1)}, bf16[128,2304]{1,0:T(8,128)(2,1)S(1)}, u32[]{:S(2)}, u32[]{:S(2)}) %collective-permute-start.21) | collective-permute-done | bytes 589856 | tf_op jit(solution)/shard_map/ppermute | solution.py:36
  145.5 2.8 %collective-permute-start.22 = (bf16[128,2304]{1,0:T(8,128)(2,1)S(1)}, bf16[128,2304]{1,0:T(8,128)(2,1)S(1)}, u32[]{:S(2)}, u32[]{:S(2)}) collective-permute-start(bf16[128,2304]{1,0:T(8,128)(2,1)S(1)} %shard_map.170), channel_id=1, source_target_pairs={{0,0},{1,1},{2,4},{3,5},{4,2},{5,3},{6,6},{7,7},{8,8},{9,9},{10,12... | collective-permute-start | bytes 1769480 | tf_op jit(solution)/shard_map/ppermute | solution.py:36
  149.2 8.2 %collective-permute-done.24.b_ref = bf16[128,2304]{1,0:T(8,128)(2,1)S(1)} collective-permute-done((bf16[128,2304]{1,0:T(8,128)(2,1)S(1)}, bf16[128,2304]{1,0:T(8,128)(2,1)S(1)}, u32[]{:S(2)}, u32[]{:S(2)}) %collective-permute-start.24) | collective-permute-done | bytes 589856 | tf_op jit(solution)/shard_map/ppermute | solution.py:36
  158.1 2.8 %collective-permute-start.25 = (bf16[128,2304]{1,0:T(8,128)(2,1)S(1)}, bf16[128,2304]{1,0:T(8,128)(2,1)S(1)}, u32[]{:S(2)}, u32[]{:S(2)}) collective-permute-start(bf16[128,2304]{1,0:T(8,128)(2,1)S(1)} %shard_map.172), channel_id=1, source_target_pairs={{0,0},{1,1},{2,4},{3,5},{4,2},{5,3},{6,6},{7,7},{8,8},{9,9},{10,12... | collective-permute-start | bytes 1769480 | tf_op jit(solution)/shard_map/ppermute | solution.py:36
  162.8 7.3 %collective-permute-done.18.near_ref = bf16[128,2304]{1,0:T(8,128)(2,1)S(1)} collective-permute-done((bf16[128,2304]{1,0:T(8,128)(2,1)S(1)}, bf16[128,2304]{1,0:T(8,128)(2,1)S(1)}, u32[]{:S(2)}, u32[]{:S(2)}) %collective-permute-start.18) | collective-permute-done | bytes 589856 | tf_op jit(solution)/shard_map/ppermute | solution.py:36
  172.5 2.1 collective-permute-done.25.mid_ref
  174.6 8.1 %collective-permute-done.23.near_ref = bf16[128,2304]{1,0:T(8,128)(2,1)S(1)} collective-permute-done((bf16[128,2304]{1,0:T(8,128)(2,1)S(1)}, bf16[128,2304]{1,0:T(8,128)(2,1)S(1)}, u32[]{:S(2)}, u32[]{:S(2)}) %collective-permute-start.23) | collective-permute-done | bytes 589856 | tf_op jit(solution)/shard_map/ppermute | solution.py:36
  186.0 7.1 %collective-permute-done.27.twin_ref = f32[2,2304]{1,0:T(2,128)S(1)} collective-permute-done((f32[2,2304]{1,0:T(2,128)S(1)}, f32[2,2304]{1,0:T(2,128)S(1)}, u32[]{:S(2)}, u32[]{:S(2)}) %collective-permute-start.27) | collective-permute-done | bytes 18464 | tf_op jit(solution)/shard_map/ppermute | solution.py:36
  194.2 1.8 shard_map.176.own_ref
  197.5 2.0 collective-permute-start.30
  199.4 2.1 collective-permute-done.28.near_ref
  201.5 1.9 collective-permute-start.29
  204.1 3.4 %collective-permute-start.37 = (bf16[64,2304]{1,0:T(8,128)(2,1)}, bf16[64,2304]{1,0:T(8,128)(2,1)}, u32[]{:S(2)}, u32[]{:S(2)}) collective-permute-start(bf16[64,2304]{1,0:T(8,128)(2,1)} %shard_map.176.own_ref), channel_id=1, source_target_pairs={{0,0},{1,1},{2,4},{3,5},{4,2},{5,3},{6,6},{7,7},{8,8},{9,9},{10,12... | collective-permute-start | bytes 884744 | tf_op jit(solution)/shard_map/ppermute | solution.py:36
  207.9 1.9 collective-permute-start.36
  209.8 4.7 %collective-permute-start.31 = (bf16[64,2304]{1,0:T(8,128)(2,1)}, bf16[64,2304]{1,0:T(8,128)(2,1)}, u32[]{:S(2)}, u32[]{:S(2)}) collective-permute-start(bf16[64,2304]{1,0:T(8,128)(2,1)} %collective-permute-done.30.last_a), channel_id=1, source_target_pairs={{2,0},{3,1},{4,6},{5,7},{10,8},{11,9},{12,14},{13,15},{18,16},{19,... | collective-permute-start | bytes 884744 | tf_op jit(solution)/shard_map/ppermute | solution.py:36
  214.6 2.0 collective-permute-start.32
  217.3 1.7 copy.45
  219.0 1.6 reshape.53
  225.4 1.6 collective-permute-start.39
  231.1 4.0 %shard_map.175 = f32[40,256]{1,0:T(8,128)S(1)} custom-call(s32[4]{0:T(128)S(1)} %pad_add_fusion.where_ref, bf16[64,2304]{1,0:T(8,128)(2,1)S(1)} %copy-done.16, bf16[64,2304]{1,0:T(8,128)(2,1)S(1)} %copy-done.24, bf16[64,2304]{1,0:T(8,128)(2,1)} %collective-permute-done.29.far_a, bf16[64,2304]{1,0:T(8,128)(2,1)} %collective-permute-done.31.far_b, ...), custom_call_target="tpu_custom_call" | custom-call | tf_op jit(solution)/shard_map/pallas_call | solution.py:167
  235.2 2.6 collective-permute-done.39.last_b
  237.8 3.9 %shard_map.177 = f32[40,256]{1,0:T(8,128)S(1)} custom-call(s32[4]{0:T(128)S(1)} %pad_add_fusion.where_ref, bf16[64,2304]{1,0:T(8,128)(2,1)} %shard_map.176.own_ref, bf16[64,2304]{1,0:T(8,128)(2,1)} %collective-permute-done.35.near_ref, bf16[64,2304]{1,0:T(8,128)(2,1)} %collective-permute-done.36.far_a, bf16[64,2304]{1,0:T(8,128)(2,1)S(1)} %collective-permute-done.38.far_b, ...), custom_call_target="tpu_custom_call" | custom-call | tf_op jit(solution)/shard_map/pallas_call | solution.py:167
  241.8 2.1 collective-permute-start.40
  245.4 2.3 collective-permute-done.41.refs_2_
  247.7 6.0 %collective-permute-start.45 = (f32[32,128]{1,0:T(8,128)S(1)}, f32[32,128]{1,0:T(8,128)S(1)}, u32[]{:S(2)}, u32[]{:S(2)}) collective-permute-start(f32[32,128]{1,0:T(8,128)S(1)} %shard_map.178), channel_id=1, source_target_pairs={{0,1},{1,3},{2,5},{3,7},{4,17},{5,19},{6,21},{7,23},{8,9},{9,11},{... | collective-permute-start | bytes 49160 | tf_op jit(solution)/shard_map/ppermute | solution.py:36
  253.6 1.9 collective-permute-start.44
  258.4 5.7 %collective-permute-done.43 = f32[32,128]{1,0:T(8,128)S(1)} collective-permute-done((f32[32,128]{1,0:T(8,128)S(1)}, f32[32,128]{1,0:T(8,128)S(1)}, u32[]{:S(2)}, u32[]{:S(2)}) %collective-permute-start.43) | collective-permute-done | bytes 16416 | tf_op jit(solution)/shard_map/ppermute | solution.py:36
  (195 shorter events, 52.0 us)
Async XLA Ops:
  0.7 28.3 %collective-permute-start.1 = (bf16[2304,1152]{1,0:T(8,128)(2,1)}, bf16[2304,1152]{1,0:T(8,128)(2,1)}, u32[]{:S(2)}, u32[]{:S(2)}) collective-permute-start(bf16[2304,1152]{1,0:T(8,128)(2,1)} %refs_2_.11), channel_id=1, source_target_pairs={{0,1},{1,0},{2,3},{3,2},{4,5},{5,4},{6,7},{7,6},{8,9},{9,8},{10,11... | collective-permute-start | bytes 15925256 | tf_op jit(solution)/shard_map/ppermute | solution.py:36
  1.4 27.6 %collective-permute-start.2 = (bf16[1152,2304]{1,0:T(8,128)(2,1)}, bf16[1152,2304]{1,0:T(8,128)(2,1)}, u32[]{:S(2)}, u32[]{:S(2)}) collective-permute-start(bf16[1152,2304]{1,0:T(8,128)(2,1)} %refs_4_.11), channel_id=1, source_target_pairs={{0,1},{1,0},{2,3},{3,2},{4,5},{5,4},{6,7},{7,6},{8,9},{9,8},{10,11... | collective-permute-start | bytes 15925256 | tf_op jit(solution)/shard_map/ppermute | solution.py:36
  3.3 14.4 %collective-permute-start = (bf16[128,2304]{1,0:T(8,128)(2,1)S(1)}, bf16[128,2304]{1,0:T(8,128)(2,1)S(1)}, u32[]{:S(2)}, u32[]{:S(2)}) collective-permute-start(bf16[128,2304]{1,0:T(8,128)(2,1)S(1)} %shard_map.158.refs_0_), channel_id=1, source_target_pairs={{0,2},{1,3},{2,0},{3,1},{4,6},{5,7},{6,4},{7,5},{8,10},{9,11},{10,... | collective-permute-start | bytes 1769480 | tf_op jit(solution)/shard_map/ppermute | solution.py:36
  3.5 22.1 %collective-permute-start.5 = (bf16[128,2304]{1,0:T(8,128)(2,1)S(1)}, bf16[128,2304]{1,0:T(8,128)(2,1)S(1)}, u32[]{:S(2)}, u32[]{:S(2)}) collective-permute-start(bf16[128,2304]{1,0:T(8,128)(2,1)S(1)} %shard_map.158.refs_0_), channel_id=1, source_target_pairs={{0,0},{1,1},{2,4},{3,5},{4,2},{5,3},{6,6},{7,7},{8,8},{9,9},{10,12... | collective-permute-start | bytes 1769480 | tf_op jit(solution)/shard_map/ppermute | solution.py:36
  17.6 26.7 %collective-permute-start.4 = (bf16[128,2304]{1,0:T(8,128)(2,1)S(1)}, bf16[128,2304]{1,0:T(8,128)(2,1)}, u32[]{:S(2)}, u32[]{:S(2)}) collective-permute-start(bf16[128,2304]{1,0:T(8,128)(2,1)S(1)} %collective-permute-done.refs_1_), channel_id=1, source_target_pairs={{0,0},{1,1},{2,4},{3,5},{4,2},{5,3},{6,6},{7,7},{8,8},{9,9},{10,12... | collective-permute-start | bytes 1769480 | tf_op jit(solution)/shard_map/ppermute | solution.py:36
  21.8 3.0 %collective-permute-start.3 = (f32[18048]{0:T(1024)}, f32[18048]{0:T(1024)}, u32[]{:S(2)}, u32[]{:S(2)}) collective-permute-start(f32[18048]{0:T(1024)} %pad_maximum_fusion.2), channel_id=1, source_target_pairs={{0,1},{1,0},{2,3},{3,2},{4,5},{5,4},{6,7},{7,6},{8,9},{9,8},{10,11... | collective-permute-start | bytes 216584 | tf_op jit(solution)/shard_map/ppermute | solution.py:36
  25.5 36.4 %collective-permute-start.7 = (bf16[128,2304]{1,0:T(8,128)(2,1)S(1)}, bf16[128,2304]{1,0:T(8,128)(2,1)S(1)}, u32[]{:S(2)}, u32[]{:S(2)}) collective-permute-start(bf16[128,2304]{1,0:T(8,128)(2,1)S(1)} %shard_map.161.refs_0_), channel_id=1, source_target_pairs={{0,2},{1,3},{2,0},{3,1},{4,6},{5,7},{6,4},{7,5},{8,10},{9,11},{10,... | collective-permute-start | bytes 1769480 | tf_op jit(solution)/shard_map/ppermute | solution.py:36
  25.6 25.3 %collective-permute-start.6 = (bf16[128,2304]{1,0:T(8,128)(2,1)S(1)}, bf16[128,2304]{1,0:T(8,128)(2,1)S(1)}, u32[]{:S(2)}, u32[]{:S(2)}) collective-permute-start(bf16[128,2304]{1,0:T(8,128)(2,1)S(1)} %collective-permute-done.5.refs_0_), channel_id=1, source_target_pairs={{2,0},{3,1},{4,6},{5,7},{10,8},{11,9},{12,14},{13,15},{18,16},{19,... | collective-permute-start | bytes 1769480 | tf_op jit(solution)/shard_map/ppermute | solution.py:36
  44.3 22.0 %collective-permute-start.9 = (bf16[128,2304]{1,0:T(8,128)(2,1)}, bf16[128,2304]{1,0:T(8,128)(2,1)S(1)}, u32[]{:S(2)}, u32[]{:S(2)}) collective-permute-start(bf16[128,2304]{1,0:T(8,128)(2,1)} %collective-permute-done.4.refs_0_), channel_id=1, source_target_pairs={{2,0},{3,1},{4,6},{5,7},{10,8},{11,9},{12,14},{13,15},{18,16},{19,... | collective-permute-start | bytes 1769480 | tf_op jit(solution)/shard_map/ppermute | solution.py:36
  46.7 18.6 %collective-permute-start.11 = (f32[2,2,64,512]{3,2,1,0:T(8,128)S(1)}, f32[2,2,64,512]{3,2,1,0:T(8,128)S(1)}, u32[]{:S(2)}, u32[]{:S(2)}) collective-permute-start(f32[2,2,64,512]{3,2,1,0:T(8,128)S(1)} %get-tuple-element.35), channel_id=1, source_target_pairs={{0,1},{1,0},{2,3},{3,2},{4,5},{5,4},{6,7},{7,6},{8,9},{9,8},{10,11... | collective-permute-start | bytes 1572872 | tf_op jit(solution)/shard_map/ppermute | solution.py:36
  58.4 33.6 %collective-permute-start.10 = (bf16[128,2304]{1,0:T(8,128)(2,1)S(1)}, bf16[128,2304]{1,0:T(8,128)(2,1)S(1)}, u32[]{:S(2)}, u32[]{:S(2)}) collective-permute-start(bf16[128,2304]{1,0:T(8,128)(2,1)S(1)} %shard_map.160.a_ref), channel_id=1, source_target_pairs={{0,2},{1,3},{6,4},{7,5},{8,10},{9,11},{14,12},{15,13},{16,18},{17,... | collective-permute-start | bytes 1769480 | tf_op jit(solution)/shard_map/ppermute | solution.py:36
  59.7 32.3 %collective-permute-start.14 = (bf16[128,2304]{1,0:T(8,128)(2,1)S(1)}, bf16[128,2304]{1,0:T(8,128)(2,1)S(1)}, u32[]{:S(2)}, u32[]{:S(2)}) collective-permute-start(bf16[128,2304]{1,0:T(8,128)(2,1)S(1)} %shard_map.161.refs_0_), channel_id=1, source_target_pairs={{0,0},{1,1},{2,4},{3,5},{4,2},{5,3},{6,6},{7,7},{8,8},{9,9},{10,12... | collective-permute-start | bytes 1769480 | tf_op jit(solution)/shard_map/ppermute | solution.py:36
  61.9 41.7 %collective-permute-start.8 = (bf16[128,2304]{1,0:T(8,128)(2,1)S(1)}, bf16[128,2304]{1,0:T(8,128)(2,1)S(1)}, u32[]{:S(2)}, u32[]{:S(2)}) collective-permute-start(bf16[128,2304]{1,0:T(8,128)(2,1)S(1)} %collective-permute-done.7.refs_1_), channel_id=1, source_target_pairs={{0,0},{1,1},{2,4},{3,5},{4,2},{5,3},{6,6},{7,7},{8,8},{9,9},{10,12... | collective-permute-start | bytes 1769480 | tf_op jit(solution)/shard_map/ppermute | solution.py:36
  66.1 11.6 %collective-permute-start.12 = (f32[2,2,64,512]{3,2,1,0:T(8,128)S(1)}, f32[2,2,64,512]{3,2,1,0:T(8,128)S(1)}, u32[]{:S(2)}, u32[]{:S(2)}) collective-permute-start(f32[2,2,64,512]{3,2,1,0:T(8,128)S(1)} %get-tuple-element.36), channel_id=1, source_target_pairs={{0,16},{1,17},{2,18},{3,19},{4,20},{5,21},{6,22},{7,23},{8,24},{9,... | collective-permute-start | bytes 1572872 | tf_op jit(solution)/shard_map/ppermute | solution.py:36
  66.3 25.0 %collective-permute-start.13 = (f32[2,2,64,512]{3,2,1,0:T(8,128)S(1)}, f32[2,2,64,512]{3,2,1,0:T(8,128)S(1)}, u32[]{:S(2)}, u32[]{:S(2)}) collective-permute-start(f32[2,2,64,512]{3,2,1,0:T(8,128)S(1)} %get-tuple-element.37), channel_id=1, source_target_pairs={{0,17},{1,16},{2,19},{3,18},{4,21},{5,20},{6,23},{7,22},{8,25},{9,... | collective-permute-start | bytes 1572872 | tf_op jit(solution)/shard_map/ppermute | solution.py:36
  78.5 36.9 %collective-permute-start.16 = (bf16[128,2304]{1,0:T(8,128)(2,1)S(1)}, bf16[128,2304]{1,0:T(8,128)(2,1)S(1)}, u32[]{:S(2)}, u32[]{:S(2)}) collective-permute-start(bf16[128,2304]{1,0:T(8,128)(2,1)S(1)} %shard_map.162.a_ref), channel_id=1, source_target_pairs={{0,2},{1,3},{6,4},{7,5},{8,10},{9,11},{14,12},{15,13},{16,18},{17,... | collective-permute-start | bytes 1769480 | tf_op jit(solution)/shard_map/ppermute | solution.py:36
  92.1 16.0 %collective-permute-start.15 = (bf16[128,2304]{1,0:T(8,128)(2,1)S(1)}, bf16[128,2304]{1,0:T(8,128)(2,1)S(1)}, u32[]{:S(2)}, u32[]{:S(2)}) collective-permute-start(bf16[128,2304]{1,0:T(8,128)(2,1)S(1)} %collective-permute-done.14.refs_0_), channel_id=1, source_target_pairs={{2,0},{3,1},{4,6},{5,7},{10,8},{11,9},{12,14},{13,15},{18,16},{19,... | collective-permute-start | bytes 1769480 | tf_op jit(solution)/shard_map/ppermute | solution.py:36
  104.4 15.8 %collective-permute-start.19 = (bf16[128,2304]{1,0:T(8,128)(2,1)S(1)}, bf16[128,2304]{1,0:T(8,128)(2,1)S(1)}, u32[]{:S(2)}, u32[]{:S(2)}) collective-permute-start(bf16[128,2304]{1,0:T(8,128)(2,1)S(1)} %shard_map.164), channel_id=1, source_target_pairs={{0,0},{1,1},{2,4},{3,5},{4,2},{5,3},{6,6},{7,7},{8,8},{9,9},{10,12... | collective-permute-start | bytes 1769480 | tf_op jit(solution)/shard_map/ppermute | solution.py:36
  106.5 13.7 %collective-permute-start.20 = (bf16[128,2304]{1,0:T(8,128)(2,1)S(1)}, bf16[128,2304]{1,0:T(8,128)(2,1)S(1)}, u32[]{:S(2)}, u32[]{:S(2)}) collective-permute-start(bf16[128,2304]{1,0:T(8,128)(2,1)S(1)} %collective-permute-done.8.refs_0_), channel_id=1, source_target_pairs={{2,0},{3,1},{4,6},{5,7},{10,8},{11,9},{12,14},{13,15},{18,16},{19,... | collective-permute-start | bytes 1769480 | tf_op jit(solution)/shard_map/ppermute | solution.py:36
  127.5 17.2 %collective-permute-start.21 = (bf16[128,2304]{1,0:T(8,128)(2,1)S(1)}, bf16[128,2304]{1,0:T(8,128)(2,1)S(1)}, u32[]{:S(2)}, u32[]{:S(2)}) collective-permute-start(bf16[128,2304]{1,0:T(8,128)(2,1)S(1)} %shard_map.169.a_ref), channel_id=1, source_target_pairs={{0,2},{1,3},{6,4},{7,5},{8,10},{9,11},{14,12},{15,13},{16,18},{17,... | collective-permute-start | bytes 1769480 | tf_op jit(solution)/shard_map/ppermute | solution.py:36
  128.8 19.6 %collective-permute-start.17 = (bf16[128,2304]{1,0:T(8,128)(2,1)S(1)}, bf16[128,2304]{1,0:T(8,128)(2,1)S(1)}, u32[]{:S(2)}, u32[]{:S(2)}) collective-permute-start(bf16[128,2304]{1,0:T(8,128)(2,1)S(1)} %shard_map.166), channel_id=1, source_target_pairs={{0,0},{1,1},{2,4},{3,5},{4,2},{5,3},{6,6},{7,7},{8,8},{9,9},{10,12... | collective-permute-start | bytes 1769480 | tf_op jit(solution)/shard_map/ppermute | solution.py:36
  131.6 25.8 %collective-permute-start.24 = (bf16[128,2304]{1,0:T(8,128)(2,1)S(1)}, bf16[128,2304]{1,0:T(8,128)(2,1)S(1)}, u32[]{:S(2)}, u32[]{:S(2)}) collective-permute-start(bf16[128,2304]{1,0:T(8,128)(2,1)S(1)} %shard_map.165.a_ref), channel_id=1, source_target_pairs={{0,2},{1,3},{6,4},{7,5},{8,10},{9,11},{14,12},{15,13},{16,18},{17,... | collective-permute-start | bytes 1769480 | tf_op jit(solution)/shard_map/ppermute | solution.py:36
  145.5 16.4 %collective-permute-start.22 = (bf16[128,2304]{1,0:T(8,128)(2,1)S(1)}, bf16[128,2304]{1,0:T(8,128)(2,1)S(1)}, u32[]{:S(2)}, u32[]{:S(2)}) collective-permute-start(bf16[128,2304]{1,0:T(8,128)(2,1)S(1)} %shard_map.170), channel_id=1, source_target_pairs={{0,0},{1,1},{2,4},{3,5},{4,2},{5,3},{6,6},{7,7},{8,8},{9,9},{10,12... | collective-permute-start | bytes 1769480 | tf_op jit(solution)/shard_map/ppermute | solution.py:36
  148.3 78.8 %collective-permute-start.33 = (bf16[2304,512]{1,0:T(8,128)(2,1)S(1)}, bf16[2304,512]{1,0:T(8,128)(2,1)}, u32[]{:S(2)}, u32[]{:S(2)}) collective-permute-start(bf16[2304,512]{1,0:T(8,128)(2,1)S(1)} %copy-done.5), channel_id=1, source_target_pairs={{0,1},{1,0},{2,3},{3,2},{4,5},{5,4},{6,7},{7,6},{8,9},{9,8},{10,11... | collective-permute-start | bytes 7077896 | tf_op jit(solution)/shard_map/ppermute | solution.py:36
  149.1 20.9 %collective-permute-start.18 = (bf16[128,2304]{1,0:T(8,128)(2,1)S(1)}, bf16[128,2304]{1,0:T(8,128)(2,1)S(1)}, u32[]{:S(2)}, u32[]{:S(2)}) collective-permute-start(bf16[128,2304]{1,0:T(8,128)(2,1)S(1)} %shard_map.167), channel_id=1, source_target_pairs={{0,2},{1,3},{2,0},{3,1},{4,6},{5,7},{6,4},{7,5},{8,10},{9,11},{10,... | collective-permute-start | bytes 1769480 | tf_op jit(solution)/shard_map/ppermute | solution.py:36
  158.1 16.4 %collective-permute-start.25 = (bf16[128,2304]{1,0:T(8,128)(2,1)S(1)}, bf16[128,2304]{1,0:T(8,128)(2,1)S(1)}, u32[]{:S(2)}, u32[]{:S(2)}) collective-permute-start(bf16[128,2304]{1,0:T(8,128)(2,1)S(1)} %shard_map.172), channel_id=1, source_target_pairs={{0,0},{1,1},{2,4},{3,5},{4,2},{5,3},{6,6},{7,7},{8,8},{9,9},{10,12... | collective-permute-start | bytes 1769480 | tf_op jit(solution)/shard_map/ppermute | solution.py:36
  162.6 20.1 %collective-permute-start.23 = (bf16[128,2304]{1,0:T(8,128)(2,1)S(1)}, bf16[128,2304]{1,0:T(8,128)(2,1)S(1)}, u32[]{:S(2)}, u32[]{:S(2)}) collective-permute-start(bf16[128,2304]{1,0:T(8,128)(2,1)S(1)} %shard_map.171), channel_id=1, source_target_pairs={{0,2},{1,3},{2,0},{3,1},{4,6},{5,7},{6,4},{7,5},{8,10},{9,11},{10,... | collective-permute-start | bytes 1769480 | tf_op jit(solution)/shard_map/ppermute | solution.py:36
  171.9 44.7 %copy-start.29 = (bf16[512,32]{1,0:T(8,128)(2,1)S(1)}, bf16[512,32]{1,0:T(8,128)(2,1)}, u32[]{:S(2)}) copy-start(bf16[512,32]{1,0:T(8,128)(2,1)} %copy-done.28) | copy-start | bytes 98308
  171.9 21.2 %collective-permute-start.26 = (bf16[64,2304]{1,0:T(8,128)(2,1)S(1)}, bf16[64,2304]{1,0:T(8,128)(2,1)S(1)}, u32[]{:S(2)}, u32[]{:S(2)}) collective-permute-start(bf16[64,2304]{1,0:T(8,128)(2,1)S(1)} %get-tuple-element.52), channel_id=1, source_target_pairs={{0,16},{1,17},{2,18},{3,19},{4,20},{5,21},{6,22},{7,23},{8,24},{9,... | collective-permute-start | bytes 884744 | tf_op jit(solution)/shard_map/ppermute | solution.py:36
  184.5 42.6 %copy-start.8 = (f32[2,2,64,512]{3,2,1,0:T(8,128)S(1)}, f32[2,2,64,512]{3,2,1,0:T(8,128)}, u32[]{:S(2)}) copy-start(f32[2,2,64,512]{3,2,1,0:T(8,128)} %copy-done.7) | copy-start | bytes 1572868
  184.5 9.7 %collective-permute-start.34 = (bf16[64,2304]{1,0:T(8,128)(2,1)S(1)}, bf16[64,2304]{1,0:T(8,128)(2,1)S(1)}, u32[]{:S(2)}, u32[]{:S(2)}) collective-permute-start(bf16[64,2304]{1,0:T(8,128)(2,1)S(1)} %get-tuple-element.55), channel_id=1, source_target_pairs={{0,16},{1,17},{2,18},{3,19},{4,20},{5,21},{6,22},{7,23},{8,24},{9,... | collective-permute-start | bytes 884744 | tf_op jit(solution)/shard_map/ppermute | solution.py:36
  185.1 8.0 %collective-permute-start.27 = (f32[2,2304]{1,0:T(2,128)S(1)}, f32[2,2304]{1,0:T(2,128)S(1)}, u32[]{:S(2)}, u32[]{:S(2)}) collective-permute-start(f32[2,2304]{1,0:T(2,128)S(1)} %dynamic-slice_bitcast_fusion.4.ada_ref), channel_id=1, source_target_pairs={{0,16},{1,17},{2,18},{3,19},{4,20},{5,21},{6,22},{7,23},{8,24},{9,... | collective-permute-start | bytes 55304 | tf_op jit(solution)/shard_map/ppermute | solution.py:36
  194.2 7.3 %collective-permute-start.28 = (bf16[64,2304]{1,0:T(8,128)(2,1)S(1)}, bf16[64,2304]{1,0:T(8,128)(2,1)S(1)}, u32[]{:S(2)}, u32[]{:S(2)}) collective-permute-start(bf16[64,2304]{1,0:T(8,128)(2,1)S(1)} %shard_map.174.own_ref), channel_id=1, source_target_pairs={{0,2},{1,3},{2,0},{3,1},{4,6},{5,7},{6,4},{7,5},{8,10},{9,11},{10,... | collective-permute-start | bytes 884744 | tf_op jit(solution)/shard_map/ppermute | solution.py:36
  196.0 11.9 %collective-permute-start.35 = (bf16[64,2304]{1,0:T(8,128)(2,1)}, bf16[64,2304]{1,0:T(8,128)(2,1)}, u32[]{:S(2)}, u32[]{:S(2)}) collective-permute-start(bf16[64,2304]{1,0:T(8,128)(2,1)} %shard_map.176.own_ref), channel_id=1, source_target_pairs={{0,2},{1,3},{2,0},{3,1},{4,6},{5,7},{6,4},{7,5},{8,10},{9,11},{10,... | collective-permute-start | bytes 884744 | tf_op jit(solution)/shard_map/ppermute | solution.py:36
  197.5 12.4 %collective-permute-start.30 = (bf16[64,2304]{1,0:T(8,128)(2,1)S(1)}, bf16[64,2304]{1,0:T(8,128)(2,1)}, u32[]{:S(2)}, u32[]{:S(2)}) collective-permute-start(bf16[64,2304]{1,0:T(8,128)(2,1)S(1)} %shard_map.174.own_ref), channel_id=1, source_target_pairs={{0,0},{1,1},{2,4},{3,5},{4,2},{5,3},{6,6},{7,7},{8,8},{9,9},{10,12... | collective-permute-start | bytes 884744 | tf_op jit(solution)/shard_map/ppermute | solution.py:36
  201.5 13.1 %collective-permute-start.29 = (bf16[64,2304]{1,0:T(8,128)(2,1)S(1)}, bf16[64,2304]{1,0:T(8,128)(2,1)}, u32[]{:S(2)}, u32[]{:S(2)}) collective-permute-start(bf16[64,2304]{1,0:T(8,128)(2,1)S(1)} %collective-permute-done.28.near_ref), channel_id=1, source_target_pairs={{0,0},{1,1},{2,4},{3,5},{4,2},{5,3},{6,6},{7,7},{8,8},{9,9},{10,12... | collective-permute-start | bytes 884744 | tf_op jit(solution)/shard_map/ppermute | solution.py:36
  204.1 20.0 %collective-permute-start.37 = (bf16[64,2304]{1,0:T(8,128)(2,1)}, bf16[64,2304]{1,0:T(8,128)(2,1)}, u32[]{:S(2)}, u32[]{:S(2)}) collective-permute-start(bf16[64,2304]{1,0:T(8,128)(2,1)} %shard_map.176.own_ref), channel_id=1, source_target_pairs={{0,0},{1,1},{2,4},{3,5},{4,2},{5,3},{6,6},{7,7},{8,8},{9,9},{10,12... | collective-permute-start | bytes 884744 | tf_op jit(solution)/shard_map/ppermute | solution.py:36
  207.9 17.5 %collective-permute-start.36 = (bf16[64,2304]{1,0:T(8,128)(2,1)}, bf16[64,2304]{1,0:T(8,128)(2,1)}, u32[]{:S(2)}, u32[]{:S(2)}) collective-permute-start(bf16[64,2304]{1,0:T(8,128)(2,1)} %collective-permute-done.35.near_ref), channel_id=1, source_target_pairs={{0,0},{1,1},{2,4},{3,5},{4,2},{5,3},{6,6},{7,7},{8,8},{9,9},{10,12... | collective-permute-start | bytes 884744 | tf_op jit(solution)/shard_map/ppermute | solution.py:36
  209.8 17.2 %collective-permute-start.31 = (bf16[64,2304]{1,0:T(8,128)(2,1)}, bf16[64,2304]{1,0:T(8,128)(2,1)}, u32[]{:S(2)}, u32[]{:S(2)}) collective-permute-start(bf16[64,2304]{1,0:T(8,128)(2,1)} %collective-permute-done.30.last_a), channel_id=1, source_target_pairs={{2,0},{3,1},{4,6},{5,7},{10,8},{11,9},{12,14},{13,15},{18,16},{19,... | collective-permute-start | bytes 884744 | tf_op jit(solution)/shard_map/ppermute | solution.py:36
  214.6 12.5 %collective-permute-start.32 = (bf16[64,2304]{1,0:T(8,128)(2,1)}, bf16[64,2304]{1,0:T(8,128)(2,1)}, u32[]{:S(2)}, u32[]{:S(2)}) collective-permute-start(bf16[64,2304]{1,0:T(8,128)(2,1)} %collective-permute-done.29.far_a), channel_id=1, source_target_pairs={{2,0},{3,1},{4,6},{5,7},{10,8},{11,9},{12,14},{13,15},{18,16},{19,... | collective-permute-start | bytes 884744 | tf_op jit(solution)/shard_map/ppermute | solution.py:36
  224.1 11.0 %collective-permute-start.38 = (bf16[64,2304]{1,0:T(8,128)(2,1)}, bf16[64,2304]{1,0:T(8,128)(2,1)S(1)}, u32[]{:S(2)}, u32[]{:S(2)}) collective-permute-start(bf16[64,2304]{1,0:T(8,128)(2,1)} %collective-permute-done.37.last_a), channel_id=1, source_target_pairs={{2,0},{3,1},{4,6},{5,7},{10,8},{11,9},{12,14},{13,15},{18,16},{19,... | collective-permute-start | bytes 884744 | tf_op jit(solution)/shard_map/ppermute | solution.py:36
  225.4 12.3 %collective-permute-start.39 = (bf16[64,2304]{1,0:T(8,128)(2,1)}, bf16[64,2304]{1,0:T(8,128)(2,1)S(1)}, u32[]{:S(2)}, u32[]{:S(2)}) collective-permute-start(bf16[64,2304]{1,0:T(8,128)(2,1)} %collective-permute-done.36.far_a), channel_id=1, source_target_pairs={{2,0},{3,1},{4,6},{5,7},{10,8},{11,9},{12,14},{13,15},{18,16},{19,... | collective-permute-start | bytes 884744 | tf_op jit(solution)/shard_map/ppermute | solution.py:36
  241.8 3.6 %collective-permute-start.40 = (f32[40,128]{1,0:T(8,128)S(1)}, f32[40,128]{1,0:T(8,128)S(1)}, u32[]{:S(2)}, u32[]{:S(2)}) collective-permute-start(f32[40,128]{1,0:T(8,128)S(1)} %pad_maximum_fusion.4), channel_id=1, source_target_pairs={{0,2},{1,3},{2,0},{3,1},{4,6},{5,7},{6,4},{7,5},{8,10},{9,11},{10,... | collective-permute-start | bytes 61448 | tf_op jit(solution)/shard_map/ppermute | solution.py:36
  244.0 3.6 %collective-permute-start.41 = (f32[40,128]{1,0:T(8,128)S(1)}, f32[40,128]{1,0:T(8,128)S(1)}, u32[]{:S(2)}, u32[]{:S(2)}) collective-permute-start(f32[40,128]{1,0:T(8,128)S(1)} %pad_maximum_fusion.5), channel_id=1, source_target_pairs={{0,4},{1,5},{2,6},{3,7},{4,0},{5,1},{6,2},{7,3},{8,12},{9,13},{10,... | collective-permute-start | bytes 61448 | tf_op jit(solution)/shard_map/ppermute | solution.py:36
  244.1 3.5 %collective-permute-start.42 = (f32[40,128]{1,0:T(8,128)S(1)}, f32[40,128]{1,0:T(8,128)S(1)}, u32[]{:S(2)}, u32[]{:S(2)}) collective-permute-start(f32[40,128]{1,0:T(8,128)S(1)} %pad_maximum_fusion.6), channel_id=1, source_target_pairs={{0,6},{1,7},{2,4},{3,5},{4,2},{5,3},{6,0},{7,1},{8,14},{9,15},{10,... | collective-permute-start | bytes 61448 | tf_op jit(solution)/shard_map/ppermute | solution.py:36
  247.7 10.4 %collective-permute-start.45 = (f32[32,128]{1,0:T(8,128)S(1)}, f32[32,128]{1,0:T(8,128)S(1)}, u32[]{:S(2)}, u32[]{:S(2)}) collective-permute-start(f32[32,128]{1,0:T(8,128)S(1)} %shard_map.178), channel_id=1, source_target_pairs={{0,1},{1,3},{2,5},{3,7},{4,17},{5,19},{6,21},{7,23},{8,9},{9,11},{... | collective-permute-start | bytes 49160 | tf_op jit(solution)/shard_map/ppermute | solution.py:36
  253.6 4.5 %collective-permute-start.44 = (f32[32,128]{1,0:T(8,128)S(1)}, f32[32,128]{1,0:T(8,128)S(1)}, u32[]{:S(2)}, u32[]{:S(2)}) collective-permute-start(f32[32,128]{1,0:T(8,128)S(1)} %shard_map.178), channel_id=1, source_target_pairs={{0,0},{1,2},{2,4},{3,6},{4,16},{5,18},{6,20},{7,22},{8,8},{9,10},{... | collective-permute-start | bytes 49160 | tf_op jit(solution)/shard_map/ppermute | solution.py:36
  256.7 7.4 %collective-permute-start.43 = (f32[32,128]{1,0:T(8,128)S(1)}, f32[32,128]{1,0:T(8,128)S(1)}, u32[]{:S(2)}, u32[]{:S(2)}) collective-permute-start(f32[32,128]{1,0:T(8,128)S(1)} %shard_map.178), channel_id=1, source_target_pairs={{1,1},{2,3},{3,5},{5,17},{6,19},{7,21},{9,9},{10,11},{11,13},{13,2... | collective-permute-start | bytes 49160 | tf_op jit(solution)/shard_map/ppermute | solution.py:36
  (39 other events, 447.0 us)
where the time goes:
time: 269 us; the launch traced here: 267 us
  waiting for transfers between devices  88.2 us (33%)
  starting transfers between devices  78.6 us (29%)
  Pallas kernels  67.9 us (25%)
  local copies, waits for them, and re-layouts  25.3 us (9%)
  other arithmetic  4.03 us (1%)
    ppermute x46, waiting for transfers between devices, permute_devices(): return lax.ppermute(value, ('dp', 'mp'), pairs)  88.2 us
    ppermute x46, starting transfers between devices, permute_devices(): return lax.ppermute(value, ('dp', 'mp'), pairs)  78.6 us
    pallas_call x21, Pallas kernels, call(): pl.pallas_call(kernel, out_shape=outs, in_specs=[SCALARS] * scalars + [ON...  67.9 us
    unnamed x92, local copies, waits for them, and re-layouts  17.1 us
  transfers between devices with their start and end apart: 46, of which 17 were waited for; matrix products, arithmetic and copies ran while one was open for 5% of the time, Pallas kernels for 21%

commit v1 on v0

--- a/solution.py
+++ b/solution.py
@@ -195,71 +195,57 @@
     return call(norm_kernel, (tokens, ada), [shape_of(tokens.shape)])[0]
 
 
-def ffn_kernel(groups, tile, where_ref, *refs):
-    count = sum(groups)
-    parts = refs[:count]
-    up_refs, down_refs = refs[count : count + 2], refs[count + 2 : count + 4]
-    bias_ref = refs[count + 4]
-    outs = refs[count + 5 : count + 5 + len(groups)]
-    x_ref, hidden_ref = refs[count + 5 + len(groups) :]
-    panel, width = down_refs[0].shape
+def ffn_kernel(slots, tile, where_ref, rows_ref, up_a, up_b, down_a, down_b, bias_ref, *refs):
+    outs, (x_ref, hidden_ref) = refs[: len(slots)], refs[len(slots) :]
+    panel, width = down_a.shape
     step = outs[0].shape[0]
-    place = 0
-    for g, size in enumerate(groups):
-        if size == 1:
-            value = parts[place][...]
-        else:
-            value = jnp.where(where_ref[0] == 1, parts[place][...], parts[place + 1][...])
-        x_ref[g * step : (g + 1) * step, :] = value
-        place += size
+    for g, slot in enumerate(slots):
+        place = where_ref[4 + slot] * step
+        x_ref[g * step : (g + 1) * step, :] = rows_ref[pl.ds(pl.multiple_of(place, step), step), :]
     for begin in range(0, 2 * panel, tile):
         end = begin + tile
         if end <= panel:
-            weight = up_refs[0][:, begin:end]
+            weight = up_a[:, begin:end]
         elif begin >= panel:
-            weight = up_refs[1][:, begin - panel : end - panel]
+            weight = up_b[:, begin - panel : end - panel]
         else:
-            weight = jnp.concatenate([up_refs[0][:, begin:], up_refs[1][:, : end - panel]], axis=1)
+            weight = jnp.concatenate([up_a[:, begin:], up_b[:, : end - panel]], axis=1)
         v = jnp.dot(x_ref[...], weight, preferred_element_type=jnp.float32) + bias_ref[:, begin:end]
         hidden_ref[:, begin:end] = jax.nn.gelu(v, approximate=True).astype(jnp.bfloat16)
     for begin in range(0, width, tile):
         cols = slice(begin, begin + tile)
-        weight = jnp.concatenate([down_refs[0][:, cols], down_refs[1][:, cols]], axis=0)
+        weight = jnp.concatenate([down_a[:, cols], down_b[:, cols]], axis=0)
         result = jnp.dot(hidden_ref[...], weight, preferred_element_type=jnp.float32)
-        for g in range(len(groups)):
+        for g in range(len(slots)):
             outs[g][:, cols] = result[g * step : (g + 1) * step].astype(jnp.bfloat16)
 
 
-def ffn(where, slots, ups, downs, bias):
-    groups = tuple(len(slot) for slot in slots)
-    parts = [part for slot in slots for part in slot]
-    rows, width = parts[0].shape
+def ffn(where, gathered, slots, ups, downs, bias):
+    rows, width = gathered.shape
     panel = ups[0].shape[1]
-    total = rows * len(slots)
+    step = rows // 4
     return call(
-        functools.partial(ffn_kernel, groups, 256),
-        (where, *parts, *ups, *downs, bias),
-        [shape_of((rows, width))] * len(slots),
+        functools.partial(ffn_kernel, slots, 256),
+        (where, gathered, *ups, *downs, bias),
+        [shape_of((step, width))] * len(slots),
         scalars=1,
         scratch=[
-            pltpu.VMEM((total, width), jnp.bfloat16),
-            pltpu.VMEM((total, 2 * panel), jnp.bfloat16),
+            pltpu.VMEM((step * len(slots), width), jnp.bfloat16),
+            pltpu.VMEM((step * len(slots), 2 * panel), jnp.bfloat16),
         ],
     )
 
 
-def add_kernel(where_ref, a_ref, b_ref, out_ref):
-    b = jnp.where(where_ref[0] == 1, b_ref[...].astype(jnp.float32), 0.0)
-    out_ref[...] = (a_ref[...].astype(jnp.float32) + b).astype(jnp.bfloat16)
-
-
-def add_mid(where, a, b):
-    return call(add_kernel, (where, a, b), [shape_of(a.shape)], scalars=1)[0]
-
-
-def out_kernel(where_ref, own_ref, near_ref, mid_ref, tokens_ref, gate_ref, bias_ref, out_ref, kept_ref, sent_ref):
-    from_mid = jnp.where(where_ref[0] == 1, mid_ref[...].astype(jnp.float32), 0.0)
-    summed = own_ref[...].astype(jnp.float32) + near_ref[...].astype(jnp.float32) + from_mid
+def add_kernel(a_ref, b_ref, out_ref):
+    out_ref[...] = (a_ref[...].astype(jnp.float32) + b_ref[...].astype(jnp.float32)).astype(jnp.bfloat16)
+
+
+def add(a, b):
+    return call(add_kernel, (a, b), [shape_of(a.shape)])[0]
+
+
+def out_kernel(where_ref, own_ref, near_ref, far_ref, tokens_ref, gate_ref, bias_ref, out_ref, kept_ref, sent_ref):
+    summed = own_ref[...].astype(jnp.float32) + near_ref[...].astype(jnp.float32) + far_ref[...].astype(jnp.float32)
     value = tokens_ref[...].astype(jnp.float32) + gate_ref[...] * (summed + bias_ref[...])
     value = value.astype(jnp.bfloat16)
     out_ref[...] = value
@@ -269,11 +255,11 @@
     sent_ref[...] = jnp.where(lower, value[half:], value[:half])
 
 
-def block_rows(where, own, near, mid, tokens, gate, bias):
+def block_rows(where, own, near, far, tokens, gate, bias):
     rows, width = own.shape
     return call(
         out_kernel,
-        (where, own, near, mid, tokens, gate, bias),
+        (where, own, near, far, tokens, gate, bias),
         [shape_of((rows, width)), shape_of((rows // 2, width)), shape_of((rows // 2, width))],
         scalars=1,
     )
@@ -292,16 +278,15 @@
 
 
 def head_kernel(
-    chunk, where_ref, own_ref, near_ref, far_a, far_b, last_a, last_b, weight_a, weight_b, bias_ref, code_ref,
+    chunk, where_ref, own_ref, near_ref, far_ref, last_ref, weight_a, weight_b, bias_ref, code_ref,
     noise_own, noise_core, noise_twin, noise_both, stats_ref, x_ref
 ):
     step = own_ref.shape[0]
     panel = weight_a.shape[1]
-    mid = where_ref[0] == 1
     x_ref[0:step, :] = own_ref[...]
     x_ref[step : 2 * step, :] = near_ref[...]
-    x_ref[2 * step : 3 * step, :] = jnp.where(mid, far_a[...], far_b[...])
-    x_ref[3 * step : 4 * step, :] = jnp.where(mid, last_a[...], last_b[...])
+    x_ref[2 * step : 3 * step, :] = far_ref[...]
+    x_ref[3 * step : 4 * step, :] = last_ref[...]
     x = x_ref[...]
     odd = where_ref[2]
     even = 1 - odd
@@ -393,7 +378,7 @@
     upper = d_index // half_dp
     z_index, core = m_index // 2, m_index % 2
     where = jnp.stack(
-        [(z_index == 1) | (z_index == 2), upper, z_index % 2, z_index // 2 == upper]
+        [z_index, upper, z_index % 2, z_index // 2 == upper] + [z_index ^ r for r in range(4)]
     ).astype(jnp.int32)
 
     def along_z(value, target):
@@ -406,14 +391,8 @@
     def near(value):
         return along_z(value, lambda z: z ^ 1)
 
-    def middle(value):
-        return along_z(value, lambda z: 3 - z if z in (1, 2) else z)
-
-    def outward(value):
-        return along_z(value, lambda z: {1: 0, 2: 3}.get(z))
-
-    def inward(value):
-        return along_z(value, lambda z: {0: 1, 3: 2}.get(z))
+    def across(value):
+        return along_z(value, lambda z: z ^ 2)
 
     def swap_cores(value):
         return permute_devices(value, dp, mp, lambda d, m: (d, m ^ 1))
@@ -432,6 +411,7 @@
     ups, downs = (up_weight, swap_cores(up_weight)), (down_weight, swap_cores(down_weight))
     small = jnp.concatenate([up_bias, head_bias, codebook.astype(jnp.float32).reshape(-1)])
     small_other = swap_cores(small)
+    head_other = swap_cores(head_weight)
     head_twin = swap_twins(head_own)
     hid, voc = up_bias.shape[0], head_bias.shape[0]
     bias_up = jnp.concatenate([up_bias, small_other[:hid]])[None]
@@ -449,62 +429,49 @@
         )
         return picked.reshape(2, CHUNKS, half, voc)
 
+    noises = (
+        noise_for(core, upper),
+        swap_cores(noise_for(1 - core, upper)),
+        swap_twins(noise_for(core, 1 - upper)),
+        swap_both(noise_for(1 - core, 1 - upper)),
+    )
+    phi = phi_weight.reshape(channels, channels * 9)
+
     step = rows // CHUNKS
     rows_a, rows_b = tokens[:step], tokens[step:]
-    own_a = norm_part(rows_a, ada_own)
-    near_a, mid_a = near(own_a), middle(own_a)
-    own_b = norm_part(rows_b, ada_own)
-    far_mid_a, far_end_a = middle(near_a), outward(mid_a)
-    near_b = near(after(own_b, near_a))
-    noises = (
-        noise_for(core, upper),
-        swap_cores(after(noise_for(1 - core, upper), mid_a)),
-        swap_twins(after(noise_for(core, 1 - upper), mid_a)),
-        swap_both(after(noise_for(1 - core, 1 - upper), mid_a)),
-    )
-    sum_own_a, sum_near_a = ffn(where, [[own_a], [near_a]], ups, downs, bias_up)
-    head_other = swap_cores(after(head_weight, ups[1], downs[1]))
-    far_a = (after(far_mid_a, sum_near_a), far_end_a)
-    last_end_a = outward(far_a[0])
-    mid_b = middle(after(own_b, far_a[0]))
-    (sum_far_a,) = ffn(where, [far_a], ups, downs, bias_up)
-    came_far_a = inward(sum_far_a)
-    near_b, mid_b = after(near_b, sum_far_a), after(mid_b, sum_far_a)
-    far_mid_b, far_end_b = middle(near_b), outward(mid_b)
-    (sum_last_a,) = ffn(where, [(mid_a, after(last_end_a, sum_far_a))], ups, downs, bias_up)
-    came_last_a = inward(sum_last_a)
-    sum_own_b, sum_near_b = ffn(where, [[after(own_b, sum_last_a, came_far_a, *noises)], [near_b]], ups, downs, bias_up)
-    far_b = (after(far_mid_b, sum_near_b), far_end_b)
-    last_end_b = outward(far_b[0])
-    both_last_a = add_mid(where, after(sum_last_a, far_b[0]), came_far_a)
-    went_last_a = middle(both_last_a)
-    (sum_far_b,) = ffn(where, [(after(far_b[0], both_last_a), far_b[1])], ups, downs, bias_up)
-    came_far_b = inward(sum_far_b)
-    both_far_a = add_mid(where, after(sum_far_a, sum_far_b), came_last_a)
-    went_far_a = middle(both_far_a)
-    (sum_last_b,) = ffn(where, [(after(mid_b, went_last_a, both_far_a), after(last_end_b, sum_far_b))], ups, downs, bias_up)
-    came_last_b = inward(sum_last_b)
-    came_near_a = near(add_mid(where, sum_near_a, went_far_a))
-    went_last_b = middle(add_mid(where, sum_last_b, came_far_b))
-    went_far_b = middle(add_mid(where, sum_far_b, came_last_b))
-
-    def finish(own, came_near, went_last, part):
-        return block_rows(where, own, came_near, went_last, part, gate_own, down_bias[None])
-
-    def gather(own):
-        from_near, from_mid = near(own), middle(own)
-        far_mid, far_end = middle(from_near), outward(from_mid)
-        return own, from_near, far_mid, far_end, from_mid, outward(far_mid)
-
-    out_a, kept_a, sent_a = finish(sum_own_a, came_near_a, went_last_a, rows_a)
-    came_a = swap_twins(sent_a)
-    mixed_a = mix_twins(where, kept_a, came_a, head_own, head_twin)
-    came_near_b = near(add_mid(where, sum_near_b, went_far_b))
-    slots_a = gather(mixed_a)
-    out_b, kept_b, sent_b = finish(sum_own_b, came_near_b, went_last_b, rows_b)
-    came_b = swap_twins(sent_b)
-    mixed_b = mix_twins(where, kept_b, came_b, head_own, head_twin)
-    slots_b = gather(mixed_b)
+    lanes = [[2 * z + c for z in range(mp // 2)] for c in range(2)]
+
+    def gather_line(value):
+        return lax.all_gather(value, "mp", axis=0, tiled=True, axis_index_groups=lanes)
+
+    all_a = gather_line(norm_part(rows_a, ada_own))
+    all_b = gather_line(norm_part(rows_b, ada_own))
+    (
+        all_a, ups, downs, noises, head_other, head_twin, bias_up, bias_head, codes, phi
+    ) = lax.optimization_barrier(
+        (all_a, ups, downs, noises, head_other, head_twin, bias_up, bias_head, codes, phi)
+    )
+
+    def spread(own):
+        from_near, from_far = near(own), across(own)
+        return own, from_near, from_far, near(from_far)
+
+    def finish(own, came_near, came_far, part):
+        out, kept, sent = block_rows(where, own, came_near, came_far, part, gate_own, down_bias[None])
+        return out, mix_twins(where, kept, swap_twins(sent), head_own, head_twin)
+
+    last_a, far_a, near_a, own_a = ffn(where, all_a, (3, 2, 1, 0), ups, downs, bias_up)
+    came_last_a, came_near_a = near(last_a), near(near_a)
+    came_far_a = across(add(far_a, came_last_a))
+    last_b, far_b = ffn(where, after(all_b, own_a), (3, 2), ups, downs, bias_up)
+    came_last_b = near(last_b)
+    near_b, own_b = ffn(where, after(all_b, far_b), (1, 0), ups, downs, bias_up)
+    came_far_b = across(add(far_b, came_last_b))
+    came_near_b = near(near_b)
+    out_a, mixed_a = finish(own_a, came_near_a, after(came_far_a, own_b), rows_a)
+    slots_a = spread(mixed_a)
+    out_b, mixed_b = finish(own_b, came_near_b, came_far_b, rows_b)
+    slots_b = spread(mixed_b)
     heads = (head_weight, head_other)
     stats = [
         head_stats(0, where, slots_a, heads, bias_head, codes, noises),
@@ -548,7 +515,7 @@
         [wide[:, i : i + band, j : j + SIDE] for i in range(3) for j in range(3)], axis=1
     ).reshape(channels * 9, cells)
     conv = jnp.dot(
-        phi_weight.reshape(channels, channels * 9),
+        phi,
         taps,
         precision=lax.Precision.HIGHEST,
         preferred_element_type=jnp.float32,

time: 269 us -> 297 us (1.10)
  waiting for transfers between devices: 88.2 us -> 146 us
  starting transfers between devices: 78.6 us -> 31.6 us
  local copies, waits for them, and re-layouts: 25.3 us -> 41.6 us
  Pallas kernels: 67.9 us -> 54.1 us
  between operations: 1.63 us -> 14.4 us
    ppermute x46 -> x28, starting transfers between devices: 78.6 us -> 31.6 us  [permute_devices(): return lax.ppermute(value, ('dp', 'mp'), pairs)]
    all_gather x0 -> x2, waiting for transfers between devices: none -> 43.5 us  [gather_line(): lax.all_gather(value, 'mp', axis=0, tiled=True, axis_index_groups=lanes)]
    ppermute x46 -> x28, waiting for transfers between devices: 88.2 us -> 103 us  [permute_devices(): return lax.ppermute(value, ('dp', 'mp'), pairs)]
    pallas_call x21 -> x14, Pallas kernels: 67.9 us -> 54.1 us  [call(): pl.pallas_call(kernel, out_shape=outs, in_specs=[SCALARS] * scalars + [ON...]
    unnamed x92 -> x69, local copies, waits for them, and re-layouts: 17.1 us -> 22.7 us
  transfers between devices with their start and end apart: 46 -> 30, of which waited for: 17 -> 19; matrix products, arithmetic and copies ran while one was open for 5% -> 8% of each run, Pallas kernels for 21% -> 17%
where the time goes in v1:
time: 297 us; the launch traced here: 296 us
  waiting for transfers between devices  146 us (49%)
  Pallas kernels  54.1 us (18%)
  local copies, waits for them, and re-layouts  41.6 us (14%)
  starting transfers between devices  31.6 us (11%)
  between operations  14.4 us (5%)
  other arithmetic  6.68 us (2%)
    ppermute x28, waiting for transfers between devices, permute_devices(): return lax.ppermute(value, ('dp', 'mp'), pairs)  103 us
    pallas_call x14, Pallas kernels, call(): pl.pallas_call(kernel, out_shape=outs, in_specs=[SCALARS] * scalars + [ON...  54.1 us
    all_gather x2, waiting for transfers between devices, gather_line(): lax.all_gather(value, 'mp', axis=0, tiled=True, axis_index_groups=lanes)  43.5 us
    ppermute x28, starting transfers between devices, permute_devices(): return lax.ppermute(value, ('dp', 'mp'), pairs)  31.6 us
    unnamed x69, local copies, waits for them, and re-layouts  22.7 us
  transfers between devices with their start and end apart: 30, of which 19 were waited for; matrix products, arithmetic and copies ran while one was open for 8% of the time, Pallas kernels for 17%

profile of v1, /device:TPU:13, one launch (start us, length us, event | category | flops | bytes accessed | tf_op | source)
XLA Modules:
  0.0 295.7 jit_solution(13157496543570571715)
XLA Ops:
  7.2 2.1 fusion.18
  14.6 2.7 dynamic-slice_bitcast_fusion
  18.3 1.6 copy.33
  19.9 1.7 reshape.50
  23.2 4.9 %collective-permute-done.7 = f32[18048]{0:T(1024)} collective-permute-done((f32[18048]{0:T(1024)S(1)}, f32[18048]{0:T(1024)}, u32[]{:S(2)}, u32[]{:S(2)}) %collective-permute-start.7) | collective-permute-done | bytes 72224 | tf_op jit(solution)/shard_map/ppermute | solution.py:36
  28.4 4.8 %collective-permute-done.2.noise_core = f32[2,2,64,512]{3,2,1,0:T(8,128)} collective-permute-done((f32[2,2,64,512]{3,2,1,0:T(8,128)}, f32[2,2,64,512]{3,2,1,0:T(8,128)}, u32[]{:S(2)}, u32[]{:S(2)}) %collective-permute-start.2) | collective-permute-done | bytes 524320 | tf_op jit(solution)/shard_map/ppermute | solution.py:36
  35.1 1.7 copy.35
  36.8 1.6 reshape.52
  38.5 1.5 slice.137
  40.0 1.7 reshape.51
  41.7 1.7 copy.34
  46.1 1.5 pad_maximum_fusion.1
  47.7 5.7 %collective-permute-done.4.noise_both = f32[2,2,64,512]{3,2,1,0:T(8,128)} collective-permute-done((f32[2,2,64,512]{3,2,1,0:T(8,128)}, f32[2,2,64,512]{3,2,1,0:T(8,128)}, u32[]{:S(2)}, u32[]{:S(2)}) %collective-permute-start.4) | collective-permute-done | bytes 524320 | tf_op jit(solution)/shard_map/ppermute | solution.py:36
  53.4 8.6 %all-gather.3.cloned.1.call-done.rows_ref = bf16[512,2304]{1,0:T(8,128)(2,1)} async-done(((bf16[128,2304]{1,0:T(8,128)(2,1)}), bf16[512,2304]{1,0:T(8,128)(2,1)}) %all-gather.3.cloned.1.call-update) | async-done | bytes 2359312 | tf_op jit(solution)/shard_map/all_gather | solution.py:445
  62.0 2.5 copy-done.1
  64.5 2.5 copy-done.3
  67.0 1.7 copy-done.9
  68.6 16.9 %shard_map.159 = (bf16[128,2304]{1,0:T(8,128)(2,1)}, bf16[128,2304]{1,0:T(8,128)(2,1)S(1)}, bf16[128,2304]{1,0:T(8,128)(2,1)S(1)}, bf16[128,2304]{1,0:T(8,128)(2,1)S(1)}) custom-call(s32[8]{0:T(128)S(1)} %stack.66.where_ref, bf16[512,2304]{1,0:T(8,128)(2,1)S(1)} %copy-done.9, bf16[2304,1152]{1,0:T(8,128)(2,1)S(1)} %copy-done.1, ...), custom_call_target="tpu_custom_call" | custom-call | tf_op jit(solution)/shard_map/pallas_call | solution.py:167
  88.0 2.1 collective-permute-start.9
  90.1 34.9 %all-gather.5.cloned.1.call-done.rows_ref = bf16[512,2304]{1,0:T(8,128)(2,1)} async-done(((bf16[128,2304]{1,0:T(8,128)(2,1)}), bf16[512,2304]{1,0:T(8,128)(2,1)}) %all-gather.5.cloned.1.call-update) | async-done | bytes 2359312 | tf_op jit(solution)/shard_map/all_gather | solution.py:445
  125.0 2.5 copy-done.2
  127.5 2.5 copy-done.4
  130.0 1.7 copy-done.5
  131.7 10.4 %shard_map.162 = (bf16[128,2304]{1,0:T(8,128)(2,1)S(1)}, bf16[128,2304]{1,0:T(8,128)(2,1)S(1)}) custom-call(s32[8]{0:T(128)S(1)} %stack.66.where_ref, bf16[512,2304]{1,0:T(8,128)(2,1)S(1)} %copy-done.5, bf16[2304,1152]{1,0:T(8,128)(2,1)S(1)} %copy-done.2, bf16[2304,1152]{1,0:T(8,128)(2,1)} %collective-permute-done.up_b, bf16[1152,2304]{1,0:T(8,128)(2,1)S(1)} %copy-done.4, ...), custom_call_target="tpu_custom_call" | custom-call | tf_op jit(solution)/shard_map/pallas_call | solution.py:167
  143.5 3.1 %collective-permute-start.10 = (bf16[128,2304]{1,0:T(8,128)(2,1)S(1)}, bf16[128,2304]{1,0:T(8,128)(2,1)S(1)}, u32[]{:S(2)}, u32[]{:S(2)}) collective-permute-start(bf16[128,2304]{1,0:T(8,128)(2,1)S(1)} %shard_map.160), channel_id=1, source_target_pairs={{0,4},{1,5},{2,6},{3,7},{4,0},{5,1},{6,2},{7,3},{8,12},{9,13},{10,... | collective-permute-start | bytes 1769480 | tf_op jit(solution)/shard_map/ppermute | solution.py:36
  146.6 10.2 %shard_map.163 = (bf16[128,2304]{1,0:T(8,128)(2,1)S(1)}, bf16[128,2304]{1,0:T(8,128)(2,1)S(1)}) custom-call(s32[8]{0:T(128)S(1)} %stack.66.where_ref, bf16[512,2304]{1,0:T(8,128)(2,1)S(1)} %copy-done.5, bf16[2304,1152]{1,0:T(8,128)(2,1)S(1)} %copy-done.2, bf16[2304,1152]{1,0:T(8,128)(2,1)} %collective-permute-done.up_b, bf16[1152,2304]{1,0:T(8,128)(2,1)S(1)} %copy-done.4, ...), custom_call_target="tpu_custom_call" | custom-call | tf_op jit(solution)/shard_map/pallas_call | solution.py:167
  156.8 1.5 collective-permute-start.11
  158.3 7.6 %collective-permute-done.12.b_ref = bf16[128,2304]{1,0:T(8,128)(2,1)S(1)} collective-permute-done((bf16[128,2304]{1,0:T(8,128)(2,1)S(1)}, bf16[128,2304]{1,0:T(8,128)(2,1)S(1)}, u32[]{:S(2)}, u32[]{:S(2)}) %collective-permute-start.12) | collective-permute-done | bytes 589856 | tf_op jit(solution)/shard_map/ppermute | solution.py:36
  166.1 1.9 collective-permute-start.13
  168.0 2.8 collective-permute-done.10.far_ref
  170.8 21.3 %collective-permute-done.8.near_ref = bf16[128,2304]{1,0:T(8,128)(2,1)S(1)} collective-permute-done((bf16[128,2304]{1,0:T(8,128)(2,1)S(1)}, bf16[128,2304]{1,0:T(8,128)(2,1)S(1)}, u32[]{:S(2)}, u32[]{:S(2)}) %collective-permute-start.8) | collective-permute-done | bytes 589856 | tf_op jit(solution)/shard_map/ppermute | solution.py:36
  194.2 10.5 %collective-permute-done.11.near_ref = bf16[128,2304]{1,0:T(8,128)(2,1)S(1)} collective-permute-done((bf16[128,2304]{1,0:T(8,128)(2,1)S(1)}, bf16[128,2304]{1,0:T(8,128)(2,1)S(1)}, u32[]{:S(2)}, u32[]{:S(2)}) %collective-permute-start.11) | collective-permute-done | bytes 589856 | tf_op jit(solution)/shard_map/ppermute | solution.py:36
  204.8 3.8 %collective-permute-done.13.far_ref = bf16[128,2304]{1,0:T(8,128)(2,1)S(1)} collective-permute-done((bf16[128,2304]{1,0:T(8,128)(2,1)S(1)}, bf16[128,2304]{1,0:T(8,128)(2,1)S(1)}, u32[]{:S(2)}, u32[]{:S(2)}) %collective-permute-start.13) | collective-permute-done | bytes 589856 | tf_op jit(solution)/shard_map/ppermute | solution.py:36
  210.7 1.8 shard_map.167.own_ref
  212.7 4.6 %collective-permute-done.18.came_ref = bf16[64,2304]{1,0:T(8,128)(2,1)S(1)} collective-permute-done((bf16[64,2304]{1,0:T(8,128)(2,1)S(1)}, bf16[64,2304]{1,0:T(8,128)(2,1)S(1)}, u32[]{:S(2)}, u32[]{:S(2)}) %collective-permute-start.18) | collective-permute-done | bytes 294944 | tf_op jit(solution)/shard_map/ppermute | solution.py:36
  217.3 1.7 shard_map.169.own_ref
  219.7 12.6 %collective-permute-done.16.far_ref = bf16[64,2304]{1,0:T(8,128)(2,1)} collective-permute-done((bf16[64,2304]{1,0:T(8,128)(2,1)}, bf16[64,2304]{1,0:T(8,128)(2,1)}, u32[]{:S(2)}, u32[]{:S(2)}) %collective-permute-start.16) | collective-permute-done | bytes 294944 | tf_op jit(solution)/shard_map/ppermute | solution.py:36
  233.8 4.9 %collective-permute-done.20.far_ref = bf16[64,2304]{1,0:T(8,128)(2,1)} collective-permute-done((bf16[64,2304]{1,0:T(8,128)(2,1)}, bf16[64,2304]{1,0:T(8,128)(2,1)}, u32[]{:S(2)}, u32[]{:S(2)}) %collective-permute-start.20) | collective-permute-done | bytes 294944 | tf_op jit(solution)/shard_map/ppermute | solution.py:36
  239.7 4.3 %collective-permute-done.17.last_ref = bf16[64,2304]{1,0:T(8,128)(2,1)} collective-permute-done((bf16[64,2304]{1,0:T(8,128)(2,1)}, bf16[64,2304]{1,0:T(8,128)(2,1)}, u32[]{:S(2)}, u32[]{:S(2)}) %collective-permute-start.17) | collective-permute-done | bytes 294944 | tf_op jit(solution)/shard_map/ppermute | solution.py:36
  244.0 4.6 %shard_map.168 = f32[40,256]{1,0:T(8,128)S(1)} custom-call(s32[8]{0:T(128)S(1)} %stack.66.where_ref, bf16[64,2304]{1,0:T(8,128)(2,1)} %shard_map.167.own_ref, bf16[64,2304]{1,0:T(8,128)(2,1)} %collective-permute-done.15.near_ref, bf16[64,2304]{1,0:T(8,128)(2,1)} %collective-permute-done.16.far_ref, bf16[64,2304]{1,0:T(8,128)(2,1)} %collective-permute-done.17.last_ref, ...), custom_call_target="tpu_custom_call" | custom-call | tf_op jit(solution)/shard_map/pallas_call | solution.py:167
  248.7 1.7 collective-permute-done.19.near_ref
  250.3 6.3 %collective-permute-done.21.last_ref = bf16[64,2304]{1,0:T(8,128)(2,1)} collective-permute-done((bf16[64,2304]{1,0:T(8,128)(2,1)}, bf16[64,2304]{1,0:T(8,128)(2,1)}, u32[]{:S(2)}, u32[]{:S(2)}) %collective-permute-start.21) | collective-permute-done | bytes 294944 | tf_op jit(solution)/shard_map/ppermute | solution.py:36
  256.7 4.3 %shard_map.170 = f32[40,256]{1,0:T(8,128)S(1)} custom-call(s32[8]{0:T(128)S(1)} %stack.66.where_ref, bf16[64,2304]{1,0:T(8,128)(2,1)} %shard_map.169.own_ref, bf16[64,2304]{1,0:T(8,128)(2,1)} %collective-permute-done.19.near_ref, bf16[64,2304]{1,0:T(8,128)(2,1)} %collective-permute-done.20.far_ref, bf16[64,2304]{1,0:T(8,128)(2,1)} %collective-permute-done.21.last_ref, ...), custom_call_target="tpu_custom_call" | custom-call | tf_op jit(solution)/shard_map/pallas_call | solution.py:167
  261.1 2.3 collective-permute-start.24
  263.5 2.0 collective-permute-start.23
  268.3 5.4 %collective-permute-start.26 = (f32[32,128]{1,0:T(8,128)S(1)}, f32[32,128]{1,0:T(8,128)S(1)}, u32[]{:S(2)}, u32[]{:S(2)}) collective-permute-start(f32[32,128]{1,0:T(8,128)S(1)} %shard_map.171), channel_id=1, source_target_pairs={{0,0},{1,2},{2,4},{3,6},{4,16},{5,18},{6,20},{7,22},{8,8},{9,10},{... | collective-permute-start | bytes 49160 | tf_op jit(solution)/shard_map/ppermute | solution.py:36
  273.7 4.6 %collective-permute-start.27 = (f32[32,128]{1,0:T(8,128)S(1)}, f32[32,128]{1,0:T(8,128)S(1)}, u32[]{:S(2)}, u32[]{:S(2)}) collective-permute-start(f32[32,128]{1,0:T(8,128)S(1)} %shard_map.171), channel_id=1, source_target_pairs={{0,1},{1,3},{2,5},{3,7},{4,17},{5,19},{6,21},{7,23},{8,9},{9,11},{... | collective-permute-start | bytes 49160 | tf_op jit(solution)/shard_map/ppermute | solution.py:36
  281.1 5.3 %collective-permute-done.25 = f32[32,128]{1,0:T(8,128)S(1)} collective-permute-done((f32[32,128]{1,0:T(8,128)S(1)}, f32[32,128]{1,0:T(8,128)S(1)}, u32[]{:S(2)}, u32[]{:S(2)}) %collective-permute-start.25) | collective-permute-done | bytes 16416 | tf_op jit(solution)/shard_map/ppermute | solution.py:36
  (137 shorter events, 32.6 us)
Async XLA Ops:
  7.2 54.8 %all-gather.3.cloned.1.call-start = ((), (), s32[]{:S(2)}) async-start(), calls=%async_computation | async-start | bytes 2949120 | tf_op jit(solution)/shard_map/all_gather | solution.py:445
  9.4 4.7 %copy-start.6 = (bf16[2304,512]{1,0:T(8,128)(2,1)S(1)}, bf16[2304,512]{1,0:T(8,128)(2,1)}, u32[]{:S(2)}) copy-start(bf16[2304,512]{1,0:T(8,128)(2,1)} %weight_a.3) | copy-start | bytes 7077892
  11.9 113.1 %all-gather.5.cloned.1.call-start = ((), (), s32[]{:S(2)}) async-start(), calls=%async_computation.1 | async-start | bytes 2949120 | tf_op jit(solution)/shard_map/all_gather | solution.py:445
  11.9 50.0 %collective-permute-start = (bf16[2304,1152]{1,0:T(8,128)(2,1)}, bf16[2304,1152]{1,0:T(8,128)(2,1)}, u32[]{:S(2)}, u32[]{:S(2)}) collective-permute-start(bf16[2304,1152]{1,0:T(8,128)(2,1)} %up_a.2), channel_id=1, source_target_pairs={{0,1},{1,0},{2,3},{3,2},{4,5},{5,4},{6,7},{7,6},{8,9},{9,8},{10,11... | collective-permute-start | bytes 15925256 | tf_op jit(solution)/shard_map/ppermute | solution.py:36
  12.7 49.3 %collective-permute-start.1 = (bf16[1152,2304]{1,0:T(8,128)(2,1)}, bf16[1152,2304]{1,0:T(8,128)(2,1)}, u32[]{:S(2)}, u32[]{:S(2)}) collective-permute-start(bf16[1152,2304]{1,0:T(8,128)(2,1)} %down_a.2), channel_id=1, source_target_pairs={{0,1},{1,0},{2,3},{3,2},{4,5},{5,4},{6,7},{7,6},{8,9},{9,8},{10,11... | collective-permute-start | bytes 15925256 | tf_op jit(solution)/shard_map/ppermute | solution.py:36
  14.1 39.3 %collective-permute-start.5 = (bf16[2304,512]{1,0:T(8,128)(2,1)S(1)}, bf16[2304,512]{1,0:T(8,128)(2,1)}, u32[]{:S(2)}, u32[]{:S(2)}) collective-permute-start(bf16[2304,512]{1,0:T(8,128)(2,1)S(1)} %copy-done.6), channel_id=1, source_target_pairs={{0,1},{1,0},{2,3},{3,2},{4,5},{5,4},{6,7},{7,6},{8,9},{9,8},{10,11... | collective-permute-start | bytes 7077896 | tf_op jit(solution)/shard_map/ppermute | solution.py:36
  14.6 7.0 %copy-start.27 = (f32[512]{0:T(512)S(1)}, f32[512]{0:T(512)}, u32[]{:S(2)}) copy-start(f32[512]{0:T(512)} %param.24) | copy-start | bytes 6148
  17.3 16.0 %collective-permute-start.2 = (f32[2,2,64,512]{3,2,1,0:T(8,128)}, f32[2,2,64,512]{3,2,1,0:T(8,128)}, u32[]{:S(2)}, u32[]{:S(2)}) collective-permute-start(f32[2,2,64,512]{3,2,1,0:T(8,128)} %get-tuple-element.68), channel_id=1, source_target_pairs={{0,1},{1,0},{2,3},{3,2},{4,5},{5,4},{6,7},{7,6},{8,9},{9,8},{10,11... | collective-permute-start | bytes 1572872 | tf_op jit(solution)/shard_map/ppermute | solution.py:36
  18.1 4.4 %collective-permute-start.6 = (f32[2,2304]{1,0:T(2,128)S(1)}, f32[2,2304]{1,0:T(2,128)S(1)}, u32[]{:S(2)}, u32[]{:S(2)}) collective-permute-start(f32[2,2304]{1,0:T(2,128)S(1)} %dynamic-slice_bitcast_fusion.4.ada_ref), channel_id=1, source_target_pairs={{0,16},{1,17},{2,18},{3,19},{4,20},{5,21},{6,22},{7,23},{8,24},{9,... | collective-permute-start | bytes 55304 | tf_op jit(solution)/shard_map/ppermute | solution.py:36
  22.4 21.6 %copy-start.20 = (f32[2,2304]{1,0:T(2,128)}, f32[2,2304]{1,0:T(2,128)S(1)}, u32[]{:S(2)}) copy-start(f32[2,2304]{1,0:T(2,128)S(1)} %collective-permute-done.6.twin_ref) | copy-start | bytes 55300
  22.4 5.7 %collective-permute-start.7 = (f32[18048]{0:T(1024)S(1)}, f32[18048]{0:T(1024)}, u32[]{:S(2)}, u32[]{:S(2)}) collective-permute-start(f32[18048]{0:T(1024)S(1)} %pad_maximum_fusion.2), channel_id=1, source_target_pairs={{0,1},{1,0},{2,3},{3,2},{4,5},{5,4},{6,7},{7,6},{8,9},{9,8},{10,11... | collective-permute-start | bytes 216584 | tf_op jit(solution)/shard_map/ppermute | solution.py:36
  28.2 19.5 %collective-permute-start.3 = (f32[2,2,64,512]{3,2,1,0:T(8,128)}, f32[2,2,64,512]{3,2,1,0:T(8,128)}, u32[]{:S(2)}, u32[]{:S(2)}) collective-permute-start(f32[2,2,64,512]{3,2,1,0:T(8,128)} %get-tuple-element.67), channel_id=1, source_target_pairs={{0,16},{1,17},{2,18},{3,19},{4,20},{5,21},{6,22},{7,23},{8,24},{9,... | collective-permute-start | bytes 1572872 | tf_op jit(solution)/shard_map/ppermute | solution.py:36
  33.2 20.1 %collective-permute-start.4 = (f32[2,2,64,512]{3,2,1,0:T(8,128)}, f32[2,2,64,512]{3,2,1,0:T(8,128)}, u32[]{:S(2)}, u32[]{:S(2)}) collective-permute-start(f32[2,2,64,512]{3,2,1,0:T(8,128)} %get-tuple-element.66), channel_id=1, source_target_pairs={{0,17},{1,16},{2,19},{3,18},{4,21},{5,20},{6,23},{7,22},{8,25},{9,... | collective-permute-start | bytes 1572872 | tf_op jit(solution)/shard_map/ppermute | solution.py:36
  62.0 2.5 copy-start.1
  64.5 2.5 copy-start.3
  88.0 54.2 %collective-permute-start.9 = (bf16[128,2304]{1,0:T(8,128)(2,1)}, bf16[128,2304]{1,0:T(8,128)(2,1)}, u32[]{:S(2)}, u32[]{:S(2)}) collective-permute-start(bf16[128,2304]{1,0:T(8,128)(2,1)} %get-tuple-element.43), channel_id=1, source_target_pairs={{0,2},{1,3},{2,0},{3,1},{4,6},{5,7},{6,4},{7,5},{8,10},{9,11},{10,... | collective-permute-start | bytes 1769480 | tf_op jit(solution)/shard_map/ppermute | solution.py:36
  127.5 2.5 copy-start.4
  131.7 10.5 %copy-start.13 = (bf16[128,2304]{1,0:T(8,128)(2,1)S(1)}, bf16[128,2304]{1,0:T(8,128)(2,1)}, u32[]{:S(2)}) copy-start(bf16[128,2304]{1,0:T(8,128)(2,1)} %copy-done.12) | copy-start | bytes 1769476
  131.7 14.9 %copy-start.23 = (bf16[128,2304]{1,0:T(8,128)(2,1)S(1)}, bf16[128,2304]{1,0:T(8,128)(2,1)}, u32[]{:S(2)}) copy-start(bf16[128,2304]{1,0:T(8,128)(2,1)} %copy-done.22) | copy-start | bytes 1769476
  142.1 23.9 %collective-permute-start.12 = (bf16[128,2304]{1,0:T(8,128)(2,1)S(1)}, bf16[128,2304]{1,0:T(8,128)(2,1)S(1)}, u32[]{:S(2)}, u32[]{:S(2)}) collective-permute-start(bf16[128,2304]{1,0:T(8,128)(2,1)S(1)} %get-tuple-element.51), channel_id=1, source_target_pairs={{0,2},{1,3},{2,0},{3,1},{4,6},{5,7},{6,4},{7,5},{8,10},{9,11},{10,... | collective-permute-start | bytes 1769480 | tf_op jit(solution)/shard_map/ppermute | solution.py:36
  143.5 27.4 %collective-permute-start.10 = (bf16[128,2304]{1,0:T(8,128)(2,1)S(1)}, bf16[128,2304]{1,0:T(8,128)(2,1)S(1)}, u32[]{:S(2)}, u32[]{:S(2)}) collective-permute-start(bf16[128,2304]{1,0:T(8,128)(2,1)S(1)} %shard_map.160), channel_id=1, source_target_pairs={{0,4},{1,5},{2,6},{3,7},{4,0},{5,1},{6,2},{7,3},{8,12},{9,13},{10,... | collective-permute-start | bytes 1769480 | tf_op jit(solution)/shard_map/ppermute | solution.py:36
  146.6 45.5 %collective-permute-start.8 = (bf16[128,2304]{1,0:T(8,128)(2,1)S(1)}, bf16[128,2304]{1,0:T(8,128)(2,1)S(1)}, u32[]{:S(2)}, u32[]{:S(2)}) collective-permute-start(bf16[128,2304]{1,0:T(8,128)(2,1)S(1)} %copy-done.23), channel_id=1, source_target_pairs={{0,2},{1,3},{2,0},{3,1},{4,6},{5,7},{6,4},{7,5},{8,10},{9,11},{10,... | collective-permute-start | bytes 1769480 | tf_op jit(solution)/shard_map/ppermute | solution.py:36
  146.6 21.4 %copy-start.26 = (f32[2304]{0:T(1024)S(1)}, f32[2304]{0:T(1024)}, u32[]{:S(2)}) copy-start(f32[2304]{0:T(1024)} %param.21) | copy-start | bytes 27652
  146.6 21.4 %copy-start.28 = (f32[2,2304]{1,0:T(2,128)S(1)}, f32[2,2304]{1,0:T(2,128)}, u32[]{:S(2)}) copy-start(f32[2,2304]{1,0:T(2,128)} %param.17) | copy-start | bytes 55300
  146.6 45.5 %copy-start.8 = (bf16[128,2304]{1,0:T(8,128)(2,1)S(1)}, bf16[128,2304]{1,0:T(8,128)(2,1)}, u32[]{:S(2)}) copy-start(bf16[128,2304]{1,0:T(8,128)(2,1)} %get-tuple-element.70.tokens_ref) | copy-start | bytes 1769476
  146.6 45.5 %copy-start.19 = (bf16[128,2304]{1,0:T(8,128)(2,1)S(1)}, bf16[128,2304]{1,0:T(8,128)(2,1)}, u32[]{:S(2)}) copy-start(bf16[128,2304]{1,0:T(8,128)(2,1)} %copy-done.18) | copy-start | bytes 1769476
  156.8 47.9 %collective-permute-start.11 = (bf16[128,2304]{1,0:T(8,128)(2,1)S(1)}, bf16[128,2304]{1,0:T(8,128)(2,1)S(1)}, u32[]{:S(2)}, u32[]{:S(2)}) collective-permute-start(bf16[128,2304]{1,0:T(8,128)(2,1)S(1)} %get-tuple-element.50), channel_id=1, source_target_pairs={{0,2},{1,3},{2,0},{3,1},{4,6},{5,7},{6,4},{7,5},{8,10},{9,11},{10,... | collective-permute-start | bytes 1769480 | tf_op jit(solution)/shard_map/ppermute | solution.py:36
  166.1 42.5 %collective-permute-start.13 = (bf16[128,2304]{1,0:T(8,128)(2,1)S(1)}, bf16[128,2304]{1,0:T(8,128)(2,1)S(1)}, u32[]{:S(2)}, u32[]{:S(2)}) collective-permute-start(bf16[128,2304]{1,0:T(8,128)(2,1)S(1)} %shard_map.165), channel_id=1, source_target_pairs={{0,4},{1,5},{2,6},{3,7},{4,0},{5,1},{6,2},{7,3},{8,12},{9,13},{10,... | collective-permute-start | bytes 1769480 | tf_op jit(solution)/shard_map/ppermute | solution.py:36
  170.8 39.8 %copy-start.21 = (f32[2,2304]{1,0:T(2,128)S(1)}, f32[2,2304]{1,0:T(2,128)}, u32[]{:S(2)}) copy-start(f32[2,2304]{1,0:T(2,128)} %copy-done.20) | copy-start | bytes 55300
  194.0 16.7 %collective-permute-start.14 = (bf16[64,2304]{1,0:T(8,128)(2,1)S(1)}, bf16[64,2304]{1,0:T(8,128)(2,1)S(1)}, u32[]{:S(2)}, u32[]{:S(2)}) collective-permute-start(bf16[64,2304]{1,0:T(8,128)(2,1)S(1)} %get-tuple-element.54), channel_id=1, source_target_pairs={{0,16},{1,17},{2,18},{3,19},{4,20},{5,21},{6,22},{7,23},{8,24},{9,... | collective-permute-start | bytes 884744 | tf_op jit(solution)/shard_map/ppermute | solution.py:36
  210.4 7.0 %collective-permute-start.18 = (bf16[64,2304]{1,0:T(8,128)(2,1)S(1)}, bf16[64,2304]{1,0:T(8,128)(2,1)S(1)}, u32[]{:S(2)}, u32[]{:S(2)}) collective-permute-start(bf16[64,2304]{1,0:T(8,128)(2,1)S(1)} %get-tuple-element.64), channel_id=1, source_target_pairs={{0,16},{1,17},{2,18},{3,19},{4,20},{5,21},{6,22},{7,23},{8,24},{9,... | collective-permute-start | bytes 884744 | tf_op jit(solution)/shard_map/ppermute | solution.py:36
  212.4 19.9 %collective-permute-start.16 = (bf16[64,2304]{1,0:T(8,128)(2,1)}, bf16[64,2304]{1,0:T(8,128)(2,1)}, u32[]{:S(2)}, u32[]{:S(2)}) collective-permute-start(bf16[64,2304]{1,0:T(8,128)(2,1)} %shard_map.167.own_ref), channel_id=1, source_target_pairs={{0,4},{1,5},{2,6},{3,7},{4,0},{5,1},{6,2},{7,3},{8,12},{9,13},{10,... | collective-permute-start | bytes 884744 | tf_op jit(solution)/shard_map/ppermute | solution.py:36
  219.1 19.5 %collective-permute-start.20 = (bf16[64,2304]{1,0:T(8,128)(2,1)}, bf16[64,2304]{1,0:T(8,128)(2,1)}, u32[]{:S(2)}, u32[]{:S(2)}) collective-permute-start(bf16[64,2304]{1,0:T(8,128)(2,1)} %shard_map.169.own_ref), channel_id=1, source_target_pairs={{0,4},{1,5},{2,6},{3,7},{4,0},{5,1},{6,2},{7,3},{8,12},{9,13},{10,... | collective-permute-start | bytes 884744 | tf_op jit(solution)/shard_map/ppermute | solution.py:36
  219.7 20.0 %collective-permute-start.15 = (bf16[64,2304]{1,0:T(8,128)(2,1)}, bf16[64,2304]{1,0:T(8,128)(2,1)}, u32[]{:S(2)}, u32[]{:S(2)}) collective-permute-start(bf16[64,2304]{1,0:T(8,128)(2,1)} %shard_map.167.own_ref), channel_id=1, source_target_pairs={{0,2},{1,3},{2,0},{3,1},{4,6},{5,7},{6,4},{7,5},{8,10},{9,11},{10,... | collective-permute-start | bytes 884744 | tf_op jit(solution)/shard_map/ppermute | solution.py:36
  232.3 11.7 %collective-permute-start.17 = (bf16[64,2304]{1,0:T(8,128)(2,1)}, bf16[64,2304]{1,0:T(8,128)(2,1)}, u32[]{:S(2)}, u32[]{:S(2)}) collective-permute-start(bf16[64,2304]{1,0:T(8,128)(2,1)} %collective-permute-done.16.far_ref), channel_id=1, source_target_pairs={{0,2},{1,3},{2,0},{3,1},{4,6},{5,7},{6,4},{7,5},{8,10},{9,11},{10,... | collective-permute-start | bytes 884744 | tf_op jit(solution)/shard_map/ppermute | solution.py:36
  232.3 18.1 %collective-permute-start.19 = (bf16[64,2304]{1,0:T(8,128)(2,1)}, bf16[64,2304]{1,0:T(8,128)(2,1)}, u32[]{:S(2)}, u32[]{:S(2)}) collective-permute-start(bf16[64,2304]{1,0:T(8,128)(2,1)} %shard_map.169.own_ref), channel_id=1, source_target_pairs={{0,2},{1,3},{2,0},{3,1},{4,6},{5,7},{6,4},{7,5},{8,10},{9,11},{10,... | collective-permute-start | bytes 884744 | tf_op jit(solution)/shard_map/ppermute | solution.py:36
  238.6 18.1 %collective-permute-start.21 = (bf16[64,2304]{1,0:T(8,128)(2,1)}, bf16[64,2304]{1,0:T(8,128)(2,1)}, u32[]{:S(2)}, u32[]{:S(2)}) collective-permute-start(bf16[64,2304]{1,0:T(8,128)(2,1)} %collective-permute-done.20.far_ref), channel_id=1, source_target_pairs={{0,2},{1,3},{2,0},{3,1},{4,6},{5,7},{6,4},{7,5},{8,10},{9,11},{10,... | collective-permute-start | bytes 884744 | tf_op jit(solution)/shard_map/ppermute | solution.py:36
  248.7 29.6 %copy-start.15 = (bf16[128,2304]{1,0:T(8,128)(2,1)S(1)}, bf16[128,2304]{1,0:T(8,128)(2,1)}, u32[]{:S(2)}) copy-start(bf16[128,2304]{1,0:T(8,128)(2,1)} %copy-done.14) | copy-start | bytes 1769476
  248.7 29.6 %copy-start.17 = (bf16[128,2304]{1,0:T(8,128)(2,1)S(1)}, bf16[128,2304]{1,0:T(8,128)(2,1)}, u32[]{:S(2)}) copy-start(bf16[128,2304]{1,0:T(8,128)(2,1)} %copy-done.16) | copy-start | bytes 1769476
  261.1 5.7 %collective-permute-start.24 = (f32[40,128]{1,0:T(8,128)S(1)}, f32[40,128]{1,0:T(8,128)S(1)}, u32[]{:S(2)}, u32[]{:S(2)}) collective-permute-start(f32[40,128]{1,0:T(8,128)S(1)} %pad_maximum_fusion.6), channel_id=1, source_target_pairs={{0,6},{1,7},{2,4},{3,5},{4,2},{5,3},{6,0},{7,1},{8,14},{9,15},{10,... | collective-permute-start | bytes 61448 | tf_op jit(solution)/shard_map/ppermute | solution.py:36
  263.5 3.5 %collective-permute-start.23 = (f32[40,128]{1,0:T(8,128)S(1)}, f32[40,128]{1,0:T(8,128)S(1)}, u32[]{:S(2)}, u32[]{:S(2)}) collective-permute-start(f32[40,128]{1,0:T(8,128)S(1)} %pad_maximum_fusion.5), channel_id=1, source_target_pairs={{0,4},{1,5},{2,6},{3,7},{4,0},{5,1},{6,2},{7,3},{8,12},{9,13},{10,... | collective-permute-start | bytes 61448 | tf_op jit(solution)/shard_map/ppermute | solution.py:36
  265.6 2.6 collective-permute-start.22
  268.3 12.6 %collective-permute-start.26 = (f32[32,128]{1,0:T(8,128)S(1)}, f32[32,128]{1,0:T(8,128)S(1)}, u32[]{:S(2)}, u32[]{:S(2)}) collective-permute-start(f32[32,128]{1,0:T(8,128)S(1)} %shard_map.171), channel_id=1, source_target_pairs={{0,0},{1,2},{2,4},{3,6},{4,16},{5,18},{6,20},{7,22},{8,8},{9,10},{... | collective-permute-start | bytes 49160 | tf_op jit(solution)/shard_map/ppermute | solution.py:36
  273.7 7.2 %collective-permute-start.27 = (f32[32,128]{1,0:T(8,128)S(1)}, f32[32,128]{1,0:T(8,128)S(1)}, u32[]{:S(2)}, u32[]{:S(2)}) collective-permute-start(f32[32,128]{1,0:T(8,128)S(1)} %shard_map.171), channel_id=1, source_target_pairs={{0,1},{1,3},{2,5},{3,7},{4,17},{5,19},{6,21},{7,23},{8,9},{9,11},{... | collective-permute-start | bytes 49160 | tf_op jit(solution)/shard_map/ppermute | solution.py:36
  279.4 8.5 %copy-start.24 = (f32[32,288]{0,1:T(8,128)S(1)}, f32[32,288]{0,1:T(8,128)}, u32[]{:S(2)}) copy-start(f32[32,288]{0,1:T(8,128)} %reshape.52) | copy-start | bytes 110596
  279.4 8.5 %copy-start.25 = (f32[1,32,128]{2,1,0:T(8,128)S(1)}, f32[1,32,128]{2,1,0:T(8,128)}, u32[]{:S(2)}) copy-start(f32[1,32,128]{2,1,0:T(8,128)} %param.29) | copy-start | bytes 49156
  279.4 8.5 %copy-start.29 = (f32[32]{0:T(128)S(1)}, f32[32]{0:T(128)}, u32[]{:S(2)}) copy-start(f32[32]{0:T(128)} %param.28) | copy-start | bytes 388
  279.4 7.0 %collective-permute-start.25 = (f32[32,128]{1,0:T(8,128)S(1)}, f32[32,128]{1,0:T(8,128)S(1)}, u32[]{:S(2)}, u32[]{:S(2)}) collective-permute-start(f32[32,128]{1,0:T(8,128)S(1)} %shard_map.171), channel_id=1, source_target_pairs={{1,1},{2,3},{3,5},{5,17},{6,19},{7,21},{9,9},{10,11},{11,13},{13,2... | collective-permute-start | bytes 49160 | tf_op jit(solution)/shard_map/ppermute | solution.py:36
  (12 other events, 15.1 us)
Sparse Core Ops, SparseCore 0:
  12.0 49.8 all-gather.2
  63.5 61.4 all-gather.4

commit v2 on v0

v2 whole, which is shorter than its diff:
```python
import functools

import jax
import jax.numpy as jnp
from jax import lax
from jax.experimental import pallas as pl
from jax.experimental.pallas import tpu as pltpu
from jax.sharding import PartitionSpec as P

SIDE = 32
NEW = 1024
GUIDE = 1.5
CHUNKS = 2
FLOWS = 4
HEAD_FLOWS = 2


def norm_rows(values):
    row_mean = jnp.mean(values, axis=-1, keepdims=True)
    centred = values - row_mean
    spread = jnp.mean(centred * centred, axis=-1, keepdims=True)
    return centred * lax.rsqrt(spread + 1e-06)


def modulate(values, ada):
    return norm_rows(values.astype(jnp.float32)) * (1.0 + ada[1]) + ada[0]


def permute_devices(value, dp, mp, target):
    pairs = []
    for d in range(dp):
        for m in range(mp):
            to = target(d, m)
            if to is not None:
                pairs.append((d * mp + m, to[0] * mp + to[1]))
    return lax.ppermute(value, ("dp", "mp"), pairs)


def general_body(
    tokens,
    ada_ffn,
    ffn_gate,
    up_weight,
    up_bias,
    down_weight,
    down_bias,
    ada_head,
    head_weight,
    head_bias,
    gumbel_noise,
    codebook,
    phi_weight,
    phi_bias,
    f_hat,
):
    rows, width = tokens.shape
    dp, mp = lax.axis_size("dp"), lax.axis_size("mp")
    d_index, m_index = lax.axis_index("dp"), lax.axis_index("mp")
    images = ada_ffn.shape[0]
    pairs = f_hat.shape[0]
    channels = f_hat.shape[1]
    vocab = head_weight.shape[1]
    own_image = (m_index * rows) // NEW
    ada_own = lax.dynamic_index_in_dim(ada_ffn, own_image, 0, keepdims=False)
    gate_own = lax.dynamic_index_in_dim(ffn_gate, own_image, 0, keepdims=False)
    head_own = lax.dynamic_index_in_dim(ada_head, own_image, 0, keepdims=False)
    half_dp, half_mp = dp // 2, mp // 2
    upper = d_index // half_dp

    def swap(d, m):
        return ((d + half_dp) % dp, m)

    def cross(d, m):
        if d // half_dp == m // half_mp:
            return None
        return ((d + half_dp) % dp, (m + half_mp) % mp)

    stays = upper == m_index // half_mp
    head_twin = permute_devices(head_own, dp, mp, swap)
    head_cond = jnp.where(upper == 0, head_own, head_twin)
    head_uncond = jnp.where(upper == 0, head_twin, head_own)

    step = rows // FLOWS
    normed = modulate(tokens, ada_own).astype(jnp.bfloat16)
    outs = []
    for c in range(FLOWS):
        part = lax.slice_in_dim(normed, c * step, (c + 1) * step, axis=0)
        gathered = lax.all_gather(part, "mp", axis=0, tiled=True)
        hidden = jax.nn.gelu(
            jnp.dot(gathered, up_weight, preferred_element_type=jnp.float32) + up_bias,
            approximate=True,
        ).astype(jnp.bfloat16)
        partial = jnp.dot(hidden, down_weight, preferred_element_type=jnp.float32).astype(jnp.bfloat16)
        summed = lax.psum_scatter(partial, "mp", scatter_dimension=0, tiled=True).astype(jnp.float32)
        own = lax.slice_in_dim(tokens, c * step, (c + 1) * step, axis=0).astype(jnp.float32)
        outs.append((own + gate_own * (summed + down_bias)).astype(jnp.bfloat16))
    block_out = jnp.concatenate(outs, axis=0)

    group = FLOWS // HEAD_FLOWS
    half = rows // HEAD_FLOWS // 2
    noise = gumbel_noise.reshape(pairs, NEW // rows, HEAD_FLOWS, 2, half, vocab)
    peaks, totals, codes = [], [], []
    for c in range(HEAD_FLOWS):
        part = jnp.concatenate(outs[c * group : (c + 1) * group], axis=0)
        first, second = part[:half], part[half:]
        kept = jnp.where(upper == 0, first, second)
        sent = jnp.where(upper == 0, second, first)
        came = permute_devices(sent, dp, mp, swap)
        cond = jnp.where(upper == 0, kept, came)
        uncond = jnp.where(upper == 0, came, kept)
        mixed = (
            (1.0 + GUIDE) * modulate(cond, head_cond) - GUIDE * modulate(uncond, head_uncond)
        ).astype(jnp.bfloat16)
        crossed = permute_devices(mixed, dp, mp, cross)
        mixed = jnp.where(stays, mixed, crossed)
        gathered = lax.all_gather(mixed, "mp", axis=0, tiled=True)
        logits = jnp.dot(gathered, head_weight, preferred_element_type=jnp.float32) + head_bias
        logits = logits.reshape(2, half_mp, half, vocab)
        order = jnp.transpose(logits, (1, 0, 2, 3)).reshape(pairs, NEW // rows, 2, half, vocab)
        scores = order + noise[:, :, c]
        peak = jnp.max(scores, axis=-1)
        weights = jnp.exp(scores - peak[..., None]).astype(jnp.bfloat16)
        totals.append(jnp.sum(weights.astype(jnp.float32), axis=-1))
        codes.append(jnp.dot(weights, codebook, preferred_element_type=jnp.float32))
        peaks.append(peak)
    stack = lambda parts: jnp.stack(parts, axis=2)
    peak = stack(peaks).reshape(pairs, 1, NEW)
    total = stack(totals).reshape(pairs, 1, NEW)
    code = stack(codes).reshape(pairs, NEW, channels).transpose(0, 2, 1)
    stats = jnp.concatenate([code, total, peak], axis=1)

    cells = f_hat.shape[2]
    band = cells // SIDE
    padded = jnp.pad(stats, ((0, 0), (0, 0), (SIDE, SIDE)))
    windows = jnp.stack(
        [padded[:, :, m * cells : m * cells + cells + 2 * SIDE] for m in range(mp)], axis=0
    )
    parts = lax.all_to_all(windows, "mp", 0, 0, tiled=True)
    top = jnp.max(parts[:, :, channels + 1], axis=0)
    factor = jnp.exp(parts[:, :, channels + 1] - top[None])[:, :, None]
    sums = jnp.sum(parts[:, :, : channels + 1] * factor, axis=0)
    cell_index = m_index * cells - SIDE + jnp.arange(cells + 2 * SIDE)
    inside = (cell_index >= 0) & (cell_index < NEW)
    soft = jnp.where(inside, sums[:, :channels] / jnp.where(inside, sums[:, channels:], 1.0), 0.0)
    code_map = soft.reshape(pairs, channels, band + 2, SIDE)
    wide = jnp.pad(code_map, ((0, 0), (0, 0), (0, 0), (1, 1)))
    taps = jnp.stack(
        [wide[:, :, i : i + band, j : j + SIDE] for i in range(3) for j in range(3)], axis=2
    ).reshape(pairs, channels * 9, cells)
    conv = jnp.einsum(
        "ok,pkn->pon",
        phi_weight.reshape(channels, channels * 9),
        taps,
        precision=lax.Precision.HIGHEST,
        preferred_element_type=jnp.float32,
    ) + phi_bias[None, :, None]
    f_hat_out = f_hat + 0.5 * soft[:, :, SIDE : SIDE + cells] + 0.5 * conv
    return (block_out, f_hat_out)


SCALARS = pl.BlockSpec(memory_space=pltpu.SMEM)
ON_CHIP = pl.BlockSpec(memory_space=pltpu.VMEM)
VMEM_LIMIT = 16 * 1024 * 1024
MID, UPPER, IMAGE, ODD, SAME, CORE = range(6)


def call(kernel, where, args, outs, scratch=()):
    return pl.pallas_call(
        kernel,
        out_shape=outs,
        in_specs=[SCALARS] + [ON_CHIP] * len(args),
        out_specs=[ON_CHIP] * len(outs),
        scratch_shapes=scratch,
        compiler_params=pltpu.CompilerParams(vmem_limit_bytes=VMEM_LIMIT),
        cost_estimate=pl.CostEstimate(flops=0, bytes_accessed=0, transcendentals=0),
    )(where, *args)


def shape_of(shape, kind=jnp.bfloat16):
    return jax.ShapeDtypeStruct(shape, kind)


def after(value, *others):
    return lax.optimization_barrier((value, *others))[0]


def modulated(values, ada_ref, image):
    shift, scale = ada_ref[image, 0:1, :], ada_ref[image, 1:2, :]
    return norm_rows(values.astype(jnp.float32)) * (1.0 + scale) + shift


def norm_kernel(begin, where_ref, tokens_ref, ada_ref, out_ref):
    values = tokens_ref[begin : begin + out_ref.shape[0], :]
    out_ref[...] = modulated(values, ada_ref, where_ref[IMAGE]).astype(jnp.bfloat16)


def norm_part(where, tokens, ada, begin, size):
    outs = [shape_of((size, tokens.shape[1]))]
    return call(functools.partial(norm_kernel, begin), where, (tokens, ada), outs)[0]


def ffn_kernel(groups, tile, where_ref, *refs):
    count = sum(groups)
    parts = refs[:count]
    up_a, up_b, down_a, down_b, bias_a, bias_b = refs[count : count + 6]
    outs = refs[count + 6 : count + 6 + len(groups)]
    x_ref, hidden_ref = refs[count + 6 + len(groups) :]
    panel, width = down_a.shape
    step = outs[0].shape[0]
    place = 0
    for g, size in enumerate(groups):
        if size == 1:
            value = parts[place][...]
        else:
            value = jnp.where(where_ref[MID] == 1, parts[place][...], parts[place + 1][...])
        x_ref[g * step : (g + 1) * step, :] = value
        place += size

    def columns(first, second, begin, end):
        if end <= panel:
            return first[:, begin:end]
        if begin >= panel:
            return second[:, begin - panel : end - panel]
        return jnp.concatenate([first[:, begin:panel], second[:, : end - panel]], axis=1)

    for begin in range(0, 2 * panel, tile):
        end = begin + tile
        v = jnp.dot(x_ref[...], columns(up_a, up_b, begin, end), preferred_element_type=jnp.float32)
        v = v + columns(bias_a, bias_b, begin, end)
        hidden_ref[:, begin:end] = jax.nn.gelu(v, approximate=True).astype(jnp.bfloat16)
    for begin in range(0, width, tile):
        cols = slice(begin, begin + tile)
        weight = jnp.concatenate([down_a[:, cols], down_b[:, cols]], axis=0)
        result = jnp.dot(hidden_ref[...], weight, preferred_element_type=jnp.float32)
        for g in range(len(groups)):
            outs[g][:, cols] = result[g * step : (g + 1) * step].astype(jnp.bfloat16)


def ffn(where, slots, panels):
    groups = tuple(len(slot) for slot in slots)
    parts = [part for slot in slots for part in slot]
    rows, width = parts[0].shape
    total = rows * len(slots)
    return call(
        functools.partial(ffn_kernel, groups, 256),
        where,
        (*parts, *panels),
        [shape_of((rows, width))] * len(slots),
        scratch=[
            pltpu.VMEM((total, width), jnp.bfloat16),
            pltpu.VMEM((total, 2 * panels[2].shape[0]), jnp.bfloat16),
        ],
    )


def add_kernel(always, where_ref, a_ref, b_ref, out_ref):
    b = b_ref[...].astype(jnp.float32)
    if not always:
        b = jnp.where(where_ref[MID] == 1, b, 0.0)
    out_ref[...] = (a_ref[...].astype(jnp.float32) + b).astype(jnp.bfloat16)


def add(where, a, b, always=False):
    return call(functools.partial(add_kernel, always), where, (a, b), [shape_of(a.shape)])[0]


def out_kernel(begin, always, where_ref, own_ref, near_ref, far_ref, tokens_ref, gate_ref, bias_ref, *refs):
    out_ref, kept_ref, sent_ref = refs[-3:]
    far = far_ref[...].astype(jnp.float32)
    if not always:
        far = jnp.where(where_ref[MID] == 1, far, 0.0)
    summed = own_ref[...].astype(jnp.float32) + near_ref[...].astype(jnp.float32) + far
    rows = summed.shape[0]
    tokens = tokens_ref[begin : begin + rows, :].astype(jnp.float32)
    gate = gate_ref[pl.ds(where_ref[IMAGE], 1), :]
    value = (tokens + gate * (summed + bias_ref[...])).astype(jnp.bfloat16)
    if len(refs) > 3:
        out_ref[0:begin, :] = refs[0][...]
        out_ref[begin : begin + rows, :] = value
    else:
        out_ref[...] = value
    half = rows // 2
    lower = where_ref[UPPER] == 0
    kept_ref[...] = jnp.where(lower, value[:half], value[half:])
    sent_ref[...] = jnp.where(lower, value[half:], value[:half])


def block_rows(where, begin, always, own, near, far, tokens, gate, bias, earlier=()):
    rows, width = own.shape
    full = rows + begin if earlier else rows
    return call(
        functools.partial(out_kernel, begin, always),
        where,
        (own, near, far, tokens, gate, bias, *earlier),
        [shape_of((full, width)), shape_of((rows // 2, width)), shape_of((rows // 2, width))],
    )


def mix_kernel(where_ref, kept_ref, came_ref, ada_ref, twin_ref, out_ref):
    image = where_ref[IMAGE]
    kept, came = modulated(kept_ref[...], ada_ref, image), modulated(came_ref[...], twin_ref, image)
    lower = where_ref[UPPER] == 0
    share = jnp.where(lower, 1.0 + GUIDE, -GUIDE)
    other = jnp.where(lower, -GUIDE, 1.0 + GUIDE)
    out_ref[...] = (share * kept + other * came).astype(jnp.bfloat16)


def mix_twins(where, kept, came, ada, twin):
    return call(mix_kernel, where, (kept, came, ada, twin), [shape_of(kept.shape)])[0]


def head_kernel(
    begin, where_ref, own_ref, near_ref, far_ref, last_ref, weight_a, weight_b, bias_a, bias_b, code_a, code_b,
    noise_own, noise_core, noise_twin, noise_both, stats_ref, x_ref
):
    step = own_ref.shape[0]
    for r, ref in enumerate((own_ref, near_ref, far_ref, last_ref)):
        x_ref[r * step : (r + 1) * step, :] = ref[...]
    x = x_ref[...]
    odd = where_ref[ODD]
    even = 1 - odd
    same = where_ref[SAME] == 1
    scores = []
    for weight, bias, ours, theirs in (
        (weight_a, bias_a, noise_own, noise_twin),
        (weight_b, bias_b, noise_core, noise_both),
    ):
        picked = []
        for first in (True, False):
            for block in (odd, even):
                a, b = ours[block, begin : begin + step, :], theirs[block, begin : begin + step, :]
                picked.append(jnp.where(same, a, b) if first else jnp.where(same, b, a))
        logits = jnp.dot(x, weight[...], preferred_element_type=jnp.float32)
        scores.append(logits + bias[:, bias.shape[1] - weight.shape[1] :] + jnp.concatenate(picked, axis=0))
    peak = jnp.max(jnp.maximum(scores[0], scores[1]), axis=1, keepdims=True)
    sums = 0.0
    total = 0.0
    for score, code in zip(scores, (code_a, code_b)):
        weights = jnp.exp(score - peak).astype(jnp.bfloat16)
        total = total + jnp.sum(weights.astype(jnp.float32), axis=1, keepdims=True)
        sums = sums + lax.dot_general(
            weights, code[...], (((1,), (1,)), ((), ())), preferred_element_type=jnp.float32
        )
    channels = code_a.shape[0]
    pad = jnp.zeros((4 * step, 128 - channels), jnp.float32)
    table = jnp.concatenate([sums, pad], axis=1)
    lane = lax.broadcasted_iota(jnp.int32, table.shape, 1)
    table = jnp.where(lane == channels, total, table)
    table = jnp.where(lane == channels + 1, peak, table)
    stats_ref[...] = jnp.transpose(table)[: stats_ref.shape[0], :]


def head_stats(where, begin, slots, heads, noises):
    step, width = slots[0].shape
    height = -(-(heads[-1].shape[0] + 2) // 8) * 8
    return call(
        functools.partial(head_kernel, begin),
        where,
        (*slots, *heads, *noises),
        [shape_of((height, 4 * step), jnp.float32)],
        scratch=[pltpu.VMEM((4 * step, width), jnp.bfloat16)],
    )[0]


def soft_kernel(channels, where_ref, *refs):
    parts, out_ref = refs[:-1], refs[-1]
    tops = [part[channels + 1 : channels + 2, :] for part in parts]
    top = functools.reduce(jnp.maximum, tops)
    code = 0.0
    total = 0.0
    for part, peak in zip(parts, tops):
        factor = jnp.exp(peak - top)
        code = code + part[0:channels, :] * factor
        total = total + part[channels : channels + 1, :] * factor
    out_ref[...] = code / total


def soft_codes(where, parts, channels):
    outs = [shape_of((channels, parts[0].shape[1]), jnp.float32)]
    return call(functools.partial(soft_kernel, channels), where, tuple(parts), outs)[0]


def refine_kernel(where_ref, first_ref, second_ref, halo_ref, phi_ref, bias_ref, map_ref, out_ref):
    first, second, halo = first_ref[...], second_ref[...], halo_ref[...]
    cells = first.shape[1]
    half = cells // 2
    lane = lax.broadcasted_iota(jnp.int32, first.shape, 1)
    shift = lambda value, by: pltpu.roll(value, by % cells, 1)
    early = where_ref[CORE] == 0
    lower, higher = jnp.where(early, first, second), jnp.where(early, second, first)
    centre = jnp.where(
        early,
        jnp.where(lane < half, lower, shift(higher, half)),
        jnp.where(lane < half, shift(lower, half), higher),
    )
    above = jnp.where(early, shift(halo, SIDE), shift(higher, SIDE - half))
    below = jnp.where(early, shift(lower, half - SIDE), shift(halo, -SIDE))
    rows = (
        jnp.where(lane < SIDE, above, shift(centre, SIDE)),
        centre,
        jnp.where(lane >= cells - SIDE, below, shift(centre, -SIDE)),
    )
    column = lane % SIDE
    conv = jnp.zeros(out_ref.shape, jnp.float32) + bias_ref[...]
    for i, row in enumerate(rows):
        left = jnp.where(column == 0, 0.0, shift(row, 1))
        right = jnp.where(column == SIDE - 1, 0.0, shift(row, -1))
        for j, tap in enumerate((left, row, right)):
            conv = conv + jnp.dot(
                phi_ref[i, j], tap, precision=lax.Precision.HIGHEST, preferred_element_type=jnp.float32
            )
    out_ref[...] = map_ref[...] + 0.5 * centre + 0.5 * conv


def line_body(
    tokens,
    ada_ffn,
    ffn_gate,
    up_weight,
    up_bias,
    down_weight,
    down_bias,
    ada_head,
    head_weight,
    head_bias,
    gumbel_noise,
    codebook,
    phi_weight,
    phi_bias,
    f_hat,
):
    rows = tokens.shape[0]
    dp, mp = lax.axis_size("dp"), lax.axis_size("mp")
    d_index, m_index = lax.axis_index("dp"), lax.axis_index("mp")
    channels = f_hat.shape[1]
    half_dp = dp // 2
    upper = d_index // half_dp
    z_index, core = m_index // 2, m_index % 2
    where = jnp.stack(
        [
            (z_index == 1) | (z_index == 2),
            upper,
            (m_index * rows) // NEW,
            z_index % 2,
            z_index // 2 == upper,
            core,
        ]
    ).astype(jnp.int32)

    def along_z(value, target):
        def to(d, m):
            z = target(m // 2)
            return None if z is None else (d, 2 * z + m % 2)

        return permute_devices(value, dp, mp, to)

    def near(value):
        return along_z(value, lambda z: z ^ 1)

    def across(value):
        return along_z(value, lambda z: z ^ 2)

    def middle(value):
        return along_z(value, lambda z: 3 - z if z in (1, 2) else z)

    def outward(value):
        return along_z(value, lambda z: {1: 0, 2: 3}.get(z))

    def inward(value):
        return along_z(value, lambda z: {0: 1, 3: 2}.get(z))

    def swap_cores(value):
        return permute_devices(value, dp, mp, lambda d, m: (d, m ^ 1))

    def swap_twins(value):
        return permute_devices(value, dp, mp, lambda d, m: ((d + half_dp) % dp, m))

    def swap_both(value):
        return permute_devices(value, dp, mp, lambda d, m: ((d + half_dp) % dp, m ^ 1))

    step = rows // CHUNKS
    half = step // 2
    voc = head_bias.shape[0]
    noise = gumbel_noise.reshape(2, 2, CHUNKS, 2, half, voc)

    def noise_for(to_core, to_upper):
        picked = lax.dynamic_slice(
            noise, (0, to_core, 0, to_upper, 0, 0), (2, 1, CHUNKS, 1, half, voc)
        )
        return picked.reshape(2, CHUNKS * half, voc)

    gate, bias_out = ffn_gate, down_bias[None]
    up_other, down_other = swap_cores(up_weight), swap_cores(down_weight)
    biases = jnp.concatenate([up_bias, head_bias])[None]
    codes = codebook.T
    bias_other = swap_cores(biases)

    own_a = norm_part(where, tokens, ada_ffn, 0, step)
    near_a, far_a = near(own_a), across(own_a)
    own_b = norm_part(where, tokens, ada_ffn, step, step)
    up_other, down_other, bias_other, near_a, far_a = lax.optimization_barrier(
        (up_other, down_other, bias_other, near_a, far_a)
    )
    panels = (up_weight, up_other, down_weight, down_other, biases, bias_other)
    last_a = near(far_a)
    mid_b = middle(after(own_b, far_a))
    noise_twin = swap_twins(after(noise_for(core, 1 - upper), far_a))
    sum_own_a, sum_near_a = ffn(where, [[own_a], [near_a]], panels)
    noise_core = swap_cores(after(noise_for(1 - core, upper), noise_twin))
    (sum_far_a,) = ffn(where, [[after(far_a, sum_near_a, noise_twin)]], panels)
    came_far_a = inward(sum_far_a)
    near_b = near(after(own_b, last_a))
    (sum_last_a,) = ffn(where, [[after(last_a, sum_far_a)]], panels)
    came_last_a = inward(sum_last_a)
    mid_b, near_b = lax.optimization_barrier((mid_b, near_b, sum_last_a))[:2]
    far_mid_b, far_end_b = middle(near_b), outward(mid_b)
    noise_both = swap_both(after(noise_for(1 - core, 1 - upper), noise_core))
    sum_own_b, sum_near_b = ffn(where, [[own_b], [after(near_b, noise_core)]], panels)
    both_last_a = add(where, after(sum_last_a, sum_near_b), came_far_a)
    went_last_a = middle(both_last_a)
    far_mid_b, far_end_b = lax.optimization_barrier((far_mid_b, far_end_b, both_last_a))[:2]
    last_end_b = outward(far_mid_b)
    (sum_far_b,) = ffn(where, [[far_mid_b, far_end_b]], panels)
    both_far_a = add(where, after(sum_far_a, sum_far_b), came_last_a)
    went_far_a = middle(both_far_a)
    (sum_last_b,) = ffn(where, [[after(mid_b, both_far_a, noise_both, went_last_a), last_end_b]], panels)
    came_last_b = near(sum_last_b)
    head_other = swap_cores(after(head_weight, sum_last_b))
    head_twin = swap_twins(after(ada_head, sum_last_b))
    code_other = swap_cores(after(codes, sum_last_b))
    both_far_b = add(where, sum_far_b, came_last_b, True)
    went_far_b = across(both_far_b)
    came_near_b = near(after(sum_near_b, both_far_b))
    both_near_a = add(where, sum_near_a, after(went_far_a, went_last_a, both_far_b))
    came_near_a = near(both_near_a)
    out_a, kept_a, sent_a = block_rows(
        where, 0, False, sum_own_a, after(came_near_a, head_twin), went_last_a, tokens, gate, bias_out
    )
    came_a = swap_twins(sent_a)
    mixed_a = mix_twins(where, kept_a, came_a, ada_head, head_twin)
    mix_near_a, mix_far_a = near(mixed_a), across(mixed_a)
    block_out, kept_b, sent_b = block_rows(
        where, step, True, sum_own_b, after(came_near_b, mix_far_a, mix_near_a, head_other, code_other), went_far_b, tokens, gate, bias_out, (out_a,)
    )
    came_b = swap_twins(sent_b)
    mix_last_a = near(after(mix_far_a, sent_b))
    mixed_b = mix_twins(where, kept_b, came_b, ada_head, head_twin)
    mix_near_b, mix_far_b = near(mixed_b), across(mixed_b)
    heads = (head_weight, head_other, biases, bias_other, codes, code_other)
    noises = (noise_for(core, upper), noise_core, noise_twin, noise_both)
    stats_a = head_stats(
        where, 0, (after(mixed_a, mixed_b), mix_near_a, mix_far_a, mix_last_a), heads, noises
    )
    mix_last_b = near(mix_far_b)
    stats_b = head_stats(where, half, (after(mixed_b, stats_a), mix_near_b, mix_far_b, mix_last_b), heads, noises)

    slots = [
        jnp.concatenate([part[:, r * half : (r + 1) * half] for part in (stats_a, stats_b)], axis=1) for r in range(4)
    ]
    parts = [slots[0]] + [along_z(slots[r], lambda z, r=r: z ^ r) for r in (1, 2, 3)]
    soft = soft_codes(where, parts, channels)

    def to_cells(d, m, core_of):
        y, x = d // half_dp, d % half_dp
        z, c = m // 2, m % 2
        return ((z // 2) * half_dp + x, 2 * (2 * (z % 2) + c) + core_of(y))

    def to_halo(d, m):
        y, x = d // half_dp, d % half_dp
        z, c = m // 2, m % 2
        block = 2 * (z % 2) + c + (1 if y == 1 else -1)
        if block < 0 or block > 3:
            return None
        return ((z // 2) * half_dp + x, 2 * block + (0 if y == 1 else 1))

    first = permute_devices(soft, dp, mp, lambda d, m: to_cells(d, m, lambda y: y))
    second = permute_devices(soft, dp, mp, lambda d, m: to_cells(d, m, lambda y: 1 - y))
    halo = permute_devices(soft, dp, mp, to_halo)
    f_hat_out = call(
        refine_kernel,
        where,
        (first, second, halo, jnp.transpose(phi_weight, (2, 3, 0, 1)), phi_bias[:, None], f_hat[0]),
        [shape_of(f_hat.shape[1:], jnp.float32)],
    )[0]
    return (block_out, f_hat_out[None])


def solution(mesh):
    in_specs = (
        P(("dp", "mp"), None),
        P("dp", None, None),
        P("dp", None),
        P(None, "mp"),
        P("mp"),
        P("mp", None),
        P(),
        P("dp", None, None),
        P(None, "mp"),
        P("mp"),
        P("dp", None, "mp"),
        P("mp", None),
        P(),
        P(),
        P("dp", None, "mp"),
    )
    out_specs = (P(("dp", "mp"), None), P("dp", None, "mp"))
    line = mesh.shape["dp"] == 4 and mesh.shape["mp"] == 8
    body = line_body if line else general_body
    return jax.shard_map(body, mesh=mesh, in_specs=in_specs, out_specs=out_specs, check_vma=False)
```

time: 269 us -> 263 us (0.978)
  waiting for transfers between devices: 88.2 us -> 117 us
  local copies, waits for them, and re-layouts: 25.3 us -> 9.96 us
  starting transfers between devices: 78.6 us -> 66.9 us
  other arithmetic: 4.03 us -> 1.03 us
    ppermute x46 -> x39, waiting for transfers between devices: 88.2 us -> 117 us  [permute_devices(): return lax.ppermute(value, ('dp', 'mp'), pairs)]
    ppermute x46 -> x39, starting transfers between devices: 78.6 us -> 66.9 us  [permute_devices(): return lax.ppermute(value, ('dp', 'mp'), pairs)]
    unnamed x92 -> x36, local copies, waits for them, and re-layouts: 17.1 us -> 7.89 us
    slice x8 -> x0, local copies, waits for them, and re-layouts: 3.89 us -> none  [the longest x1 1.33 us: line_body(): rows_a, rows_b = (tokens[:step], tokens[step:])]
    reshape x5 -> x0, local copies, waits for them, and re-layouts: 3.86 us -> none  [the longest x1 1.64 us: line_body(): phi_weight.reshape(channels, channels * 9)]
    pallas_call x21 -> x20, Pallas kernels: 67.9 us -> 66.6 us  [call(): pl.pallas_call(kernel, out_shape=outs, in_specs=[SCALARS] + [ON_CHIP] * l...]
  transfers between devices with their start and end apart: 46 -> 39, of which waited for: 17 -> 18; matrix products, arithmetic and copies ran while one was open for 5% -> 1% of each run, Pallas kernels for 21% -> 20%
where the time goes in v2:
time: 263 us
  waiting for transfers between devices  117 us (44%)
  starting transfers between devices  66.9 us (25%)
  Pallas kernels  66.6 us (25%)
  local copies, waits for them, and re-layouts  9.96 us (4%)
    ppermute x39, waiting for transfers between devices, permute_devices(): return lax.ppermute(value, ('dp', 'mp'), pairs)  117 us
    ppermute x39, starting transfers between devices, permute_devices(): return lax.ppermute(value, ('dp', 'mp'), pairs)  66.9 us
    pallas_call x20, Pallas kernels, call(): pl.pallas_call(kernel, out_shape=outs, in_specs=[SCALARS] + [ON_CHIP] * l...  66.6 us
    unnamed x36, local copies, waits for them, and re-layouts  7.89 us
  transfers between devices with their start and end apart: 39, of which 18 were waited for; matrix products, arithmetic and copies ran while one was open for 1% of the time, Pallas kernels for 20%

profile of v2, /device:TPU:13, one launch (start us, length us, event | category | flops | bytes accessed | tf_op | source)
XLA Modules:
  0.0 262.7 jit_solution(2261842224087763718)
XLA Ops:
  4.8 2.3 collective-permute-start.4
  9.8 19.8 %collective-permute-done.3.refs_1_ = bf16[128,2304]{1,0:T(8,128)(2,1)S(1)} collective-permute-done((bf16[128,2304]{1,0:T(8,128)(2,1)S(1)}, bf16[128,2304]{1,0:T(8,128)(2,1)S(1)}, u32[]{:S(2)}, u32[]{:S(2)}) %collective-permute-start.3) | collective-permute-done | bytes 589856 | tf_op jit(solution)/shard_map/ppermute | solution.py:36
  29.6 3.2 %collective-permute-done.4.refs_0_ = bf16[128,2304]{1,0:T(8,128)(2,1)S(1)} collective-permute-done((bf16[128,2304]{1,0:T(8,128)(2,1)S(1)}, bf16[128,2304]{1,0:T(8,128)(2,1)S(1)}, u32[]{:S(2)}, u32[]{:S(2)}) %collective-permute-start.4) | collective-permute-done | bytes 589856 | tf_op jit(solution)/shard_map/ppermute | solution.py:36
  34.6 4.3 %collective-permute-start.5 = (bf16[128,2304]{1,0:T(8,128)(2,1)S(1)}, bf16[128,2304]{1,0:T(8,128)(2,1)S(1)}, u32[]{:S(2)}, u32[]{:S(2)}) collective-permute-start(bf16[128,2304]{1,0:T(8,128)(2,1)S(1)} %shard_map.158.refs_0_), channel_id=1, source_target_pairs={{0,0},{1,1},{2,4},{3,5},{4,2},{5,3},{6,6},{7,7},{8,8},{9,9},{10,12... | collective-permute-start | bytes 1769480 | tf_op jit(solution)/shard_map/ppermute | solution.py:36
  38.9 7.4 %collective-permute-done.6.refs_0_ = bf16[128,2304]{1,0:T(8,128)(2,1)S(1)} collective-permute-done((bf16[128,2304]{1,0:T(8,128)(2,1)S(1)}, bf16[128,2304]{1,0:T(8,128)(2,1)S(1)}, u32[]{:S(2)}, u32[]{:S(2)}) %collective-permute-start.6) | collective-permute-done | bytes 589856 | tf_op jit(solution)/shard_map/ppermute | solution.py:36
  46.3 1.7 constant_dynamic-slice_fusion
  48.3 2.5 copy-done
  50.9 2.5 copy-done.1
  53.4 10.0 %shard_map.160 = (bf16[128,2304]{1,0:T(8,128)(2,1)S(1)}, bf16[128,2304]{1,0:T(8,128)(2,1)S(1)}) custom-call(s32[6]{0:T(128)S(1)} %stack.35.where_ref, bf16[128,2304]{1,0:T(8,128)(2,1)S(1)} %shard_map.159.refs_0_, bf16[128,2304]{1,0:T(8,128)(2,1)S(1)} %collective-permute-done.3.refs_1_, bf16[2304,1152]{1,0:T(8,128)(2,1)S(1)} %copy-done, ...), custom_call_target="tpu_custom_call" | custom-call | tf_op jit(solution)/shard_map/pallas_call | solution.py:168
  63.4 7.4 %shard_map.161.a_ref = bf16[128,2304]{1,0:T(8,128)(2,1)S(1)} custom-call(s32[6]{0:T(128)S(1)} %stack.35.where_ref, bf16[128,2304]{1,0:T(8,128)(2,1)S(1)} %collective-permute-done.4.refs_0_, bf16[2304,1152]{1,0:T(8,128)(2,1)S(1)} %copy-done, bf16[2304,1152]{1,0:T(8,128)(2,1)} %collective-permute-done.refs_3_.refs_2_, bf16[1152,2304]{1,0:T(8,128)(2,1)S(1)} %copy-done.1, ...), custom_call_target="tpu_custom_call" | custom-call | tf_op jit(solution)/shard_map/pallas_call | solution.py:168
  70.9 1.6 collective-permute-start.12
  72.5 7.3 %shard_map.162.a_ref = bf16[128,2304]{1,0:T(8,128)(2,1)S(1)} custom-call(s32[6]{0:T(128)S(1)} %stack.35.where_ref, bf16[128,2304]{1,0:T(8,128)(2,1)S(1)} %collective-permute-done.6.refs_0_, bf16[2304,1152]{1,0:T(8,128)(2,1)S(1)} %copy-done, bf16[2304,1152]{1,0:T(8,128)(2,1)} %collective-permute-done.refs_3_.refs_2_, bf16[1152,2304]{1,0:T(8,128)(2,1)S(1)} %copy-done.1, ...), custom_call_target="tpu_custom_call" | custom-call | tf_op jit(solution)/shard_map/pallas_call | solution.py:168
  79.8 4.1 %collective-permute-start.10 = (bf16[128,2304]{1,0:T(8,128)(2,1)S(1)}, bf16[128,2304]{1,0:T(8,128)(2,1)S(1)}, u32[]{:S(2)}, u32[]{:S(2)}) collective-permute-start(bf16[128,2304]{1,0:T(8,128)(2,1)S(1)} %collective-permute-done.7.refs_1_), channel_id=1, source_target_pairs={{0,0},{1,1},{2,4},{3,5},{4,2},{5,3},{6,6},{7,7},{8,8},{9,9},{10,12... | collective-permute-start | bytes 1769480 | tf_op jit(solution)/shard_map/ppermute | solution.py:36
  83.9 1.3 collective-permute-start.11
  85.2 3.4 %collective-permute-start.9 = (f32[2,128,512]{2,1,0:T(8,128)S(1)}, f32[2,128,512]{2,1,0:T(8,128)S(1)}, u32[]{:S(2)}, u32[]{:S(2)}) collective-permute-start(f32[2,128,512]{2,1,0:T(8,128)S(1)} %bitcast.37), channel_id=1, source_target_pairs={{0,1},{1,0},{2,3},{3,2},{4,5},{5,4},{6,7},{7,6},{8,9},{9,8},{10,11... | collective-permute-start | bytes 1572872 | tf_op jit(solution)/shard_map/ppermute | solution.py:36
  90.1 10.0 %shard_map.163 = (bf16[128,2304]{1,0:T(8,128)(2,1)S(1)}, bf16[128,2304]{1,0:T(8,128)(2,1)S(1)}) custom-call(s32[6]{0:T(128)S(1)} %stack.35.where_ref, bf16[128,2304]{1,0:T(8,128)(2,1)S(1)} %shard_map.158.refs_0_, bf16[128,2304]{1,0:T(8,128)(2,1)S(1)} %collective-permute-done.7.refs_1_, bf16[2304,1152]{1,0:T(8,128)(2,1)S(1)} %bitcast.25, ...), custom_call_target="tpu_custom_call" | custom-call | tf_op jit(solution)/shard_map/pallas_call | solution.py:168
  100.9 3.7 %collective-permute-start.15 = (bf16[128,2304]{1,0:T(8,128)(2,1)S(1)}, bf16[128,2304]{1,0:T(8,128)(2,1)S(1)}, u32[]{:S(2)}, u32[]{:S(2)}) collective-permute-start(bf16[128,2304]{1,0:T(8,128)(2,1)S(1)} %shard_map.164), channel_id=1, source_target_pairs={{0,0},{1,1},{2,4},{3,5},{4,2},{5,3},{6,6},{7,7},{8,8},{9,9},{10,12... | collective-permute-start | bytes 1769480 | tf_op jit(solution)/shard_map/ppermute | solution.py:36
  104.7 1.5 collective-permute-start.16
  106.2 1.8 collective-permute-start.14
  108.1 7.2 %shard_map.165.a_ref = bf16[128,2304]{1,0:T(8,128)(2,1)S(1)} custom-call(s32[6]{0:T(128)S(1)} %stack.35.where_ref, bf16[128,2304]{1,0:T(8,128)(2,1)S(1)} %collective-permute-done.10.refs_0_, bf16[128,2304]{1,0:T(8,128)(2,1)S(1)} %collective-permute-done.11.refs_1_, bf16[2304,1152]{1,0:T(8,128)(2,1)S(1)} %bitcast.25, ...), custom_call_target="tpu_custom_call" | custom-call | tf_op jit(solution)/shard_map/pallas_call | solution.py:168
  116.0 4.7 %collective-permute-done.14.noise_both = f32[2,128,512]{2,1,0:T(8,128)S(1)} collective-permute-done((f32[2,128,512]{2,1,0:T(8,128)S(1)}, f32[2,128,512]{2,1,0:T(8,128)S(1)}, u32[]{:S(2)}, u32[]{:S(2)}) %collective-permute-start.14) | collective-permute-done | bytes 524320 | tf_op jit(solution)/shard_map/ppermute | solution.py:36
  120.7 7.2 %shard_map.167 = bf16[128,2304]{1,0:T(8,128)(2,1)S(1)} custom-call(s32[6]{0:T(128)S(1)} %stack.35.where_ref, bf16[128,2304]{1,0:T(8,128)(2,1)S(1)} %collective-permute-done.5.refs_0_, bf16[128,2304]{1,0:T(8,128)(2,1)S(1)} %collective-permute-done.16.refs_1_, bf16[2304,1152]{1,0:T(8,128)(2,1)S(1)} %bitcast.25, ...), custom_call_target="tpu_custom_call" | custom-call | tf_op jit(solution)/shard_map/pallas_call | solution.py:168
  129.0 3.5 %collective-permute-start.19 = (bf16[128,2304]{1,0:T(8,128)(2,1)S(1)}, bf16[128,2304]{1,0:T(8,128)(2,1)S(1)}, u32[]{:S(2)}, u32[]{:S(2)}) collective-permute-start(bf16[128,2304]{1,0:T(8,128)(2,1)S(1)} %shard_map.166), channel_id=1, source_target_pairs={{0,0},{1,1},{2,4},{3,5},{4,2},{5,3},{6,6},{7,7},{8,8},{9,9},{10,12... | collective-permute-start | bytes 1769480 | tf_op jit(solution)/shard_map/ppermute | solution.py:36
  132.5 10.9 %collective-permute-done.17.b_ref = bf16[128,2304]{1,0:T(8,128)(2,1)S(1)} collective-permute-done((bf16[128,2304]{1,0:T(8,128)(2,1)S(1)}, bf16[128,2304]{1,0:T(8,128)(2,1)S(1)}, u32[]{:S(2)}, u32[]{:S(2)}) %collective-permute-start.17) | collective-permute-done | bytes 589856 | tf_op jit(solution)/shard_map/ppermute | solution.py:36
  144.0 1.4 collective-permute-done.19.b_ref
  146.3 1.3 collective-permute-start.21
  147.6 1.5 collective-permute-done.21.twin_ref
  149.1 10.7 %collective-permute-done.20.near_ref = bf16[128,2304]{1,0:T(8,128)(2,1)S(1)} collective-permute-done((bf16[128,2304]{1,0:T(8,128)(2,1)S(1)}, bf16[128,2304]{1,0:T(8,128)(2,1)S(1)}, u32[]{:S(2)}, u32[]{:S(2)}) %collective-permute-start.20) | collective-permute-done | bytes 589856 | tf_op jit(solution)/shard_map/ppermute | solution.py:36
  162.5 2.2 collective-permute-start.27
  164.7 2.9 %collective-permute-start.26 = (bf16[32,512]{1,0:T(8,128)(2,1)S(1)}, bf16[32,512]{1,0:T(8,128)(2,1)S(1)}, u32[]{:S(2)}, u32[]{:S(2)}) collective-permute-start(bf16[32,512]{1,0:T(8,128)(2,1)S(1)} %bitcast.31), channel_id=1, source_target_pairs={{0,1},{1,0},{2,3},{3,2},{4,5},{5,4},{6,7},{7,6},{8,9},{9,8},{10,11... | collective-permute-start | bytes 98312 | tf_op jit(solution)/shard_map/ppermute | solution.py:36
  168.7 1.4 collective-permute-start.23
  171.0 15.0 %collective-permute-done.18.near_ref = bf16[128,2304]{1,0:T(8,128)(2,1)S(1)} collective-permute-done((bf16[128,2304]{1,0:T(8,128)(2,1)S(1)}, bf16[128,2304]{1,0:T(8,128)(2,1)S(1)}, u32[]{:S(2)}, u32[]{:S(2)}) %collective-permute-start.18) | collective-permute-done | bytes 589856 | tf_op jit(solution)/shard_map/ppermute | solution.py:36
  186.0 14.1 %collective-permute-done.23.far_ref = bf16[64,2304]{1,0:T(8,128)(2,1)S(1)} collective-permute-done((bf16[64,2304]{1,0:T(8,128)(2,1)S(1)}, bf16[64,2304]{1,0:T(8,128)(2,1)S(1)}, u32[]{:S(2)}, u32[]{:S(2)}) %collective-permute-start.23) | collective-permute-done | bytes 294944 | tf_op jit(solution)/shard_map/ppermute | solution.py:36
  200.1 2.0 shard_map.172
  202.3 5.3 %collective-permute-done.28.came_ref = bf16[64,2304]{1,0:T(8,128)(2,1)S(1)} collective-permute-done((bf16[64,2304]{1,0:T(8,128)(2,1)S(1)}, bf16[64,2304]{1,0:T(8,128)(2,1)S(1)}, u32[]{:S(2)}, u32[]{:S(2)}) %collective-permute-start.28) | collective-permute-done | bytes 294944 | tf_op jit(solution)/shard_map/ppermute | solution.py:36
  208.7 3.2 %collective-permute-start.31 = (bf16[64,2304]{1,0:T(8,128)(2,1)S(1)}, bf16[64,2304]{1,0:T(8,128)(2,1)S(1)}, u32[]{:S(2)}, u32[]{:S(2)}) collective-permute-start(bf16[64,2304]{1,0:T(8,128)(2,1)S(1)} %shard_map.173.own_ref), channel_id=1, source_target_pairs={{0,4},{1,5},{2,6},{3,7},{4,0},{5,1},{6,2},{7,3},{8,12},{9,13},{10,... | collective-permute-start | bytes 884744 | tf_op jit(solution)/shard_map/ppermute | solution.py:36
  211.9 1.5 collective-permute-start.30
  213.3 6.9 %collective-permute-done.31.far_ref = bf16[64,2304]{1,0:T(8,128)(2,1)S(1)} collective-permute-done((bf16[64,2304]{1,0:T(8,128)(2,1)S(1)}, bf16[64,2304]{1,0:T(8,128)(2,1)S(1)}, u32[]{:S(2)}, u32[]{:S(2)}) %collective-permute-start.31) | collective-permute-done | bytes 294944 | tf_op jit(solution)/shard_map/ppermute | solution.py:36
  220.2 4.3 %collective-permute-start.32 = (bf16[64,2304]{1,0:T(8,128)(2,1)S(1)}, bf16[64,2304]{1,0:T(8,128)(2,1)S(1)}, u32[]{:S(2)}, u32[]{:S(2)}) collective-permute-start(bf16[64,2304]{1,0:T(8,128)(2,1)S(1)} %collective-permute-done.31.far_ref), channel_id=1, source_target_pairs={{0,2},{1,3},{2,0},{3,1},{4,6},{5,7},{6,4},{7,5},{8,10},{9,11},{10,... | collective-permute-start | bytes 884744 | tf_op jit(solution)/shard_map/ppermute | solution.py:36
  224.5 2.6 %shard_map.174 = f32[40,256]{1,0:T(8,128)S(1)} custom-call(s32[6]{0:T(128)S(1)} %stack.35.where_ref, bf16[64,2304]{1,0:T(8,128)(2,1)S(1)} %shard_map.171.own_ref, bf16[64,2304]{1,0:T(8,128)(2,1)S(1)} %collective-permute-done.24.near_ref, bf16[64,2304]{1,0:T(8,128)(2,1)S(1)} %collective-permute-done.23.far_ref, ...), custom_call_target="tpu_custom_call" | custom-call | tf_op jit(solution)/shard_map/pallas_call | solution.py:168
  228.1 6.3 %collective-permute-done.32.last_ref = bf16[64,2304]{1,0:T(8,128)(2,1)S(1)} collective-permute-done((bf16[64,2304]{1,0:T(8,128)(2,1)S(1)}, bf16[64,2304]{1,0:T(8,128)(2,1)S(1)}, u32[]{:S(2)}, u32[]{:S(2)}) %collective-permute-start.32) | collective-permute-done | bytes 294944 | tf_op jit(solution)/shard_map/ppermute | solution.py:36
  234.4 2.6 %shard_map.175 = f32[40,256]{1,0:T(8,128)S(1)} custom-call(s32[6]{0:T(128)S(1)} %stack.35.where_ref, bf16[64,2304]{1,0:T(8,128)(2,1)S(1)} %shard_map.173.own_ref, bf16[64,2304]{1,0:T(8,128)(2,1)S(1)} %collective-permute-done.30.near_ref, bf16[64,2304]{1,0:T(8,128)(2,1)S(1)} %collective-permute-done.31.far_ref, ...), custom_call_target="tpu_custom_call" | custom-call | tf_op jit(solution)/shard_map/pallas_call | solution.py:168
  237.2 2.2 collective-permute-start.33
  240.9 2.2 collective-permute-done.34.refs_2_
  243.6 5.3 %collective-permute-start.36 = (f32[32,128]{1,0:T(8,128)S(1)}, f32[32,128]{1,0:T(8,128)S(1)}, u32[]{:S(2)}, u32[]{:S(2)}) collective-permute-start(f32[32,128]{1,0:T(8,128)S(1)} %shard_map.176), channel_id=1, source_target_pairs={{0,0},{1,2},{2,4},{3,6},{4,16},{5,18},{6,20},{7,22},{8,8},{9,10},{... | collective-permute-start | bytes 49160 | tf_op jit(solution)/shard_map/ppermute | solution.py:36
  248.9 5.2 %collective-permute-start.37 = (f32[32,128]{1,0:T(8,128)S(1)}, f32[32,128]{1,0:T(8,128)S(1)}, u32[]{:S(2)}, u32[]{:S(2)}) collective-permute-start(f32[32,128]{1,0:T(8,128)S(1)} %shard_map.176), channel_id=1, source_target_pairs={{0,1},{1,3},{2,5},{3,7},{4,17},{5,19},{6,21},{7,23},{8,9},{9,11},{... | collective-permute-start | bytes 49160 | tf_op jit(solution)/shard_map/ppermute | solution.py:36
  255.5 5.5 %collective-permute-done.38.halo_ref = f32[32,128]{1,0:T(8,128)S(1)} collective-permute-done((f32[32,128]{1,0:T(8,128)S(1)}, f32[32,128]{1,0:T(8,128)S(1)}, u32[]{:S(2)}, u32[]{:S(2)}) %collective-permute-start.38) | collective-permute-done | bytes 16416 | tf_op jit(solution)/shard_map/ppermute | solution.py:36
  261.0 1.7 shard_map.177
  (100 shorter events, 24.8 us)
Async XLA Ops:
  0.6 32.2 %collective-permute-start = (bf16[2304,1152]{1,0:T(8,128)(2,1)}, bf16[2304,1152]{1,0:T(8,128)(2,1)}, u32[]{:S(2)}, u32[]{:S(2)}) collective-permute-start(bf16[2304,1152]{1,0:T(8,128)(2,1)} %refs_2_.7), channel_id=1, source_target_pairs={{0,1},{1,0},{2,3},{3,2},{4,5},{5,4},{6,7},{7,6},{8,9},{9,8},{10,11... | collective-permute-start | bytes 15925256 | tf_op jit(solution)/shard_map/ppermute | solution.py:36
  1.4 31.4 %collective-permute-start.1 = (bf16[1152,2304]{1,0:T(8,128)(2,1)}, bf16[1152,2304]{1,0:T(8,128)(2,1)}, u32[]{:S(2)}, u32[]{:S(2)}) collective-permute-start(bf16[1152,2304]{1,0:T(8,128)(2,1)} %refs_4_.7), channel_id=1, source_target_pairs={{0,1},{1,0},{2,3},{3,2},{4,5},{5,4},{6,7},{7,6},{8,9},{9,8},{10,11... | collective-permute-start | bytes 15925256 | tf_op jit(solution)/shard_map/ppermute | solution.py:36
  4.6 25.0 %collective-permute-start.3 = (bf16[128,2304]{1,0:T(8,128)(2,1)S(1)}, bf16[128,2304]{1,0:T(8,128)(2,1)S(1)}, u32[]{:S(2)}, u32[]{:S(2)}) collective-permute-start(bf16[128,2304]{1,0:T(8,128)(2,1)S(1)} %shard_map.159.refs_0_), channel_id=1, source_target_pairs={{0,2},{1,3},{2,0},{3,1},{4,6},{5,7},{6,4},{7,5},{8,10},{9,11},{10,... | collective-permute-start | bytes 1769480 | tf_op jit(solution)/shard_map/ppermute | solution.py:36
  4.8 28.0 %collective-permute-start.4 = (bf16[128,2304]{1,0:T(8,128)(2,1)S(1)}, bf16[128,2304]{1,0:T(8,128)(2,1)S(1)}, u32[]{:S(2)}, u32[]{:S(2)}) collective-permute-start(bf16[128,2304]{1,0:T(8,128)(2,1)S(1)} %shard_map.159.refs_0_), channel_id=1, source_target_pairs={{0,4},{1,5},{2,6},{3,7},{4,0},{5,1},{6,2},{7,3},{8,12},{9,13},{10,... | collective-permute-start | bytes 1769480 | tf_op jit(solution)/shard_map/ppermute | solution.py:36
  7.8 1.9 collective-permute-start.2
  32.8 13.5 %collective-permute-start.6 = (bf16[128,2304]{1,0:T(8,128)(2,1)S(1)}, bf16[128,2304]{1,0:T(8,128)(2,1)S(1)}, u32[]{:S(2)}, u32[]{:S(2)}) collective-permute-start(bf16[128,2304]{1,0:T(8,128)(2,1)S(1)} %collective-permute-done.4.refs_0_), channel_id=1, source_target_pairs={{0,2},{1,3},{2,0},{3,1},{4,6},{5,7},{6,4},{7,5},{8,10},{9,11},{10,... | collective-permute-start | bytes 1769480 | tf_op jit(solution)/shard_map/ppermute | solution.py:36
  34.6 45.2 %collective-permute-start.5 = (bf16[128,2304]{1,0:T(8,128)(2,1)S(1)}, bf16[128,2304]{1,0:T(8,128)(2,1)S(1)}, u32[]{:S(2)}, u32[]{:S(2)}) collective-permute-start(bf16[128,2304]{1,0:T(8,128)(2,1)S(1)} %shard_map.158.refs_0_), channel_id=1, source_target_pairs={{0,0},{1,1},{2,4},{3,5},{4,2},{5,3},{6,6},{7,7},{8,8},{9,9},{10,12... | collective-permute-start | bytes 1769480 | tf_op jit(solution)/shard_map/ppermute | solution.py:36
  46.3 33.5 %collective-permute-start.7 = (bf16[128,2304]{1,0:T(8,128)(2,1)S(1)}, bf16[128,2304]{1,0:T(8,128)(2,1)S(1)}, u32[]{:S(2)}, u32[]{:S(2)}) collective-permute-start(bf16[128,2304]{1,0:T(8,128)(2,1)S(1)} %shard_map.158.refs_0_), channel_id=1, source_target_pairs={{0,2},{1,3},{2,0},{3,1},{4,6},{5,7},{6,4},{7,5},{8,10},{9,11},{10,... | collective-permute-start | bytes 1769480 | tf_op jit(solution)/shard_map/ppermute | solution.py:36
  48.1 15.4 %collective-permute-start.8 = (f32[2,128,512]{2,1,0:T(8,128)S(1)}, f32[2,128,512]{2,1,0:T(8,128)S(1)}, u32[]{:S(2)}, u32[]{:S(2)}) collective-permute-start(f32[2,128,512]{2,1,0:T(8,128)S(1)} %bitcast.38), channel_id=1, source_target_pairs={{0,16},{1,17},{2,18},{3,19},{4,20},{5,21},{6,22},{7,23},{8,24},{9,... | collective-permute-start | bytes 1572872 | tf_op jit(solution)/shard_map/ppermute | solution.py:36
  63.4 26.7 %slice-start = ((s8[5308416]{0:T(1024)(128)(4,1)}), s8[4194304]{0:T(1024)(128)(4,1)S(1)}, s32[]{:S(2)}) async-start(s8[5308416]{0:T(1024)(128)(4,1)} %bitcast.24), calls=%async_computation | async-start | bytes 8388608
  63.4 26.7 %slice-start.2 = ((s8[5308416]{0:T(1024)(128)(4,1)}), s8[4194304]{0:T(1024)(128)(4,1)S(1)}, s32[]{:S(2)}) async-start(s8[5308416]{0:T(1024)(128)(4,1)} %bitcast.26), calls=%async_computation.2 | async-start | bytes 8388608
  70.9 29.3 %collective-permute-start.12 = (bf16[128,2304]{1,0:T(8,128)(2,1)S(1)}, bf16[128,2304]{1,0:T(8,128)(2,1)S(1)}, u32[]{:S(2)}, u32[]{:S(2)}) collective-permute-start(bf16[128,2304]{1,0:T(8,128)(2,1)S(1)} %shard_map.161.a_ref), channel_id=1, source_target_pairs={{0,2},{1,3},{6,4},{7,5},{8,10},{9,11},{14,12},{15,13},{16,18},{17,... | collective-permute-start | bytes 1769480 | tf_op jit(solution)/shard_map/ppermute | solution.py:36
  79.8 24.8 %collective-permute-start.10 = (bf16[128,2304]{1,0:T(8,128)(2,1)S(1)}, bf16[128,2304]{1,0:T(8,128)(2,1)S(1)}, u32[]{:S(2)}, u32[]{:S(2)}) collective-permute-start(bf16[128,2304]{1,0:T(8,128)(2,1)S(1)} %collective-permute-done.7.refs_1_), channel_id=1, source_target_pairs={{0,0},{1,1},{2,4},{3,5},{4,2},{5,3},{6,6},{7,7},{8,8},{9,9},{10,12... | collective-permute-start | bytes 1769480 | tf_op jit(solution)/shard_map/ppermute | solution.py:36
  83.9 20.8 %collective-permute-start.11 = (bf16[128,2304]{1,0:T(8,128)(2,1)S(1)}, bf16[128,2304]{1,0:T(8,128)(2,1)S(1)}, u32[]{:S(2)}, u32[]{:S(2)}) collective-permute-start(bf16[128,2304]{1,0:T(8,128)(2,1)S(1)} %collective-permute-done.5.refs_0_), channel_id=1, source_target_pairs={{2,0},{3,1},{4,6},{5,7},{10,8},{11,9},{12,14},{13,15},{18,16},{19,... | collective-permute-start | bytes 1769480 | tf_op jit(solution)/shard_map/ppermute | solution.py:36
  85.2 4.9 %collective-permute-start.9 = (f32[2,128,512]{2,1,0:T(8,128)S(1)}, f32[2,128,512]{2,1,0:T(8,128)S(1)}, u32[]{:S(2)}, u32[]{:S(2)}) collective-permute-start(f32[2,128,512]{2,1,0:T(8,128)S(1)} %bitcast.37), channel_id=1, source_target_pairs={{0,1},{1,0},{2,3},{3,2},{4,5},{5,4},{6,7},{7,6},{8,9},{9,8},{10,11... | collective-permute-start | bytes 1572872 | tf_op jit(solution)/shard_map/ppermute | solution.py:36
  88.6 26.7 %collective-permute-start.13 = (bf16[128,2304]{1,0:T(8,128)(2,1)S(1)}, bf16[128,2304]{1,0:T(8,128)(2,1)S(1)}, u32[]{:S(2)}, u32[]{:S(2)}) collective-permute-start(bf16[128,2304]{1,0:T(8,128)(2,1)S(1)} %shard_map.162.a_ref), channel_id=1, source_target_pairs={{0,2},{1,3},{6,4},{7,5},{8,10},{9,11},{14,12},{15,13},{16,18},{17,... | collective-permute-start | bytes 1769480 | tf_op jit(solution)/shard_map/ppermute | solution.py:36
  100.9 19.8 %collective-permute-start.15 = (bf16[128,2304]{1,0:T(8,128)(2,1)S(1)}, bf16[128,2304]{1,0:T(8,128)(2,1)S(1)}, u32[]{:S(2)}, u32[]{:S(2)}) collective-permute-start(bf16[128,2304]{1,0:T(8,128)(2,1)S(1)} %shard_map.164), channel_id=1, source_target_pairs={{0,0},{1,1},{2,4},{3,5},{4,2},{5,3},{6,6},{7,7},{8,8},{9,9},{10,12... | collective-permute-start | bytes 1769480 | tf_op jit(solution)/shard_map/ppermute | solution.py:36
  104.7 16.1 %collective-permute-start.16 = (bf16[128,2304]{1,0:T(8,128)(2,1)S(1)}, bf16[128,2304]{1,0:T(8,128)(2,1)S(1)}, u32[]{:S(2)}, u32[]{:S(2)}) collective-permute-start(bf16[128,2304]{1,0:T(8,128)(2,1)S(1)} %collective-permute-done.10.refs_0_), channel_id=1, source_target_pairs={{2,0},{3,1},{4,6},{5,7},{10,8},{11,9},{12,14},{13,15},{18,16},{19,... | collective-permute-start | bytes 1769480 | tf_op jit(solution)/shard_map/ppermute | solution.py:36
  106.2 14.5 %collective-permute-start.14 = (f32[2,128,512]{2,1,0:T(8,128)S(1)}, f32[2,128,512]{2,1,0:T(8,128)S(1)}, u32[]{:S(2)}, u32[]{:S(2)}) collective-permute-start(f32[2,128,512]{2,1,0:T(8,128)S(1)} %bitcast.36), channel_id=1, source_target_pairs={{0,17},{1,16},{2,19},{3,18},{4,21},{5,20},{6,23},{7,22},{8,25},{9,... | collective-permute-start | bytes 1572872 | tf_op jit(solution)/shard_map/ppermute | solution.py:36
  127.9 19.7 %copy-start.12 = (f32[2304]{0:T(1024)S(1)}, f32[2304]{0:T(1024)}, u32[]{:S(2)}) copy-start(f32[2304]{0:T(1024)} %param.21) | copy-start | bytes 27652
  127.9 32.0 %copy-start.3 = (bf16[256,2304]{1,0:T(8,128)(2,1)S(1)}, bf16[256,2304]{1,0:T(8,128)(2,1)}, u32[]{:S(2)}) copy-start(bf16[256,2304]{1,0:T(8,128)(2,1)} %tokens_ref.7) | copy-start | bytes 3538948
  128.0 31.9 %copy-start.10 = (f32[2,2304]{1,0:T(2,128)S(1)}, f32[2,2304]{1,0:T(2,128)}, u32[]{:S(2)}) copy-start(f32[2,2304]{1,0:T(2,128)} %gate_ref.3) | copy-start | bytes 55300
  128.0 72.1 %collective-permute-start.25 = (bf16[2304,512]{1,0:T(8,128)(2,1)S(1)}, bf16[2304,512]{1,0:T(8,128)(2,1)S(1)}, u32[]{:S(2)}, u32[]{:S(2)}) collective-permute-start(bf16[2304,512]{1,0:T(8,128)(2,1)S(1)} %copy-done.4), channel_id=1, source_target_pairs={{0,1},{1,0},{2,3},{3,2},{4,5},{5,4},{6,7},{7,6},{8,9},{9,8},{10,11... | collective-permute-start | bytes 7077896 | tf_op jit(solution)/shard_map/ppermute | solution.py:36
  128.4 14.9 %collective-permute-start.17 = (bf16[128,2304]{1,0:T(8,128)(2,1)S(1)}, bf16[128,2304]{1,0:T(8,128)(2,1)S(1)}, u32[]{:S(2)}, u32[]{:S(2)}) collective-permute-start(bf16[128,2304]{1,0:T(8,128)(2,1)S(1)} %shard_map.167), channel_id=1, source_target_pairs={{0,2},{1,3},{2,0},{3,1},{4,6},{5,7},{6,4},{7,5},{8,10},{9,11},{10,... | collective-permute-start | bytes 1769480 | tf_op jit(solution)/shard_map/ppermute | solution.py:36
  129.0 16.5 %collective-permute-start.19 = (bf16[128,2304]{1,0:T(8,128)(2,1)S(1)}, bf16[128,2304]{1,0:T(8,128)(2,1)S(1)}, u32[]{:S(2)}, u32[]{:S(2)}) collective-permute-start(bf16[128,2304]{1,0:T(8,128)(2,1)S(1)} %shard_map.166), channel_id=1, source_target_pairs={{0,0},{1,1},{2,4},{3,5},{4,2},{5,3},{6,6},{7,7},{8,8},{9,9},{10,12... | collective-permute-start | bytes 1769480 | tf_op jit(solution)/shard_map/ppermute | solution.py:36
  144.0 20.7 %copy-start.9 = (bf16[512,32]{0,1:T(8,128)(2,1)S(1)}, bf16[512,32]{0,1:T(8,128)(2,1)}, u32[]{:S(2)}) copy-start(bf16[512,32]{0,1:T(8,128)(2,1)} %param.26) | copy-start | bytes 98308
  146.2 13.7 %collective-permute-start.20 = (bf16[128,2304]{1,0:T(8,128)(2,1)S(1)}, bf16[128,2304]{1,0:T(8,128)(2,1)S(1)}, u32[]{:S(2)}, u32[]{:S(2)}) collective-permute-start(bf16[128,2304]{1,0:T(8,128)(2,1)S(1)} %shard_map.169), channel_id=1, source_target_pairs={{0,2},{1,3},{2,0},{3,1},{4,6},{5,7},{6,4},{7,5},{8,10},{9,11},{10,... | collective-permute-start | bytes 1769480 | tf_op jit(solution)/shard_map/ppermute | solution.py:36
  146.3 2.9 %collective-permute-start.21 = (f32[2,2,2304]{2,1,0:T(2,128)S(1)}, f32[2,2,2304]{2,1,0:T(2,128)S(1)}, u32[]{:S(2)}, u32[]{:S(2)}) collective-permute-start(f32[2,2,2304]{2,1,0:T(2,128)S(1)} %copy-done.5), channel_id=1, source_target_pairs={{0,16},{1,17},{2,18},{3,19},{4,20},{5,21},{6,22},{7,23},{8,24},{9,... | collective-permute-start | bytes 110600 | tf_op jit(solution)/shard_map/ppermute | solution.py:36
  160.9 6.7 %collective-permute-start.22 = (bf16[64,2304]{1,0:T(8,128)(2,1)S(1)}, bf16[64,2304]{1,0:T(8,128)(2,1)S(1)}, u32[]{:S(2)}, u32[]{:S(2)}) collective-permute-start(bf16[64,2304]{1,0:T(8,128)(2,1)S(1)} %get-tuple-element.71), channel_id=1, source_target_pairs={{0,16},{1,17},{2,18},{3,19},{4,20},{5,21},{6,22},{7,23},{8,24},{9,... | collective-permute-start | bytes 884744 | tf_op jit(solution)/shard_map/ppermute | solution.py:36
  162.2 23.7 %collective-permute-start.18 = (bf16[128,2304]{1,0:T(8,128)(2,1)S(1)}, bf16[128,2304]{1,0:T(8,128)(2,1)S(1)}, u32[]{:S(2)}, u32[]{:S(2)}) collective-permute-start(bf16[128,2304]{1,0:T(8,128)(2,1)S(1)} %get-tuple-element.65), channel_id=1, source_target_pairs={{0,2},{1,3},{2,0},{3,1},{4,6},{5,7},{6,4},{7,5},{8,10},{9,11},{10,... | collective-permute-start | bytes 1769480 | tf_op jit(solution)/shard_map/ppermute | solution.py:36
  162.5 37.5 %collective-permute-start.27 = (bf16[128,2304]{1,0:T(8,128)(2,1)S(1)}, bf16[128,2304]{1,0:T(8,128)(2,1)S(1)}, u32[]{:S(2)}, u32[]{:S(2)}) collective-permute-start(bf16[128,2304]{1,0:T(8,128)(2,1)S(1)} %shard_map.168), channel_id=1, source_target_pairs={{0,4},{1,5},{2,6},{3,7},{4,0},{5,1},{6,2},{7,3},{8,12},{9,13},{10,... | collective-permute-start | bytes 1769480 | tf_op jit(solution)/shard_map/ppermute | solution.py:36
  164.7 5.4 %collective-permute-start.26 = (bf16[32,512]{1,0:T(8,128)(2,1)S(1)}, bf16[32,512]{1,0:T(8,128)(2,1)S(1)}, u32[]{:S(2)}, u32[]{:S(2)}) collective-permute-start(bf16[32,512]{1,0:T(8,128)(2,1)S(1)} %bitcast.31), channel_id=1, source_target_pairs={{0,1},{1,0},{2,3},{3,2},{4,5},{5,4},{6,7},{7,6},{8,9},{9,8},{10,11... | collective-permute-start | bytes 98312 | tf_op jit(solution)/shard_map/ppermute | solution.py:36
  168.7 31.4 %collective-permute-start.23 = (bf16[64,2304]{1,0:T(8,128)(2,1)S(1)}, bf16[64,2304]{1,0:T(8,128)(2,1)S(1)}, u32[]{:S(2)}, u32[]{:S(2)}) collective-permute-start(bf16[64,2304]{1,0:T(8,128)(2,1)S(1)} %shard_map.171.own_ref), channel_id=1, source_target_pairs={{0,4},{1,5},{2,6},{3,7},{4,0},{5,1},{6,2},{7,3},{8,12},{9,13},{10,... | collective-permute-start | bytes 884744 | tf_op jit(solution)/shard_map/ppermute | solution.py:36
  170.1 29.9 %collective-permute-start.24 = (bf16[64,2304]{1,0:T(8,128)(2,1)S(1)}, bf16[64,2304]{1,0:T(8,128)(2,1)S(1)}, u32[]{:S(2)}, u32[]{:S(2)}) collective-permute-start(bf16[64,2304]{1,0:T(8,128)(2,1)S(1)} %shard_map.171.own_ref), channel_id=1, source_target_pairs={{0,2},{1,3},{2,0},{3,1},{4,6},{5,7},{6,4},{7,5},{8,10},{9,11},{10,... | collective-permute-start | bytes 884744 | tf_op jit(solution)/shard_map/ppermute | solution.py:36
  202.1 5.6 %collective-permute-start.28 = (bf16[64,2304]{1,0:T(8,128)(2,1)S(1)}, bf16[64,2304]{1,0:T(8,128)(2,1)S(1)}, u32[]{:S(2)}, u32[]{:S(2)}) collective-permute-start(bf16[64,2304]{1,0:T(8,128)(2,1)S(1)} %get-tuple-element.78), channel_id=1, source_target_pairs={{0,16},{1,17},{2,18},{3,19},{4,20},{5,21},{6,22},{7,23},{8,24},{9,... | collective-permute-start | bytes 884744 | tf_op jit(solution)/shard_map/ppermute | solution.py:36
  208.7 11.5 %collective-permute-start.31 = (bf16[64,2304]{1,0:T(8,128)(2,1)S(1)}, bf16[64,2304]{1,0:T(8,128)(2,1)S(1)}, u32[]{:S(2)}, u32[]{:S(2)}) collective-permute-start(bf16[64,2304]{1,0:T(8,128)(2,1)S(1)} %shard_map.173.own_ref), channel_id=1, source_target_pairs={{0,4},{1,5},{2,6},{3,7},{4,0},{5,1},{6,2},{7,3},{8,12},{9,13},{10,... | collective-permute-start | bytes 884744 | tf_op jit(solution)/shard_map/ppermute | solution.py:36
  211.9 12.6 %collective-permute-start.29 = (bf16[64,2304]{1,0:T(8,128)(2,1)S(1)}, bf16[64,2304]{1,0:T(8,128)(2,1)S(1)}, u32[]{:S(2)}, u32[]{:S(2)}) collective-permute-start(bf16[64,2304]{1,0:T(8,128)(2,1)S(1)} %collective-permute-done.23.far_ref), channel_id=1, source_target_pairs={{0,2},{1,3},{2,0},{3,1},{4,6},{5,7},{6,4},{7,5},{8,10},{9,11},{10,... | collective-permute-start | bytes 884744 | tf_op jit(solution)/shard_map/ppermute | solution.py:36
  211.9 16.2 %collective-permute-start.30 = (bf16[64,2304]{1,0:T(8,128)(2,1)S(1)}, bf16[64,2304]{1,0:T(8,128)(2,1)S(1)}, u32[]{:S(2)}, u32[]{:S(2)}) collective-permute-start(bf16[64,2304]{1,0:T(8,128)(2,1)S(1)} %shard_map.173.own_ref), channel_id=1, source_target_pairs={{0,2},{1,3},{2,0},{3,1},{4,6},{5,7},{6,4},{7,5},{8,10},{9,11},{10,... | collective-permute-start | bytes 884744 | tf_op jit(solution)/shard_map/ppermute | solution.py:36
  220.2 14.2 %collective-permute-start.32 = (bf16[64,2304]{1,0:T(8,128)(2,1)S(1)}, bf16[64,2304]{1,0:T(8,128)(2,1)S(1)}, u32[]{:S(2)}, u32[]{:S(2)}) collective-permute-start(bf16[64,2304]{1,0:T(8,128)(2,1)S(1)} %collective-permute-done.31.far_ref), channel_id=1, source_target_pairs={{0,2},{1,3},{2,0},{3,1},{4,6},{5,7},{6,4},{7,5},{8,10},{9,11},{10,... | collective-permute-start | bytes 884744 | tf_op jit(solution)/shard_map/ppermute | solution.py:36
  227.2 28.2 %copy-start.13 = (f32[32]{0:T(128)S(1)}, f32[32]{0:T(128)}, u32[]{:S(2)}) copy-start(f32[32]{0:T(128)} %param.28) | copy-start | bytes 388
  227.2 33.8 %copy-start.6 = (f32[32,32,3,3]{1,0,3,2:T(8,128)S(1)}, f32[32,32,3,3]{1,0,3,2:T(8,128)}, u32[]{:S(2)}) copy-start(f32[32,32,3,3]{1,0,3,2:T(8,128)} %param.27) | copy-start | bytes 110596
  227.2 33.8 %copy-start.11 = (f32[1,32,128]{2,1,0:T(8,128)S(1)}, f32[1,32,128]{2,1,0:T(8,128)}, u32[]{:S(2)}) copy-start(f32[1,32,128]{2,1,0:T(8,128)} %param.29) | copy-start | bytes 49156
  237.2 3.7 %collective-permute-start.33 = (f32[40,128]{1,0:T(8,128)S(1)}, f32[40,128]{1,0:T(8,128)S(1)}, u32[]{:S(2)}, u32[]{:S(2)}) collective-permute-start(f32[40,128]{1,0:T(8,128)S(1)} %pad_maximum_fusion.1), channel_id=1, source_target_pairs={{0,2},{1,3},{2,0},{3,1},{4,6},{5,7},{6,4},{7,5},{8,10},{9,11},{10,... | collective-permute-start | bytes 61448 | tf_op jit(solution)/shard_map/ppermute | solution.py:36
  239.5 3.5 %collective-permute-start.34 = (f32[40,128]{1,0:T(8,128)S(1)}, f32[40,128]{1,0:T(8,128)S(1)}, u32[]{:S(2)}, u32[]{:S(2)}) collective-permute-start(f32[40,128]{1,0:T(8,128)S(1)} %pad_maximum_fusion.2), channel_id=1, source_target_pairs={{0,4},{1,5},{2,6},{3,7},{4,0},{5,1},{6,2},{7,3},{8,12},{9,13},{10,... | collective-permute-start | bytes 61448 | tf_op jit(solution)/shard_map/ppermute | solution.py:36
  239.6 3.4 %collective-permute-start.35 = (f32[40,128]{1,0:T(8,128)S(1)}, f32[40,128]{1,0:T(8,128)S(1)}, u32[]{:S(2)}, u32[]{:S(2)}) collective-permute-start(f32[40,128]{1,0:T(8,128)S(1)} %pad_maximum_fusion.3), channel_id=1, source_target_pairs={{0,6},{1,7},{2,4},{3,5},{4,2},{5,3},{6,0},{7,1},{8,14},{9,15},{10,... | collective-permute-start | bytes 61448 | tf_op jit(solution)/shard_map/ppermute | solution.py:36
  243.6 11.9 %collective-permute-start.36 = (f32[32,128]{1,0:T(8,128)S(1)}, f32[32,128]{1,0:T(8,128)S(1)}, u32[]{:S(2)}, u32[]{:S(2)}) collective-permute-start(f32[32,128]{1,0:T(8,128)S(1)} %shard_map.176), channel_id=1, source_target_pairs={{0,0},{1,2},{2,4},{3,6},{4,16},{5,18},{6,20},{7,22},{8,8},{9,10},{... | collective-permute-start | bytes 49160 | tf_op jit(solution)/shard_map/ppermute | solution.py:36
  248.9 6.6 %collective-permute-start.37 = (f32[32,128]{1,0:T(8,128)S(1)}, f32[32,128]{1,0:T(8,128)S(1)}, u32[]{:S(2)}, u32[]{:S(2)}) collective-permute-start(f32[32,128]{1,0:T(8,128)S(1)} %shard_map.176), channel_id=1, source_target_pairs={{0,1},{1,3},{2,5},{3,7},{4,17},{5,19},{6,21},{7,23},{8,9},{9,11},{... | collective-permute-start | bytes 49160 | tf_op jit(solution)/shard_map/ppermute | solution.py:36
  254.1 6.8 %collective-permute-start.38 = (f32[32,128]{1,0:T(8,128)S(1)}, f32[32,128]{1,0:T(8,128)S(1)}, u32[]{:S(2)}, u32[]{:S(2)}) collective-permute-start(f32[32,128]{1,0:T(8,128)S(1)} %shard_map.176), channel_id=1, source_target_pairs={{1,1},{2,3},{3,5},{5,17},{6,19},{7,21},{9,9},{10,11},{11,13},{13,2... | collective-permute-start | bytes 49160 | tf_op jit(solution)/shard_map/ppermute | solution.py:36
  (9 other events, 76.6 us)

commit v3 on v2

--- a/solution.py
+++ b/solution.py
@@ -495,35 +495,45 @@
     codes = codebook.T
     bias_other = swap_cores(biases)
 
+    barrier = lax.optimization_barrier
     own_a = norm_part(where, tokens, ada_ffn, 0, step)
-    near_a, far_a = near(own_a), across(own_a)
+    near_a, mid_a = near(own_a), middle(own_a)
     own_b = norm_part(where, tokens, ada_ffn, step, step)
-    up_other, down_other, bias_other, near_a, far_a = lax.optimization_barrier(
-        (up_other, down_other, bias_other, near_a, far_a)
-    )
+    noise_own, noise_twin, noise_core, noise_both = (
+        noise_for(core, upper),
+        noise_for(core, 1 - upper),
+        noise_for(1 - core, upper),
+        noise_for(1 - core, 1 - upper),
+    )
+    noise_twin, noise_core, noise_both, _ = barrier((noise_twin, noise_core, noise_both, own_b))
+    noise_twin = swap_twins(noise_twin)
+    up_other, down_other, bias_other, near_a = barrier((up_other, down_other, bias_other, near_a))
     panels = (up_weight, up_other, down_weight, down_other, biases, bias_other)
-    last_a = near(far_a)
-    mid_b = middle(after(own_b, far_a))
-    noise_twin = swap_twins(after(noise_for(core, 1 - upper), far_a))
-    sum_own_a, sum_near_a = ffn(where, [[own_a], [near_a]], panels)
-    noise_core = swap_cores(after(noise_for(1 - core, upper), noise_twin))
-    (sum_far_a,) = ffn(where, [[after(far_a, sum_near_a, noise_twin)]], panels)
+    far_mid_a = middle(near_a)
+    near_b = near(after(own_b, near_a))
+    mid_a = after(mid_a, near_a)
+    far_end_a = outward(mid_a)
+    sum_own_a, sum_near_a = ffn(where, [[own_a], [after(near_a, mid_a)]], panels)
+    noise_core = swap_cores(after(noise_core, sum_near_a))
+    far_mid_a = after(far_mid_a, sum_near_a)
+    last_end_a = outward(far_mid_a)
+    mid_b = middle(after(own_b, far_mid_a))
+    (sum_far_a,) = ffn(where, [[far_mid_a, far_end_a]], panels)
     came_far_a = inward(sum_far_a)
-    near_b = near(after(own_b, last_a))
-    (sum_last_a,) = ffn(where, [[after(last_a, sum_far_a)]], panels)
+    near_b, mid_b = barrier((near_b, mid_b, sum_far_a))[:2]
+    far_mid_b, far_end_b = middle(near_b), outward(mid_b)
+    (sum_last_a,) = ffn(where, [[mid_a, after(last_end_a, near_b, mid_b, noise_twin)]], panels)
     came_last_a = inward(sum_last_a)
-    mid_b, near_b = lax.optimization_barrier((mid_b, near_b, sum_last_a))[:2]
-    far_mid_b, far_end_b = middle(near_b), outward(mid_b)
-    noise_both = swap_both(after(noise_for(1 - core, 1 - upper), noise_core))
-    sum_own_b, sum_near_b = ffn(where, [[own_b], [after(near_b, noise_core)]], panels)
+    noise_both = swap_both(after(noise_both, sum_last_a))
+    sum_own_b, sum_near_b = ffn(where, [[after(own_b, sum_last_a, noise_core)], [near_b]], panels)
     both_last_a = add(where, after(sum_last_a, sum_near_b), came_far_a)
     went_last_a = middle(both_last_a)
-    far_mid_b, far_end_b = lax.optimization_barrier((far_mid_b, far_end_b, both_last_a))[:2]
+    far_mid_b, far_end_b = barrier((far_mid_b, far_end_b, both_last_a))[:2]
     last_end_b = outward(far_mid_b)
     (sum_far_b,) = ffn(where, [[far_mid_b, far_end_b]], panels)
     both_far_a = add(where, after(sum_far_a, sum_far_b), came_last_a)
     went_far_a = middle(both_far_a)
-    (sum_last_b,) = ffn(where, [[after(mid_b, both_far_a, noise_both, went_last_a), last_end_b]], panels)
+    (sum_last_b,) = ffn(where, [[after(mid_b, both_far_a, went_last_a), last_end_b]], panels)
     came_last_b = near(sum_last_b)
     head_other = swap_cores(after(head_weight, sum_last_b))
     head_twin = swap_twins(after(ada_head, sum_last_b))
@@ -540,14 +550,14 @@
     mixed_a = mix_twins(where, kept_a, came_a, ada_head, head_twin)
     mix_near_a, mix_far_a = near(mixed_a), across(mixed_a)
     block_out, kept_b, sent_b = block_rows(
-        where, step, True, sum_own_b, after(came_near_b, mix_far_a, mix_near_a, head_other, code_other), went_far_b, tokens, gate, bias_out, (out_a,)
+        where, step, True, sum_own_b, after(came_near_b, mixed_a, head_other, code_other, noise_both), went_far_b, tokens, gate, bias_out, (out_a,)
     )
     came_b = swap_twins(sent_b)
-    mix_last_a = near(after(mix_far_a, sent_b))
+    mix_last_a = near(mix_far_a)
     mixed_b = mix_twins(where, kept_b, came_b, ada_head, head_twin)
     mix_near_b, mix_far_b = near(mixed_b), across(mixed_b)
     heads = (head_weight, head_other, biases, bias_other, codes, code_other)
-    noises = (noise_for(core, upper), noise_core, noise_twin, noise_both)
+    noises = (noise_own, noise_core, noise_twin, noise_both)
     stats_a = head_stats(
         where, 0, (after(mixed_a, mixed_b), mix_near_a, mix_far_a, mix_last_a), heads, noises
     )

time: 263 us -> 242 us (0.920)
  waiting for transfers between devices: 117 us -> 93.1 us
  starting transfers between devices: 66.9 us -> 70.6 us
    ppermute x39 -> x41, waiting for transfers between devices: 117 us -> 93.1 us  [permute_devices(): return lax.ppermute(value, ('dp', 'mp'), pairs)]
    ppermute x39 -> x41, starting transfers between devices: 66.9 us -> 70.6 us  [permute_devices(): return lax.ppermute(value, ('dp', 'mp'), pairs)]
  transfers between devices with their start and end apart: 39 -> 41, of which waited for: 18 -> 20; matrix products, arithmetic and copies ran while one was open for 1% -> 1% of each run, Pallas kernels for 20% -> 22%
where the time goes in v3:
time: 242 us; the launch traced here: 241 us
  waiting for transfers between devices  93.1 us (38%)
  starting transfers between devices  70.6 us (29%)
  Pallas kernels  67 us (28%)
  local copies, waits for them, and re-layouts  8.45 us (3%)
    ppermute x41, waiting for transfers between devices, permute_devices(): return lax.ppermute(value, ('dp', 'mp'), pairs)  93.1 us
    ppermute x41, starting transfers between devices, permute_devices(): return lax.ppermute(value, ('dp', 'mp'), pairs)  70.6 us
    pallas_call x20, Pallas kernels, call(): pl.pallas_call(kernel, out_shape=outs, in_specs=[SCALARS] + [ON_CHIP] * l...  67 us
    unnamed x36, local copies, waits for them, and re-layouts  7.88 us
  transfers between devices with their start and end apart: 41, of which 20 were waited for; matrix products, arithmetic and copies ran while one was open for 1% of the time, Pallas kernels for 22%

profile of v3, /device:TPU:13, one launch (start us, length us, event | category | flops | bytes accessed | tf_op | source)
XLA Modules:
  0.0 241.4 jit_solution(15857352869607245365)
XLA Ops:
  6.3 4.3 %collective-permute-start = (bf16[128,2304]{1,0:T(8,128)(2,1)S(1)}, bf16[128,2304]{1,0:T(8,128)(2,1)S(1)}, u32[]{:S(2)}, u32[]{:S(2)}) collective-permute-start(bf16[128,2304]{1,0:T(8,128)(2,1)S(1)} %shard_map.159.refs_0_), channel_id=1, source_target_pairs={{0,0},{1,1},{2,4},{3,5},{4,2},{5,3},{6,6},{7,7},{8,8},{9,9},{10,12... | collective-permute-start | bytes 1769480 | tf_op jit(solution)/shard_map/ppermute | solution.py:36
  10.6 8.5 %collective-permute-done.4.refs_1_ = bf16[128,2304]{1,0:T(8,128)(2,1)S(1)} collective-permute-done((bf16[128,2304]{1,0:T(8,128)(2,1)S(1)}, bf16[128,2304]{1,0:T(8,128)(2,1)S(1)}, u32[]{:S(2)}, u32[]{:S(2)}) %collective-permute-start.4) | collective-permute-done | bytes 589856 | tf_op jit(solution)/shard_map/ppermute | solution.py:36
  19.1 3.2 %collective-permute-start.5 = (bf16[128,2304]{1,0:T(8,128)(2,1)S(1)}, bf16[128,2304]{1,0:T(8,128)(2,1)S(1)}, u32[]{:S(2)}, u32[]{:S(2)}) collective-permute-start(bf16[128,2304]{1,0:T(8,128)(2,1)S(1)} %collective-permute-done.4.refs_1_), channel_id=1, source_target_pairs={{0,0},{1,1},{2,4},{3,5},{4,2},{5,3},{6,6},{7,7},{8,8},{9,9},{10,12... | collective-permute-start | bytes 1769480 | tf_op jit(solution)/shard_map/ppermute | solution.py:36
  25.7 2.5 %copy-done = bf16[2304,1152]{1,0:T(8,128)(2,1)S(1)} copy-done((bf16[2304,1152]{1,0:T(8,128)(2,1)S(1)}, bf16[2304,1152]{1,0:T(8,128)(2,1)}, u32[]{:S(2)}) %copy-start) | copy-done | bytes 5308440
  28.2 2.5 %copy-done.2 = bf16[1152,2304]{1,0:T(8,128)(2,1)S(1)} copy-done((bf16[1152,2304]{1,0:T(8,128)(2,1)S(1)}, bf16[1152,2304]{1,0:T(8,128)(2,1)}, u32[]{:S(2)}) %copy-start.2) | copy-done | bytes 5308440
  30.7 10.2 %shard_map.160 = (bf16[128,2304]{1,0:T(8,128)(2,1)S(1)}, bf16[128,2304]{1,0:T(8,128)(2,1)S(1)}) custom-call(s32[6]{0:T(128)S(1)} %stack.35.where_ref, bf16[128,2304]{1,0:T(8,128)(2,1)S(1)} %shard_map.159.refs_0_, bf16[128,2304]{1,0:T(8,128)(2,1)S(1)} %collective-permute-done.4.refs_1_, bf16[2304,1152]{1,0:T(8,128)(2,1)S(1)} %copy-done, ...), custom_call_target="tpu_custom_call" | custom-call | tf_op jit(solution)/shard_map/pallas_call | solution.py:168
  40.9 3.2 %collective-permute-start.8 = (bf16[128,2304]{1,0:T(8,128)(2,1)S(1)}, bf16[128,2304]{1,0:T(8,128)(2,1)S(1)}, u32[]{:S(2)}, u32[]{:S(2)}) collective-permute-start(bf16[128,2304]{1,0:T(8,128)(2,1)S(1)} %shard_map.158.refs_0_), channel_id=1, source_target_pairs={{0,0},{1,1},{2,4},{3,5},{4,2},{5,3},{6,6},{7,7},{8,8},{9,9},{10,12... | collective-permute-start | bytes 1769480 | tf_op jit(solution)/shard_map/ppermute | solution.py:36
  46.0 7.4 %shard_map.161.a_ref = bf16[128,2304]{1,0:T(8,128)(2,1)S(1)} custom-call(s32[6]{0:T(128)S(1)} %stack.35.where_ref, bf16[128,2304]{1,0:T(8,128)(2,1)S(1)} %collective-permute-done.5.refs_0_, bf16[128,2304]{1,0:T(8,128)(2,1)S(1)} %collective-permute-done.9.refs_1_, bf16[2304,1152]{1,0:T(8,128)(2,1)S(1)} %copy-done.1, ...), custom_call_target="tpu_custom_call" | custom-call | tf_op jit(solution)/shard_map/pallas_call | solution.py:168
  53.4 1.4 collective-permute-start.14
  56.3 3.3 %collective-permute-start.12 = (bf16[128,2304]{1,0:T(8,128)(2,1)S(1)}, bf16[128,2304]{1,0:T(8,128)(2,1)S(1)}, u32[]{:S(2)}, u32[]{:S(2)}) collective-permute-start(bf16[128,2304]{1,0:T(8,128)(2,1)S(1)} %collective-permute-done.7.refs_1_), channel_id=1, source_target_pairs={{0,0},{1,1},{2,4},{3,5},{4,2},{5,3},{6,6},{7,7},{8,8},{9,9},{10,12... | collective-permute-start | bytes 1769480 | tf_op jit(solution)/shard_map/ppermute | solution.py:36
  59.6 1.5 collective-permute-start.13
  61.1 2.5 %collective-permute-start.11 = (f32[2,128,512]{2,1,0:T(8,128)S(1)}, f32[2,128,512]{2,1,0:T(8,128)S(1)}, u32[]{:S(2)}, u32[]{:S(2)}) collective-permute-start(f32[2,128,512]{2,1,0:T(8,128)S(1)} %bitcast.35), channel_id=1, source_target_pairs={{0,1},{1,0},{2,3},{3,2},{4,5},{5,4},{6,7},{7,6},{8,9},{9,8},{10,11... | collective-permute-start | bytes 1572872 | tf_op jit(solution)/shard_map/ppermute | solution.py:36
  63.6 7.3 %shard_map.162.a_ref = bf16[128,2304]{1,0:T(8,128)(2,1)S(1)} custom-call(s32[6]{0:T(128)S(1)} %stack.35.where_ref, bf16[128,2304]{1,0:T(8,128)(2,1)S(1)} %collective-permute-done.refs_0_, bf16[128,2304]{1,0:T(8,128)(2,1)S(1)} %collective-permute-done.6.refs_1_, bf16[2304,1152]{1,0:T(8,128)(2,1)S(1)} %copy-done.1, ...), custom_call_target="tpu_custom_call" | custom-call | tf_op jit(solution)/shard_map/pallas_call | solution.py:168
  72.2 10.1 %shard_map.163 = (bf16[128,2304]{1,0:T(8,128)(2,1)S(1)}, bf16[128,2304]{1,0:T(8,128)(2,1)S(1)}) custom-call(s32[6]{0:T(128)S(1)} %stack.35.where_ref, bf16[128,2304]{1,0:T(8,128)(2,1)S(1)} %shard_map.158.refs_0_, bf16[128,2304]{1,0:T(8,128)(2,1)S(1)} %collective-permute-done.7.refs_1_, bf16[2304,1152]{1,0:T(8,128)(2,1)S(1)} %copy-done.1, ...), custom_call_target="tpu_custom_call" | custom-call | tf_op jit(solution)/shard_map/pallas_call | solution.py:168
  83.1 2.1 collective-permute-start.16
  85.2 2.9 %collective-permute-start.17 = (bf16[128,2304]{1,0:T(8,128)(2,1)S(1)}, bf16[128,2304]{1,0:T(8,128)(2,1)S(1)}, u32[]{:S(2)}, u32[]{:S(2)}) collective-permute-start(bf16[128,2304]{1,0:T(8,128)(2,1)S(1)} %collective-permute-done.12.refs_0_), channel_id=1, source_target_pairs={{2,0},{3,1},{4,6},{5,7},{10,8},{11,9},{12,14},{13,15},{18,16},{19,... | collective-permute-start | bytes 1769480 | tf_op jit(solution)/shard_map/ppermute | solution.py:36
  88.1 7.3 %shard_map.165.a_ref = bf16[128,2304]{1,0:T(8,128)(2,1)S(1)} custom-call(s32[6]{0:T(128)S(1)} %stack.35.where_ref, bf16[128,2304]{1,0:T(8,128)(2,1)S(1)} %collective-permute-done.12.refs_0_, bf16[128,2304]{1,0:T(8,128)(2,1)S(1)} %collective-permute-done.13.refs_1_, bf16[2304,1152]{1,0:T(8,128)(2,1)S(1)} %copy-done.1, ...), custom_call_target="tpu_custom_call" | custom-call | tf_op jit(solution)/shard_map/pallas_call | solution.py:168
  97.7 7.3 %shard_map.167 = bf16[128,2304]{1,0:T(8,128)(2,1)S(1)} custom-call(s32[6]{0:T(128)S(1)} %stack.35.where_ref, bf16[128,2304]{1,0:T(8,128)(2,1)S(1)} %collective-permute-done.8.refs_0_, bf16[128,2304]{1,0:T(8,128)(2,1)S(1)} %collective-permute-done.17.refs_1_, bf16[2304,1152]{1,0:T(8,128)(2,1)S(1)} %copy-done.1, ...), custom_call_target="tpu_custom_call" | custom-call | tf_op jit(solution)/shard_map/pallas_call | solution.py:168
  105.1 3.7 %collective-permute-start.24 = (bf16[2304,512]{1,0:T(8,128)(2,1)S(1)}, bf16[2304,512]{1,0:T(8,128)(2,1)S(1)}, u32[]{:S(2)}, u32[]{:S(2)}) collective-permute-start(bf16[2304,512]{1,0:T(8,128)(2,1)S(1)} %copy-done.5), channel_id=1, source_target_pairs={{0,1},{1,0},{2,3},{3,2},{4,5},{5,4},{6,7},{7,6},{8,9},{9,8},{10,11... | collective-permute-start | bytes 7077896 | tf_op jit(solution)/shard_map/ppermute | solution.py:36
  108.8 2.2 collective-permute-start.18
  111.0 2.5 %collective-permute-start.20 = (bf16[128,2304]{1,0:T(8,128)(2,1)S(1)}, bf16[128,2304]{1,0:T(8,128)(2,1)S(1)}, u32[]{:S(2)}, u32[]{:S(2)}) collective-permute-start(bf16[128,2304]{1,0:T(8,128)(2,1)S(1)} %shard_map.166), channel_id=1, source_target_pairs={{0,0},{1,1},{2,4},{3,5},{4,2},{5,3},{6,6},{7,7},{8,8},{9,9},{10,12... | collective-permute-start | bytes 1769480 | tf_op jit(solution)/shard_map/ppermute | solution.py:36
  113.4 11.1 %collective-permute-done.18.b_ref = bf16[128,2304]{1,0:T(8,128)(2,1)S(1)} collective-permute-done((bf16[128,2304]{1,0:T(8,128)(2,1)S(1)}, bf16[128,2304]{1,0:T(8,128)(2,1)S(1)}, u32[]{:S(2)}, u32[]{:S(2)}) %collective-permute-start.18) | collective-permute-done | bytes 589856 | tf_op jit(solution)/shard_map/ppermute | solution.py:36
  125.3 2.1 collective-permute-done.20.b_ref
  128.2 1.5 collective-permute-start.19
  130.5 2.4 collective-permute-done.22.twin_ref
  132.9 3.2 %collective-permute-start.26 = (f32[2,128,512]{2,1,0:T(8,128)S(1)}, f32[2,128,512]{2,1,0:T(8,128)S(1)}, u32[]{:S(2)}, u32[]{:S(2)}) collective-permute-start(f32[2,128,512]{2,1,0:T(8,128)S(1)} %bitcast.34), channel_id=1, source_target_pairs={{0,17},{1,16},{2,19},{3,18},{4,21},{5,20},{6,23},{7,22},{8,25},{9,... | collective-permute-start | bytes 1572872 | tf_op jit(solution)/shard_map/ppermute | solution.py:36
  136.1 16.5 %collective-permute-done.21.near_ref = bf16[128,2304]{1,0:T(8,128)(2,1)S(1)} collective-permute-done((bf16[128,2304]{1,0:T(8,128)(2,1)S(1)}, bf16[128,2304]{1,0:T(8,128)(2,1)S(1)}, u32[]{:S(2)}, u32[]{:S(2)}) %collective-permute-start.21) | collective-permute-done | bytes 589856 | tf_op jit(solution)/shard_map/ppermute | solution.py:36
  153.9 5.6 %collective-permute-done.23.came_ref = bf16[64,2304]{1,0:T(8,128)(2,1)S(1)} collective-permute-done((bf16[64,2304]{1,0:T(8,128)(2,1)S(1)}, bf16[64,2304]{1,0:T(8,128)(2,1)S(1)}, u32[]{:S(2)}, u32[]{:S(2)}) %collective-permute-start.23) | collective-permute-done | bytes 294944 | tf_op jit(solution)/shard_map/ppermute | solution.py:36
  159.6 4.1 %collective-permute-start.25 = (bf16[32,512]{1,0:T(8,128)(2,1)S(1)}, bf16[32,512]{1,0:T(8,128)(2,1)S(1)}, u32[]{:S(2)}, u32[]{:S(2)}) collective-permute-start(bf16[32,512]{1,0:T(8,128)(2,1)S(1)} %bitcast.29), channel_id=1, source_target_pairs={{0,1},{1,0},{2,3},{3,2},{4,5},{5,4},{6,7},{7,6},{8,9},{9,8},{10,11... | collective-permute-start | bytes 98312 | tf_op jit(solution)/shard_map/ppermute | solution.py:36
  165.2 1.9 collective-permute-done.27.far_ref
  167.2 2.0 shard_map.172
  170.2 5.4 %collective-permute-done.28.came_ref = bf16[64,2304]{1,0:T(8,128)(2,1)S(1)} collective-permute-done((bf16[64,2304]{1,0:T(8,128)(2,1)S(1)}, bf16[64,2304]{1,0:T(8,128)(2,1)S(1)}, u32[]{:S(2)}, u32[]{:S(2)}) %collective-permute-start.28) | collective-permute-done | bytes 294944 | tf_op jit(solution)/shard_map/ppermute | solution.py:36
  177.3 1.7 collective-permute-start.29
  179.0 7.9 %collective-permute-done.30.far_ref = bf16[64,2304]{1,0:T(8,128)(2,1)S(1)} collective-permute-done((bf16[64,2304]{1,0:T(8,128)(2,1)S(1)}, bf16[64,2304]{1,0:T(8,128)(2,1)S(1)}, u32[]{:S(2)}, u32[]{:S(2)}) %collective-permute-start.30) | collective-permute-done | bytes 294944 | tf_op jit(solution)/shard_map/ppermute | solution.py:36
  186.9 3.1 %collective-permute-start.31 = (bf16[64,2304]{1,0:T(8,128)(2,1)S(1)}, bf16[64,2304]{1,0:T(8,128)(2,1)S(1)}, u32[]{:S(2)}, u32[]{:S(2)}) collective-permute-start(bf16[64,2304]{1,0:T(8,128)(2,1)S(1)} %collective-permute-done.30.far_ref), channel_id=1, source_target_pairs={{0,2},{1,3},{2,0},{3,1},{4,6},{5,7},{6,4},{7,5},{8,10},{9,11},{10,... | collective-permute-start | bytes 884744 | tf_op jit(solution)/shard_map/ppermute | solution.py:36
  190.1 4.5 %collective-permute-done.33.far_ref = bf16[64,2304]{1,0:T(8,128)(2,1)S(1)} collective-permute-done((bf16[64,2304]{1,0:T(8,128)(2,1)S(1)}, bf16[64,2304]{1,0:T(8,128)(2,1)S(1)}, u32[]{:S(2)}, u32[]{:S(2)}) %collective-permute-start.33) | collective-permute-done | bytes 294944 | tf_op jit(solution)/shard_map/ppermute | solution.py:36
  194.6 2.4 %collective-permute-start.34 = (bf16[64,2304]{1,0:T(8,128)(2,1)S(1)}, bf16[64,2304]{1,0:T(8,128)(2,1)S(1)}, u32[]{:S(2)}, u32[]{:S(2)}) collective-permute-start(bf16[64,2304]{1,0:T(8,128)(2,1)S(1)} %collective-permute-done.33.far_ref), channel_id=1, source_target_pairs={{0,2},{1,3},{2,0},{3,1},{4,6},{5,7},{6,4},{7,5},{8,10},{9,11},{10,... | collective-permute-start | bytes 884744 | tf_op jit(solution)/shard_map/ppermute | solution.py:36
  197.0 5.8 %collective-permute-done.31.last_ref = bf16[64,2304]{1,0:T(8,128)(2,1)S(1)} collective-permute-done((bf16[64,2304]{1,0:T(8,128)(2,1)S(1)}, bf16[64,2304]{1,0:T(8,128)(2,1)S(1)}, u32[]{:S(2)}, u32[]{:S(2)}) %collective-permute-start.31) | collective-permute-done | bytes 294944 | tf_op jit(solution)/shard_map/ppermute | solution.py:36
  202.8 2.6 %shard_map.174 = f32[40,256]{1,0:T(8,128)S(1)} custom-call(s32[6]{0:T(128)S(1)} %stack.35.where_ref, bf16[64,2304]{1,0:T(8,128)(2,1)S(1)} %shard_map.171.own_ref, bf16[64,2304]{1,0:T(8,128)(2,1)S(1)} %collective-permute-done.29.near_ref, bf16[64,2304]{1,0:T(8,128)(2,1)S(1)} %collective-permute-done.30.far_ref, ...), custom_call_target="tpu_custom_call" | custom-call | tf_op jit(solution)/shard_map/pallas_call | solution.py:168
  205.5 3.6 %collective-permute-done.32.near_ref = bf16[64,2304]{1,0:T(8,128)(2,1)S(1)} collective-permute-done((bf16[64,2304]{1,0:T(8,128)(2,1)S(1)}, bf16[64,2304]{1,0:T(8,128)(2,1)S(1)}, u32[]{:S(2)}, u32[]{:S(2)}) %collective-permute-start.32) | collective-permute-done | bytes 294944 | tf_op jit(solution)/shard_map/ppermute | solution.py:36
  209.1 6.3 %collective-permute-done.34.last_ref = bf16[64,2304]{1,0:T(8,128)(2,1)S(1)} collective-permute-done((bf16[64,2304]{1,0:T(8,128)(2,1)S(1)}, bf16[64,2304]{1,0:T(8,128)(2,1)S(1)}, u32[]{:S(2)}, u32[]{:S(2)}) %collective-permute-start.34) | collective-permute-done | bytes 294944 | tf_op jit(solution)/shard_map/ppermute | solution.py:36
  215.4 2.6 %shard_map.175 = f32[40,256]{1,0:T(8,128)S(1)} custom-call(s32[6]{0:T(128)S(1)} %stack.35.where_ref, bf16[64,2304]{1,0:T(8,128)(2,1)S(1)} %shard_map.173.own_ref, bf16[64,2304]{1,0:T(8,128)(2,1)S(1)} %collective-permute-done.32.near_ref, bf16[64,2304]{1,0:T(8,128)(2,1)S(1)} %collective-permute-done.33.far_ref, ...), custom_call_target="tpu_custom_call" | custom-call | tf_op jit(solution)/shard_map/pallas_call | solution.py:168
  218.2 2.2 collective-permute-start.35
  221.9 2.2 collective-permute-done.36.refs_2_
  224.7 6.0 %collective-permute-start.38 = (f32[32,128]{1,0:T(8,128)S(1)}, f32[32,128]{1,0:T(8,128)S(1)}, u32[]{:S(2)}, u32[]{:S(2)}) collective-permute-start(f32[32,128]{1,0:T(8,128)S(1)} %shard_map.176), channel_id=1, source_target_pairs={{0,0},{1,2},{2,4},{3,6},{4,16},{5,18},{6,20},{7,22},{8,8},{9,10},{... | collective-permute-start | bytes 49160 | tf_op jit(solution)/shard_map/ppermute | solution.py:36
  230.7 2.1 collective-permute-start.39
  234.2 5.4 %collective-permute-done.40.halo_ref = f32[32,128]{1,0:T(8,128)S(1)} collective-permute-done((f32[32,128]{1,0:T(8,128)S(1)}, f32[32,128]{1,0:T(8,128)S(1)}, u32[]{:S(2)}, u32[]{:S(2)}) %collective-permute-start.40) | collective-permute-done | bytes 16416 | tf_op jit(solution)/shard_map/ppermute | solution.py:36
  239.6 1.7 shard_map.177
  (103 shorter events, 28.3 us)
Async XLA Ops:
  0.6 18.5 %collective-permute-start.1 = (bf16[2304,1152]{1,0:T(8,128)(2,1)}, bf16[2304,1152]{1,0:T(8,128)(2,1)}, u32[]{:S(2)}, u32[]{:S(2)}) collective-permute-start(bf16[2304,1152]{1,0:T(8,128)(2,1)} %refs_2_.11), channel_id=1, source_target_pairs={{0,1},{1,0},{2,3},{3,2},{4,5},{5,4},{6,7},{7,6},{8,9},{9,8},{10,11... | collective-permute-start | bytes 15925256 | tf_op jit(solution)/shard_map/ppermute | solution.py:36
  1.4 17.7 %collective-permute-start.2 = (bf16[1152,2304]{1,0:T(8,128)(2,1)}, bf16[1152,2304]{1,0:T(8,128)(2,1)}, u32[]{:S(2)}, u32[]{:S(2)}) collective-permute-start(bf16[1152,2304]{1,0:T(8,128)(2,1)} %refs_4_.11), channel_id=1, source_target_pairs={{0,1},{1,0},{2,3},{3,2},{4,5},{5,4},{6,7},{7,6},{8,9},{9,8},{10,11... | collective-permute-start | bytes 15925256 | tf_op jit(solution)/shard_map/ppermute | solution.py:36
  4.6 14.5 %collective-permute-start.4 = (bf16[128,2304]{1,0:T(8,128)(2,1)S(1)}, bf16[128,2304]{1,0:T(8,128)(2,1)S(1)}, u32[]{:S(2)}, u32[]{:S(2)}) collective-permute-start(bf16[128,2304]{1,0:T(8,128)(2,1)S(1)} %shard_map.159.refs_0_), channel_id=1, source_target_pairs={{0,2},{1,3},{2,0},{3,1},{4,6},{5,7},{6,4},{7,5},{8,10},{9,11},{10,... | collective-permute-start | bytes 1769480 | tf_op jit(solution)/shard_map/ppermute | solution.py:36
  5.5 5.1 %collective-permute-start.3 = (f32[1,1664]{1,0:T(1,128)S(1)}, f32[1,1664]{1,0:T(1,128)S(1)}, u32[]{:S(2)}, u32[]{:S(2)}) collective-permute-start(f32[1,1664]{1,0:T(1,128)S(1)} %broadcast_in_dim.12.refs_6_.bias_a), channel_id=1, source_target_pairs={{0,1},{1,0},{2,3},{3,2},{4,5},{5,4},{6,7},{7,6},{8,9},{9,8},{10,11... | collective-permute-start | bytes 19976 | tf_op jit(solution)/shard_map/ppermute | solution.py:36
  6.3 18.0 %collective-permute-start = (bf16[128,2304]{1,0:T(8,128)(2,1)S(1)}, bf16[128,2304]{1,0:T(8,128)(2,1)S(1)}, u32[]{:S(2)}, u32[]{:S(2)}) collective-permute-start(bf16[128,2304]{1,0:T(8,128)(2,1)S(1)} %shard_map.159.refs_0_), channel_id=1, source_target_pairs={{0,0},{1,1},{2,4},{3,5},{4,2},{5,3},{6,6},{7,7},{8,8},{9,9},{10,12... | collective-permute-start | bytes 1769480 | tf_op jit(solution)/shard_map/ppermute | solution.py:36
  19.1 21.8 %collective-permute-start.5 = (bf16[128,2304]{1,0:T(8,128)(2,1)S(1)}, bf16[128,2304]{1,0:T(8,128)(2,1)S(1)}, u32[]{:S(2)}, u32[]{:S(2)}) collective-permute-start(bf16[128,2304]{1,0:T(8,128)(2,1)S(1)} %collective-permute-done.4.refs_1_), channel_id=1, source_target_pairs={{0,0},{1,1},{2,4},{3,5},{4,2},{5,3},{6,6},{7,7},{8,8},{9,9},{10,12... | collective-permute-start | bytes 1769480 | tf_op jit(solution)/shard_map/ppermute | solution.py:36
  24.3 21.7 %collective-permute-start.9 = (bf16[128,2304]{1,0:T(8,128)(2,1)S(1)}, bf16[128,2304]{1,0:T(8,128)(2,1)S(1)}, u32[]{:S(2)}, u32[]{:S(2)}) collective-permute-start(bf16[128,2304]{1,0:T(8,128)(2,1)S(1)} %collective-permute-done.refs_0_), channel_id=1, source_target_pairs={{2,0},{3,1},{4,6},{5,7},{10,8},{11,9},{12,14},{13,15},{18,16},{19,... | collective-permute-start | bytes 1769480 | tf_op jit(solution)/shard_map/ppermute | solution.py:36
  25.6 29.3 %collective-permute-start.7 = (bf16[128,2304]{1,0:T(8,128)(2,1)S(1)}, bf16[128,2304]{1,0:T(8,128)(2,1)S(1)}, u32[]{:S(2)}, u32[]{:S(2)}) collective-permute-start(bf16[128,2304]{1,0:T(8,128)(2,1)S(1)} %shard_map.158.refs_0_), channel_id=1, source_target_pairs={{0,2},{1,3},{2,0},{3,1},{4,6},{5,7},{6,4},{7,5},{8,10},{9,11},{10,... | collective-permute-start | bytes 1769480 | tf_op jit(solution)/shard_map/ppermute | solution.py:36
  40.9 15.3 %collective-permute-start.8 = (bf16[128,2304]{1,0:T(8,128)(2,1)S(1)}, bf16[128,2304]{1,0:T(8,128)(2,1)S(1)}, u32[]{:S(2)}, u32[]{:S(2)}) collective-permute-start(bf16[128,2304]{1,0:T(8,128)(2,1)S(1)} %shard_map.158.refs_0_), channel_id=1, source_target_pairs={{0,0},{1,1},{2,4},{3,5},{4,2},{5,3},{6,6},{7,7},{8,8},{9,9},{10,12... | collective-permute-start | bytes 1769480 | tf_op jit(solution)/shard_map/ppermute | solution.py:36
  44.3 16.8 %collective-permute-start.10 = (f32[2,128,512]{2,1,0:T(8,128)S(1)}, f32[2,128,512]{2,1,0:T(8,128)S(1)}, u32[]{:S(2)}, u32[]{:S(2)}) collective-permute-start(f32[2,128,512]{2,1,0:T(8,128)S(1)} %bitcast.36), channel_id=1, source_target_pairs={{0,16},{1,17},{2,18},{3,19},{4,20},{5,21},{6,22},{7,23},{8,24},{9,... | collective-permute-start | bytes 1572872 | tf_op jit(solution)/shard_map/ppermute | solution.py:36
  44.6 19.0 %collective-permute-start.6 = (bf16[128,2304]{1,0:T(8,128)(2,1)S(1)}, bf16[128,2304]{1,0:T(8,128)(2,1)S(1)}, u32[]{:S(2)}, u32[]{:S(2)}) collective-permute-start(bf16[128,2304]{1,0:T(8,128)(2,1)S(1)} %collective-permute-done.5.refs_0_), channel_id=1, source_target_pairs={{2,0},{3,1},{4,6},{5,7},{10,8},{11,9},{12,14},{13,15},{18,16},{19,... | collective-permute-start | bytes 1769480 | tf_op jit(solution)/shard_map/ppermute | solution.py:36
  53.4 28.9 %collective-permute-start.14 = (bf16[128,2304]{1,0:T(8,128)(2,1)S(1)}, bf16[128,2304]{1,0:T(8,128)(2,1)S(1)}, u32[]{:S(2)}, u32[]{:S(2)}) collective-permute-start(bf16[128,2304]{1,0:T(8,128)(2,1)S(1)} %shard_map.161.a_ref), channel_id=1, source_target_pairs={{0,2},{1,3},{6,4},{7,5},{8,10},{9,11},{14,12},{15,13},{16,18},{17,... | collective-permute-start | bytes 1769480 | tf_op jit(solution)/shard_map/ppermute | solution.py:36
  56.3 28.9 %collective-permute-start.12 = (bf16[128,2304]{1,0:T(8,128)(2,1)S(1)}, bf16[128,2304]{1,0:T(8,128)(2,1)S(1)}, u32[]{:S(2)}, u32[]{:S(2)}) collective-permute-start(bf16[128,2304]{1,0:T(8,128)(2,1)S(1)} %collective-permute-done.7.refs_1_), channel_id=1, source_target_pairs={{0,0},{1,1},{2,4},{3,5},{4,2},{5,3},{6,6},{7,7},{8,8},{9,9},{10,12... | collective-permute-start | bytes 1769480 | tf_op jit(solution)/shard_map/ppermute | solution.py:36
  59.6 25.6 %collective-permute-start.13 = (bf16[128,2304]{1,0:T(8,128)(2,1)S(1)}, bf16[128,2304]{1,0:T(8,128)(2,1)S(1)}, u32[]{:S(2)}, u32[]{:S(2)}) collective-permute-start(bf16[128,2304]{1,0:T(8,128)(2,1)S(1)} %collective-permute-done.8.refs_0_), channel_id=1, source_target_pairs={{2,0},{3,1},{4,6},{5,7},{10,8},{11,9},{12,14},{13,15},{18,16},{19,... | collective-permute-start | bytes 1769480 | tf_op jit(solution)/shard_map/ppermute | solution.py:36
  61.1 11.1 %collective-permute-start.11 = (f32[2,128,512]{2,1,0:T(8,128)S(1)}, f32[2,128,512]{2,1,0:T(8,128)S(1)}, u32[]{:S(2)}, u32[]{:S(2)}) collective-permute-start(f32[2,128,512]{2,1,0:T(8,128)S(1)} %bitcast.35), channel_id=1, source_target_pairs={{0,1},{1,0},{2,3},{3,2},{4,5},{5,4},{6,7},{7,6},{8,9},{9,8},{10,11... | collective-permute-start | bytes 1572872 | tf_op jit(solution)/shard_map/ppermute | solution.py:36
  70.9 24.5 %collective-permute-start.15 = (bf16[128,2304]{1,0:T(8,128)(2,1)S(1)}, bf16[128,2304]{1,0:T(8,128)(2,1)S(1)}, u32[]{:S(2)}, u32[]{:S(2)}) collective-permute-start(bf16[128,2304]{1,0:T(8,128)(2,1)S(1)} %shard_map.162.a_ref), channel_id=1, source_target_pairs={{0,2},{1,3},{6,4},{7,5},{8,10},{9,11},{14,12},{15,13},{16,18},{17,... | collective-permute-start | bytes 1769480 | tf_op jit(solution)/shard_map/ppermute | solution.py:36
  83.1 14.3 %collective-permute-start.16 = (bf16[128,2304]{1,0:T(8,128)(2,1)S(1)}, bf16[128,2304]{1,0:T(8,128)(2,1)S(1)}, u32[]{:S(2)}, u32[]{:S(2)}) collective-permute-start(bf16[128,2304]{1,0:T(8,128)(2,1)S(1)} %shard_map.164), channel_id=1, source_target_pairs={{0,0},{1,1},{2,4},{3,5},{4,2},{5,3},{6,6},{7,7},{8,8},{9,9},{10,12... | collective-permute-start | bytes 1769480 | tf_op jit(solution)/shard_map/ppermute | solution.py:36
  85.2 12.5 %collective-permute-start.17 = (bf16[128,2304]{1,0:T(8,128)(2,1)S(1)}, bf16[128,2304]{1,0:T(8,128)(2,1)S(1)}, u32[]{:S(2)}, u32[]{:S(2)}) collective-permute-start(bf16[128,2304]{1,0:T(8,128)(2,1)S(1)} %collective-permute-done.12.refs_0_), channel_id=1, source_target_pairs={{2,0},{3,1},{4,6},{5,7},{10,8},{11,9},{12,14},{13,15},{18,16},{19,... | collective-permute-start | bytes 1769480 | tf_op jit(solution)/shard_map/ppermute | solution.py:36
  105.0 31.0 %copy-start.14 = (f32[2304]{0:T(1024)S(1)}, f32[2304]{0:T(1024)}, u32[]{:S(2)}) copy-start(f32[2304]{0:T(1024)} %param.21) | copy-start | bytes 27652
  105.1 47.5 %copy-start.4 = (bf16[256,2304]{1,0:T(8,128)(2,1)S(1)}, bf16[256,2304]{1,0:T(8,128)(2,1)}, u32[]{:S(2)}) copy-start(bf16[256,2304]{1,0:T(8,128)(2,1)} %tokens_ref.7) | copy-start | bytes 3538948
  105.1 47.5 %copy-start.11 = (f32[2,2304]{1,0:T(2,128)S(1)}, f32[2,2304]{1,0:T(2,128)}, u32[]{:S(2)}) copy-start(f32[2,2304]{1,0:T(2,128)} %gate_ref.3) | copy-start | bytes 55300
  105.1 60.2 %collective-permute-start.24 = (bf16[2304,512]{1,0:T(8,128)(2,1)S(1)}, bf16[2304,512]{1,0:T(8,128)(2,1)S(1)}, u32[]{:S(2)}, u32[]{:S(2)}) collective-permute-start(bf16[2304,512]{1,0:T(8,128)(2,1)S(1)} %copy-done.5), channel_id=1, source_target_pairs={{0,1},{1,0},{2,3},{3,2},{4,5},{5,4},{6,7},{7,6},{8,9},{9,8},{10,11... | collective-permute-start | bytes 7077896 | tf_op jit(solution)/shard_map/ppermute | solution.py:36
  108.8 15.8 %collective-permute-start.18 = (bf16[128,2304]{1,0:T(8,128)(2,1)S(1)}, bf16[128,2304]{1,0:T(8,128)(2,1)S(1)}, u32[]{:S(2)}, u32[]{:S(2)}) collective-permute-start(bf16[128,2304]{1,0:T(8,128)(2,1)S(1)} %shard_map.167), channel_id=1, source_target_pairs={{0,2},{1,3},{2,0},{3,1},{4,6},{5,7},{6,4},{7,5},{8,10},{9,11},{10,... | collective-permute-start | bytes 1769480 | tf_op jit(solution)/shard_map/ppermute | solution.py:36
  111.0 16.5 %collective-permute-start.20 = (bf16[128,2304]{1,0:T(8,128)(2,1)S(1)}, bf16[128,2304]{1,0:T(8,128)(2,1)S(1)}, u32[]{:S(2)}, u32[]{:S(2)}) collective-permute-start(bf16[128,2304]{1,0:T(8,128)(2,1)S(1)} %shard_map.166), channel_id=1, source_target_pairs={{0,0},{1,1},{2,4},{3,5},{4,2},{5,3},{6,6},{7,7},{8,8},{9,9},{10,12... | collective-permute-start | bytes 1769480 | tf_op jit(solution)/shard_map/ppermute | solution.py:36
  125.3 34.3 %copy-start.10 = (bf16[512,32]{0,1:T(8,128)(2,1)S(1)}, bf16[512,32]{0,1:T(8,128)(2,1)}, u32[]{:S(2)}) copy-start(bf16[512,32]{0,1:T(8,128)(2,1)} %param.26) | copy-start | bytes 98308
  128.1 24.5 %collective-permute-start.21 = (bf16[128,2304]{1,0:T(8,128)(2,1)S(1)}, bf16[128,2304]{1,0:T(8,128)(2,1)S(1)}, u32[]{:S(2)}, u32[]{:S(2)}) collective-permute-start(bf16[128,2304]{1,0:T(8,128)(2,1)S(1)} %shard_map.169), channel_id=1, source_target_pairs={{0,2},{1,3},{2,0},{3,1},{4,6},{5,7},{6,4},{7,5},{8,10},{9,11},{10,... | collective-permute-start | bytes 1769480 | tf_op jit(solution)/shard_map/ppermute | solution.py:36
  128.2 37.0 %collective-permute-start.19 = (bf16[128,2304]{1,0:T(8,128)(2,1)S(1)}, bf16[128,2304]{1,0:T(8,128)(2,1)S(1)}, u32[]{:S(2)}, u32[]{:S(2)}) collective-permute-start(bf16[128,2304]{1,0:T(8,128)(2,1)S(1)} %get-tuple-element.68), channel_id=1, source_target_pairs={{0,2},{1,3},{2,0},{3,1},{4,6},{5,7},{6,4},{7,5},{8,10},{9,11},{10,... | collective-permute-start | bytes 1769480 | tf_op jit(solution)/shard_map/ppermute | solution.py:36
  129.7 37.5 %collective-permute-start.27 = (bf16[128,2304]{1,0:T(8,128)(2,1)S(1)}, bf16[128,2304]{1,0:T(8,128)(2,1)S(1)}, u32[]{:S(2)}, u32[]{:S(2)}) collective-permute-start(bf16[128,2304]{1,0:T(8,128)(2,1)S(1)} %shard_map.168), channel_id=1, source_target_pairs={{0,4},{1,5},{2,6},{3,7},{4,0},{5,1},{6,2},{7,3},{8,12},{9,13},{10,... | collective-permute-start | bytes 1769480 | tf_op jit(solution)/shard_map/ppermute | solution.py:36
  129.8 3.1 %collective-permute-start.22 = (f32[2,2,2304]{2,1,0:T(2,128)S(1)}, f32[2,2,2304]{2,1,0:T(2,128)S(1)}, u32[]{:S(2)}, u32[]{:S(2)}) collective-permute-start(f32[2,2,2304]{2,1,0:T(2,128)S(1)} %copy-done.6), channel_id=1, source_target_pairs={{0,16},{1,17},{2,18},{3,19},{4,20},{5,21},{6,22},{7,23},{8,24},{9,... | collective-permute-start | bytes 110600 | tf_op jit(solution)/shard_map/ppermute | solution.py:36
  132.9 31.8 %collective-permute-start.26 = (f32[2,128,512]{2,1,0:T(8,128)S(1)}, f32[2,128,512]{2,1,0:T(8,128)S(1)}, u32[]{:S(2)}, u32[]{:S(2)}) collective-permute-start(f32[2,128,512]{2,1,0:T(8,128)S(1)} %bitcast.34), channel_id=1, source_target_pairs={{0,17},{1,16},{2,19},{3,18},{4,21},{5,20},{6,23},{7,22},{8,25},{9,... | collective-permute-start | bytes 1572872 | tf_op jit(solution)/shard_map/ppermute | solution.py:36
  153.6 5.9 %collective-permute-start.23 = (bf16[64,2304]{1,0:T(8,128)(2,1)S(1)}, bf16[64,2304]{1,0:T(8,128)(2,1)S(1)}, u32[]{:S(2)}, u32[]{:S(2)}) collective-permute-start(bf16[64,2304]{1,0:T(8,128)(2,1)S(1)} %get-tuple-element.74), channel_id=1, source_target_pairs={{0,16},{1,17},{2,18},{3,19},{4,20},{5,21},{6,22},{7,23},{8,24},{9,... | collective-permute-start | bytes 884744 | tf_op jit(solution)/shard_map/ppermute | solution.py:36
  159.6 5.1 %collective-permute-start.25 = (bf16[32,512]{1,0:T(8,128)(2,1)S(1)}, bf16[32,512]{1,0:T(8,128)(2,1)S(1)}, u32[]{:S(2)}, u32[]{:S(2)}) collective-permute-start(bf16[32,512]{1,0:T(8,128)(2,1)S(1)} %bitcast.29), channel_id=1, source_target_pairs={{0,1},{1,0},{2,3},{3,2},{4,5},{5,4},{6,7},{7,6},{8,9},{9,8},{10,11... | collective-permute-start | bytes 98312 | tf_op jit(solution)/shard_map/ppermute | solution.py:36
  169.2 6.4 %collective-permute-start.28 = (bf16[64,2304]{1,0:T(8,128)(2,1)S(1)}, bf16[64,2304]{1,0:T(8,128)(2,1)S(1)}, u32[]{:S(2)}, u32[]{:S(2)}) collective-permute-start(bf16[64,2304]{1,0:T(8,128)(2,1)S(1)} %get-tuple-element.83), channel_id=1, source_target_pairs={{0,16},{1,17},{2,18},{3,19},{4,20},{5,21},{6,22},{7,23},{8,24},{9,... | collective-permute-start | bytes 884744 | tf_op jit(solution)/shard_map/ppermute | solution.py:36
  169.9 17.0 %collective-permute-start.30 = (bf16[64,2304]{1,0:T(8,128)(2,1)S(1)}, bf16[64,2304]{1,0:T(8,128)(2,1)S(1)}, u32[]{:S(2)}, u32[]{:S(2)}) collective-permute-start(bf16[64,2304]{1,0:T(8,128)(2,1)S(1)} %shard_map.171.own_ref), channel_id=1, source_target_pairs={{0,4},{1,5},{2,6},{3,7},{4,0},{5,1},{6,2},{7,3},{8,12},{9,13},{10,... | collective-permute-start | bytes 884744 | tf_op jit(solution)/shard_map/ppermute | solution.py:36
  176.6 18.0 %collective-permute-start.33 = (bf16[64,2304]{1,0:T(8,128)(2,1)S(1)}, bf16[64,2304]{1,0:T(8,128)(2,1)S(1)}, u32[]{:S(2)}, u32[]{:S(2)}) collective-permute-start(bf16[64,2304]{1,0:T(8,128)(2,1)S(1)} %shard_map.173.own_ref), channel_id=1, source_target_pairs={{0,4},{1,5},{2,6},{3,7},{4,0},{5,1},{6,2},{7,3},{8,12},{9,13},{10,... | collective-permute-start | bytes 884744 | tf_op jit(solution)/shard_map/ppermute | solution.py:36
  177.3 19.7 %collective-permute-start.29 = (bf16[64,2304]{1,0:T(8,128)(2,1)S(1)}, bf16[64,2304]{1,0:T(8,128)(2,1)S(1)}, u32[]{:S(2)}, u32[]{:S(2)}) collective-permute-start(bf16[64,2304]{1,0:T(8,128)(2,1)S(1)} %shard_map.171.own_ref), channel_id=1, source_target_pairs={{0,2},{1,3},{2,0},{3,1},{4,6},{5,7},{6,4},{7,5},{8,10},{9,11},{10,... | collective-permute-start | bytes 884744 | tf_op jit(solution)/shard_map/ppermute | solution.py:36
  186.9 15.9 %collective-permute-start.31 = (bf16[64,2304]{1,0:T(8,128)(2,1)S(1)}, bf16[64,2304]{1,0:T(8,128)(2,1)S(1)}, u32[]{:S(2)}, u32[]{:S(2)}) collective-permute-start(bf16[64,2304]{1,0:T(8,128)(2,1)S(1)} %collective-permute-done.30.far_ref), channel_id=1, source_target_pairs={{0,2},{1,3},{2,0},{3,1},{4,6},{5,7},{6,4},{7,5},{8,10},{9,11},{10,... | collective-permute-start | bytes 884744 | tf_op jit(solution)/shard_map/ppermute | solution.py:36
  190.0 19.1 %collective-permute-start.32 = (bf16[64,2304]{1,0:T(8,128)(2,1)S(1)}, bf16[64,2304]{1,0:T(8,128)(2,1)S(1)}, u32[]{:S(2)}, u32[]{:S(2)}) collective-permute-start(bf16[64,2304]{1,0:T(8,128)(2,1)S(1)} %shard_map.173.own_ref), channel_id=1, source_target_pairs={{0,2},{1,3},{2,0},{3,1},{4,6},{5,7},{6,4},{7,5},{8,10},{9,11},{10,... | collective-permute-start | bytes 884744 | tf_op jit(solution)/shard_map/ppermute | solution.py:36
  194.6 20.9 %collective-permute-start.34 = (bf16[64,2304]{1,0:T(8,128)(2,1)S(1)}, bf16[64,2304]{1,0:T(8,128)(2,1)S(1)}, u32[]{:S(2)}, u32[]{:S(2)}) collective-permute-start(bf16[64,2304]{1,0:T(8,128)(2,1)S(1)} %collective-permute-done.33.far_ref), channel_id=1, source_target_pairs={{0,2},{1,3},{2,0},{3,1},{4,6},{5,7},{6,4},{7,5},{8,10},{9,11},{10,... | collective-permute-start | bytes 884744 | tf_op jit(solution)/shard_map/ppermute | solution.py:36
  205.5 28.6 %copy-start.15 = (f32[32]{0:T(128)S(1)}, f32[32]{0:T(128)}, u32[]{:S(2)}) copy-start(f32[32]{0:T(128)} %param.28) | copy-start | bytes 388
  205.5 34.1 %copy-start.7 = (f32[32,32,3,3]{1,0,3,2:T(8,128)S(1)}, f32[32,32,3,3]{1,0,3,2:T(8,128)}, u32[]{:S(2)}) copy-start(f32[32,32,3,3]{1,0,3,2:T(8,128)} %param.27) | copy-start | bytes 110596
  205.5 34.1 %copy-start.12 = (f32[1,32,128]{2,1,0:T(8,128)S(1)}, f32[1,32,128]{2,1,0:T(8,128)}, u32[]{:S(2)}) copy-start(f32[1,32,128]{2,1,0:T(8,128)} %param.29) | copy-start | bytes 49156
  218.2 3.7 %collective-permute-start.35 = (f32[40,128]{1,0:T(8,128)S(1)}, f32[40,128]{1,0:T(8,128)S(1)}, u32[]{:S(2)}, u32[]{:S(2)}) collective-permute-start(f32[40,128]{1,0:T(8,128)S(1)} %pad_maximum_fusion.1), channel_id=1, source_target_pairs={{0,2},{1,3},{2,0},{3,1},{4,6},{5,7},{6,4},{7,5},{8,10},{9,11},{10,... | collective-permute-start | bytes 61448 | tf_op jit(solution)/shard_map/ppermute | solution.py:36
  220.5 3.6 %collective-permute-start.36 = (f32[40,128]{1,0:T(8,128)S(1)}, f32[40,128]{1,0:T(8,128)S(1)}, u32[]{:S(2)}, u32[]{:S(2)}) collective-permute-start(f32[40,128]{1,0:T(8,128)S(1)} %pad_maximum_fusion.2), channel_id=1, source_target_pairs={{0,4},{1,5},{2,6},{3,7},{4,0},{5,1},{6,2},{7,3},{8,12},{9,13},{10,... | collective-permute-start | bytes 61448 | tf_op jit(solution)/shard_map/ppermute | solution.py:36
  221.0 3.1 %collective-permute-start.37 = (f32[40,128]{1,0:T(8,128)S(1)}, f32[40,128]{1,0:T(8,128)S(1)}, u32[]{:S(2)}, u32[]{:S(2)}) collective-permute-start(f32[40,128]{1,0:T(8,128)S(1)} %pad_maximum_fusion.3), channel_id=1, source_target_pairs={{0,6},{1,7},{2,4},{3,5},{4,2},{5,3},{6,0},{7,1},{8,14},{9,15},{10,... | collective-permute-start | bytes 61448 | tf_op jit(solution)/shard_map/ppermute | solution.py:36
  224.7 9.5 %collective-permute-start.38 = (f32[32,128]{1,0:T(8,128)S(1)}, f32[32,128]{1,0:T(8,128)S(1)}, u32[]{:S(2)}, u32[]{:S(2)}) collective-permute-start(f32[32,128]{1,0:T(8,128)S(1)} %shard_map.176), channel_id=1, source_target_pairs={{0,0},{1,2},{2,4},{3,6},{4,16},{5,18},{6,20},{7,22},{8,8},{9,10},{... | collective-permute-start | bytes 49160 | tf_op jit(solution)/shard_map/ppermute | solution.py:36
  230.7 3.5 %collective-permute-start.39 = (f32[32,128]{1,0:T(8,128)S(1)}, f32[32,128]{1,0:T(8,128)S(1)}, u32[]{:S(2)}, u32[]{:S(2)}) collective-permute-start(f32[32,128]{1,0:T(8,128)S(1)} %shard_map.176), channel_id=1, source_target_pairs={{0,1},{1,3},{2,5},{3,7},{4,17},{5,19},{6,21},{7,23},{8,9},{9,11},{... | collective-permute-start | bytes 49160 | tf_op jit(solution)/shard_map/ppermute | solution.py:36
  232.8 6.8 %collective-permute-start.40 = (f32[32,128]{1,0:T(8,128)S(1)}, f32[32,128]{1,0:T(8,128)S(1)}, u32[]{:S(2)}, u32[]{:S(2)}) collective-permute-start(f32[32,128]{1,0:T(8,128)S(1)} %shard_map.176), channel_id=1, source_target_pairs={{1,1},{2,3},{3,5},{5,17},{6,19},{7,21},{9,9},{10,11},{11,13},{13,2... | collective-permute-start | bytes 49160 | tf_op jit(solution)/shard_map/ppermute | solution.py:36
  (11 other events, 115.2 us)

commit v4 on v3

--- a/solution.py
+++ b/solution.py
@@ -164,7 +164,7 @@
 MID, UPPER, IMAGE, ODD, SAME, CORE = range(6)
 
 
-def call(kernel, where, args, outs, scratch=()):
+def call(kernel, where, args, outs, scratch=(), flops=0):
     return pl.pallas_call(
         kernel,
         out_shape=outs,
@@ -172,7 +172,7 @@
         out_specs=[ON_CHIP] * len(outs),
         scratch_shapes=scratch,
         compiler_params=pltpu.CompilerParams(vmem_limit_bytes=VMEM_LIMIT),
-        cost_estimate=pl.CostEstimate(flops=0, bytes_accessed=0, transcendentals=0),
+        cost_estimate=pl.CostEstimate(flops=flops, bytes_accessed=0, transcendentals=0),
     )(where, *args)
 
 
@@ -197,6 +197,29 @@
 def norm_part(where, tokens, ada, begin, size):
     outs = [shape_of((size, tokens.shape[1]))]
     return call(functools.partial(norm_kernel, begin), where, (tokens, ada), outs)[0]
+
+
+def stage_kernel(where_ref, up_ref, down_ref, up_out, down_out, sems):
+    copies = [
+        pltpu.make_async_copy(up_ref, up_out, sems.at[0]),
+        pltpu.make_async_copy(down_ref, down_out, sems.at[1]),
+    ]
+    for copy in copies:
+        copy.start()
+    for copy in copies:
+        copy.wait()
+
+
+def stage(where, up, down):
+    return pl.pallas_call(
+        stage_kernel,
+        out_shape=[shape_of(up.shape), shape_of(down.shape)],
+        in_specs=[SCALARS] + [pl.BlockSpec(memory_space=pltpu.HBM)] * 2,
+        out_specs=[ON_CHIP] * 2,
+        scratch_shapes=[pltpu.SemaphoreType.DMA((2,))],
+        compiler_params=pltpu.CompilerParams(vmem_limit_bytes=VMEM_LIMIT),
+        cost_estimate=pl.CostEstimate(flops=0, bytes_accessed=0, transcendentals=0),
+    )(where, up, down)
 
 
 def ffn_kernel(groups, tile, where_ref, *refs):
@@ -260,8 +283,8 @@
     out_ref[...] = (a_ref[...].astype(jnp.float32) + b).astype(jnp.bfloat16)
 
 
-def add(where, a, b, always=False):
-    return call(functools.partial(add_kernel, always), where, (a, b), [shape_of(a.shape)])[0]
+def add(where, a, b, always=False, flops=0):
+    return call(functools.partial(add_kernel, always), where, (a, b), [shape_of(a.shape)], flops=flops)[0]
 
 
 def out_kernel(begin, always, where_ref, own_ref, near_ref, far_ref, tokens_ref, gate_ref, bias_ref, *refs):
@@ -507,17 +530,20 @@
     )
     noise_twin, noise_core, noise_both, _ = barrier((noise_twin, noise_core, noise_both, own_b))
     noise_twin = swap_twins(noise_twin)
-    up_other, down_other, bias_other, near_a = barrier((up_other, down_other, bias_other, near_a))
-    panels = (up_weight, up_other, down_weight, down_other, biases, bias_other)
+    up_own, down_own = stage(where, up_weight, down_weight)
+    up_own, down_own, up_other, down_other, bias_other, near_a, own_b = barrier(
+        (up_own, down_own, up_other, down_other, bias_other, near_a, own_b)
+    )
+    panels = (up_own, up_other, down_own, down_other, biases, bias_other)
     far_mid_a = middle(near_a)
     near_b = near(after(own_b, near_a))
     mid_a = after(mid_a, near_a)
     far_end_a = outward(mid_a)
     sum_own_a, sum_near_a = ffn(where, [[own_a], [after(near_a, mid_a)]], panels)
-    noise_core = swap_cores(after(noise_core, sum_near_a))
     far_mid_a = after(far_mid_a, sum_near_a)
     last_end_a = outward(far_mid_a)
     mid_b = middle(after(own_b, far_mid_a))
+    noise_core = swap_cores(after(noise_core, far_mid_a))
     (sum_far_a,) = ffn(where, [[far_mid_a, far_end_a]], panels)
     came_far_a = inward(sum_far_a)
     near_b, mid_b = barrier((near_b, mid_b, sum_far_a))[:2]
@@ -535,14 +561,14 @@
     went_far_a = middle(both_far_a)
     (sum_last_b,) = ffn(where, [[after(mid_b, both_far_a, went_last_a), last_end_b]], panels)
     came_last_b = near(sum_last_b)
+    came_near_b = near(after(sum_near_b, last_end_b))
     head_other = swap_cores(after(head_weight, sum_last_b))
     head_twin = swap_twins(after(ada_head, sum_last_b))
     code_other = swap_cores(after(codes, sum_last_b))
-    both_far_b = add(where, sum_far_b, came_last_b, True)
+    both_near_a = add(where, sum_near_a, after(went_far_a, went_last_a, came_near_b), flops=40000000000)
+    came_near_a = near(both_near_a)
+    both_far_b = add(where, after(sum_far_b, both_near_a), came_last_b, True)
     went_far_b = across(both_far_b)
-    came_near_b = near(after(sum_near_b, both_far_b))
-    both_near_a = add(where, sum_near_a, after(went_far_a, went_last_a, both_far_b))
-    came_near_a = near(both_near_a)
     out_a, kept_a, sent_a = block_rows(
         where, 0, False, sum_own_a, after(came_near_a, head_twin), went_last_a, tokens, gate, bias_out
     )
@@ -552,7 +578,7 @@
     block_out, kept_b, sent_b = block_rows(
         where, step, True, sum_own_b, after(came_near_b, mixed_a, head_other, code_other, noise_both), went_far_b, tokens, gate, bias_out, (out_a,)
     )
-    came_b = swap_twins(sent_b)
+    came_b = after(swap_twins(sent_b), mix_far_a)
     mix_last_a = near(mix_far_a)
     mixed_b = mix_twins(where, kept_b, came_b, ada_head, head_twin)
     mix_near_b, mix_far_b = near(mixed_b), across(mixed_b)

time: 242 us -> 242 us (level)
  waiting for transfers between devices: 93.1 us -> 74.7 us
  local copies, waits for them, and re-layouts: 8.45 us -> 19.3 us
  starting transfers between devices: 70.6 us -> 76.2 us
    ppermute x41, waiting for transfers between devices: 93.1 us -> 74.7 us  [permute_devices(): return lax.ppermute(value, ('dp', 'mp'), pairs)]
    unnamed x36 -> x52, local copies, waits for them, and re-layouts: 7.88 us -> 18.7 us
    ppermute x41, starting transfers between devices: 70.6 us -> 76.2 us  [permute_devices(): return lax.ppermute(value, ('dp', 'mp'), pairs)]
  transfers between devices with their start and end apart: 41 -> 41, of which waited for: 20 -> 14; matrix products, arithmetic and copies ran while one was open for 1% -> 1% of each run, Pallas kernels for 22% -> 26%
where the time goes in v4:
time: 242 us; the launch traced here: 241 us
  starting transfers between devices  76.2 us (31%)
  waiting for transfers between devices  74.7 us (31%)
  Pallas kernels  68.5 us (28%)
  local copies, waits for them, and re-layouts  19.3 us (8%)
    ppermute x41, starting transfers between devices, permute_devices(): return lax.ppermute(value, ('dp', 'mp'), pairs)  76.2 us
    ppermute x41, waiting for transfers between devices, permute_devices(): return lax.ppermute(value, ('dp', 'mp'), pairs)  74.7 us
    pallas_call x20, Pallas kernels, call(): pl.pallas_call(kernel, out_shape=outs, in_specs=[SCALARS] + [ON_CHIP] * l...  67.1 us
    unnamed x52, local copies, waits for them, and re-layouts  18.7 us
  transfers between devices with their start and end apart: 41, of which 14 were waited for; matrix products, arithmetic and copies ran while one was open for 1% of the time, Pallas kernels for 26%

profile of v4, /device:TPU:13, one launch (start us, length us, event | category | flops | bytes accessed | tf_op | source)
XLA Modules:
  0.0 241.0 jit_solution(12964140285140561380)
XLA Ops:
  6.3 4.3 %collective-permute-start.4 = (bf16[128,2304]{1,0:T(8,128)(2,1)S(1)}, bf16[128,2304]{1,0:T(8,128)(2,1)S(1)}, u32[]{:S(2)}, u32[]{:S(2)}) collective-permute-start(bf16[128,2304]{1,0:T(8,128)(2,1)S(1)} %shard_map.159.refs_0_), channel_id=1, source_target_pairs={{0,0},{1,1},{2,4},{3,5},{4,2},{5,3},{6,6},{7,7},{8,8},{9,9},{10,12... | collective-permute-start | bytes 1769480 | tf_op jit(solution)/shard_map/ppermute | solution.py:36
  10.7 2.5 %copy-done.8 = bf16[2304,1152]{1,0:T(8,128)(2,1)S(1)} copy-done((bf16[2304,1152]{1,0:T(8,128)(2,1)S(1)}, bf16[2304,1152]{1,0:T(8,128)(2,1)}, u32[]{:S(2)}) %copy-start.8) | copy-done | bytes 5308440
  13.2 2.5 %copy-done.9 = bf16[1152,2304]{1,0:T(8,128)(2,1)S(1)} copy-done((bf16[1152,2304]{1,0:T(8,128)(2,1)S(1)}, bf16[1152,2304]{1,0:T(8,128)(2,1)}, u32[]{:S(2)}) %copy-start.9) | copy-done | bytes 5308440
  15.7 1.4 shard_map.158
  17.1 2.3 copy-done
  19.4 2.4 copy-done.3
  23.5 1.9 collective-permute-start.5
  25.4 1.3 collective-permute-start.9
  26.9 2.5 %copy-done.1 = bf16[2304,1152]{1,0:T(8,128)(2,1)S(1)} copy-done((bf16[2304,1152]{1,0:T(8,128)(2,1)S(1)}, bf16[2304,1152]{1,0:T(8,128)(2,1)}, u32[]{:S(2)}) %copy-start.1) | copy-done | bytes 5308440
  29.4 2.5 %copy-done.4 = bf16[1152,2304]{1,0:T(8,128)(2,1)S(1)} copy-done((bf16[1152,2304]{1,0:T(8,128)(2,1)S(1)}, bf16[1152,2304]{1,0:T(8,128)(2,1)}, u32[]{:S(2)}) %copy-start.4) | copy-done | bytes 5308440
  32.5 10.2 %shard_map.161 = (bf16[128,2304]{1,0:T(8,128)(2,1)S(1)}, bf16[128,2304]{1,0:T(8,128)(2,1)S(1)}) custom-call(s32[6]{0:T(128)S(1)} %copy-done.12, bf16[128,2304]{1,0:T(8,128)(2,1)S(1)} %shard_map.159.refs_0_, bf16[128,2304]{1,0:T(8,128)(2,1)S(1)} %collective-permute-done.3.refs_1_, bf16[2304,1152]{1,0:T(8,128)(2,1)S(1)} %copy-done.1, ...), custom_call_target="tpu_custom_call" | custom-call | tf_op jit(solution)/shard_map/pallas_call | solution.py:168
  42.7 3.4 %collective-permute-start.8 = (bf16[128,2304]{1,0:T(8,128)(2,1)S(1)}, bf16[128,2304]{1,0:T(8,128)(2,1)S(1)}, u32[]{:S(2)}, u32[]{:S(2)}) collective-permute-start(bf16[128,2304]{1,0:T(8,128)(2,1)S(1)} %shard_map.160.refs_0_), channel_id=1, source_target_pairs={{0,0},{1,1},{2,4},{3,5},{4,2},{5,3},{6,6},{7,7},{8,8},{9,9},{10,12... | collective-permute-start | bytes 1769480 | tf_op jit(solution)/shard_map/ppermute | solution.py:36
  46.6 1.3 collective-permute-start.6
  48.6 7.5 %shard_map.162.a_ref = bf16[128,2304]{1,0:T(8,128)(2,1)S(1)} custom-call(s32[6]{0:T(128)S(1)} %copy-done.13, bf16[128,2304]{1,0:T(8,128)(2,1)} %collective-permute-done.5.refs_0_, bf16[128,2304]{1,0:T(8,128)(2,1)S(1)} %collective-permute-done.9.refs_1_, bf16[2304,1152]{1,0:T(8,128)(2,1)S(1)} %copy-done.2, bf16[2304,1152]{1,0:T(8,128)(2,1)} %collective-permute-done.refs_3_, ...), custom_call_target="tpu_custom_call" | custom-call | tf_op jit(solution)/shard_map/pallas_call | solution.py:168
  57.4 1.7 collective-permute-done.8.refs_0_
  59.1 3.0 %collective-permute-start.12 = (bf16[128,2304]{1,0:T(8,128)(2,1)S(1)}, bf16[128,2304]{1,0:T(8,128)(2,1)S(1)}, u32[]{:S(2)}, u32[]{:S(2)}) collective-permute-start(bf16[128,2304]{1,0:T(8,128)(2,1)S(1)} %collective-permute-done.7.refs_1_), channel_id=1, source_target_pairs={{0,0},{1,1},{2,4},{3,5},{4,2},{5,3},{6,6},{7,7},{8,8},{9,9},{10,12... | collective-permute-start | bytes 1769480 | tf_op jit(solution)/shard_map/ppermute | solution.py:36
  62.1 1.5 collective-permute-start.13
  63.7 1.9 collective-permute-start.11
  65.6 7.3 %shard_map.163.a_ref = bf16[128,2304]{1,0:T(8,128)(2,1)S(1)} custom-call(s32[6]{0:T(128)S(1)} %copy-done.13, bf16[128,2304]{1,0:T(8,128)(2,1)S(1)} %collective-permute-done.4.refs_0_, bf16[128,2304]{1,0:T(8,128)(2,1)S(1)} %collective-permute-done.6.refs_1_, bf16[2304,1152]{1,0:T(8,128)(2,1)S(1)} %copy-done.2, ...), custom_call_target="tpu_custom_call" | custom-call | tf_op jit(solution)/shard_map/pallas_call | solution.py:168
  74.2 10.1 %shard_map.164 = (bf16[128,2304]{1,0:T(8,128)(2,1)S(1)}, bf16[128,2304]{1,0:T(8,128)(2,1)S(1)}) custom-call(s32[6]{0:T(128)S(1)} %copy-done.14, bf16[128,2304]{1,0:T(8,128)(2,1)S(1)} %shard_map.160.refs_0_, bf16[128,2304]{1,0:T(8,128)(2,1)S(1)} %collective-permute-done.7.refs_1_, bf16[2304,1152]{1,0:T(8,128)(2,1)S(1)} %copy-done.2, ...), custom_call_target="tpu_custom_call" | custom-call | tf_op jit(solution)/shard_map/pallas_call | solution.py:168
  85.1 4.1 %collective-permute-start.15 = (bf16[128,2304]{1,0:T(8,128)(2,1)S(1)}, bf16[128,2304]{1,0:T(8,128)(2,1)S(1)}, u32[]{:S(2)}, u32[]{:S(2)}) collective-permute-start(bf16[128,2304]{1,0:T(8,128)(2,1)S(1)} %collective-permute-done.12.refs_0_), channel_id=1, source_target_pairs={{2,0},{3,1},{4,6},{5,7},{10,8},{11,9},{12,14},{13,15},{18,16},{19,... | collective-permute-start | bytes 1769480 | tf_op jit(solution)/shard_map/ppermute | solution.py:36
  89.1 2.1 collective-permute-start.19
  91.3 7.3 %shard_map.166.a_ref = bf16[128,2304]{1,0:T(8,128)(2,1)S(1)} custom-call(s32[6]{0:T(128)S(1)} %copy-done.14, bf16[128,2304]{1,0:T(8,128)(2,1)S(1)} %collective-permute-done.12.refs_0_, bf16[128,2304]{1,0:T(8,128)(2,1)S(1)} %collective-permute-done.13.refs_1_, bf16[2304,1152]{1,0:T(8,128)(2,1)S(1)} %copy-done.2, ...), custom_call_target="tpu_custom_call" | custom-call | tf_op jit(solution)/shard_map/pallas_call | solution.py:168
  99.3 3.5 %collective-permute-start.18 = (bf16[128,2304]{1,0:T(8,128)(2,1)S(1)}, bf16[128,2304]{1,0:T(8,128)(2,1)S(1)}, u32[]{:S(2)}, u32[]{:S(2)}) collective-permute-start(bf16[128,2304]{1,0:T(8,128)(2,1)S(1)} %shard_map.167), channel_id=1, source_target_pairs={{0,0},{1,1},{2,4},{3,5},{4,2},{5,3},{6,6},{7,7},{8,8},{9,9},{10,12... | collective-permute-start | bytes 1769480 | tf_op jit(solution)/shard_map/ppermute | solution.py:36
  103.0 1.6 collective-permute-done.19.far_ref
  104.7 7.3 %shard_map.169 = bf16[128,2304]{1,0:T(8,128)(2,1)S(1)} custom-call(s32[6]{0:T(128)S(1)} %copy-done.14, bf16[128,2304]{1,0:T(8,128)(2,1)S(1)} %collective-permute-done.8.refs_0_, bf16[128,2304]{1,0:T(8,128)(2,1)S(1)} %collective-permute-done.15.refs_1_, bf16[2304,1152]{1,0:T(8,128)(2,1)S(1)} %copy-done.2, bf16[2304,1152]{1,0:T(8,128)(2,1)} %collective-permute-done.refs_3_, ...), custom_call_target="tpu_custom_call" | custom-call | tf_op jit(solution)/shard_map/pallas_call | solution.py:168
  112.1 3.9 %collective-permute-start.23 = (bf16[2304,512]{1,0:T(8,128)(2,1)S(1)}, bf16[2304,512]{1,0:T(8,128)(2,1)S(1)}, u32[]{:S(2)}, u32[]{:S(2)}) collective-permute-start(bf16[2304,512]{1,0:T(8,128)(2,1)S(1)} %copy-done.7), channel_id=1, source_target_pairs={{0,1},{1,0},{2,3},{3,2},{4,5},{5,4},{6,7},{7,6},{8,9},{9,8},{10,11... | collective-permute-start | bytes 7077896 | tf_op jit(solution)/shard_map/ppermute | solution.py:36
  118.4 10.2 %collective-permute-done.26.b_ref = bf16[128,2304]{1,0:T(8,128)(2,1)S(1)} collective-permute-done((bf16[128,2304]{1,0:T(8,128)(2,1)S(1)}, bf16[128,2304]{1,0:T(8,128)(2,1)S(1)}, u32[]{:S(2)}, u32[]{:S(2)}) %collective-permute-start.26) | collective-permute-done | bytes 589856 | tf_op jit(solution)/shard_map/ppermute | solution.py:36
  129.4 12.8 %collective-permute-start.25 = (f32[2,128,512]{2,1,0:T(8,128)S(1)}, f32[2,128,512]{2,1,0:T(8,128)S(1)}, u32[]{:S(2)}, u32[]{:S(2)}) collective-permute-start(f32[2,128,512]{2,1,0:T(8,128)S(1)} %bitcast.32), channel_id=1, source_target_pairs={{0,17},{1,16},{2,19},{3,18},{4,21},{5,20},{6,23},{7,22},{8,25},{9,... | collective-permute-start | bytes 1572872 | tf_op jit(solution)/shard_map/ppermute | solution.py:36
  143.5 12.3 %collective-permute-done.21.twin_ref = f32[2,2,2304]{2,1,0:T(2,128)S(1)} collective-permute-done((f32[2,2,2304]{2,1,0:T(2,128)S(1)}, f32[2,2,2304]{2,1,0:T(2,128)S(1)}, u32[]{:S(2)}, u32[]{:S(2)}) %collective-permute-start.21) | collective-permute-done | bytes 36896 | tf_op jit(solution)/shard_map/ppermute | solution.py:36
  158.7 6.9 %collective-permute-done.22.came_ref = bf16[64,2304]{1,0:T(8,128)(2,1)S(1)} collective-permute-done((bf16[64,2304]{1,0:T(8,128)(2,1)S(1)}, bf16[64,2304]{1,0:T(8,128)(2,1)S(1)}, u32[]{:S(2)}, u32[]{:S(2)}) %collective-permute-start.22) | collective-permute-done | bytes 294944 | tf_op jit(solution)/shard_map/ppermute | solution.py:36
  166.8 2.0 shard_map.173
  169.2 9.7 %collective-permute-done.29.far_ref = bf16[64,2304]{1,0:T(8,128)(2,1)S(1)} collective-permute-done((bf16[64,2304]{1,0:T(8,128)(2,1)S(1)}, bf16[64,2304]{1,0:T(8,128)(2,1)S(1)}, u32[]{:S(2)}, u32[]{:S(2)}) %collective-permute-start.29) | collective-permute-done | bytes 294944 | tf_op jit(solution)/shard_map/ppermute | solution.py:36
  180.0 3.2 %collective-permute-start.33 = (bf16[64,2304]{1,0:T(8,128)(2,1)S(1)}, bf16[64,2304]{1,0:T(8,128)(2,1)S(1)}, u32[]{:S(2)}, u32[]{:S(2)}) collective-permute-start(bf16[64,2304]{1,0:T(8,128)(2,1)S(1)} %shard_map.174.own_ref), channel_id=1, source_target_pairs={{0,4},{1,5},{2,6},{3,7},{4,0},{5,1},{6,2},{7,3},{8,12},{9,13},{10,... | collective-permute-start | bytes 884744 | tf_op jit(solution)/shard_map/ppermute | solution.py:36
  183.2 1.5 collective-permute-start.31
  184.7 10.3 %collective-permute-done.33.far_ref = bf16[64,2304]{1,0:T(8,128)(2,1)S(1)} collective-permute-done((bf16[64,2304]{1,0:T(8,128)(2,1)S(1)}, bf16[64,2304]{1,0:T(8,128)(2,1)S(1)}, u32[]{:S(2)}, u32[]{:S(2)}) %collective-permute-start.33) | collective-permute-done | bytes 294944 | tf_op jit(solution)/shard_map/ppermute | solution.py:36
  195.0 3.2 %collective-permute-start.34 = (bf16[64,2304]{1,0:T(8,128)(2,1)S(1)}, bf16[64,2304]{1,0:T(8,128)(2,1)S(1)}, u32[]{:S(2)}, u32[]{:S(2)}) collective-permute-start(bf16[64,2304]{1,0:T(8,128)(2,1)S(1)} %collective-permute-done.33.far_ref), channel_id=1, source_target_pairs={{0,2},{1,3},{2,0},{3,1},{4,6},{5,7},{6,4},{7,5},{8,10},{9,11},{10,... | collective-permute-start | bytes 884744 | tf_op jit(solution)/shard_map/ppermute | solution.py:36
  198.2 2.7 %collective-permute-done.31.last_ref = bf16[64,2304]{1,0:T(8,128)(2,1)S(1)} collective-permute-done((bf16[64,2304]{1,0:T(8,128)(2,1)S(1)}, bf16[64,2304]{1,0:T(8,128)(2,1)S(1)}, u32[]{:S(2)}, u32[]{:S(2)}) %collective-permute-start.31) | collective-permute-done | bytes 294944 | tf_op jit(solution)/shard_map/ppermute | solution.py:36
  200.9 2.6 %shard_map.175 = f32[40,256]{1,0:T(8,128)S(1)} custom-call(s32[6]{0:T(128)S(1)} %copy-done.14, bf16[64,2304]{1,0:T(8,128)(2,1)S(1)} %shard_map.171.own_ref, bf16[64,2304]{1,0:T(8,128)(2,1)S(1)} %collective-permute-done.30.near_ref, bf16[64,2304]{1,0:T(8,128)(2,1)S(1)} %collective-permute-done.29.far_ref, ...), custom_call_target="tpu_custom_call" | custom-call | tf_op jit(solution)/shard_map/pallas_call | solution.py:168
  203.6 3.6 %collective-permute-done.32.near_ref = bf16[64,2304]{1,0:T(8,128)(2,1)S(1)} collective-permute-done((bf16[64,2304]{1,0:T(8,128)(2,1)S(1)}, bf16[64,2304]{1,0:T(8,128)(2,1)S(1)}, u32[]{:S(2)}, u32[]{:S(2)}) %collective-permute-start.32) | collective-permute-done | bytes 294944 | tf_op jit(solution)/shard_map/ppermute | solution.py:36
  207.2 6.3 %collective-permute-done.34.last_ref = bf16[64,2304]{1,0:T(8,128)(2,1)S(1)} collective-permute-done((bf16[64,2304]{1,0:T(8,128)(2,1)S(1)}, bf16[64,2304]{1,0:T(8,128)(2,1)S(1)}, u32[]{:S(2)}, u32[]{:S(2)}) %collective-permute-start.34) | collective-permute-done | bytes 294944 | tf_op jit(solution)/shard_map/ppermute | solution.py:36
  213.5 2.6 %shard_map.176 = f32[40,256]{1,0:T(8,128)S(1)} custom-call(s32[6]{0:T(128)S(1)} %copy-done.14, bf16[64,2304]{1,0:T(8,128)(2,1)S(1)} %shard_map.174.own_ref, bf16[64,2304]{1,0:T(8,128)(2,1)S(1)} %collective-permute-done.32.near_ref, bf16[64,2304]{1,0:T(8,128)(2,1)S(1)} %collective-permute-done.33.far_ref, ...), custom_call_target="tpu_custom_call" | custom-call | tf_op jit(solution)/shard_map/pallas_call | solution.py:168
  217.7 3.0 %collective-permute-start.36 = (f32[40,128]{1,0:T(8,128)S(1)}, f32[40,128]{1,0:T(8,128)S(1)}, u32[]{:S(2)}, u32[]{:S(2)}) collective-permute-start(f32[40,128]{1,0:T(8,128)S(1)} %pad_maximum_fusion.2), channel_id=1, source_target_pairs={{0,4},{1,5},{2,6},{3,7},{4,0},{5,1},{6,2},{7,3},{8,12},{9,13},{10,... | collective-permute-start | bytes 61448 | tf_op jit(solution)/shard_map/ppermute | solution.py:36
  222.0 1.4 collective-permute-done.35.refs_1_
  224.0 2.1 collective-permute-start.38
  226.1 6.3 %collective-permute-start.39 = (f32[32,128]{1,0:T(8,128)S(1)}, f32[32,128]{1,0:T(8,128)S(1)}, u32[]{:S(2)}, u32[]{:S(2)}) collective-permute-start(f32[32,128]{1,0:T(8,128)S(1)} %shard_map.177), channel_id=1, source_target_pairs={{0,1},{1,3},{2,5},{3,7},{4,17},{5,19},{6,21},{7,23},{8,9},{9,11},{... | collective-permute-start | bytes 49160 | tf_op jit(solution)/shard_map/ppermute | solution.py:36
  233.8 5.5 %collective-permute-done.40.halo_ref = f32[32,128]{1,0:T(8,128)S(1)} collective-permute-done((f32[32,128]{1,0:T(8,128)S(1)}, f32[32,128]{1,0:T(8,128)S(1)}, u32[]{:S(2)}, u32[]{:S(2)}) %collective-permute-start.40) | collective-permute-done | bytes 16416 | tf_op jit(solution)/shard_map/ppermute | solution.py:36
  239.3 1.7 shard_map.178
  (119 shorter events, 28.5 us)
Async XLA Ops:
  0.6 22.8 %collective-permute-start = (bf16[2304,1152]{1,0:T(8,128)(2,1)}, bf16[2304,1152]{1,0:T(8,128)(2,1)}, u32[]{:S(2)}, u32[]{:S(2)}) collective-permute-start(bf16[2304,1152]{1,0:T(8,128)(2,1)} %up_ref.1), channel_id=1, source_target_pairs={{0,1},{1,0},{2,3},{3,2},{4,5},{5,4},{6,7},{7,6},{8,9},{9,8},{10,11... | collective-permute-start | bytes 15925256 | tf_op jit(solution)/shard_map/ppermute | solution.py:36
  1.4 22.1 %collective-permute-start.1 = (bf16[1152,2304]{1,0:T(8,128)(2,1)}, bf16[1152,2304]{1,0:T(8,128)(2,1)}, u32[]{:S(2)}, u32[]{:S(2)}) collective-permute-start(bf16[1152,2304]{1,0:T(8,128)(2,1)} %down_ref.1), channel_id=1, source_target_pairs={{0,1},{1,0},{2,3},{3,2},{4,5},{5,4},{6,7},{7,6},{8,9},{9,8},{10,11... | collective-permute-start | bytes 15925256 | tf_op jit(solution)/shard_map/ppermute | solution.py:36
  4.6 18.9 %collective-permute-start.3 = (bf16[128,2304]{1,0:T(8,128)(2,1)S(1)}, bf16[128,2304]{1,0:T(8,128)(2,1)S(1)}, u32[]{:S(2)}, u32[]{:S(2)}) collective-permute-start(bf16[128,2304]{1,0:T(8,128)(2,1)S(1)} %shard_map.159.refs_0_), channel_id=1, source_target_pairs={{0,2},{1,3},{2,0},{3,1},{4,6},{5,7},{6,4},{7,5},{8,10},{9,11},{10,... | collective-permute-start | bytes 1769480 | tf_op jit(solution)/shard_map/ppermute | solution.py:36
  5.5 17.9 %collective-permute-start.2 = (f32[1,1664]{1,0:T(1,128)S(1)}, f32[1,1664]{1,0:T(1,128)S(1)}, u32[]{:S(2)}, u32[]{:S(2)}) collective-permute-start(f32[1,1664]{1,0:T(1,128)S(1)} %broadcast_in_dim.12.refs_6_.bias_a), channel_id=1, source_target_pairs={{0,1},{1,0},{2,3},{3,2},{4,5},{5,4},{6,7},{7,6},{8,9},{9,8},{10,11... | collective-permute-start | bytes 19976 | tf_op jit(solution)/shard_map/ppermute | solution.py:36
  6.3 19.1 %collective-permute-start.4 = (bf16[128,2304]{1,0:T(8,128)(2,1)S(1)}, bf16[128,2304]{1,0:T(8,128)(2,1)S(1)}, u32[]{:S(2)}, u32[]{:S(2)}) collective-permute-start(bf16[128,2304]{1,0:T(8,128)(2,1)S(1)} %shard_map.159.refs_0_), channel_id=1, source_target_pairs={{0,0},{1,1},{2,4},{3,5},{4,2},{5,3},{6,6},{7,7},{8,8},{9,9},{10,12... | collective-permute-start | bytes 1769480 | tf_op jit(solution)/shard_map/ppermute | solution.py:36
  23.5 19.3 %collective-permute-start.5 = (bf16[128,2304]{1,0:T(8,128)(2,1)S(1)}, bf16[128,2304]{1,0:T(8,128)(2,1)}, u32[]{:S(2)}, u32[]{:S(2)}) collective-permute-start(bf16[128,2304]{1,0:T(8,128)(2,1)S(1)} %collective-permute-done.3.refs_1_), channel_id=1, source_target_pairs={{0,0},{1,1},{2,4},{3,5},{4,2},{5,3},{6,6},{7,7},{8,8},{9,9},{10,12... | collective-permute-start | bytes 1769480 | tf_op jit(solution)/shard_map/ppermute | solution.py:36
  25.4 22.5 %collective-permute-start.9 = (bf16[128,2304]{1,0:T(8,128)(2,1)S(1)}, bf16[128,2304]{1,0:T(8,128)(2,1)S(1)}, u32[]{:S(2)}, u32[]{:S(2)}) collective-permute-start(bf16[128,2304]{1,0:T(8,128)(2,1)S(1)} %collective-permute-done.4.refs_0_), channel_id=1, source_target_pairs={{2,0},{3,1},{4,6},{5,7},{10,8},{11,9},{12,14},{13,15},{18,16},{19,... | collective-permute-start | bytes 1769480 | tf_op jit(solution)/shard_map/ppermute | solution.py:36
  26.8 30.7 %collective-permute-start.7 = (bf16[128,2304]{1,0:T(8,128)(2,1)S(1)}, bf16[128,2304]{1,0:T(8,128)(2,1)S(1)}, u32[]{:S(2)}, u32[]{:S(2)}) collective-permute-start(bf16[128,2304]{1,0:T(8,128)(2,1)S(1)} %shard_map.160.refs_0_), channel_id=1, source_target_pairs={{0,2},{1,3},{2,0},{3,1},{4,6},{5,7},{6,4},{7,5},{8,10},{9,11},{10,... | collective-permute-start | bytes 1769480 | tf_op jit(solution)/shard_map/ppermute | solution.py:36
  42.7 16.4 %collective-permute-start.8 = (bf16[128,2304]{1,0:T(8,128)(2,1)S(1)}, bf16[128,2304]{1,0:T(8,128)(2,1)S(1)}, u32[]{:S(2)}, u32[]{:S(2)}) collective-permute-start(bf16[128,2304]{1,0:T(8,128)(2,1)S(1)} %shard_map.160.refs_0_), channel_id=1, source_target_pairs={{0,0},{1,1},{2,4},{3,5},{4,2},{5,3},{6,6},{7,7},{8,8},{9,9},{10,12... | collective-permute-start | bytes 1769480 | tf_op jit(solution)/shard_map/ppermute | solution.py:36
  46.4 17.3 %collective-permute-start.10 = (f32[2,128,512]{2,1,0:T(8,128)S(1)}, f32[2,128,512]{2,1,0:T(8,128)S(1)}, u32[]{:S(2)}, u32[]{:S(2)}) collective-permute-start(f32[2,128,512]{2,1,0:T(8,128)S(1)} %bitcast.34), channel_id=1, source_target_pairs={{0,16},{1,17},{2,18},{3,19},{4,20},{5,21},{6,22},{7,23},{8,24},{9,... | collective-permute-start | bytes 1572872 | tf_op jit(solution)/shard_map/ppermute | solution.py:36
  46.6 19.0 %collective-permute-start.6 = (bf16[128,2304]{1,0:T(8,128)(2,1)}, bf16[128,2304]{1,0:T(8,128)(2,1)S(1)}, u32[]{:S(2)}, u32[]{:S(2)}) collective-permute-start(bf16[128,2304]{1,0:T(8,128)(2,1)} %collective-permute-done.5.refs_0_), channel_id=1, source_target_pairs={{2,0},{3,1},{4,6},{5,7},{10,8},{11,9},{12,14},{13,15},{18,16},{19,... | collective-permute-start | bytes 1769480 | tf_op jit(solution)/shard_map/ppermute | solution.py:36
  56.1 28.2 %collective-permute-start.14 = (bf16[128,2304]{1,0:T(8,128)(2,1)S(1)}, bf16[128,2304]{1,0:T(8,128)(2,1)S(1)}, u32[]{:S(2)}, u32[]{:S(2)}) collective-permute-start(bf16[128,2304]{1,0:T(8,128)(2,1)S(1)} %shard_map.162.a_ref), channel_id=1, source_target_pairs={{0,2},{1,3},{6,4},{7,5},{8,10},{9,11},{14,12},{15,13},{16,18},{17,... | collective-permute-start | bytes 1769480 | tf_op jit(solution)/shard_map/ppermute | solution.py:36
  59.1 26.0 %collective-permute-start.12 = (bf16[128,2304]{1,0:T(8,128)(2,1)S(1)}, bf16[128,2304]{1,0:T(8,128)(2,1)S(1)}, u32[]{:S(2)}, u32[]{:S(2)}) collective-permute-start(bf16[128,2304]{1,0:T(8,128)(2,1)S(1)} %collective-permute-done.7.refs_1_), channel_id=1, source_target_pairs={{0,0},{1,1},{2,4},{3,5},{4,2},{5,3},{6,6},{7,7},{8,8},{9,9},{10,12... | collective-permute-start | bytes 1769480 | tf_op jit(solution)/shard_map/ppermute | solution.py:36
  62.1 22.9 %collective-permute-start.13 = (bf16[128,2304]{1,0:T(8,128)(2,1)S(1)}, bf16[128,2304]{1,0:T(8,128)(2,1)S(1)}, u32[]{:S(2)}, u32[]{:S(2)}) collective-permute-start(bf16[128,2304]{1,0:T(8,128)(2,1)S(1)} %collective-permute-done.8.refs_0_), channel_id=1, source_target_pairs={{2,0},{3,1},{4,6},{5,7},{10,8},{11,9},{12,14},{13,15},{18,16},{19,... | collective-permute-start | bytes 1769480 | tf_op jit(solution)/shard_map/ppermute | solution.py:36
  63.7 10.5 %collective-permute-start.11 = (f32[2,128,512]{2,1,0:T(8,128)S(1)}, f32[2,128,512]{2,1,0:T(8,128)S(1)}, u32[]{:S(2)}, u32[]{:S(2)}) collective-permute-start(f32[2,128,512]{2,1,0:T(8,128)S(1)} %bitcast.33), channel_id=1, source_target_pairs={{0,1},{1,0},{2,3},{3,2},{4,5},{5,4},{6,7},{7,6},{8,9},{9,8},{10,11... | collective-permute-start | bytes 1572872 | tf_op jit(solution)/shard_map/ppermute | solution.py:36
  72.9 25.7 %collective-permute-start.17 = (bf16[128,2304]{1,0:T(8,128)(2,1)S(1)}, bf16[128,2304]{1,0:T(8,128)(2,1)S(1)}, u32[]{:S(2)}, u32[]{:S(2)}) collective-permute-start(bf16[128,2304]{1,0:T(8,128)(2,1)S(1)} %shard_map.163.a_ref), channel_id=1, source_target_pairs={{0,2},{1,3},{6,4},{7,5},{8,10},{9,11},{14,12},{15,13},{16,18},{17,... | collective-permute-start | bytes 1769480 | tf_op jit(solution)/shard_map/ppermute | solution.py:36
  85.1 17.8 %collective-permute-start.15 = (bf16[128,2304]{1,0:T(8,128)(2,1)S(1)}, bf16[128,2304]{1,0:T(8,128)(2,1)S(1)}, u32[]{:S(2)}, u32[]{:S(2)}) collective-permute-start(bf16[128,2304]{1,0:T(8,128)(2,1)S(1)} %collective-permute-done.12.refs_0_), channel_id=1, source_target_pairs={{2,0},{3,1},{4,6},{5,7},{10,8},{11,9},{12,14},{13,15},{18,16},{19,... | collective-permute-start | bytes 1769480 | tf_op jit(solution)/shard_map/ppermute | solution.py:36
  89.1 15.5 %collective-permute-start.19 = (bf16[128,2304]{1,0:T(8,128)(2,1)S(1)}, bf16[128,2304]{1,0:T(8,128)(2,1)S(1)}, u32[]{:S(2)}, u32[]{:S(2)}) collective-permute-start(bf16[128,2304]{1,0:T(8,128)(2,1)S(1)} %shard_map.165), channel_id=1, source_target_pairs={{0,0},{1,1},{2,4},{3,5},{4,2},{5,3},{6,6},{7,7},{8,8},{9,9},{10,12... | collective-permute-start | bytes 1769480 | tf_op jit(solution)/shard_map/ppermute | solution.py:36
  99.3 18.0 %collective-permute-start.18 = (bf16[128,2304]{1,0:T(8,128)(2,1)S(1)}, bf16[128,2304]{1,0:T(8,128)(2,1)S(1)}, u32[]{:S(2)}, u32[]{:S(2)}) collective-permute-start(bf16[128,2304]{1,0:T(8,128)(2,1)S(1)} %shard_map.167), channel_id=1, source_target_pairs={{0,0},{1,1},{2,4},{3,5},{4,2},{5,3},{6,6},{7,7},{8,8},{9,9},{10,12... | collective-permute-start | bytes 1769480 | tf_op jit(solution)/shard_map/ppermute | solution.py:36
  102.8 14.4 %collective-permute-start.16 = (bf16[128,2304]{1,0:T(8,128)(2,1)S(1)}, bf16[128,2304]{1,0:T(8,128)(2,1)S(1)}, u32[]{:S(2)}, u32[]{:S(2)}) collective-permute-start(bf16[128,2304]{1,0:T(8,128)(2,1)S(1)} %get-tuple-element.77), channel_id=1, source_target_pairs={{0,2},{1,3},{2,0},{3,1},{4,6},{5,7},{6,4},{7,5},{8,10},{9,11},{10,... | collective-permute-start | bytes 1769480 | tf_op jit(solution)/shard_map/ppermute | solution.py:36
  112.0 30.2 %copy-start.16 = (f32[2,2,2304]{2,1,0:T(2,128)S(1)}, f32[2,2,2304]{2,1,0:T(2,128)}, u32[]{:S(2)}) copy-start(f32[2,2,2304]{2,1,0:T(2,128)} %ada_ref.7) | copy-start | bytes 110596
  112.0 31.5 %copy-start.24 = (f32[2304]{0:T(1024)S(1)}, f32[2304]{0:T(1024)}, u32[]{:S(2)}) copy-start(f32[2304]{0:T(1024)} %param.21) | copy-start | bytes 27652
  112.0 43.8 %copy-start.21 = (f32[2,2304]{1,0:T(2,128)S(1)}, f32[2,2304]{1,0:T(2,128)}, u32[]{:S(2)}) copy-start(f32[2,2304]{1,0:T(2,128)} %gate_ref.3) | copy-start | bytes 55300
  112.0 46.0 %copy-start.20 = (bf16[512,32]{0,1:T(8,128)(2,1)S(1)}, bf16[512,32]{0,1:T(8,128)(2,1)}, u32[]{:S(2)}) copy-start(bf16[512,32]{0,1:T(8,128)(2,1)} %param.26) | copy-start | bytes 98308
  112.0 16.6 %collective-permute-start.26 = (bf16[128,2304]{1,0:T(8,128)(2,1)S(1)}, bf16[128,2304]{1,0:T(8,128)(2,1)S(1)}, u32[]{:S(2)}, u32[]{:S(2)}) collective-permute-start(bf16[128,2304]{1,0:T(8,128)(2,1)S(1)} %shard_map.169), channel_id=1, source_target_pairs={{0,2},{1,3},{2,0},{3,1},{4,6},{5,7},{6,4},{7,5},{8,10},{9,11},{10,... | collective-permute-start | bytes 1769480 | tf_op jit(solution)/shard_map/ppermute | solution.py:36
  112.1 54.7 %collective-permute-start.23 = (bf16[2304,512]{1,0:T(8,128)(2,1)S(1)}, bf16[2304,512]{1,0:T(8,128)(2,1)S(1)}, u32[]{:S(2)}, u32[]{:S(2)}) collective-permute-start(bf16[2304,512]{1,0:T(8,128)(2,1)S(1)} %copy-done.7), channel_id=1, source_target_pairs={{0,1},{1,0},{2,3},{3,2},{4,5},{5,4},{6,7},{7,6},{8,9},{9,8},{10,11... | collective-permute-start | bytes 7077896 | tf_op jit(solution)/shard_map/ppermute | solution.py:36
  118.0 37.7 %collective-permute-start.20 = (bf16[128,2304]{1,0:T(8,128)(2,1)S(1)}, bf16[128,2304]{1,0:T(8,128)(2,1)S(1)}, u32[]{:S(2)}, u32[]{:S(2)}) collective-permute-start(bf16[128,2304]{1,0:T(8,128)(2,1)S(1)} %shard_map.168), channel_id=1, source_target_pairs={{0,2},{1,3},{2,0},{3,1},{4,6},{5,7},{6,4},{7,5},{8,10},{9,11},{10,... | collective-permute-start | bytes 1769480 | tf_op jit(solution)/shard_map/ppermute | solution.py:36
  129.3 37.5 %collective-permute-start.27 = (bf16[128,2304]{1,0:T(8,128)(2,1)S(1)}, bf16[128,2304]{1,0:T(8,128)(2,1)S(1)}, u32[]{:S(2)}, u32[]{:S(2)}) collective-permute-start(bf16[128,2304]{1,0:T(8,128)(2,1)S(1)} %shard_map.172), channel_id=1, source_target_pairs={{0,4},{1,5},{2,6},{3,7},{4,0},{5,1},{6,2},{7,3},{8,12},{9,13},{10,... | collective-permute-start | bytes 1769480 | tf_op jit(solution)/shard_map/ppermute | solution.py:36
  129.4 37.4 %collective-permute-start.25 = (f32[2,128,512]{2,1,0:T(8,128)S(1)}, f32[2,128,512]{2,1,0:T(8,128)S(1)}, u32[]{:S(2)}, u32[]{:S(2)}) collective-permute-start(f32[2,128,512]{2,1,0:T(8,128)S(1)} %bitcast.32), channel_id=1, source_target_pairs={{0,17},{1,16},{2,19},{3,18},{4,21},{5,20},{6,23},{7,22},{8,25},{9,... | collective-permute-start | bytes 1572872 | tf_op jit(solution)/shard_map/ppermute | solution.py:36
  142.2 13.6 %collective-permute-start.21 = (f32[2,2,2304]{2,1,0:T(2,128)S(1)}, f32[2,2,2304]{2,1,0:T(2,128)S(1)}, u32[]{:S(2)}, u32[]{:S(2)}) collective-permute-start(f32[2,2,2304]{2,1,0:T(2,128)S(1)} %copy-done.16), channel_id=1, source_target_pairs={{0,16},{1,17},{2,18},{3,19},{4,20},{5,21},{6,22},{7,23},{8,24},{9,... | collective-permute-start | bytes 110600 | tf_op jit(solution)/shard_map/ppermute | solution.py:36
  156.8 8.8 %collective-permute-start.22 = (bf16[64,2304]{1,0:T(8,128)(2,1)S(1)}, bf16[64,2304]{1,0:T(8,128)(2,1)S(1)}, u32[]{:S(2)}, u32[]{:S(2)}) collective-permute-start(bf16[64,2304]{1,0:T(8,128)(2,1)S(1)} %get-tuple-element.86), channel_id=1, source_target_pairs={{0,16},{1,17},{2,18},{3,19},{4,20},{5,21},{6,22},{7,23},{8,24},{9,... | collective-permute-start | bytes 884744 | tf_op jit(solution)/shard_map/ppermute | solution.py:36
  158.0 8.8 %collective-permute-start.24 = (bf16[32,512]{1,0:T(8,128)(2,1)S(1)}, bf16[32,512]{1,0:T(8,128)(2,1)S(1)}, u32[]{:S(2)}, u32[]{:S(2)}) collective-permute-start(bf16[32,512]{1,0:T(8,128)(2,1)S(1)} %bitcast.27), channel_id=1, source_target_pairs={{0,1},{1,0},{2,3},{3,2},{4,5},{5,4},{6,7},{7,6},{8,9},{9,8},{10,11... | collective-permute-start | bytes 98312 | tf_op jit(solution)/shard_map/ppermute | solution.py:36
  166.7 12.3 %collective-permute-start.29 = (bf16[64,2304]{1,0:T(8,128)(2,1)S(1)}, bf16[64,2304]{1,0:T(8,128)(2,1)S(1)}, u32[]{:S(2)}, u32[]{:S(2)}) collective-permute-start(bf16[64,2304]{1,0:T(8,128)(2,1)S(1)} %shard_map.171.own_ref), channel_id=1, source_target_pairs={{0,4},{1,5},{2,6},{3,7},{4,0},{5,1},{6,2},{7,3},{8,12},{9,13},{10,... | collective-permute-start | bytes 884744 | tf_op jit(solution)/shard_map/ppermute | solution.py:36
  168.8 10.2 %collective-permute-start.28 = (bf16[64,2304]{1,0:T(8,128)(2,1)S(1)}, bf16[64,2304]{1,0:T(8,128)(2,1)S(1)}, u32[]{:S(2)}, u32[]{:S(2)}) collective-permute-start(bf16[64,2304]{1,0:T(8,128)(2,1)S(1)} %get-tuple-element.96), channel_id=1, source_target_pairs={{0,16},{1,17},{2,18},{3,19},{4,20},{5,21},{6,22},{7,23},{8,24},{9,... | collective-permute-start | bytes 884744 | tf_op jit(solution)/shard_map/ppermute | solution.py:36
  180.0 15.0 %collective-permute-start.33 = (bf16[64,2304]{1,0:T(8,128)(2,1)S(1)}, bf16[64,2304]{1,0:T(8,128)(2,1)S(1)}, u32[]{:S(2)}, u32[]{:S(2)}) collective-permute-start(bf16[64,2304]{1,0:T(8,128)(2,1)S(1)} %shard_map.174.own_ref), channel_id=1, source_target_pairs={{0,4},{1,5},{2,6},{3,7},{4,0},{5,1},{6,2},{7,3},{8,12},{9,13},{10,... | collective-permute-start | bytes 884744 | tf_op jit(solution)/shard_map/ppermute | solution.py:36
  183.2 15.0 %collective-permute-start.30 = (bf16[64,2304]{1,0:T(8,128)(2,1)S(1)}, bf16[64,2304]{1,0:T(8,128)(2,1)S(1)}, u32[]{:S(2)}, u32[]{:S(2)}) collective-permute-start(bf16[64,2304]{1,0:T(8,128)(2,1)S(1)} %shard_map.171.own_ref), channel_id=1, source_target_pairs={{0,2},{1,3},{2,0},{3,1},{4,6},{5,7},{6,4},{7,5},{8,10},{9,11},{10,... | collective-permute-start | bytes 884744 | tf_op jit(solution)/shard_map/ppermute | solution.py:36
  183.2 17.7 %collective-permute-start.31 = (bf16[64,2304]{1,0:T(8,128)(2,1)S(1)}, bf16[64,2304]{1,0:T(8,128)(2,1)S(1)}, u32[]{:S(2)}, u32[]{:S(2)}) collective-permute-start(bf16[64,2304]{1,0:T(8,128)(2,1)S(1)} %collective-permute-done.29.far_ref), channel_id=1, source_target_pairs={{0,2},{1,3},{2,0},{3,1},{4,6},{5,7},{6,4},{7,5},{8,10},{9,11},{10,... | collective-permute-start | bytes 884744 | tf_op jit(solution)/shard_map/ppermute | solution.py:36
  184.6 22.6 %collective-permute-start.32 = (bf16[64,2304]{1,0:T(8,128)(2,1)S(1)}, bf16[64,2304]{1,0:T(8,128)(2,1)S(1)}, u32[]{:S(2)}, u32[]{:S(2)}) collective-permute-start(bf16[64,2304]{1,0:T(8,128)(2,1)S(1)} %shard_map.174.own_ref), channel_id=1, source_target_pairs={{0,2},{1,3},{2,0},{3,1},{4,6},{5,7},{6,4},{7,5},{8,10},{9,11},{10,... | collective-permute-start | bytes 884744 | tf_op jit(solution)/shard_map/ppermute | solution.py:36
  195.0 18.5 %collective-permute-start.34 = (bf16[64,2304]{1,0:T(8,128)(2,1)S(1)}, bf16[64,2304]{1,0:T(8,128)(2,1)S(1)}, u32[]{:S(2)}, u32[]{:S(2)}) collective-permute-start(bf16[64,2304]{1,0:T(8,128)(2,1)S(1)} %collective-permute-done.33.far_ref), channel_id=1, source_target_pairs={{0,2},{1,3},{2,0},{3,1},{4,6},{5,7},{6,4},{7,5},{8,10},{9,11},{10,... | collective-permute-start | bytes 884744 | tf_op jit(solution)/shard_map/ppermute | solution.py:36
  203.5 35.7 %copy-start.15 = (s32[6]{0:T(128)S(1)}, s32[6]{0:T(128)}, u32[]{:S(2)}) copy-start(s32[6]{0:T(128)} %copy-done.10) | copy-start | bytes 76
  203.5 35.7 %copy-start.17 = (f32[32,32,3,3]{1,0,3,2:T(8,128)S(1)}, f32[32,32,3,3]{1,0,3,2:T(8,128)}, u32[]{:S(2)}) copy-start(f32[32,32,3,3]{1,0,3,2:T(8,128)} %param.27) | copy-start | bytes 110596
  203.5 35.7 %copy-start.22 = (f32[1,32,128]{2,1,0:T(8,128)S(1)}, f32[1,32,128]{2,1,0:T(8,128)}, u32[]{:S(2)}) copy-start(f32[1,32,128]{2,1,0:T(8,128)} %param.29) | copy-start | bytes 49156
  216.3 4.6 %collective-permute-start.37 = (f32[40,128]{1,0:T(8,128)S(1)}, f32[40,128]{1,0:T(8,128)S(1)}, u32[]{:S(2)}, u32[]{:S(2)}) collective-permute-start(f32[40,128]{1,0:T(8,128)S(1)} %pad_maximum_fusion.3), channel_id=1, source_target_pairs={{0,6},{1,7},{2,4},{3,5},{4,2},{5,3},{6,0},{7,1},{8,14},{9,15},{10,... | collective-permute-start | bytes 61448 | tf_op jit(solution)/shard_map/ppermute | solution.py:36
  217.7 4.4 %collective-permute-start.36 = (f32[40,128]{1,0:T(8,128)S(1)}, f32[40,128]{1,0:T(8,128)S(1)}, u32[]{:S(2)}, u32[]{:S(2)}) collective-permute-start(f32[40,128]{1,0:T(8,128)S(1)} %pad_maximum_fusion.2), channel_id=1, source_target_pairs={{0,4},{1,5},{2,6},{3,7},{4,0},{5,1},{6,2},{7,3},{8,12},{9,13},{10,... | collective-permute-start | bytes 61448 | tf_op jit(solution)/shard_map/ppermute | solution.py:36
  220.8 2.7 %collective-permute-start.35 = (f32[40,128]{1,0:T(8,128)S(1)}, f32[40,128]{1,0:T(8,128)S(1)}, u32[]{:S(2)}, u32[]{:S(2)}) collective-permute-start(f32[40,128]{1,0:T(8,128)S(1)} %pad_maximum_fusion.1), channel_id=1, source_target_pairs={{0,2},{1,3},{2,0},{3,1},{4,6},{5,7},{6,4},{7,5},{8,10},{9,11},{10,... | collective-permute-start | bytes 61448 | tf_op jit(solution)/shard_map/ppermute | solution.py:36
  224.0 9.8 %collective-permute-start.38 = (f32[32,128]{1,0:T(8,128)S(1)}, f32[32,128]{1,0:T(8,128)S(1)}, u32[]{:S(2)}, u32[]{:S(2)}) collective-permute-start(f32[32,128]{1,0:T(8,128)S(1)} %shard_map.177), channel_id=1, source_target_pairs={{0,0},{1,2},{2,4},{3,6},{4,16},{5,18},{6,20},{7,22},{8,8},{9,10},{... | collective-permute-start | bytes 49160 | tf_op jit(solution)/shard_map/ppermute | solution.py:36
  226.1 7.7 %collective-permute-start.39 = (f32[32,128]{1,0:T(8,128)S(1)}, f32[32,128]{1,0:T(8,128)S(1)}, u32[]{:S(2)}, u32[]{:S(2)}) collective-permute-start(f32[32,128]{1,0:T(8,128)S(1)} %shard_map.177), channel_id=1, source_target_pairs={{0,1},{1,3},{2,5},{3,7},{4,17},{5,19},{6,21},{7,23},{8,9},{9,11},{... | collective-permute-start | bytes 49160 | tf_op jit(solution)/shard_map/ppermute | solution.py:36
  232.4 6.8 %collective-permute-start.40 = (f32[32,128]{1,0:T(8,128)S(1)}, f32[32,128]{1,0:T(8,128)S(1)}, u32[]{:S(2)}, u32[]{:S(2)}) collective-permute-start(f32[32,128]{1,0:T(8,128)S(1)} %shard_map.177), channel_id=1, source_target_pairs={{1,1},{2,3},{3,5},{5,17},{6,19},{7,21},{9,9},{10,11},{11,13},{13,2... | collective-permute-start | bytes 49160 | tf_op jit(solution)/shard_map/ppermute | solution.py:36
  (19 other events, 138.3 us)

commit v5 on v3

--- a/solution.py
+++ b/solution.py
@@ -161,18 +161,19 @@
 SCALARS = pl.BlockSpec(memory_space=pltpu.SMEM)
 ON_CHIP = pl.BlockSpec(memory_space=pltpu.VMEM)
 VMEM_LIMIT = 16 * 1024 * 1024
+AHEAD = 40_000_000_000
 MID, UPPER, IMAGE, ODD, SAME, CORE = range(6)
 
 
-def call(kernel, where, args, outs, scratch=()):
+def call(kernel, where, args, outs, scratch=(), flops=0, specs=None, limit=VMEM_LIMIT):
     return pl.pallas_call(
         kernel,
         out_shape=outs,
-        in_specs=[SCALARS] + [ON_CHIP] * len(args),
+        in_specs=[SCALARS] + (specs or [ON_CHIP] * len(args)),
         out_specs=[ON_CHIP] * len(outs),
         scratch_shapes=scratch,
-        compiler_params=pltpu.CompilerParams(vmem_limit_bytes=VMEM_LIMIT),
-        cost_estimate=pl.CostEstimate(flops=0, bytes_accessed=0, transcendentals=0),
+        compiler_params=pltpu.CompilerParams(vmem_limit_bytes=limit),
+        cost_estimate=pl.CostEstimate(flops=flops, bytes_accessed=0, transcendentals=0),
     )(where, *args)
 
 
@@ -199,12 +200,24 @@
     return call(functools.partial(norm_kernel, begin), where, (tokens, ada), outs)[0]
 
 
-def ffn_kernel(groups, tile, where_ref, *refs):
+def ffn_kernel(groups, tile, fetch, where_ref, *refs):
     count = sum(groups)
     parts = refs[:count]
     up_a, up_b, down_a, down_b, bias_a, bias_b = refs[count : count + 6]
     outs = refs[count + 6 : count + 6 + len(groups)]
-    x_ref, hidden_ref = refs[count + 6 + len(groups) :]
+    x_ref, hidden_ref, *own = refs[count + 6 + len(groups) :]
+    order = list(range(0, 2 * down_a.shape[0], tile))
+    copies = []
+    if fetch:
+        up_own, down_own, sems = own
+        copies = [
+            pltpu.make_async_copy(up_a, up_own, sems.at[0]),
+            pltpu.make_async_copy(down_a, down_own, sems.at[1]),
+        ]
+        for copy in copies:
+            copy.start()
+        up_a, down_a = up_own, down_own
+        order = [t for t in order if t >= down_a.shape[0]] + [t for t in order if t < down_a.shape[0]]
     panel, width = down_a.shape
     step = outs[0].shape[0]
     place = 0
@@ -223,11 +236,15 @@
             return second[:, begin - panel : end - panel]
         return jnp.concatenate([first[:, begin:panel], second[:, : end - panel]], axis=1)
 
-    for begin in range(0, 2 * panel, tile):
+    for begin in order:
         end = begin + tile
+        if fetch and begin == 0:
+            copies[0].wait()
         v = jnp.dot(x_ref[...], columns(up_a, up_b, begin, end), preferred_element_type=jnp.float32)
         v = v + columns(bias_a, bias_b, begin, end)
         hidden_ref[:, begin:end] = jax.nn.gelu(v, approximate=True).astype(jnp.bfloat16)
+    if fetch:
+        copies[1].wait()
     for begin in range(0, width, tile):
         cols = slice(begin, begin + tile)
         weight = jnp.concatenate([down_a[:, cols], down_b[:, cols]], axis=0)
@@ -236,20 +253,31 @@
             outs[g][:, cols] = result[g * step : (g + 1) * step].astype(jnp.bfloat16)
 
 
-def ffn(where, slots, panels):
+def ffn(where, slots, panels, fetch=False):
     groups = tuple(len(slot) for slot in slots)
     parts = [part for slot in slots for part in slot]
     rows, width = parts[0].shape
     total = rows * len(slots)
+    up, down = panels[0], panels[2]
+    if fetch:
+        panels = [
+            pltpu.with_memory_space_constraint(p, pltpu.HBM) if i in (0, 2) else p for i, p in enumerate(panels)
+        ]
+    own = [pltpu.VMEM(up.shape, up.dtype), pltpu.VMEM(down.shape, down.dtype), pltpu.SemaphoreType.DMA((2,))]
+    in_place = pl.BlockSpec(memory_space=pltpu.HBM)
+    specs = [in_place if fetch and i in (0, 2) else ON_CHIP for i in range(len(panels))]
     return call(
-        functools.partial(ffn_kernel, groups, 256),
+        functools.partial(ffn_kernel, groups, 256, fetch),
         where,
         (*parts, *panels),
         [shape_of((rows, width))] * len(slots),
         scratch=[
             pltpu.VMEM((total, width), jnp.bfloat16),
-            pltpu.VMEM((total, 2 * panels[2].shape[0]), jnp.bfloat16),
+            pltpu.VMEM((total, 2 * down.shape[0]), jnp.bfloat16),
+            *(own if fetch else []),
         ],
+        specs=[ON_CHIP] * len(parts) + specs,
+        limit=VMEM_LIMIT + 8 * 1024 * 1024 if fetch else VMEM_LIMIT,
     )
 
 
@@ -260,8 +288,8 @@
     out_ref[...] = (a_ref[...].astype(jnp.float32) + b).astype(jnp.bfloat16)
 
 
-def add(where, a, b, always=False):
-    return call(functools.partial(add_kernel, always), where, (a, b), [shape_of(a.shape)])[0]
+def add(where, a, b, always=False, flops=0):
+    return call(functools.partial(add_kernel, always), where, (a, b), [shape_of(a.shape)], flops=flops)[0]
 
 
 def out_kernel(begin, always, where_ref, own_ref, near_ref, far_ref, tokens_ref, gate_ref, bias_ref, *refs):
@@ -350,7 +378,7 @@
     stats_ref[...] = jnp.transpose(table)[: stats_ref.shape[0], :]
 
 
-def head_stats(where, begin, slots, heads, noises):
+def head_stats(where, begin, slots, heads, noises, flops=0):
     step, width = slots[0].shape
     height = -(-(heads[-1].shape[0] + 2) // 8) * 8
     return call(
@@ -359,6 +387,7 @@
         (*slots, *heads, *noises),
         [shape_of((height, 4 * step), jnp.float32)],
         scratch=[pltpu.VMEM((4 * step, width), jnp.bfloat16)],
+        flops=flops,
     )[0]
 
 
@@ -507,24 +536,25 @@
     )
     noise_twin, noise_core, noise_both, _ = barrier((noise_twin, noise_core, noise_both, own_b))
     noise_twin = swap_twins(noise_twin)
-    up_other, down_other, bias_other, near_a = barrier((up_other, down_other, bias_other, near_a))
+    up_other, down_other, bias_other, near_a, own_b = barrier((up_other, down_other, bias_other, near_a, own_b))
     panels = (up_weight, up_other, down_weight, down_other, biases, bias_other)
     far_mid_a = middle(near_a)
     near_b = near(after(own_b, near_a))
     mid_a = after(mid_a, near_a)
     far_end_a = outward(mid_a)
-    sum_own_a, sum_near_a = ffn(where, [[own_a], [after(near_a, mid_a)]], panels)
-    noise_core = swap_cores(after(noise_core, sum_near_a))
+    sum_own_a, sum_near_a = ffn(where, [[own_a], [after(near_a, mid_a)]], panels, fetch=True)
     far_mid_a = after(far_mid_a, sum_near_a)
     last_end_a = outward(far_mid_a)
     mid_b = middle(after(own_b, far_mid_a))
+    noise_core = swap_cores(after(noise_core, far_mid_a))
+    head_twin = swap_twins(after(ada_head, far_mid_a))
     (sum_far_a,) = ffn(where, [[far_mid_a, far_end_a]], panels)
     came_far_a = inward(sum_far_a)
     near_b, mid_b = barrier((near_b, mid_b, sum_far_a))[:2]
     far_mid_b, far_end_b = middle(near_b), outward(mid_b)
-    (sum_last_a,) = ffn(where, [[mid_a, after(last_end_a, near_b, mid_b, noise_twin)]], panels)
+    (sum_last_a,) = ffn(where, [[mid_a, after(last_end_a, near_b, mid_b, noise_twin, head_twin)]], panels)
     came_last_a = inward(sum_last_a)
-    noise_both = swap_both(after(noise_both, sum_last_a))
+    noise_both = swap_both(after(noise_both, noise_twin))
     sum_own_b, sum_near_b = ffn(where, [[after(own_b, sum_last_a, noise_core)], [near_b]], panels)
     both_last_a = add(where, after(sum_last_a, sum_near_b), came_far_a)
     went_last_a = middle(both_last_a)
@@ -536,32 +566,31 @@
     (sum_last_b,) = ffn(where, [[after(mid_b, both_far_a, went_last_a), last_end_b]], panels)
     came_last_b = near(sum_last_b)
     head_other = swap_cores(after(head_weight, sum_last_b))
-    head_twin = swap_twins(after(ada_head, sum_last_b))
     code_other = swap_cores(after(codes, sum_last_b))
-    both_far_b = add(where, sum_far_b, came_last_b, True)
+    came_near_b = near(after(sum_near_b, last_end_b))
+    both_near_a = add(where, sum_near_a, after(went_far_a, went_last_a, came_near_b), flops=AHEAD)
+    came_near_a = near(both_near_a)
+    both_far_b = add(where, after(sum_far_b, both_near_a), came_last_b, True)
     went_far_b = across(both_far_b)
-    came_near_b = near(after(sum_near_b, both_far_b))
-    both_near_a = add(where, sum_near_a, after(went_far_a, went_last_a, both_far_b))
-    came_near_a = near(both_near_a)
     out_a, kept_a, sent_a = block_rows(
-        where, 0, False, sum_own_a, after(came_near_a, head_twin), went_last_a, tokens, gate, bias_out
+        where, 0, False, sum_own_a, after(came_near_a, noise_both), went_last_a, tokens, gate, bias_out
     )
     came_a = swap_twins(sent_a)
     mixed_a = mix_twins(where, kept_a, came_a, ada_head, head_twin)
     mix_near_a, mix_far_a = near(mixed_a), across(mixed_a)
     block_out, kept_b, sent_b = block_rows(
-        where, step, True, sum_own_b, after(came_near_b, mixed_a, head_other, code_other, noise_both), went_far_b, tokens, gate, bias_out, (out_a,)
-    )
-    came_b = swap_twins(sent_b)
+        where, step, True, sum_own_b, after(came_near_b, mixed_a, head_other, code_other), went_far_b, tokens, gate, bias_out, (out_a,)
+    )
+    came_b = after(swap_twins(sent_b), mix_far_a)
     mix_last_a = near(mix_far_a)
     mixed_b = mix_twins(where, kept_b, came_b, ada_head, head_twin)
     mix_near_b, mix_far_b = near(mixed_b), across(mixed_b)
     heads = (head_weight, head_other, biases, bias_other, codes, code_other)
     noises = (noise_own, noise_core, noise_twin, noise_both)
     stats_a = head_stats(
-        where, 0, (after(mixed_a, mixed_b), mix_near_a, mix_far_a, mix_last_a), heads, noises
-    )
-    mix_last_b = near(mix_far_b)
+        where, 0, (after(mixed_a, mixed_b), mix_near_a, mix_far_a, mix_last_a), heads, noises, flops=AHEAD
+    )
+    mix_last_b = near(after(mix_far_b, stats_a))
     stats_b = head_stats(where, half, (after(mixed_b, stats_a), mix_near_b, mix_far_b, mix_last_b), heads, noises)
 
     slots = [

time: 242 us -> 234 us (0.967)
  waiting for transfers between devices: 93.1 us -> 81.5 us
  starting transfers between devices: 70.6 us -> 74.7 us
  local copies, waits for them, and re-layouts: 8.45 us -> 5.97 us
    ppermute x41, waiting for transfers between devices: 93.1 us -> 81.5 us  [permute_devices(): return lax.ppermute(value, ('dp', 'mp'), pairs)]
    ppermute x41, starting transfers between devices: 70.6 us -> 74.7 us  [permute_devices(): return lax.ppermute(value, ('dp', 'mp'), pairs)]
    unnamed x36, local copies, waits for them, and re-layouts: 7.88 us -> 5.38 us
  transfers between devices with their start and end apart: 41 -> 41, of which waited for: 20 -> 18; matrix products, arithmetic and copies ran while one was open for 1% -> 1% of each run, Pallas kernels for 22% -> 27%
where the time goes in v5:
time: 234 us; the launch traced here: 233 us
  waiting for transfers between devices  81.5 us (35%)
  starting transfers between devices  74.7 us (32%)
  Pallas kernels  68.7 us (29%)
  local copies, waits for them, and re-layouts  5.97 us (3%)
    ppermute x41, waiting for transfers between devices, permute_devices(): return lax.ppermute(value, ('dp', 'mp'), pairs)  81.5 us
    ppermute x41, starting transfers between devices, permute_devices(): return lax.ppermute(value, ('dp', 'mp'), pairs)  74.7 us
    pallas_call x20, Pallas kernels, call(): pl.pallas_call(kernel, out_shape=outs, in_specs=[SCALARS] + (specs or [ON...  68.7 us
    unnamed x36, local copies, waits for them, and re-layouts  5.38 us
  transfers between devices with their start and end apart: 41, of which 18 were waited for; matrix products, arithmetic and copies ran while one was open for 1% of the time, Pallas kernels for 27%

profile of v5, /device:TPU:13, one launch (start us, length us, event | category | flops | bytes accessed | tf_op | source)
XLA Modules:
  0.0 233.1 jit_solution(17293799223746976115)
XLA Ops:
  6.3 4.3 %collective-permute-start.4 = (bf16[128,2304]{1,0:T(8,128)(2,1)S(1)}, bf16[128,2304]{1,0:T(8,128)(2,1)S(1)}, u32[]{:S(2)}, u32[]{:S(2)}) collective-permute-start(bf16[128,2304]{1,0:T(8,128)(2,1)S(1)} %shard_map.158.refs_0_), channel_id=1, source_target_pairs={{0,0},{1,1},{2,4},{3,5},{4,2},{5,3},{6,6},{7,7},{8,8},{9,9},{10,12... | collective-permute-start | bytes 1769480 | tf_op jit(solution)/shard_map/ppermute | solution.py:36
  12.4 6.7 %collective-permute-done.3.refs_1_ = bf16[128,2304]{1,0:T(8,128)(2,1)S(1)} collective-permute-done((bf16[128,2304]{1,0:T(8,128)(2,1)S(1)}, bf16[128,2304]{1,0:T(8,128)(2,1)S(1)}, u32[]{:S(2)}, u32[]{:S(2)}) %collective-permute-start.3) | collective-permute-done | bytes 589856 | tf_op jit(solution)/shard_map/ppermute | solution.py:36
  19.1 3.2 %collective-permute-start.5 = (bf16[128,2304]{1,0:T(8,128)(2,1)S(1)}, bf16[128,2304]{1,0:T(8,128)(2,1)}, u32[]{:S(2)}, u32[]{:S(2)}) collective-permute-start(bf16[128,2304]{1,0:T(8,128)(2,1)S(1)} %collective-permute-done.3.refs_1_), channel_id=1, source_target_pairs={{0,0},{1,1},{2,4},{3,5},{4,2},{5,3},{6,6},{7,7},{8,8},{9,9},{10,12... | collective-permute-start | bytes 1769480 | tf_op jit(solution)/shard_map/ppermute | solution.py:36
  22.4 1.9 collective-permute-done.4.refs_0_
  24.3 1.4 collective-permute-start.9
  25.8 11.9 %shard_map.160 = (bf16[128,2304]{1,0:T(8,128)(2,1)S(1)}, bf16[128,2304]{1,0:T(8,128)(2,1)S(1)}) custom-call(s32[6]{0:T(128)S(1)} %stack.35.where_ref, bf16[128,2304]{1,0:T(8,128)(2,1)S(1)} %shard_map.158.refs_0_, bf16[128,2304]{1,0:T(8,128)(2,1)S(1)} %collective-permute-done.3.refs_1_, bf16[2304,1152]{1,0:T(8,128)(2,1)} %refs_2_.11, ...), custom_call_target="tpu_custom_call" | custom-call | tf_op jit(solution)/shard_map/pallas_call | solution.py:169
  37.7 3.0 %collective-permute-start.8 = (bf16[128,2304]{1,0:T(8,128)(2,1)S(1)}, bf16[128,2304]{1,0:T(8,128)(2,1)S(1)}, u32[]{:S(2)}, u32[]{:S(2)}) collective-permute-start(bf16[128,2304]{1,0:T(8,128)(2,1)S(1)} %shard_map.159.refs_0_), channel_id=1, source_target_pairs={{0,0},{1,1},{2,4},{3,5},{4,2},{5,3},{6,6},{7,7},{8,8},{9,9},{10,12... | collective-permute-start | bytes 1769480 | tf_op jit(solution)/shard_map/ppermute | solution.py:36
  42.7 2.5 %copy-done = bf16[1152,2304]{1,0:T(8,128)(2,1)S(1)} copy-done((bf16[1152,2304]{1,0:T(8,128)(2,1)S(1)}, bf16[1152,2304]{1,0:T(8,128)(2,1)}, u32[]{:S(2)}) %copy-start) | copy-done | bytes 5308440
  45.2 7.6 %shard_map.161.a_ref = bf16[128,2304]{1,0:T(8,128)(2,1)S(1)} custom-call(s32[6]{0:T(128)S(1)} %stack.35.where_ref, bf16[128,2304]{1,0:T(8,128)(2,1)} %collective-permute-done.5.refs_0_, bf16[128,2304]{1,0:T(8,128)(2,1)S(1)} %collective-permute-done.9.refs_1_, bf16[2304,1152]{1,0:T(8,128)(2,1)S(1)} %bitcast.25, ...), custom_call_target="tpu_custom_call" | custom-call | tf_op jit(solution)/shard_map/pallas_call | solution.py:169
  52.8 1.4 collective-permute-start.15
  54.2 2.8 %collective-permute-start.13 = (bf16[128,2304]{1,0:T(8,128)(2,1)S(1)}, bf16[128,2304]{1,0:T(8,128)(2,1)S(1)}, u32[]{:S(2)}, u32[]{:S(2)}) collective-permute-start(bf16[128,2304]{1,0:T(8,128)(2,1)S(1)} %collective-permute-done.7.refs_1_), channel_id=1, source_target_pairs={{0,0},{1,1},{2,4},{3,5},{4,2},{5,3},{6,6},{7,7},{8,8},{9,9},{10,12... | collective-permute-start | bytes 1769480 | tf_op jit(solution)/shard_map/ppermute | solution.py:36
  57.0 2.2 collective-permute-start.14
  60.5 1.9 collective-permute-done.11.twin_ref
  62.4 3.2 %collective-permute-start.12 = (f32[2,128,512]{2,1,0:T(8,128)S(1)}, f32[2,128,512]{2,1,0:T(8,128)S(1)}, u32[]{:S(2)}, u32[]{:S(2)}) collective-permute-start(f32[2,128,512]{2,1,0:T(8,128)S(1)} %bitcast.37), channel_id=1, source_target_pairs={{0,1},{1,0},{2,3},{3,2},{4,5},{5,4},{6,7},{7,6},{8,9},{9,8},{10,11... | collective-permute-start | bytes 1572872 | tf_op jit(solution)/shard_map/ppermute | solution.py:36
  65.5 7.3 %shard_map.162.a_ref = bf16[128,2304]{1,0:T(8,128)(2,1)S(1)} custom-call(s32[6]{0:T(128)S(1)} %stack.35.where_ref, bf16[128,2304]{1,0:T(8,128)(2,1)S(1)} %collective-permute-done.4.refs_0_, bf16[128,2304]{1,0:T(8,128)(2,1)S(1)} %collective-permute-done.6.refs_1_, bf16[2304,1152]{1,0:T(8,128)(2,1)S(1)} %bitcast.25, ...), custom_call_target="tpu_custom_call" | custom-call | tf_op jit(solution)/shard_map/pallas_call | solution.py:169
  74.1 10.0 %shard_map.163 = (bf16[128,2304]{1,0:T(8,128)(2,1)S(1)}, bf16[128,2304]{1,0:T(8,128)(2,1)S(1)}) custom-call(s32[6]{0:T(128)S(1)} %stack.35.where_ref, bf16[128,2304]{1,0:T(8,128)(2,1)S(1)} %shard_map.159.refs_0_, bf16[128,2304]{1,0:T(8,128)(2,1)S(1)} %collective-permute-done.7.refs_1_, bf16[2304,1152]{1,0:T(8,128)(2,1)S(1)} %bitcast.25, ...), custom_call_target="tpu_custom_call" | custom-call | tf_op jit(solution)/shard_map/pallas_call | solution.py:169
  85.0 4.1 %collective-permute-start.16 = (bf16[128,2304]{1,0:T(8,128)(2,1)S(1)}, bf16[128,2304]{1,0:T(8,128)(2,1)S(1)}, u32[]{:S(2)}, u32[]{:S(2)}) collective-permute-start(bf16[128,2304]{1,0:T(8,128)(2,1)S(1)} %collective-permute-done.13.refs_0_), channel_id=1, source_target_pairs={{2,0},{3,1},{4,6},{5,7},{10,8},{11,9},{12,14},{13,15},{18,16},{19,... | collective-permute-start | bytes 1769480 | tf_op jit(solution)/shard_map/ppermute | solution.py:36
  89.0 3.0 %collective-permute-start.20 = (bf16[128,2304]{1,0:T(8,128)(2,1)S(1)}, bf16[128,2304]{1,0:T(8,128)(2,1)S(1)}, u32[]{:S(2)}, u32[]{:S(2)}) collective-permute-start(bf16[128,2304]{1,0:T(8,128)(2,1)S(1)} %shard_map.164), channel_id=1, source_target_pairs={{0,0},{1,1},{2,4},{3,5},{4,2},{5,3},{6,6},{7,7},{8,8},{9,9},{10,12... | collective-permute-start | bytes 1769480 | tf_op jit(solution)/shard_map/ppermute | solution.py:36
  92.0 7.2 %shard_map.165.a_ref = bf16[128,2304]{1,0:T(8,128)(2,1)S(1)} custom-call(s32[6]{0:T(128)S(1)} %stack.35.where_ref, bf16[128,2304]{1,0:T(8,128)(2,1)S(1)} %collective-permute-done.13.refs_0_, bf16[128,2304]{1,0:T(8,128)(2,1)S(1)} %collective-permute-done.14.refs_1_, bf16[2304,1152]{1,0:T(8,128)(2,1)S(1)} %bitcast.25, ...), custom_call_target="tpu_custom_call" | custom-call | tf_op jit(solution)/shard_map/pallas_call | solution.py:169
  100.1 2.6 %collective-permute-start.19 = (bf16[128,2304]{1,0:T(8,128)(2,1)S(1)}, bf16[128,2304]{1,0:T(8,128)(2,1)S(1)}, u32[]{:S(2)}, u32[]{:S(2)}) collective-permute-start(bf16[128,2304]{1,0:T(8,128)(2,1)S(1)} %shard_map.166), channel_id=1, source_target_pairs={{0,0},{1,1},{2,4},{3,5},{4,2},{5,3},{6,6},{7,7},{8,8},{9,9},{10,12... | collective-permute-start | bytes 1769480 | tf_op jit(solution)/shard_map/ppermute | solution.py:36
  103.4 1.6 collective-permute-done.20.far_ref
  105.0 7.3 %shard_map.170 = bf16[128,2304]{1,0:T(8,128)(2,1)S(1)} custom-call(s32[6]{0:T(128)S(1)} %stack.35.where_ref, bf16[128,2304]{1,0:T(8,128)(2,1)S(1)} %collective-permute-done.8.refs_0_, bf16[128,2304]{1,0:T(8,128)(2,1)S(1)} %collective-permute-done.16.refs_1_, bf16[2304,1152]{1,0:T(8,128)(2,1)S(1)} %bitcast.25, ...), custom_call_target="tpu_custom_call" | custom-call | tf_op jit(solution)/shard_map/pallas_call | solution.py:169
  112.4 2.9 %collective-permute-start.24 = (bf16[2304,512]{1,0:T(8,128)(2,1)S(1)}, bf16[2304,512]{1,0:T(8,128)(2,1)S(1)}, u32[]{:S(2)}, u32[]{:S(2)}) collective-permute-start(bf16[2304,512]{1,0:T(8,128)(2,1)S(1)} %copy-done.3), channel_id=1, source_target_pairs={{0,1},{1,0},{2,3},{3,2},{4,5},{5,4},{6,7},{7,6},{8,9},{9,8},{10,11... | collective-permute-start | bytes 7077896 | tf_op jit(solution)/shard_map/ppermute | solution.py:36
  115.3 2.3 %collective-permute-done.19.b_ref = bf16[128,2304]{1,0:T(8,128)(2,1)S(1)} collective-permute-done((bf16[128,2304]{1,0:T(8,128)(2,1)S(1)}, bf16[128,2304]{1,0:T(8,128)(2,1)S(1)}, u32[]{:S(2)}, u32[]{:S(2)}) %collective-permute-start.19) | collective-permute-done | bytes 589856 | tf_op jit(solution)/shard_map/ppermute | solution.py:36
  118.5 4.7 %collective-permute-start.22 = (f32[2,128,512]{2,1,0:T(8,128)S(1)}, f32[2,128,512]{2,1,0:T(8,128)S(1)}, u32[]{:S(2)}, u32[]{:S(2)}) collective-permute-start(f32[2,128,512]{2,1,0:T(8,128)S(1)} %bitcast.36), channel_id=1, source_target_pairs={{0,17},{1,16},{2,19},{3,18},{4,21},{5,20},{6,23},{7,22},{8,25},{9,... | collective-permute-start | bytes 1572872 | tf_op jit(solution)/shard_map/ppermute | solution.py:36
  123.2 5.7 %collective-permute-done.26.b_ref = bf16[128,2304]{1,0:T(8,128)(2,1)S(1)} collective-permute-done((bf16[128,2304]{1,0:T(8,128)(2,1)S(1)}, bf16[128,2304]{1,0:T(8,128)(2,1)S(1)}, u32[]{:S(2)}, u32[]{:S(2)}) %collective-permute-start.26) | collective-permute-done | bytes 589856 | tf_op jit(solution)/shard_map/ppermute | solution.py:36
  130.4 5.5 %collective-permute-done.22.noise_both = f32[2,128,512]{2,1,0:T(8,128)S(1)} collective-permute-done((f32[2,128,512]{2,1,0:T(8,128)S(1)}, f32[2,128,512]{2,1,0:T(8,128)S(1)}, u32[]{:S(2)}, u32[]{:S(2)}) %collective-permute-start.22) | collective-permute-done | bytes 524320 | tf_op jit(solution)/shard_map/ppermute | solution.py:36
  135.9 15.6 %collective-permute-done.21.near_ref = bf16[128,2304]{1,0:T(8,128)(2,1)S(1)} collective-permute-done((bf16[128,2304]{1,0:T(8,128)(2,1)S(1)}, bf16[128,2304]{1,0:T(8,128)(2,1)S(1)}, u32[]{:S(2)}, u32[]{:S(2)}) %collective-permute-start.21) | collective-permute-done | bytes 589856 | tf_op jit(solution)/shard_map/ppermute | solution.py:36
  153.9 5.0 %collective-permute-done.23.came_ref = bf16[64,2304]{1,0:T(8,128)(2,1)S(1)} collective-permute-done((bf16[64,2304]{1,0:T(8,128)(2,1)S(1)}, bf16[64,2304]{1,0:T(8,128)(2,1)S(1)}, u32[]{:S(2)}, u32[]{:S(2)}) %collective-permute-start.23) | collective-permute-done | bytes 294944 | tf_op jit(solution)/shard_map/ppermute | solution.py:36
  159.9 1.9 collective-permute-start.29
  161.9 3.8 %collective-permute-start.25 = (bf16[32,512]{1,0:T(8,128)(2,1)S(1)}, bf16[32,512]{1,0:T(8,128)(2,1)S(1)}, u32[]{:S(2)}, u32[]{:S(2)}) collective-permute-start(bf16[32,512]{1,0:T(8,128)(2,1)S(1)} %bitcast.31), channel_id=1, source_target_pairs={{0,1},{1,0},{2,3},{3,2},{4,5},{5,4},{6,7},{7,6},{8,9},{9,8},{10,11... | collective-permute-start | bytes 98312 | tf_op jit(solution)/shard_map/ppermute | solution.py:36
  166.6 2.0 shard_map.172
  169.8 5.0 %collective-permute-done.29.far_ref = bf16[64,2304]{1,0:T(8,128)(2,1)S(1)} collective-permute-done((bf16[64,2304]{1,0:T(8,128)(2,1)S(1)}, bf16[64,2304]{1,0:T(8,128)(2,1)S(1)}, u32[]{:S(2)}, u32[]{:S(2)}) %collective-permute-start.29) | collective-permute-done | bytes 294944 | tf_op jit(solution)/shard_map/ppermute | solution.py:36
  174.8 2.1 collective-permute-start.31
  179.0 1.5 collective-permute-start.32
  180.5 6.4 %collective-permute-done.30.near_ref = bf16[64,2304]{1,0:T(8,128)(2,1)S(1)} collective-permute-done((bf16[64,2304]{1,0:T(8,128)(2,1)S(1)}, bf16[64,2304]{1,0:T(8,128)(2,1)S(1)}, u32[]{:S(2)}, u32[]{:S(2)}) %collective-permute-start.30) | collective-permute-done | bytes 294944 | tf_op jit(solution)/shard_map/ppermute | solution.py:36
  186.9 7.2 %collective-permute-done.31.last_ref = bf16[64,2304]{1,0:T(8,128)(2,1)S(1)} collective-permute-done((bf16[64,2304]{1,0:T(8,128)(2,1)S(1)}, bf16[64,2304]{1,0:T(8,128)(2,1)S(1)}, u32[]{:S(2)}, u32[]{:S(2)}) %collective-permute-start.31) | collective-permute-done | bytes 294944 | tf_op jit(solution)/shard_map/ppermute | solution.py:36
  194.1 2.6 %shard_map.174 = f32[40,256]{1,0:T(8,128)S(1)} custom-call(s32[6]{0:T(128)S(1)} %stack.35.where_ref, bf16[64,2304]{1,0:T(8,128)(2,1)S(1)} %shard_map.169.own_ref, bf16[64,2304]{1,0:T(8,128)(2,1)S(1)} %collective-permute-done.30.near_ref, bf16[64,2304]{1,0:T(8,128)(2,1)S(1)} %collective-permute-done.29.far_ref, ...), custom_call_target="tpu_custom_call" | custom-call | flops 40000000000 | tf_op jit(solution)/shard_map/pallas_call | solution.py:169
  196.7 2.3 collective-permute-start.34
  199.1 1.3 collective-permute-done.32.near_ref
  200.4 6.3 %collective-permute-done.34.last_ref = bf16[64,2304]{1,0:T(8,128)(2,1)S(1)} collective-permute-done((bf16[64,2304]{1,0:T(8,128)(2,1)S(1)}, bf16[64,2304]{1,0:T(8,128)(2,1)S(1)}, u32[]{:S(2)}, u32[]{:S(2)}) %collective-permute-start.34) | collective-permute-done | bytes 294944 | tf_op jit(solution)/shard_map/ppermute | solution.py:36
  206.7 2.6 %shard_map.175 = f32[40,256]{1,0:T(8,128)S(1)} custom-call(s32[6]{0:T(128)S(1)} %stack.35.where_ref, bf16[64,2304]{1,0:T(8,128)(2,1)S(1)} %shard_map.173.own_ref, bf16[64,2304]{1,0:T(8,128)(2,1)S(1)} %collective-permute-done.32.near_ref, bf16[64,2304]{1,0:T(8,128)(2,1)S(1)} %collective-permute-done.33.far_ref, ...), custom_call_target="tpu_custom_call" | custom-call | tf_op jit(solution)/shard_map/pallas_call | solution.py:169
  210.6 3.3 %collective-permute-start.36 = (f32[40,128]{1,0:T(8,128)S(1)}, f32[40,128]{1,0:T(8,128)S(1)}, u32[]{:S(2)}, u32[]{:S(2)}) collective-permute-start(f32[40,128]{1,0:T(8,128)S(1)} %pad_maximum_fusion.2), channel_id=1, source_target_pairs={{0,4},{1,5},{2,6},{3,7},{4,0},{5,1},{6,2},{7,3},{8,12},{9,13},{10,... | collective-permute-start | bytes 61448 | tf_op jit(solution)/shard_map/ppermute | solution.py:36
  215.2 1.4 collective-permute-done.35.refs_1_
  217.2 4.3 %collective-permute-start.38 = (f32[32,128]{1,0:T(8,128)S(1)}, f32[32,128]{1,0:T(8,128)S(1)}, u32[]{:S(2)}, u32[]{:S(2)}) collective-permute-start(f32[32,128]{1,0:T(8,128)S(1)} %shard_map.176), channel_id=1, source_target_pairs={{0,0},{1,2},{2,4},{3,6},{4,16},{5,18},{6,20},{7,22},{8,8},{9,10},{... | collective-permute-start | bytes 49160 | tf_op jit(solution)/shard_map/ppermute | solution.py:36
  221.5 3.0 %collective-permute-start.39 = (f32[32,128]{1,0:T(8,128)S(1)}, f32[32,128]{1,0:T(8,128)S(1)}, u32[]{:S(2)}, u32[]{:S(2)}) collective-permute-start(f32[32,128]{1,0:T(8,128)S(1)} %shard_map.176), channel_id=1, source_target_pairs={{0,1},{1,3},{2,5},{3,7},{4,17},{5,19},{6,21},{7,23},{8,9},{9,11},{... | collective-permute-start | bytes 49160 | tf_op jit(solution)/shard_map/ppermute | solution.py:36
  226.0 5.5 %collective-permute-done.40.halo_ref = f32[32,128]{1,0:T(8,128)S(1)} collective-permute-done((f32[32,128]{1,0:T(8,128)S(1)}, f32[32,128]{1,0:T(8,128)S(1)}, u32[]{:S(2)}, u32[]{:S(2)}) %collective-permute-start.40) | collective-permute-done | bytes 16416 | tf_op jit(solution)/shard_map/ppermute | solution.py:36
  231.4 1.7 shard_map.177
  (104 shorter events, 28.6 us)
Async XLA Ops:
  0.6 18.5 %collective-permute-start = (bf16[2304,1152]{1,0:T(8,128)(2,1)}, bf16[2304,1152]{1,0:T(8,128)(2,1)}, u32[]{:S(2)}, u32[]{:S(2)}) collective-permute-start(bf16[2304,1152]{1,0:T(8,128)(2,1)} %refs_2_.11), channel_id=1, source_target_pairs={{0,1},{1,0},{2,3},{3,2},{4,5},{5,4},{6,7},{7,6},{8,9},{9,8},{10,11... | collective-permute-start | bytes 15925256 | tf_op jit(solution)/shard_map/ppermute | solution.py:36
  1.4 17.7 %collective-permute-start.1 = (bf16[1152,2304]{1,0:T(8,128)(2,1)}, bf16[1152,2304]{1,0:T(8,128)(2,1)}, u32[]{:S(2)}, u32[]{:S(2)}) collective-permute-start(bf16[1152,2304]{1,0:T(8,128)(2,1)} %refs_4_.11), channel_id=1, source_target_pairs={{0,1},{1,0},{2,3},{3,2},{4,5},{5,4},{6,7},{7,6},{8,9},{9,8},{10,11... | collective-permute-start | bytes 15925256 | tf_op jit(solution)/shard_map/ppermute | solution.py:36
  4.6 14.5 %collective-permute-start.3 = (bf16[128,2304]{1,0:T(8,128)(2,1)S(1)}, bf16[128,2304]{1,0:T(8,128)(2,1)S(1)}, u32[]{:S(2)}, u32[]{:S(2)}) collective-permute-start(bf16[128,2304]{1,0:T(8,128)(2,1)S(1)} %shard_map.158.refs_0_), channel_id=1, source_target_pairs={{0,2},{1,3},{2,0},{3,1},{4,6},{5,7},{6,4},{7,5},{8,10},{9,11},{10,... | collective-permute-start | bytes 1769480 | tf_op jit(solution)/shard_map/ppermute | solution.py:36
  5.5 6.9 %collective-permute-start.2 = (f32[1,1664]{1,0:T(1,128)S(1)}, f32[1,1664]{1,0:T(1,128)S(1)}, u32[]{:S(2)}, u32[]{:S(2)}) collective-permute-start(f32[1,1664]{1,0:T(1,128)S(1)} %broadcast_in_dim.12.refs_6_.bias_a), channel_id=1, source_target_pairs={{0,1},{1,0},{2,3},{3,2},{4,5},{5,4},{6,7},{7,6},{8,9},{9,8},{10,11... | collective-permute-start | bytes 19976 | tf_op jit(solution)/shard_map/ppermute | solution.py:36
  6.3 18.0 %collective-permute-start.4 = (bf16[128,2304]{1,0:T(8,128)(2,1)S(1)}, bf16[128,2304]{1,0:T(8,128)(2,1)S(1)}, u32[]{:S(2)}, u32[]{:S(2)}) collective-permute-start(bf16[128,2304]{1,0:T(8,128)(2,1)S(1)} %shard_map.158.refs_0_), channel_id=1, source_target_pairs={{0,0},{1,1},{2,4},{3,5},{4,2},{5,3},{6,6},{7,7},{8,8},{9,9},{10,12... | collective-permute-start | bytes 1769480 | tf_op jit(solution)/shard_map/ppermute | solution.py:36
  19.1 18.6 %collective-permute-start.5 = (bf16[128,2304]{1,0:T(8,128)(2,1)S(1)}, bf16[128,2304]{1,0:T(8,128)(2,1)}, u32[]{:S(2)}, u32[]{:S(2)}) collective-permute-start(bf16[128,2304]{1,0:T(8,128)(2,1)S(1)} %collective-permute-done.3.refs_1_), channel_id=1, source_target_pairs={{0,0},{1,1},{2,4},{3,5},{4,2},{5,3},{6,6},{7,7},{8,8},{9,9},{10,12... | collective-permute-start | bytes 1769480 | tf_op jit(solution)/shard_map/ppermute | solution.py:36
  24.3 18.4 %collective-permute-start.9 = (bf16[128,2304]{1,0:T(8,128)(2,1)S(1)}, bf16[128,2304]{1,0:T(8,128)(2,1)S(1)}, u32[]{:S(2)}, u32[]{:S(2)}) collective-permute-start(bf16[128,2304]{1,0:T(8,128)(2,1)S(1)} %collective-permute-done.4.refs_0_), channel_id=1, source_target_pairs={{2,0},{3,1},{4,6},{5,7},{10,8},{11,9},{12,14},{13,15},{18,16},{19,... | collective-permute-start | bytes 1769480 | tf_op jit(solution)/shard_map/ppermute | solution.py:36
  25.7 28.5 %collective-permute-start.7 = (bf16[128,2304]{1,0:T(8,128)(2,1)S(1)}, bf16[128,2304]{1,0:T(8,128)(2,1)S(1)}, u32[]{:S(2)}, u32[]{:S(2)}) collective-permute-start(bf16[128,2304]{1,0:T(8,128)(2,1)S(1)} %shard_map.159.refs_0_), channel_id=1, source_target_pairs={{0,2},{1,3},{2,0},{3,1},{4,6},{5,7},{6,4},{7,5},{8,10},{9,11},{10,... | collective-permute-start | bytes 1769480 | tf_op jit(solution)/shard_map/ppermute | solution.py:36
  37.7 16.5 %collective-permute-start.8 = (bf16[128,2304]{1,0:T(8,128)(2,1)S(1)}, bf16[128,2304]{1,0:T(8,128)(2,1)S(1)}, u32[]{:S(2)}, u32[]{:S(2)}) collective-permute-start(bf16[128,2304]{1,0:T(8,128)(2,1)S(1)} %shard_map.159.refs_0_), channel_id=1, source_target_pairs={{0,0},{1,1},{2,4},{3,5},{4,2},{5,3},{6,6},{7,7},{8,8},{9,9},{10,12... | collective-permute-start | bytes 1769480 | tf_op jit(solution)/shard_map/ppermute | solution.py:36
  41.0 18.1 %collective-permute-start.10 = (f32[2,128,512]{2,1,0:T(8,128)S(1)}, f32[2,128,512]{2,1,0:T(8,128)S(1)}, u32[]{:S(2)}, u32[]{:S(2)}) collective-permute-start(f32[2,128,512]{2,1,0:T(8,128)S(1)} %bitcast.38), channel_id=1, source_target_pairs={{0,16},{1,17},{2,18},{3,19},{4,20},{5,21},{6,22},{7,23},{8,24},{9,... | collective-permute-start | bytes 1572872 | tf_op jit(solution)/shard_map/ppermute | solution.py:36
  41.3 24.2 %collective-permute-start.6 = (bf16[128,2304]{1,0:T(8,128)(2,1)}, bf16[128,2304]{1,0:T(8,128)(2,1)S(1)}, u32[]{:S(2)}, u32[]{:S(2)}) collective-permute-start(bf16[128,2304]{1,0:T(8,128)(2,1)} %collective-permute-done.5.refs_0_), channel_id=1, source_target_pairs={{2,0},{3,1},{4,6},{5,7},{10,8},{11,9},{12,14},{13,15},{18,16},{19,... | collective-permute-start | bytes 1769480 | tf_op jit(solution)/shard_map/ppermute | solution.py:36
  45.2 28.9 %slice-start.2 = ((s8[5308416]{0:T(1024)(128)(4,1)}), s8[4194304]{0:T(1024)(128)(4,1)S(1)}, s32[]{:S(2)}) async-start(s8[5308416]{0:T(1024)(128)(4,1)} %bitcast.26), calls=%async_computation.2 | async-start | bytes 8388608
  52.8 31.4 %collective-permute-start.15 = (bf16[128,2304]{1,0:T(8,128)(2,1)S(1)}, bf16[128,2304]{1,0:T(8,128)(2,1)S(1)}, u32[]{:S(2)}, u32[]{:S(2)}) collective-permute-start(bf16[128,2304]{1,0:T(8,128)(2,1)S(1)} %shard_map.161.a_ref), channel_id=1, source_target_pairs={{0,2},{1,3},{6,4},{7,5},{8,10},{9,11},{14,12},{15,13},{16,18},{17,... | collective-permute-start | bytes 1769480 | tf_op jit(solution)/shard_map/ppermute | solution.py:36
  54.2 30.7 %collective-permute-start.13 = (bf16[128,2304]{1,0:T(8,128)(2,1)S(1)}, bf16[128,2304]{1,0:T(8,128)(2,1)S(1)}, u32[]{:S(2)}, u32[]{:S(2)}) collective-permute-start(bf16[128,2304]{1,0:T(8,128)(2,1)S(1)} %collective-permute-done.7.refs_1_), channel_id=1, source_target_pairs={{0,0},{1,1},{2,4},{3,5},{4,2},{5,3},{6,6},{7,7},{8,8},{9,9},{10,12... | collective-permute-start | bytes 1769480 | tf_op jit(solution)/shard_map/ppermute | solution.py:36
  57.0 28.0 %collective-permute-start.14 = (bf16[128,2304]{1,0:T(8,128)(2,1)S(1)}, bf16[128,2304]{1,0:T(8,128)(2,1)S(1)}, u32[]{:S(2)}, u32[]{:S(2)}) collective-permute-start(bf16[128,2304]{1,0:T(8,128)(2,1)S(1)} %collective-permute-done.8.refs_0_), channel_id=1, source_target_pairs={{2,0},{3,1},{4,6},{5,7},{10,8},{11,9},{12,14},{13,15},{18,16},{19,... | collective-permute-start | bytes 1769480 | tf_op jit(solution)/shard_map/ppermute | solution.py:36
  59.2 3.2 %collective-permute-start.11 = (f32[2,2,2304]{2,1,0:T(2,128)S(1)}, f32[2,2,2304]{2,1,0:T(2,128)S(1)}, u32[]{:S(2)}, u32[]{:S(2)}) collective-permute-start(f32[2,2,2304]{2,1,0:T(2,128)S(1)} %copy-done.4), channel_id=1, source_target_pairs={{0,16},{1,17},{2,18},{3,19},{4,20},{5,21},{6,22},{7,23},{8,24},{9,... | collective-permute-start | bytes 110600 | tf_op jit(solution)/shard_map/ppermute | solution.py:36
  62.4 11.8 %collective-permute-start.12 = (f32[2,128,512]{2,1,0:T(8,128)S(1)}, f32[2,128,512]{2,1,0:T(8,128)S(1)}, u32[]{:S(2)}, u32[]{:S(2)}) collective-permute-start(f32[2,128,512]{2,1,0:T(8,128)S(1)} %bitcast.37), channel_id=1, source_target_pairs={{0,1},{1,0},{2,3},{3,2},{4,5},{5,4},{6,7},{7,6},{8,9},{9,8},{10,11... | collective-permute-start | bytes 1572872 | tf_op jit(solution)/shard_map/ppermute | solution.py:36
  72.8 26.5 %collective-permute-start.18 = (bf16[128,2304]{1,0:T(8,128)(2,1)S(1)}, bf16[128,2304]{1,0:T(8,128)(2,1)S(1)}, u32[]{:S(2)}, u32[]{:S(2)}) collective-permute-start(bf16[128,2304]{1,0:T(8,128)(2,1)S(1)} %shard_map.162.a_ref), channel_id=1, source_target_pairs={{0,2},{1,3},{6,4},{7,5},{8,10},{9,11},{14,12},{15,13},{16,18},{17,... | collective-permute-start | bytes 1769480 | tf_op jit(solution)/shard_map/ppermute | solution.py:36
  85.0 17.7 %collective-permute-start.16 = (bf16[128,2304]{1,0:T(8,128)(2,1)S(1)}, bf16[128,2304]{1,0:T(8,128)(2,1)S(1)}, u32[]{:S(2)}, u32[]{:S(2)}) collective-permute-start(bf16[128,2304]{1,0:T(8,128)(2,1)S(1)} %collective-permute-done.13.refs_0_), channel_id=1, source_target_pairs={{2,0},{3,1},{4,6},{5,7},{10,8},{11,9},{12,14},{13,15},{18,16},{19,... | collective-permute-start | bytes 1769480 | tf_op jit(solution)/shard_map/ppermute | solution.py:36
  89.0 16.0 %collective-permute-start.20 = (bf16[128,2304]{1,0:T(8,128)(2,1)S(1)}, bf16[128,2304]{1,0:T(8,128)(2,1)S(1)}, u32[]{:S(2)}, u32[]{:S(2)}) collective-permute-start(bf16[128,2304]{1,0:T(8,128)(2,1)S(1)} %shard_map.164), channel_id=1, source_target_pairs={{0,0},{1,1},{2,4},{3,5},{4,2},{5,3},{6,6},{7,7},{8,8},{9,9},{10,12... | collective-permute-start | bytes 1769480 | tf_op jit(solution)/shard_map/ppermute | solution.py:36
  100.1 17.6 %collective-permute-start.19 = (bf16[128,2304]{1,0:T(8,128)(2,1)S(1)}, bf16[128,2304]{1,0:T(8,128)(2,1)S(1)}, u32[]{:S(2)}, u32[]{:S(2)}) collective-permute-start(bf16[128,2304]{1,0:T(8,128)(2,1)S(1)} %shard_map.166), channel_id=1, source_target_pairs={{0,0},{1,1},{2,4},{3,5},{4,2},{5,3},{6,6},{7,7},{8,8},{9,9},{10,12... | collective-permute-start | bytes 1769480 | tf_op jit(solution)/shard_map/ppermute | solution.py:36
  102.7 15.0 %collective-permute-start.17 = (bf16[128,2304]{1,0:T(8,128)(2,1)S(1)}, bf16[128,2304]{1,0:T(8,128)(2,1)S(1)}, u32[]{:S(2)}, u32[]{:S(2)}) collective-permute-start(bf16[128,2304]{1,0:T(8,128)(2,1)S(1)} %get-tuple-element.71), channel_id=1, source_target_pairs={{0,2},{1,3},{2,0},{3,1},{4,6},{5,7},{6,4},{7,5},{8,10},{9,11},{10,... | collective-permute-start | bytes 1769480 | tf_op jit(solution)/shard_map/ppermute | solution.py:36
  112.3 39.2 %copy-start.8 = (f32[2,2304]{1,0:T(2,128)S(1)}, f32[2,2304]{1,0:T(2,128)}, u32[]{:S(2)}) copy-start(f32[2,2304]{1,0:T(2,128)} %gate_ref.3) | copy-start | bytes 55300
  112.3 16.6 %collective-permute-start.26 = (bf16[128,2304]{1,0:T(8,128)(2,1)S(1)}, bf16[128,2304]{1,0:T(8,128)(2,1)S(1)}, u32[]{:S(2)}, u32[]{:S(2)}) collective-permute-start(bf16[128,2304]{1,0:T(8,128)(2,1)S(1)} %shard_map.170), channel_id=1, source_target_pairs={{0,2},{1,3},{2,0},{3,1},{4,6},{5,7},{6,4},{7,5},{8,10},{9,11},{10,... | collective-permute-start | bytes 1769480 | tf_op jit(solution)/shard_map/ppermute | solution.py:36
  112.4 54.2 %collective-permute-start.24 = (bf16[2304,512]{1,0:T(8,128)(2,1)S(1)}, bf16[2304,512]{1,0:T(8,128)(2,1)S(1)}, u32[]{:S(2)}, u32[]{:S(2)}) collective-permute-start(bf16[2304,512]{1,0:T(8,128)(2,1)S(1)} %copy-done.3), channel_id=1, source_target_pairs={{0,1},{1,0},{2,3},{3,2},{4,5},{5,4},{6,7},{7,6},{8,9},{9,8},{10,11... | collective-permute-start | bytes 7077896 | tf_op jit(solution)/shard_map/ppermute | solution.py:36
  118.4 33.1 %copy-start.2 = (bf16[256,2304]{1,0:T(8,128)(2,1)S(1)}, bf16[256,2304]{1,0:T(8,128)(2,1)}, u32[]{:S(2)}) copy-start(bf16[256,2304]{1,0:T(8,128)(2,1)} %tokens_ref.7) | copy-start | bytes 3538948
  118.4 33.1 %collective-permute-start.21 = (bf16[128,2304]{1,0:T(8,128)(2,1)S(1)}, bf16[128,2304]{1,0:T(8,128)(2,1)S(1)}, u32[]{:S(2)}, u32[]{:S(2)}) collective-permute-start(bf16[128,2304]{1,0:T(8,128)(2,1)S(1)} %shard_map.167), channel_id=1, source_target_pairs={{0,2},{1,3},{2,0},{3,1},{4,6},{5,7},{6,4},{7,5},{8,10},{9,11},{10,... | collective-permute-start | bytes 1769480 | tf_op jit(solution)/shard_map/ppermute | solution.py:36
  118.5 17.4 %collective-permute-start.22 = (f32[2,128,512]{2,1,0:T(8,128)S(1)}, f32[2,128,512]{2,1,0:T(8,128)S(1)}, u32[]{:S(2)}, u32[]{:S(2)}) collective-permute-start(f32[2,128,512]{2,1,0:T(8,128)S(1)} %bitcast.36), channel_id=1, source_target_pairs={{0,17},{1,16},{2,19},{3,18},{4,21},{5,20},{6,23},{7,22},{8,25},{9,... | collective-permute-start | bytes 1572872 | tf_op jit(solution)/shard_map/ppermute | solution.py:36
  129.6 32.3 %copy-start.9 = (bf16[512,32]{0,1:T(8,128)(2,1)S(1)}, bf16[512,32]{0,1:T(8,128)(2,1)}, u32[]{:S(2)}) copy-start(bf16[512,32]{0,1:T(8,128)(2,1)} %param.26) | copy-start | bytes 98308
  129.6 37.0 %collective-permute-start.27 = (bf16[128,2304]{1,0:T(8,128)(2,1)S(1)}, bf16[128,2304]{1,0:T(8,128)(2,1)S(1)}, u32[]{:S(2)}, u32[]{:S(2)}) collective-permute-start(bf16[128,2304]{1,0:T(8,128)(2,1)S(1)} %shard_map.171), channel_id=1, source_target_pairs={{0,4},{1,5},{2,6},{3,7},{4,0},{5,1},{6,2},{7,3},{8,12},{9,13},{10,... | collective-permute-start | bytes 1769480 | tf_op jit(solution)/shard_map/ppermute | solution.py:36
  152.6 6.3 %collective-permute-start.23 = (bf16[64,2304]{1,0:T(8,128)(2,1)S(1)}, bf16[64,2304]{1,0:T(8,128)(2,1)S(1)}, u32[]{:S(2)}, u32[]{:S(2)}) collective-permute-start(bf16[64,2304]{1,0:T(8,128)(2,1)S(1)} %get-tuple-element.80), channel_id=1, source_target_pairs={{0,16},{1,17},{2,18},{3,19},{4,20},{5,21},{6,22},{7,23},{8,24},{9,... | collective-permute-start | bytes 884744 | tf_op jit(solution)/shard_map/ppermute | solution.py:36
  159.9 14.9 %collective-permute-start.29 = (bf16[64,2304]{1,0:T(8,128)(2,1)S(1)}, bf16[64,2304]{1,0:T(8,128)(2,1)S(1)}, u32[]{:S(2)}, u32[]{:S(2)}) collective-permute-start(bf16[64,2304]{1,0:T(8,128)(2,1)S(1)} %shard_map.169.own_ref), channel_id=1, source_target_pairs={{0,4},{1,5},{2,6},{3,7},{4,0},{5,1},{6,2},{7,3},{8,12},{9,13},{10,... | collective-permute-start | bytes 884744 | tf_op jit(solution)/shard_map/ppermute | solution.py:36
  161.9 4.7 %collective-permute-start.25 = (bf16[32,512]{1,0:T(8,128)(2,1)S(1)}, bf16[32,512]{1,0:T(8,128)(2,1)S(1)}, u32[]{:S(2)}, u32[]{:S(2)}) collective-permute-start(bf16[32,512]{1,0:T(8,128)(2,1)S(1)} %bitcast.31), channel_id=1, source_target_pairs={{0,1},{1,0},{2,3},{3,2},{4,5},{5,4},{6,7},{7,6},{8,9},{9,8},{10,11... | collective-permute-start | bytes 98312 | tf_op jit(solution)/shard_map/ppermute | solution.py:36
  168.6 8.4 %collective-permute-start.28 = (bf16[64,2304]{1,0:T(8,128)(2,1)S(1)}, bf16[64,2304]{1,0:T(8,128)(2,1)S(1)}, u32[]{:S(2)}, u32[]{:S(2)}) collective-permute-start(bf16[64,2304]{1,0:T(8,128)(2,1)S(1)} %get-tuple-element.89), channel_id=1, source_target_pairs={{0,16},{1,17},{2,18},{3,19},{4,20},{5,21},{6,22},{7,23},{8,24},{9,... | collective-permute-start | bytes 884744 | tf_op jit(solution)/shard_map/ppermute | solution.py:36
  169.8 17.1 %collective-permute-start.30 = (bf16[64,2304]{1,0:T(8,128)(2,1)S(1)}, bf16[64,2304]{1,0:T(8,128)(2,1)S(1)}, u32[]{:S(2)}, u32[]{:S(2)}) collective-permute-start(bf16[64,2304]{1,0:T(8,128)(2,1)S(1)} %shard_map.169.own_ref), channel_id=1, source_target_pairs={{0,2},{1,3},{2,0},{3,1},{4,6},{5,7},{6,4},{7,5},{8,10},{9,11},{10,... | collective-permute-start | bytes 884744 | tf_op jit(solution)/shard_map/ppermute | solution.py:36
  174.8 19.3 %collective-permute-start.31 = (bf16[64,2304]{1,0:T(8,128)(2,1)S(1)}, bf16[64,2304]{1,0:T(8,128)(2,1)S(1)}, u32[]{:S(2)}, u32[]{:S(2)}) collective-permute-start(bf16[64,2304]{1,0:T(8,128)(2,1)S(1)} %collective-permute-done.29.far_ref), channel_id=1, source_target_pairs={{0,2},{1,3},{2,0},{3,1},{4,6},{5,7},{6,4},{7,5},{8,10},{9,11},{10,... | collective-permute-start | bytes 884744 | tf_op jit(solution)/shard_map/ppermute | solution.py:36
  178.0 18.8 %collective-permute-start.33 = (bf16[64,2304]{1,0:T(8,128)(2,1)S(1)}, bf16[64,2304]{1,0:T(8,128)(2,1)S(1)}, u32[]{:S(2)}, u32[]{:S(2)}) collective-permute-start(bf16[64,2304]{1,0:T(8,128)(2,1)S(1)} %shard_map.173.own_ref), channel_id=1, source_target_pairs={{0,4},{1,5},{2,6},{3,7},{4,0},{5,1},{6,2},{7,3},{8,12},{9,13},{10,... | collective-permute-start | bytes 884744 | tf_op jit(solution)/shard_map/ppermute | solution.py:36
  179.0 21.4 %collective-permute-start.32 = (bf16[64,2304]{1,0:T(8,128)(2,1)S(1)}, bf16[64,2304]{1,0:T(8,128)(2,1)S(1)}, u32[]{:S(2)}, u32[]{:S(2)}) collective-permute-start(bf16[64,2304]{1,0:T(8,128)(2,1)S(1)} %shard_map.173.own_ref), channel_id=1, source_target_pairs={{0,2},{1,3},{2,0},{3,1},{4,6},{5,7},{6,4},{7,5},{8,10},{9,11},{10,... | collective-permute-start | bytes 884744 | tf_op jit(solution)/shard_map/ppermute | solution.py:36
  196.7 10.0 %collective-permute-start.34 = (bf16[64,2304]{1,0:T(8,128)(2,1)S(1)}, bf16[64,2304]{1,0:T(8,128)(2,1)S(1)}, u32[]{:S(2)}, u32[]{:S(2)}) collective-permute-start(bf16[64,2304]{1,0:T(8,128)(2,1)S(1)} %collective-permute-done.33.far_ref), channel_id=1, source_target_pairs={{0,2},{1,3},{2,0},{3,1},{4,6},{5,7},{6,4},{7,5},{8,10},{9,11},{10,... | collective-permute-start | bytes 884744 | tf_op jit(solution)/shard_map/ppermute | solution.py:36
  199.1 26.8 %copy-start.13 = (f32[32]{0:T(128)S(1)}, f32[32]{0:T(128)}, u32[]{:S(2)}) copy-start(f32[32]{0:T(128)} %param.28) | copy-start | bytes 388
  199.1 32.3 %copy-start.5 = (f32[32,32,3,3]{1,0,3,2:T(8,128)S(1)}, f32[32,32,3,3]{1,0,3,2:T(8,128)}, u32[]{:S(2)}) copy-start(f32[32,32,3,3]{1,0,3,2:T(8,128)} %param.27) | copy-start | bytes 110596
  199.1 32.3 %copy-start.10 = (f32[1,32,128]{2,1,0:T(8,128)S(1)}, f32[1,32,128]{2,1,0:T(8,128)}, u32[]{:S(2)}) copy-start(f32[1,32,128]{2,1,0:T(8,128)} %param.29) | copy-start | bytes 49156
  209.5 4.6 %collective-permute-start.37 = (f32[40,128]{1,0:T(8,128)S(1)}, f32[40,128]{1,0:T(8,128)S(1)}, u32[]{:S(2)}, u32[]{:S(2)}) collective-permute-start(f32[40,128]{1,0:T(8,128)S(1)} %pad_maximum_fusion.3), channel_id=1, source_target_pairs={{0,6},{1,7},{2,4},{3,5},{4,2},{5,3},{6,0},{7,1},{8,14},{9,15},{10,... | collective-permute-start | bytes 61448 | tf_op jit(solution)/shard_map/ppermute | solution.py:36
  210.6 4.6 %collective-permute-start.36 = (f32[40,128]{1,0:T(8,128)S(1)}, f32[40,128]{1,0:T(8,128)S(1)}, u32[]{:S(2)}, u32[]{:S(2)}) collective-permute-start(f32[40,128]{1,0:T(8,128)S(1)} %pad_maximum_fusion.2), channel_id=1, source_target_pairs={{0,4},{1,5},{2,6},{3,7},{4,0},{5,1},{6,2},{7,3},{8,12},{9,13},{10,... | collective-permute-start | bytes 61448 | tf_op jit(solution)/shard_map/ppermute | solution.py:36
  214.0 2.6 %collective-permute-start.35 = (f32[40,128]{1,0:T(8,128)S(1)}, f32[40,128]{1,0:T(8,128)S(1)}, u32[]{:S(2)}, u32[]{:S(2)}) collective-permute-start(f32[40,128]{1,0:T(8,128)S(1)} %pad_maximum_fusion.1), channel_id=1, source_target_pairs={{0,2},{1,3},{2,0},{3,1},{4,6},{5,7},{6,4},{7,5},{8,10},{9,11},{10,... | collective-permute-start | bytes 61448 | tf_op jit(solution)/shard_map/ppermute | solution.py:36
  217.2 8.8 %collective-permute-start.38 = (f32[32,128]{1,0:T(8,128)S(1)}, f32[32,128]{1,0:T(8,128)S(1)}, u32[]{:S(2)}, u32[]{:S(2)}) collective-permute-start(f32[32,128]{1,0:T(8,128)S(1)} %shard_map.176), channel_id=1, source_target_pairs={{0,0},{1,2},{2,4},{3,6},{4,16},{5,18},{6,20},{7,22},{8,8},{9,10},{... | collective-permute-start | bytes 49160 | tf_op jit(solution)/shard_map/ppermute | solution.py:36
  221.5 4.4 %collective-permute-start.39 = (f32[32,128]{1,0:T(8,128)S(1)}, f32[32,128]{1,0:T(8,128)S(1)}, u32[]{:S(2)}, u32[]{:S(2)}) collective-permute-start(f32[32,128]{1,0:T(8,128)S(1)} %shard_map.176), channel_id=1, source_target_pairs={{0,1},{1,3},{2,5},{3,7},{4,17},{5,19},{6,21},{7,23},{8,9},{9,11},{... | collective-permute-start | bytes 49160 | tf_op jit(solution)/shard_map/ppermute | solution.py:36
  224.6 6.8 %collective-permute-start.40 = (f32[32,128]{1,0:T(8,128)S(1)}, f32[32,128]{1,0:T(8,128)S(1)}, u32[]{:S(2)}, u32[]{:S(2)}) collective-permute-start(f32[32,128]{1,0:T(8,128)S(1)} %shard_map.176), channel_id=1, source_target_pairs={{1,1},{2,3},{3,5},{5,17},{6,19},{7,21},{9,9},{10,11},{11,13},{13,2... | collective-permute-start | bytes 49160 | tf_op jit(solution)/shard_map/ppermute | solution.py:36
  (11 other events, 130.1 us)

commit v6 on v5

--- a/solution.py
+++ b/solution.py
@@ -281,20 +281,26 @@
     )
 
 
-def add_kernel(always, where_ref, a_ref, b_ref, out_ref):
-    b = b_ref[...].astype(jnp.float32)
-    if not always:
-        b = jnp.where(where_ref[MID] == 1, b, 0.0)
-    out_ref[...] = (a_ref[...].astype(jnp.float32) + b).astype(jnp.bfloat16)
-
-
-def add(where, a, b, always=False, flops=0):
-    return call(functools.partial(add_kernel, always), where, (a, b), [shape_of(a.shape)], flops=flops)[0]
+def add_kernel(begin, always, where_ref, *refs):
+    out_ref = refs[-1]
+    rows = refs[0].shape[0]
+    for place, (a_ref, b_ref) in enumerate(zip(refs[:-1:2], refs[1:-1:2])):
+        b = b_ref[begin : begin + rows, :].astype(jnp.float32)
+        if not always:
+            b = jnp.where(where_ref[MID] == 1, b, 0.0)
+        total = (a_ref[...].astype(jnp.float32) + b).astype(jnp.bfloat16)
+        out_ref[place * rows : (place + 1) * rows, :] = total
+
+
+def add(where, *parts, begin=0, always=False, flops=0):
+    rows, width = parts[0].shape
+    outs = [shape_of((rows * len(parts) // 2, width))]
+    return call(functools.partial(add_kernel, begin, always), where, parts, outs, flops=flops)[0]
 
 
 def out_kernel(begin, always, where_ref, own_ref, near_ref, far_ref, tokens_ref, gate_ref, bias_ref, *refs):
     out_ref, kept_ref, sent_ref = refs[-3:]
-    far = far_ref[...].astype(jnp.float32)
+    far = far_ref[0 : own_ref.shape[0], :].astype(jnp.float32)
     if not always:
         far = jnp.where(where_ref[MID] == 1, far, 0.0)
     summed = own_ref[...].astype(jnp.float32) + near_ref[...].astype(jnp.float32) + far
@@ -534,46 +540,46 @@
         noise_for(1 - core, upper),
         noise_for(1 - core, 1 - upper),
     )
-    noise_twin, noise_core, noise_both, _ = barrier((noise_twin, noise_core, noise_both, own_b))
-    noise_twin = swap_twins(noise_twin)
-    up_other, down_other, bias_other, near_a, own_b = barrier((up_other, down_other, bias_other, near_a, own_b))
+    head_twin = swap_twins(after(ada_head, own_a))
+    up_other, down_other, bias_other, near_a, own_b, head_twin = barrier(
+        (up_other, down_other, bias_other, near_a, own_b, head_twin)
+    )
     panels = (up_weight, up_other, down_weight, down_other, biases, bias_other)
     far_mid_a = middle(near_a)
     near_b = near(after(own_b, near_a))
     mid_a = after(mid_a, near_a)
     far_end_a = outward(mid_a)
+    noise_twin = swap_twins(after(noise_twin, near_a))
     sum_own_a, sum_near_a = ffn(where, [[own_a], [after(near_a, mid_a)]], panels, fetch=True)
     far_mid_a = after(far_mid_a, sum_near_a)
     last_end_a = outward(far_mid_a)
     mid_b = middle(after(own_b, far_mid_a))
     noise_core = swap_cores(after(noise_core, far_mid_a))
-    head_twin = swap_twins(after(ada_head, far_mid_a))
     (sum_far_a,) = ffn(where, [[far_mid_a, far_end_a]], panels)
     came_far_a = inward(sum_far_a)
     near_b, mid_b = barrier((near_b, mid_b, sum_far_a))[:2]
     far_mid_b, far_end_b = middle(near_b), outward(mid_b)
-    (sum_last_a,) = ffn(where, [[mid_a, after(last_end_a, near_b, mid_b, noise_twin, head_twin)]], panels)
+    sum_own_b, sum_near_b = ffn(where, [[after(own_b, sum_far_a)], [after(near_b, mid_b, noise_twin)]], panels)
+    (sum_last_a,) = ffn(where, [[mid_a, after(last_end_a, sum_near_b, noise_core)]], panels)
     came_last_a = inward(sum_last_a)
+    far_mid_b, far_end_b = barrier((far_mid_b, far_end_b, sum_last_a))[:2]
+    last_end_b = outward(far_mid_b)
     noise_both = swap_both(after(noise_both, noise_twin))
-    sum_own_b, sum_near_b = ffn(where, [[after(own_b, sum_last_a, noise_core)], [near_b]], panels)
-    both_last_a = add(where, after(sum_last_a, sum_near_b), came_far_a)
-    went_last_a = middle(both_last_a)
-    far_mid_b, far_end_b = barrier((far_mid_b, far_end_b, both_last_a))[:2]
-    last_end_b = outward(far_mid_b)
-    (sum_far_b,) = ffn(where, [[far_mid_b, far_end_b]], panels)
-    both_far_a = add(where, after(sum_far_a, sum_far_b), came_last_a)
-    went_far_a = middle(both_far_a)
-    (sum_last_b,) = ffn(where, [[after(mid_b, both_far_a, went_last_a), last_end_b]], panels)
+    both_a = add(where, sum_last_a, after(came_far_a, far_mid_b), sum_far_a, came_last_a)
+    went_a = middle(both_a)
+    sum_far_b, sum_last_b = ffn(
+        where, [[after(far_mid_b, both_a), far_end_b], [mid_b, last_end_b]], panels
+    )
     came_last_b = near(sum_last_b)
     head_other = swap_cores(after(head_weight, sum_last_b))
     code_other = swap_cores(after(codes, sum_last_b))
     came_near_b = near(after(sum_near_b, last_end_b))
-    both_near_a = add(where, sum_near_a, after(went_far_a, went_last_a, came_near_b), flops=AHEAD)
+    both_near_a = add(where, sum_near_a, after(went_a, came_near_b), begin=step, flops=AHEAD)
     came_near_a = near(both_near_a)
-    both_far_b = add(where, after(sum_far_b, both_near_a), came_last_b, True)
+    both_far_b = add(where, after(sum_far_b, both_near_a), came_last_b, always=True)
     went_far_b = across(both_far_b)
     out_a, kept_a, sent_a = block_rows(
-        where, 0, False, sum_own_a, after(came_near_a, noise_both), went_last_a, tokens, gate, bias_out
+        where, 0, False, sum_own_a, after(came_near_a, noise_both), went_a, tokens, gate, bias_out
     )
     came_a = swap_twins(sent_a)
     mixed_a = mix_twins(where, kept_a, came_a, ada_head, head_twin)

time: 234 us -> 230 us (0.983)
  Pallas kernels: 68.7 us -> 64.4 us
    pallas_call x20 -> x18, Pallas kernels: 68.7 us -> 64.4 us  [call(): pl.pallas_call(kernel, out_shape=outs, in_specs=[SCALARS] + (specs or [ON...]
    ppermute x41 -> x40, starting transfers between devices: 74.7 us -> 76 us  [permute_devices(): return lax.ppermute(value, ('dp', 'mp'), pairs)]
    ppermute x41 -> x40, waiting for transfers between devices: 81.5 us -> 80.9 us  [permute_devices(): return lax.ppermute(value, ('dp', 'mp'), pairs)]
    unnamed x36 -> x34, local copies, waits for them, and re-layouts: 5.38 us -> 5.37 us
  transfers between devices with their start and end apart: 41 -> 40, of which waited for: 18 -> 18; matrix products, arithmetic and copies ran while one was open for 1% -> 1% of each run, Pallas kernels for 27% -> 26%
where the time goes in v6:
time: 230 us; the launch traced here: 229 us
  waiting for transfers between devices  80.9 us (35%)
  starting transfers between devices  76 us (33%)
  Pallas kernels  64.4 us (28%)
  local copies, waits for them, and re-layouts  5.98 us (3%)
    ppermute x40, waiting for transfers between devices, permute_devices(): return lax.ppermute(value, ('dp', 'mp'), pairs)  80.9 us
    ppermute x40, starting transfers between devices, permute_devices(): return lax.ppermute(value, ('dp', 'mp'), pairs)  76 us
    pallas_call x18, Pallas kernels, call(): pl.pallas_call(kernel, out_shape=outs, in_specs=[SCALARS] + (specs or [ON...  64.4 us
    unnamed x34, local copies, waits for them, and re-layouts  5.37 us
  transfers between devices with their start and end apart: 40, of which 18 were waited for; matrix products, arithmetic and copies ran while one was open for 1% of the time, Pallas kernels for 26%

profile of v6, /device:TPU:13, one launch (start us, length us, event | category | flops | bytes accessed | tf_op | source)
XLA Modules:
  0.0 229.4 jit_solution(11808070287489457178)
XLA Ops:
  4.8 4.3 %collective-permute-start.6 = (bf16[128,2304]{1,0:T(8,128)(2,1)S(1)}, bf16[128,2304]{1,0:T(8,128)(2,1)S(1)}, u32[]{:S(2)}, u32[]{:S(2)}) collective-permute-start(bf16[128,2304]{1,0:T(8,128)(2,1)S(1)} %shard_map.158.refs_0_), channel_id=1, source_target_pairs={{0,0},{1,1},{2,4},{3,5},{4,2},{5,3},{6,6},{7,7},{8,8},{9,9},{10,12... | collective-permute-start | bytes 1769480 | tf_op jit(solution)/shard_map/ppermute | solution.py:36
  10.9 6.4 %collective-permute-done.2.refs_7_.refs_9_.bias_b = f32[1,1664]{1,0:T(1,128)S(1)} collective-permute-done((f32[1,1664]{1,0:T(1,128)S(1)}, f32[1,1664]{1,0:T(1,128)S(1)}, u32[]{:S(2)}, u32[]{:S(2)}) %collective-permute-start.2) | collective-permute-done | bytes 6688 | tf_op jit(solution)/shard_map/ppermute | solution.py:36
  20.7 3.2 %collective-permute-start.5 = (bf16[128,2304]{1,0:T(8,128)(2,1)S(1)}, bf16[128,2304]{1,0:T(8,128)(2,1)}, u32[]{:S(2)}, u32[]{:S(2)}) collective-permute-start(bf16[128,2304]{1,0:T(8,128)(2,1)S(1)} %collective-permute-done.3.refs_1_), channel_id=1, source_target_pairs={{0,0},{1,1},{2,4},{3,5},{4,2},{5,3},{6,6},{7,7},{8,8},{9,9},{10,12... | collective-permute-start | bytes 1769480 | tf_op jit(solution)/shard_map/ppermute | solution.py:36
  23.9 2.1 collective-permute-start.7
  26.0 12.5 %shard_map.160 = (bf16[128,2304]{1,0:T(8,128)(2,1)S(1)}, bf16[128,2304]{1,0:T(8,128)(2,1)S(1)}) custom-call(s32[6]{0:T(128)S(1)} %stack.35.where_ref, bf16[128,2304]{1,0:T(8,128)(2,1)S(1)} %shard_map.158.refs_0_, bf16[128,2304]{1,0:T(8,128)(2,1)S(1)} %collective-permute-done.3.refs_1_, bf16[2304,1152]{1,0:T(8,128)(2,1)} %refs_4_.9, ...), custom_call_target="tpu_custom_call" | custom-call | tf_op jit(solution)/shard_map/pallas_call | solution.py:169
  38.5 2.8 %collective-permute-start.13 = (bf16[128,2304]{1,0:T(8,128)(2,1)}, bf16[128,2304]{1,0:T(8,128)(2,1)S(1)}, u32[]{:S(2)}, u32[]{:S(2)}) collective-permute-start(bf16[128,2304]{1,0:T(8,128)(2,1)} %collective-permute-done.5.refs_0_), channel_id=1, source_target_pairs={{2,0},{3,1},{4,6},{5,7},{10,8},{11,9},{12,14},{13,15},{18,16},{19,... | collective-permute-start | bytes 1769480 | tf_op jit(solution)/shard_map/ppermute | solution.py:36
  41.3 2.1 collective-permute-start.9
  44.0 2.6 %collective-permute-start.14 = (f32[2,128,512]{2,1,0:T(8,128)S(1)}, f32[2,128,512]{2,1,0:T(8,128)S(1)}, u32[]{:S(2)}, u32[]{:S(2)}) collective-permute-start(f32[2,128,512]{2,1,0:T(8,128)S(1)} %bitcast.35), channel_id=1, source_target_pairs={{0,1},{1,0},{2,3},{3,2},{4,5},{5,4},{6,7},{7,6},{8,9},{9,8},{10,11... | collective-permute-start | bytes 1572872 | tf_op jit(solution)/shard_map/ppermute | solution.py:36
  46.6 2.5 %copy-done = bf16[1152,2304]{1,0:T(8,128)(2,1)S(1)} copy-done((bf16[1152,2304]{1,0:T(8,128)(2,1)S(1)}, bf16[1152,2304]{1,0:T(8,128)(2,1)}, u32[]{:S(2)}) %copy-start) | copy-done | bytes 5308440
  49.2 7.7 %shard_map.161.refs_2_ = bf16[128,2304]{1,0:T(8,128)(2,1)S(1)} custom-call(s32[6]{0:T(128)S(1)} %stack.35.where_ref, bf16[128,2304]{1,0:T(8,128)(2,1)} %collective-permute-done.5.refs_0_, bf16[128,2304]{1,0:T(8,128)(2,1)} %collective-permute-done.7.refs_1_, bf16[2304,1152]{1,0:T(8,128)(2,1)S(1)} %bitcast.25, ...), custom_call_target="tpu_custom_call" | custom-call | tf_op jit(solution)/shard_map/pallas_call | solution.py:169
  58.2 3.2 %collective-permute-start.11 = (bf16[128,2304]{1,0:T(8,128)(2,1)S(1)}, bf16[128,2304]{1,0:T(8,128)(2,1)S(1)}, u32[]{:S(2)}, u32[]{:S(2)}) collective-permute-start(bf16[128,2304]{1,0:T(8,128)(2,1)S(1)} %collective-permute-done.8.refs_1_), channel_id=1, source_target_pairs={{0,0},{1,1},{2,4},{3,5},{4,2},{5,3},{6,6},{7,7},{8,8},{9,9},{10,12... | collective-permute-start | bytes 1769480 | tf_op jit(solution)/shard_map/ppermute | solution.py:36
  61.4 1.7 collective-permute-start.12
  63.1 10.0 %shard_map.162 = (bf16[128,2304]{1,0:T(8,128)(2,1)S(1)}, bf16[128,2304]{1,0:T(8,128)(2,1)S(1)}) custom-call(s32[6]{0:T(128)S(1)} %stack.35.where_ref, bf16[128,2304]{1,0:T(8,128)(2,1)S(1)} %shard_map.159.refs_0_, bf16[128,2304]{1,0:T(8,128)(2,1)S(1)} %collective-permute-done.8.refs_1_, bf16[2304,1152]{1,0:T(8,128)(2,1)S(1)} %bitcast.25, ...), custom_call_target="tpu_custom_call" | custom-call | tf_op jit(solution)/shard_map/pallas_call | solution.py:169
  73.2 7.3 %shard_map.163.refs_0_ = bf16[128,2304]{1,0:T(8,128)(2,1)S(1)} custom-call(s32[6]{0:T(128)S(1)} %stack.35.where_ref, bf16[128,2304]{1,0:T(8,128)(2,1)S(1)} %collective-permute-done.6.refs_0_, bf16[128,2304]{1,0:T(8,128)(2,1)S(1)} %collective-permute-done.13.refs_1_, bf16[2304,1152]{1,0:T(8,128)(2,1)S(1)} %bitcast.25, ...), custom_call_target="tpu_custom_call" | custom-call | tf_op jit(solution)/shard_map/pallas_call | solution.py:169
  81.8 4.1 %collective-permute-start.15 = (bf16[128,2304]{1,0:T(8,128)(2,1)S(1)}, bf16[128,2304]{1,0:T(8,128)(2,1)S(1)}, u32[]{:S(2)}, u32[]{:S(2)}) collective-permute-start(bf16[128,2304]{1,0:T(8,128)(2,1)S(1)} %collective-permute-done.11.refs_0_), channel_id=1, source_target_pairs={{2,0},{3,1},{4,6},{5,7},{10,8},{11,9},{12,14},{13,15},{18,16},{19,... | collective-permute-start | bytes 1769480 | tf_op jit(solution)/shard_map/ppermute | solution.py:36
  85.9 10.8 %collective-permute-done.18.refs_3_ = bf16[128,2304]{1,0:T(8,128)(2,1)S(1)} collective-permute-done((bf16[128,2304]{1,0:T(8,128)(2,1)S(1)}, bf16[128,2304]{1,0:T(8,128)(2,1)S(1)}, u32[]{:S(2)}, u32[]{:S(2)}) %collective-permute-start.18) | collective-permute-done | bytes 589856 | tf_op jit(solution)/shard_map/ppermute | solution.py:36
  97.6 3.5 %collective-permute-start.19 = (bf16[256,2304]{1,0:T(8,128)(2,1)S(1)}, bf16[256,2304]{1,0:T(8,128)(2,1)S(1)}, u32[]{:S(2)}, u32[]{:S(2)}) collective-permute-start(bf16[256,2304]{1,0:T(8,128)(2,1)S(1)} %shard_map.164), channel_id=1, source_target_pairs={{0,0},{1,1},{2,4},{3,5},{4,2},{5,3},{6,6},{7,7},{8,8},{9,9},{10,12... | collective-permute-start | bytes 3538952 | tf_op jit(solution)/shard_map/ppermute | solution.py:36
  101.2 10.0 %shard_map.168 = (bf16[128,2304]{1,0:T(8,128)(2,1)S(1)}, bf16[128,2304]{1,0:T(8,128)(2,1)S(1)}) custom-call(s32[6]{0:T(128)S(1)} %stack.35.where_ref, bf16[128,2304]{1,0:T(8,128)(2,1)S(1)} %collective-permute-done.11.refs_0_, bf16[128,2304]{1,0:T(8,128)(2,1)S(1)} %collective-permute-done.12.refs_1_, bf16[128,2304]{1,0:T(8,128)(2,1)S(1)} %collective-permute-done.9.refs_2_, ...), custom_call_target="tpu_custom_call" | custom-call | tf_op jit(solution)/shard_map/pallas_call | solution.py:169
  112.8 2.3 collective-permute-start.23
  115.1 10.6 %collective-permute-done.19.refs_1_.far_ref = bf16[256,2304]{1,0:T(8,128)(2,1)S(1)} collective-permute-done((bf16[256,2304]{1,0:T(8,128)(2,1)S(1)}, bf16[256,2304]{1,0:T(8,128)(2,1)S(1)}, u32[]{:S(2)}, u32[]{:S(2)}) %collective-permute-start.19) | collective-permute-done | bytes 1179680 | tf_op jit(solution)/shard_map/ppermute | solution.py:36
  126.5 3.5 %collective-permute-start.21 = (f32[2,128,512]{2,1,0:T(8,128)S(1)}, f32[2,128,512]{2,1,0:T(8,128)S(1)}, u32[]{:S(2)}, u32[]{:S(2)}) collective-permute-start(f32[2,128,512]{2,1,0:T(8,128)S(1)} %bitcast.34), channel_id=1, source_target_pairs={{0,17},{1,16},{2,19},{3,18},{4,21},{5,20},{6,23},{7,22},{8,25},{9,... | collective-permute-start | bytes 1572872 | tf_op jit(solution)/shard_map/ppermute | solution.py:36
  130.7 2.8 %collective-permute-start.26 = (bf16[128,2304]{1,0:T(8,128)(2,1)S(1)}, bf16[128,2304]{1,0:T(8,128)(2,1)S(1)}, u32[]{:S(2)}, u32[]{:S(2)}) collective-permute-start(bf16[128,2304]{1,0:T(8,128)(2,1)S(1)} %shard_map.169), channel_id=1, source_target_pairs={{0,4},{1,5},{2,6},{3,7},{4,0},{5,1},{6,2},{7,3},{8,12},{9,13},{10,... | collective-permute-start | bytes 1769480 | tf_op jit(solution)/shard_map/ppermute | solution.py:36
  133.5 9.2 %collective-permute-done.21.noise_both = f32[2,128,512]{2,1,0:T(8,128)S(1)} collective-permute-done((f32[2,128,512]{2,1,0:T(8,128)S(1)}, f32[2,128,512]{2,1,0:T(8,128)S(1)}, u32[]{:S(2)}, u32[]{:S(2)}) %collective-permute-start.21) | collective-permute-done | bytes 524320 | tf_op jit(solution)/shard_map/ppermute | solution.py:36
  142.7 3.0 %collective-permute-done.20.near_ref = bf16[128,2304]{1,0:T(8,128)(2,1)S(1)} collective-permute-done((bf16[128,2304]{1,0:T(8,128)(2,1)S(1)}, bf16[128,2304]{1,0:T(8,128)(2,1)S(1)}, u32[]{:S(2)}, u32[]{:S(2)}) %collective-permute-start.20) | collective-permute-done | bytes 589856 | tf_op jit(solution)/shard_map/ppermute | solution.py:36
  146.8 1.8 collective-permute-start.22
  148.6 4.4 %collective-permute-done.22.came_ref = bf16[64,2304]{1,0:T(8,128)(2,1)S(1)} collective-permute-done((bf16[64,2304]{1,0:T(8,128)(2,1)S(1)}, bf16[64,2304]{1,0:T(8,128)(2,1)S(1)}, u32[]{:S(2)}, u32[]{:S(2)}) %collective-permute-start.22) | collective-permute-done | bytes 294944 | tf_op jit(solution)/shard_map/ppermute | solution.py:36
  154.0 2.1 collective-permute-start.28
  156.1 3.9 %collective-permute-start.24 = (bf16[32,512]{1,0:T(8,128)(2,1)S(1)}, bf16[32,512]{1,0:T(8,128)(2,1)S(1)}, u32[]{:S(2)}, u32[]{:S(2)}) collective-permute-start(bf16[32,512]{1,0:T(8,128)(2,1)S(1)} %bitcast.29), channel_id=1, source_target_pairs={{0,1},{1,0},{2,3},{3,2},{4,5},{5,4},{6,7},{7,6},{8,9},{9,8},{10,11... | collective-permute-start | bytes 98312 | tf_op jit(solution)/shard_map/ppermute | solution.py:36
  160.9 4.7 %collective-permute-done.26.far_ref = bf16[128,2304]{1,0:T(8,128)(2,1)S(1)} collective-permute-done((bf16[128,2304]{1,0:T(8,128)(2,1)S(1)}, bf16[128,2304]{1,0:T(8,128)(2,1)S(1)}, u32[]{:S(2)}, u32[]{:S(2)}) %collective-permute-start.26) | collective-permute-done | bytes 589856 | tf_op jit(solution)/shard_map/ppermute | solution.py:36
  165.6 2.0 shard_map.170
  167.6 2.0 collective-permute-start.29
  169.6 1.6 collective-permute-done.28.far_ref
  171.3 1.9 collective-permute-start.30
  173.2 3.1 %collective-permute-done.27.came_ref = bf16[64,2304]{1,0:T(8,128)(2,1)S(1)} collective-permute-done((bf16[64,2304]{1,0:T(8,128)(2,1)S(1)}, bf16[64,2304]{1,0:T(8,128)(2,1)S(1)}, u32[]{:S(2)}, u32[]{:S(2)}) %collective-permute-start.27) | collective-permute-done | bytes 294944 | tf_op jit(solution)/shard_map/ppermute | solution.py:36
  177.3 3.2 %collective-permute-start.32 = (bf16[64,2304]{1,0:T(8,128)(2,1)S(1)}, bf16[64,2304]{1,0:T(8,128)(2,1)S(1)}, u32[]{:S(2)}, u32[]{:S(2)}) collective-permute-start(bf16[64,2304]{1,0:T(8,128)(2,1)S(1)} %shard_map.171.own_ref), channel_id=1, source_target_pairs={{0,4},{1,5},{2,6},{3,7},{4,0},{5,1},{6,2},{7,3},{8,12},{9,13},{10,... | collective-permute-start | bytes 884744 | tf_op jit(solution)/shard_map/ppermute | solution.py:36
  180.5 5.0 %collective-permute-done.30.last_ref = bf16[64,2304]{1,0:T(8,128)(2,1)S(1)} collective-permute-done((bf16[64,2304]{1,0:T(8,128)(2,1)S(1)}, bf16[64,2304]{1,0:T(8,128)(2,1)S(1)}, u32[]{:S(2)}, u32[]{:S(2)}) %collective-permute-start.30) | collective-permute-done | bytes 294944 | tf_op jit(solution)/shard_map/ppermute | solution.py:36
  185.5 2.7 %shard_map.172 = f32[40,256]{1,0:T(8,128)S(1)} custom-call(s32[6]{0:T(128)S(1)} %stack.35.where_ref, bf16[64,2304]{1,0:T(8,128)(2,1)S(1)} %shard_map.167.own_ref, bf16[64,2304]{1,0:T(8,128)(2,1)S(1)} %collective-permute-done.29.near_ref, bf16[64,2304]{1,0:T(8,128)(2,1)S(1)} %collective-permute-done.28.far_ref, ...), custom_call_target="tpu_custom_call" | custom-call | flops 40000000000 | tf_op jit(solution)/shard_map/pallas_call | solution.py:169
  188.2 5.2 %collective-permute-done.32.far_ref = bf16[64,2304]{1,0:T(8,128)(2,1)S(1)} collective-permute-done((bf16[64,2304]{1,0:T(8,128)(2,1)S(1)}, bf16[64,2304]{1,0:T(8,128)(2,1)S(1)}, u32[]{:S(2)}, u32[]{:S(2)}) %collective-permute-start.32) | collective-permute-done | bytes 294944 | tf_op jit(solution)/shard_map/ppermute | solution.py:36
  193.4 1.9 collective-permute-start.33
  195.6 6.2 %collective-permute-done.33.last_ref = bf16[64,2304]{1,0:T(8,128)(2,1)S(1)} collective-permute-done((bf16[64,2304]{1,0:T(8,128)(2,1)S(1)}, bf16[64,2304]{1,0:T(8,128)(2,1)S(1)}, u32[]{:S(2)}, u32[]{:S(2)}) %collective-permute-start.33) | collective-permute-done | bytes 294944 | tf_op jit(solution)/shard_map/ppermute | solution.py:36
  201.9 2.7 %shard_map.173 = f32[40,256]{1,0:T(8,128)S(1)} custom-call(s32[6]{0:T(128)S(1)} %stack.35.where_ref, bf16[64,2304]{1,0:T(8,128)(2,1)S(1)} %shard_map.171.own_ref, bf16[64,2304]{1,0:T(8,128)(2,1)S(1)} %collective-permute-done.31.near_ref, bf16[64,2304]{1,0:T(8,128)(2,1)S(1)} %collective-permute-done.32.far_ref, ...), custom_call_target="tpu_custom_call" | custom-call | tf_op jit(solution)/shard_map/pallas_call | solution.py:169
  204.7 1.6 collective-permute-start.36
  206.4 2.7 %collective-permute-start.35 = (f32[40,128]{1,0:T(8,128)S(1)}, f32[40,128]{1,0:T(8,128)S(1)}, u32[]{:S(2)}, u32[]{:S(2)}) collective-permute-start(f32[40,128]{1,0:T(8,128)S(1)} %pad_maximum_fusion.2), channel_id=1, source_target_pairs={{0,4},{1,5},{2,6},{3,7},{4,0},{5,1},{6,2},{7,3},{8,12},{9,13},{10,... | collective-permute-start | bytes 61448 | tf_op jit(solution)/shard_map/ppermute | solution.py:36
  210.4 1.7 collective-permute-done.34.refs_1_
  212.6 4.8 %collective-permute-start.37 = (f32[32,128]{1,0:T(8,128)S(1)}, f32[32,128]{1,0:T(8,128)S(1)}, u32[]{:S(2)}, u32[]{:S(2)}) collective-permute-start(f32[32,128]{1,0:T(8,128)S(1)} %shard_map.174), channel_id=1, source_target_pairs={{0,0},{1,2},{2,4},{3,6},{4,16},{5,18},{6,20},{7,22},{8,8},{9,10},{... | collective-permute-start | bytes 49160 | tf_op jit(solution)/shard_map/ppermute | solution.py:36
  217.4 3.4 %collective-permute-start.38 = (f32[32,128]{1,0:T(8,128)S(1)}, f32[32,128]{1,0:T(8,128)S(1)}, u32[]{:S(2)}, u32[]{:S(2)}) collective-permute-start(f32[32,128]{1,0:T(8,128)S(1)} %shard_map.174), channel_id=1, source_target_pairs={{0,1},{1,3},{2,5},{3,7},{4,17},{5,19},{6,21},{7,23},{8,9},{9,11},{... | collective-permute-start | bytes 49160 | tf_op jit(solution)/shard_map/ppermute | solution.py:36
  222.2 5.5 %collective-permute-done.39.halo_ref = f32[32,128]{1,0:T(8,128)S(1)} collective-permute-done((f32[32,128]{1,0:T(8,128)S(1)}, f32[32,128]{1,0:T(8,128)S(1)}, u32[]{:S(2)}, u32[]{:S(2)}) %collective-permute-start.39) | collective-permute-done | bytes 16416 | tf_op jit(solution)/shard_map/ppermute | solution.py:36
  227.7 1.7 shard_map.175
  (97 shorter events, 24.2 us)
Async XLA Ops:
  0.6 20.0 %collective-permute-start = (bf16[2304,1152]{1,0:T(8,128)(2,1)}, bf16[2304,1152]{1,0:T(8,128)(2,1)}, u32[]{:S(2)}, u32[]{:S(2)}) collective-permute-start(bf16[2304,1152]{1,0:T(8,128)(2,1)} %refs_4_.9), channel_id=1, source_target_pairs={{0,1},{1,0},{2,3},{3,2},{4,5},{5,4},{6,7},{7,6},{8,9},{9,8},{10,11... | collective-permute-start | bytes 15925256 | tf_op jit(solution)/shard_map/ppermute | solution.py:36
  1.4 19.3 %collective-permute-start.1 = (bf16[1152,2304]{1,0:T(8,128)(2,1)}, bf16[1152,2304]{1,0:T(8,128)(2,1)}, u32[]{:S(2)}, u32[]{:S(2)}) collective-permute-start(bf16[1152,2304]{1,0:T(8,128)(2,1)} %refs_6_.1), channel_id=1, source_target_pairs={{0,1},{1,0},{2,3},{3,2},{4,5},{5,4},{6,7},{7,6},{8,9},{9,8},{10,11... | collective-permute-start | bytes 15925256 | tf_op jit(solution)/shard_map/ppermute | solution.py:36
  4.6 16.1 %collective-permute-start.3 = (bf16[128,2304]{1,0:T(8,128)(2,1)S(1)}, bf16[128,2304]{1,0:T(8,128)(2,1)S(1)}, u32[]{:S(2)}, u32[]{:S(2)}) collective-permute-start(bf16[128,2304]{1,0:T(8,128)(2,1)S(1)} %shard_map.158.refs_0_), channel_id=1, source_target_pairs={{0,2},{1,3},{2,0},{3,1},{4,6},{5,7},{6,4},{7,5},{8,10},{9,11},{10,... | collective-permute-start | bytes 1769480 | tf_op jit(solution)/shard_map/ppermute | solution.py:36
  4.8 19.1 %collective-permute-start.6 = (bf16[128,2304]{1,0:T(8,128)(2,1)S(1)}, bf16[128,2304]{1,0:T(8,128)(2,1)S(1)}, u32[]{:S(2)}, u32[]{:S(2)}) collective-permute-start(bf16[128,2304]{1,0:T(8,128)(2,1)S(1)} %shard_map.158.refs_0_), channel_id=1, source_target_pairs={{0,0},{1,1},{2,4},{3,5},{4,2},{5,3},{6,6},{7,7},{8,8},{9,9},{10,12... | collective-permute-start | bytes 1769480 | tf_op jit(solution)/shard_map/ppermute | solution.py:36
  9.9 7.5 %collective-permute-start.2 = (f32[1,1664]{1,0:T(1,128)S(1)}, f32[1,1664]{1,0:T(1,128)S(1)}, u32[]{:S(2)}, u32[]{:S(2)}) collective-permute-start(f32[1,1664]{1,0:T(1,128)S(1)} %broadcast_in_dim.12.refs_6_.refs_8_.bias_a), channel_id=1, source_target_pairs={{0,1},{1,0},{2,3},{3,2},{4,5},{5,4},{6,7},{7,6},{8,9},{9,8},{10,11... | collective-permute-start | bytes 19976 | tf_op jit(solution)/shard_map/ppermute | solution.py:36
  17.4 3.3 %collective-permute-start.4 = (f32[2,2,2304]{2,1,0:T(2,128)}, f32[2,2,2304]{2,1,0:T(2,128)S(1)}, u32[]{:S(2)}, u32[]{:S(2)}) collective-permute-start(f32[2,2,2304]{2,1,0:T(2,128)} %ada_ref.7), channel_id=1, source_target_pairs={{0,16},{1,17},{2,18},{3,19},{4,20},{5,21},{6,22},{7,23},{8,24},{9,... | collective-permute-start | bytes 110600 | tf_op jit(solution)/shard_map/ppermute | solution.py:36
  20.7 17.8 %collective-permute-start.5 = (bf16[128,2304]{1,0:T(8,128)(2,1)S(1)}, bf16[128,2304]{1,0:T(8,128)(2,1)}, u32[]{:S(2)}, u32[]{:S(2)}) collective-permute-start(bf16[128,2304]{1,0:T(8,128)(2,1)S(1)} %collective-permute-done.3.refs_1_), channel_id=1, source_target_pairs={{0,0},{1,1},{2,4},{3,5},{4,2},{5,3},{6,6},{7,7},{8,8},{9,9},{10,12... | collective-permute-start | bytes 1769480 | tf_op jit(solution)/shard_map/ppermute | solution.py:36
  23.9 20.1 %collective-permute-start.7 = (bf16[128,2304]{1,0:T(8,128)(2,1)S(1)}, bf16[128,2304]{1,0:T(8,128)(2,1)}, u32[]{:S(2)}, u32[]{:S(2)}) collective-permute-start(bf16[128,2304]{1,0:T(8,128)(2,1)S(1)} %collective-permute-done.6.refs_0_), channel_id=1, source_target_pairs={{2,0},{3,1},{4,6},{5,7},{10,8},{11,9},{12,14},{13,15},{18,16},{19,... | collective-permute-start | bytes 1769480 | tf_op jit(solution)/shard_map/ppermute | solution.py:36
  26.0 20.6 %slice-start = ((s8[5308416]{0:T(1024)(128)(4,1)}), s8[1114112]{0:T(1024)(128)(4,1)S(1)}, s32[]{:S(2)}) async-start(s8[5308416]{0:T(1024)(128)(4,1)} %bitcast.24), calls=%async_computation | async-start | bytes 2228224
  26.0 30.8 %collective-permute-start.8 = (bf16[128,2304]{1,0:T(8,128)(2,1)S(1)}, bf16[128,2304]{1,0:T(8,128)(2,1)S(1)}, u32[]{:S(2)}, u32[]{:S(2)}) collective-permute-start(bf16[128,2304]{1,0:T(8,128)(2,1)S(1)} %shard_map.159.refs_0_), channel_id=1, source_target_pairs={{0,2},{1,3},{2,0},{3,1},{4,6},{5,7},{6,4},{7,5},{8,10},{9,11},{10,... | collective-permute-start | bytes 1769480 | tf_op jit(solution)/shard_map/ppermute | solution.py:36
  38.5 34.7 %collective-permute-start.13 = (bf16[128,2304]{1,0:T(8,128)(2,1)}, bf16[128,2304]{1,0:T(8,128)(2,1)S(1)}, u32[]{:S(2)}, u32[]{:S(2)}) collective-permute-start(bf16[128,2304]{1,0:T(8,128)(2,1)} %collective-permute-done.5.refs_0_), channel_id=1, source_target_pairs={{2,0},{3,1},{4,6},{5,7},{10,8},{11,9},{12,14},{13,15},{18,16},{19,... | collective-permute-start | bytes 1769480 | tf_op jit(solution)/shard_map/ppermute | solution.py:36
  41.3 16.8 %collective-permute-start.9 = (bf16[128,2304]{1,0:T(8,128)(2,1)S(1)}, bf16[128,2304]{1,0:T(8,128)(2,1)S(1)}, u32[]{:S(2)}, u32[]{:S(2)}) collective-permute-start(bf16[128,2304]{1,0:T(8,128)(2,1)S(1)} %shard_map.159.refs_0_), channel_id=1, source_target_pairs={{0,0},{1,1},{2,4},{3,5},{4,2},{5,3},{6,6},{7,7},{8,8},{9,9},{10,12... | collective-permute-start | bytes 1769480 | tf_op jit(solution)/shard_map/ppermute | solution.py:36
  43.7 17.7 %collective-permute-start.10 = (f32[2,128,512]{2,1,0:T(8,128)S(1)}, f32[2,128,512]{2,1,0:T(8,128)S(1)}, u32[]{:S(2)}, u32[]{:S(2)}) collective-permute-start(f32[2,128,512]{2,1,0:T(8,128)S(1)} %bitcast.36), channel_id=1, source_target_pairs={{0,16},{1,17},{2,18},{3,19},{4,20},{5,21},{6,22},{7,23},{8,24},{9,... | collective-permute-start | bytes 1572872 | tf_op jit(solution)/shard_map/ppermute | solution.py:36
  44.0 29.2 %collective-permute-start.14 = (f32[2,128,512]{2,1,0:T(8,128)S(1)}, f32[2,128,512]{2,1,0:T(8,128)S(1)}, u32[]{:S(2)}, u32[]{:S(2)}) collective-permute-start(f32[2,128,512]{2,1,0:T(8,128)S(1)} %bitcast.35), channel_id=1, source_target_pairs={{0,1},{1,0},{2,3},{3,2},{4,5},{5,4},{6,7},{7,6},{8,9},{9,8},{10,11... | collective-permute-start | bytes 1572872 | tf_op jit(solution)/shard_map/ppermute | solution.py:36
  56.8 29.0 %collective-permute-start.17 = (bf16[128,2304]{1,0:T(8,128)(2,1)S(1)}, bf16[128,2304]{1,0:T(8,128)(2,1)S(1)}, u32[]{:S(2)}, u32[]{:S(2)}) collective-permute-start(bf16[128,2304]{1,0:T(8,128)(2,1)S(1)} %shard_map.161.refs_2_), channel_id=1, source_target_pairs={{0,2},{1,3},{6,4},{7,5},{8,10},{9,11},{14,12},{15,13},{16,18},{17,... | collective-permute-start | bytes 1769480 | tf_op jit(solution)/shard_map/ppermute | solution.py:36
  58.2 23.6 %collective-permute-start.11 = (bf16[128,2304]{1,0:T(8,128)(2,1)S(1)}, bf16[128,2304]{1,0:T(8,128)(2,1)S(1)}, u32[]{:S(2)}, u32[]{:S(2)}) collective-permute-start(bf16[128,2304]{1,0:T(8,128)(2,1)S(1)} %collective-permute-done.8.refs_1_), channel_id=1, source_target_pairs={{0,0},{1,1},{2,4},{3,5},{4,2},{5,3},{6,6},{7,7},{8,8},{9,9},{10,12... | collective-permute-start | bytes 1769480 | tf_op jit(solution)/shard_map/ppermute | solution.py:36
  61.4 20.4 %collective-permute-start.12 = (bf16[128,2304]{1,0:T(8,128)(2,1)S(1)}, bf16[128,2304]{1,0:T(8,128)(2,1)S(1)}, u32[]{:S(2)}, u32[]{:S(2)}) collective-permute-start(bf16[128,2304]{1,0:T(8,128)(2,1)S(1)} %collective-permute-done.9.refs_2_), channel_id=1, source_target_pairs={{2,0},{3,1},{4,6},{5,7},{10,8},{11,9},{12,14},{13,15},{18,16},{19,... | collective-permute-start | bytes 1769480 | tf_op jit(solution)/shard_map/ppermute | solution.py:36
  80.5 16.2 %collective-permute-start.18 = (bf16[128,2304]{1,0:T(8,128)(2,1)S(1)}, bf16[128,2304]{1,0:T(8,128)(2,1)S(1)}, u32[]{:S(2)}, u32[]{:S(2)}) collective-permute-start(bf16[128,2304]{1,0:T(8,128)(2,1)S(1)} %shard_map.163.refs_0_), channel_id=1, source_target_pairs={{0,2},{1,3},{6,4},{7,5},{8,10},{9,11},{14,12},{15,13},{16,18},{17,... | collective-permute-start | bytes 1769480 | tf_op jit(solution)/shard_map/ppermute | solution.py:36
  81.8 19.4 %collective-permute-start.15 = (bf16[128,2304]{1,0:T(8,128)(2,1)S(1)}, bf16[128,2304]{1,0:T(8,128)(2,1)S(1)}, u32[]{:S(2)}, u32[]{:S(2)}) collective-permute-start(bf16[128,2304]{1,0:T(8,128)(2,1)S(1)} %collective-permute-done.11.refs_0_), channel_id=1, source_target_pairs={{2,0},{3,1},{4,6},{5,7},{10,8},{11,9},{12,14},{13,15},{18,16},{19,... | collective-permute-start | bytes 1769480 | tf_op jit(solution)/shard_map/ppermute | solution.py:36
  97.6 28.1 %collective-permute-start.19 = (bf16[256,2304]{1,0:T(8,128)(2,1)S(1)}, bf16[256,2304]{1,0:T(8,128)(2,1)S(1)}, u32[]{:S(2)}, u32[]{:S(2)}) collective-permute-start(bf16[256,2304]{1,0:T(8,128)(2,1)S(1)} %shard_map.164), channel_id=1, source_target_pairs={{0,0},{1,1},{2,4},{3,5},{4,2},{5,3},{6,6},{7,7},{8,8},{9,9},{10,12... | collective-permute-start | bytes 3538952 | tf_op jit(solution)/shard_map/ppermute | solution.py:36
  101.2 24.5 %collective-permute-start.16 = (bf16[128,2304]{1,0:T(8,128)(2,1)S(1)}, bf16[128,2304]{1,0:T(8,128)(2,1)S(1)}, u32[]{:S(2)}, u32[]{:S(2)}) collective-permute-start(bf16[128,2304]{1,0:T(8,128)(2,1)S(1)} %get-tuple-element.71), channel_id=1, source_target_pairs={{0,2},{1,3},{2,0},{3,1},{4,6},{5,7},{6,4},{7,5},{8,10},{9,11},{10,... | collective-permute-start | bytes 1769480 | tf_op jit(solution)/shard_map/ppermute | solution.py:36
  111.3 22.2 %copy-start.13 = (f32[2304]{0:T(1024)S(1)}, f32[2304]{0:T(1024)}, u32[]{:S(2)}) copy-start(f32[2304]{0:T(1024)} %param.21) | copy-start | bytes 27652
  111.3 34.5 %copy-start.9 = (f32[2,2304]{1,0:T(2,128)S(1)}, f32[2,2304]{1,0:T(2,128)}, u32[]{:S(2)}) copy-start(f32[2,2304]{1,0:T(2,128)} %gate_ref.3) | copy-start | bytes 55300
  111.3 18.7 %collective-permute-start.25 = (bf16[128,2304]{1,0:T(8,128)(2,1)S(1)}, bf16[128,2304]{1,0:T(8,128)(2,1)S(1)}, u32[]{:S(2)}, u32[]{:S(2)}) collective-permute-start(bf16[128,2304]{1,0:T(8,128)(2,1)S(1)} %get-tuple-element.82), channel_id=1, source_target_pairs={{0,2},{1,3},{2,0},{3,1},{4,6},{5,7},{6,4},{7,5},{8,10},{9,11},{10,... | collective-permute-start | bytes 1769480 | tf_op jit(solution)/shard_map/ppermute | solution.py:36
  112.8 48.1 %collective-permute-start.23 = (bf16[2304,512]{1,0:T(8,128)(2,1)S(1)}, bf16[2304,512]{1,0:T(8,128)(2,1)S(1)}, u32[]{:S(2)}, u32[]{:S(2)}) collective-permute-start(bf16[2304,512]{1,0:T(8,128)(2,1)S(1)} %copy-done.4), channel_id=1, source_target_pairs={{0,1},{1,0},{2,3},{3,2},{4,5},{5,4},{6,7},{7,6},{8,9},{9,8},{10,11... | collective-permute-start | bytes 7077896 | tf_op jit(solution)/shard_map/ppermute | solution.py:36
  126.4 19.4 %collective-permute-start.20 = (bf16[128,2304]{1,0:T(8,128)(2,1)S(1)}, bf16[128,2304]{1,0:T(8,128)(2,1)S(1)}, u32[]{:S(2)}, u32[]{:S(2)}) collective-permute-start(bf16[128,2304]{1,0:T(8,128)(2,1)S(1)} %shard_map.165), channel_id=1, source_target_pairs={{0,2},{1,3},{2,0},{3,1},{4,6},{5,7},{6,4},{7,5},{8,10},{9,11},{10,... | collective-permute-start | bytes 1769480 | tf_op jit(solution)/shard_map/ppermute | solution.py:36
  126.5 16.2 %collective-permute-start.21 = (f32[2,128,512]{2,1,0:T(8,128)S(1)}, f32[2,128,512]{2,1,0:T(8,128)S(1)}, u32[]{:S(2)}, u32[]{:S(2)}) collective-permute-start(f32[2,128,512]{2,1,0:T(8,128)S(1)} %bitcast.34), channel_id=1, source_target_pairs={{0,17},{1,16},{2,19},{3,18},{4,21},{5,20},{6,23},{7,22},{8,25},{9,... | collective-permute-start | bytes 1572872 | tf_op jit(solution)/shard_map/ppermute | solution.py:36
  130.0 23.0 %copy-start.5 = (f32[2,2,2304]{2,1,0:T(2,128)S(1)}, f32[2,2,2304]{2,1,0:T(2,128)}, u32[]{:S(2)}) copy-start(f32[2,2,2304]{2,1,0:T(2,128)} %ada_ref.7) | copy-start | bytes 110596
  130.7 25.4 %copy-start.10 = (bf16[512,32]{0,1:T(8,128)(2,1)S(1)}, bf16[512,32]{0,1:T(8,128)(2,1)}, u32[]{:S(2)}) copy-start(bf16[512,32]{0,1:T(8,128)(2,1)} %param.26) | copy-start | bytes 98308
  130.7 34.9 %collective-permute-start.26 = (bf16[128,2304]{1,0:T(8,128)(2,1)S(1)}, bf16[128,2304]{1,0:T(8,128)(2,1)S(1)}, u32[]{:S(2)}, u32[]{:S(2)}) collective-permute-start(bf16[128,2304]{1,0:T(8,128)(2,1)S(1)} %shard_map.169), channel_id=1, source_target_pairs={{0,4},{1,5},{2,6},{3,7},{4,0},{5,1},{6,2},{7,3},{8,12},{9,13},{10,... | collective-permute-start | bytes 1769480 | tf_op jit(solution)/shard_map/ppermute | solution.py:36
  146.8 6.2 %collective-permute-start.22 = (bf16[64,2304]{1,0:T(8,128)(2,1)S(1)}, bf16[64,2304]{1,0:T(8,128)(2,1)S(1)}, u32[]{:S(2)}, u32[]{:S(2)}) collective-permute-start(bf16[64,2304]{1,0:T(8,128)(2,1)S(1)} %get-tuple-element.78), channel_id=1, source_target_pairs={{0,16},{1,17},{2,18},{3,19},{4,20},{5,21},{6,22},{7,23},{8,24},{9,... | collective-permute-start | bytes 884744 | tf_op jit(solution)/shard_map/ppermute | solution.py:36
  154.0 17.2 %collective-permute-start.28 = (bf16[64,2304]{1,0:T(8,128)(2,1)S(1)}, bf16[64,2304]{1,0:T(8,128)(2,1)S(1)}, u32[]{:S(2)}, u32[]{:S(2)}) collective-permute-start(bf16[64,2304]{1,0:T(8,128)(2,1)S(1)} %shard_map.167.own_ref), channel_id=1, source_target_pairs={{0,4},{1,5},{2,6},{3,7},{4,0},{5,1},{6,2},{7,3},{8,12},{9,13},{10,... | collective-permute-start | bytes 884744 | tf_op jit(solution)/shard_map/ppermute | solution.py:36
  156.1 4.8 %collective-permute-start.24 = (bf16[32,512]{1,0:T(8,128)(2,1)S(1)}, bf16[32,512]{1,0:T(8,128)(2,1)S(1)}, u32[]{:S(2)}, u32[]{:S(2)}) collective-permute-start(bf16[32,512]{1,0:T(8,128)(2,1)S(1)} %bitcast.29), channel_id=1, source_target_pairs={{0,1},{1,0},{2,3},{3,2},{4,5},{5,4},{6,7},{7,6},{8,9},{9,8},{10,11... | collective-permute-start | bytes 98312 | tf_op jit(solution)/shard_map/ppermute | solution.py:36
  167.6 8.7 %collective-permute-start.27 = (bf16[64,2304]{1,0:T(8,128)(2,1)S(1)}, bf16[64,2304]{1,0:T(8,128)(2,1)S(1)}, u32[]{:S(2)}, u32[]{:S(2)}) collective-permute-start(bf16[64,2304]{1,0:T(8,128)(2,1)S(1)} %get-tuple-element.91), channel_id=1, source_target_pairs={{0,16},{1,17},{2,18},{3,19},{4,20},{5,21},{6,22},{7,23},{8,24},{9,... | collective-permute-start | bytes 884744 | tf_op jit(solution)/shard_map/ppermute | solution.py:36
  167.6 12.9 %collective-permute-start.29 = (bf16[64,2304]{1,0:T(8,128)(2,1)S(1)}, bf16[64,2304]{1,0:T(8,128)(2,1)S(1)}, u32[]{:S(2)}, u32[]{:S(2)}) collective-permute-start(bf16[64,2304]{1,0:T(8,128)(2,1)S(1)} %shard_map.167.own_ref), channel_id=1, source_target_pairs={{0,2},{1,3},{2,0},{3,1},{4,6},{5,7},{6,4},{7,5},{8,10},{9,11},{10,... | collective-permute-start | bytes 884744 | tf_op jit(solution)/shard_map/ppermute | solution.py:36
  171.3 14.3 %collective-permute-start.30 = (bf16[64,2304]{1,0:T(8,128)(2,1)S(1)}, bf16[64,2304]{1,0:T(8,128)(2,1)S(1)}, u32[]{:S(2)}, u32[]{:S(2)}) collective-permute-start(bf16[64,2304]{1,0:T(8,128)(2,1)S(1)} %collective-permute-done.28.far_ref), channel_id=1, source_target_pairs={{0,2},{1,3},{2,0},{3,1},{4,6},{5,7},{6,4},{7,5},{8,10},{9,11},{10,... | collective-permute-start | bytes 884744 | tf_op jit(solution)/shard_map/ppermute | solution.py:36
  177.3 16.1 %collective-permute-start.32 = (bf16[64,2304]{1,0:T(8,128)(2,1)S(1)}, bf16[64,2304]{1,0:T(8,128)(2,1)S(1)}, u32[]{:S(2)}, u32[]{:S(2)}) collective-permute-start(bf16[64,2304]{1,0:T(8,128)(2,1)S(1)} %shard_map.171.own_ref), channel_id=1, source_target_pairs={{0,4},{1,5},{2,6},{3,7},{4,0},{5,1},{6,2},{7,3},{8,12},{9,13},{10,... | collective-permute-start | bytes 884744 | tf_op jit(solution)/shard_map/ppermute | solution.py:36
  180.5 15.2 %collective-permute-start.31 = (bf16[64,2304]{1,0:T(8,128)(2,1)S(1)}, bf16[64,2304]{1,0:T(8,128)(2,1)S(1)}, u32[]{:S(2)}, u32[]{:S(2)}) collective-permute-start(bf16[64,2304]{1,0:T(8,128)(2,1)S(1)} %shard_map.171.own_ref), channel_id=1, source_target_pairs={{0,2},{1,3},{2,0},{3,1},{4,6},{5,7},{6,4},{7,5},{8,10},{9,11},{10,... | collective-permute-start | bytes 884744 | tf_op jit(solution)/shard_map/ppermute | solution.py:36
  193.4 8.5 %collective-permute-start.33 = (bf16[64,2304]{1,0:T(8,128)(2,1)S(1)}, bf16[64,2304]{1,0:T(8,128)(2,1)S(1)}, u32[]{:S(2)}, u32[]{:S(2)}) collective-permute-start(bf16[64,2304]{1,0:T(8,128)(2,1)S(1)} %collective-permute-done.32.far_ref), channel_id=1, source_target_pairs={{0,2},{1,3},{2,0},{3,1},{4,6},{5,7},{6,4},{7,5},{8,10},{9,11},{10,... | collective-permute-start | bytes 884744 | tf_op jit(solution)/shard_map/ppermute | solution.py:36
  195.4 26.8 %copy-start.14 = (f32[32]{0:T(128)S(1)}, f32[32]{0:T(128)}, u32[]{:S(2)}) copy-start(f32[32]{0:T(128)} %param.28) | copy-start | bytes 388
  195.4 32.3 %copy-start.6 = (f32[32,32,3,3]{1,0,3,2:T(8,128)S(1)}, f32[32,32,3,3]{1,0,3,2:T(8,128)}, u32[]{:S(2)}) copy-start(f32[32,32,3,3]{1,0,3,2:T(8,128)} %param.27) | copy-start | bytes 110596
  195.4 32.3 %copy-start.11 = (f32[1,32,128]{2,1,0:T(8,128)S(1)}, f32[1,32,128]{2,1,0:T(8,128)}, u32[]{:S(2)}) copy-start(f32[1,32,128]{2,1,0:T(8,128)} %param.29) | copy-start | bytes 49156
  204.7 4.8 %collective-permute-start.36 = (f32[40,128]{1,0:T(8,128)S(1)}, f32[40,128]{1,0:T(8,128)S(1)}, u32[]{:S(2)}, u32[]{:S(2)}) collective-permute-start(f32[40,128]{1,0:T(8,128)S(1)} %pad_maximum_fusion.3), channel_id=1, source_target_pairs={{0,6},{1,7},{2,4},{3,5},{4,2},{5,3},{6,0},{7,1},{8,14},{9,15},{10,... | collective-permute-start | bytes 61448 | tf_op jit(solution)/shard_map/ppermute | solution.py:36
  206.4 4.0 %collective-permute-start.35 = (f32[40,128]{1,0:T(8,128)S(1)}, f32[40,128]{1,0:T(8,128)S(1)}, u32[]{:S(2)}, u32[]{:S(2)}) collective-permute-start(f32[40,128]{1,0:T(8,128)S(1)} %pad_maximum_fusion.2), channel_id=1, source_target_pairs={{0,4},{1,5},{2,6},{3,7},{4,0},{5,1},{6,2},{7,3},{8,12},{9,13},{10,... | collective-permute-start | bytes 61448 | tf_op jit(solution)/shard_map/ppermute | solution.py:36
  209.1 2.9 %collective-permute-start.34 = (f32[40,128]{1,0:T(8,128)S(1)}, f32[40,128]{1,0:T(8,128)S(1)}, u32[]{:S(2)}, u32[]{:S(2)}) collective-permute-start(f32[40,128]{1,0:T(8,128)S(1)} %pad_maximum_fusion.1), channel_id=1, source_target_pairs={{0,2},{1,3},{2,0},{3,1},{4,6},{5,7},{6,4},{7,5},{8,10},{9,11},{10,... | collective-permute-start | bytes 61448 | tf_op jit(solution)/shard_map/ppermute | solution.py:36
  212.6 9.6 %collective-permute-start.37 = (f32[32,128]{1,0:T(8,128)S(1)}, f32[32,128]{1,0:T(8,128)S(1)}, u32[]{:S(2)}, u32[]{:S(2)}) collective-permute-start(f32[32,128]{1,0:T(8,128)S(1)} %shard_map.174), channel_id=1, source_target_pairs={{0,0},{1,2},{2,4},{3,6},{4,16},{5,18},{6,20},{7,22},{8,8},{9,10},{... | collective-permute-start | bytes 49160 | tf_op jit(solution)/shard_map/ppermute | solution.py:36
  217.4 4.8 %collective-permute-start.38 = (f32[32,128]{1,0:T(8,128)S(1)}, f32[32,128]{1,0:T(8,128)S(1)}, u32[]{:S(2)}, u32[]{:S(2)}) collective-permute-start(f32[32,128]{1,0:T(8,128)S(1)} %shard_map.174), channel_id=1, source_target_pairs={{0,1},{1,3},{2,5},{3,7},{4,17},{5,19},{6,21},{7,23},{8,9},{9,11},{... | collective-permute-start | bytes 49160 | tf_op jit(solution)/shard_map/ppermute | solution.py:36
  220.8 6.8 %collective-permute-start.39 = (f32[32,128]{1,0:T(8,128)S(1)}, f32[32,128]{1,0:T(8,128)S(1)}, u32[]{:S(2)}, u32[]{:S(2)}) collective-permute-start(f32[32,128]{1,0:T(8,128)S(1)} %shard_map.174), channel_id=1, source_target_pairs={{1,1},{2,3},{3,5},{5,17},{6,19},{7,21},{9,9},{10,11},{11,13},{13,2... | collective-permute-start | bytes 49160 | tf_op jit(solution)/shard_map/ppermute | solution.py:36
  (9 other events, 91.9 us)

commit v7 on v5

--- a/solution.py
+++ b/solution.py
@@ -292,7 +292,7 @@
     return call(functools.partial(add_kernel, always), where, (a, b), [shape_of(a.shape)], flops=flops)[0]
 
 
-def out_kernel(begin, always, where_ref, own_ref, near_ref, far_ref, tokens_ref, gate_ref, bias_ref, *refs):
+def out_kernel(begin, always, where_ref, own_ref, near_ref, far_ref, tokens_ref, gate_ref, bias_ref, ada_ref, *refs):
     out_ref, kept_ref, sent_ref = refs[-3:]
     far = far_ref[...].astype(jnp.float32)
     if not always:
@@ -310,31 +310,31 @@
     half = rows // 2
     lower = where_ref[UPPER] == 0
     kept_ref[...] = jnp.where(lower, value[:half], value[half:])
-    sent_ref[...] = jnp.where(lower, value[half:], value[:half])
-
-
-def block_rows(where, begin, always, own, near, far, tokens, gate, bias, earlier=()):
+    sent = jnp.where(lower, value[half:], value[:half])
+    sent_ref[...] = modulated(sent, ada_ref, where_ref[IMAGE]).astype(jnp.bfloat16)
+
+
+def block_rows(where, begin, always, own, near, far, tokens, gate, bias, ada, earlier=()):
     rows, width = own.shape
     full = rows + begin if earlier else rows
     return call(
         functools.partial(out_kernel, begin, always),
         where,
-        (own, near, far, tokens, gate, bias, *earlier),
+        (own, near, far, tokens, gate, bias, ada, *earlier),
         [shape_of((full, width)), shape_of((rows // 2, width)), shape_of((rows // 2, width))],
     )
 
 
-def mix_kernel(where_ref, kept_ref, came_ref, ada_ref, twin_ref, out_ref):
-    image = where_ref[IMAGE]
-    kept, came = modulated(kept_ref[...], ada_ref, image), modulated(came_ref[...], twin_ref, image)
+def mix_kernel(where_ref, kept_ref, came_ref, ada_ref, out_ref):
+    kept, came = modulated(kept_ref[...], ada_ref, where_ref[IMAGE]), came_ref[...].astype(jnp.float32)
     lower = where_ref[UPPER] == 0
     share = jnp.where(lower, 1.0 + GUIDE, -GUIDE)
     other = jnp.where(lower, -GUIDE, 1.0 + GUIDE)
     out_ref[...] = (share * kept + other * came).astype(jnp.bfloat16)
 
 
-def mix_twins(where, kept, came, ada, twin):
-    return call(mix_kernel, where, (kept, came, ada, twin), [shape_of(kept.shape)])[0]
+def mix_twins(where, kept, came, ada):
+    return call(mix_kernel, where, (kept, came, ada), [shape_of(kept.shape)])[0]
 
 
 def head_kernel(
@@ -534,56 +534,54 @@
         noise_for(1 - core, upper),
         noise_for(1 - core, 1 - upper),
     )
-    noise_twin, noise_core, noise_both, _ = barrier((noise_twin, noise_core, noise_both, own_b))
-    noise_twin = swap_twins(noise_twin)
     up_other, down_other, bias_other, near_a, own_b = barrier((up_other, down_other, bias_other, near_a, own_b))
     panels = (up_weight, up_other, down_weight, down_other, biases, bias_other)
     far_mid_a = middle(near_a)
     near_b = near(after(own_b, near_a))
     mid_a = after(mid_a, near_a)
     far_end_a = outward(mid_a)
+    noise_twin = swap_twins(after(noise_twin, near_a))
     sum_own_a, sum_near_a = ffn(where, [[own_a], [after(near_a, mid_a)]], panels, fetch=True)
     far_mid_a = after(far_mid_a, sum_near_a)
     last_end_a = outward(far_mid_a)
     mid_b = middle(after(own_b, far_mid_a))
     noise_core = swap_cores(after(noise_core, far_mid_a))
-    head_twin = swap_twins(after(ada_head, far_mid_a))
     (sum_far_a,) = ffn(where, [[far_mid_a, far_end_a]], panels)
     came_far_a = inward(sum_far_a)
     near_b, mid_b = barrier((near_b, mid_b, sum_far_a))[:2]
     far_mid_b, far_end_b = middle(near_b), outward(mid_b)
-    (sum_last_a,) = ffn(where, [[mid_a, after(last_end_a, near_b, mid_b, noise_twin, head_twin)]], panels)
+    sum_own_b, sum_near_b = ffn(where, [[after(own_b, sum_far_a)], [after(near_b, mid_b)]], panels)
+    (sum_last_a,) = ffn(where, [[mid_a, after(last_end_a, sum_near_b, noise_twin, far_mid_b)]], panels)
     came_last_a = inward(sum_last_a)
+    last_end_b = outward(after(far_mid_b, sum_near_b))
     noise_both = swap_both(after(noise_both, noise_twin))
-    sum_own_b, sum_near_b = ffn(where, [[after(own_b, sum_last_a, noise_core)], [near_b]], panels)
-    both_last_a = add(where, after(sum_last_a, sum_near_b), came_far_a)
+    both_last_a = add(where, sum_last_a, came_far_a)
     went_last_a = middle(both_last_a)
-    far_mid_b, far_end_b = barrier((far_mid_b, far_end_b, both_last_a))[:2]
-    last_end_b = outward(far_mid_b)
-    (sum_far_b,) = ffn(where, [[far_mid_b, far_end_b]], panels)
-    both_far_a = add(where, after(sum_far_a, sum_far_b), came_last_a)
+    sum_far_b, sum_last_b = ffn(
+        where, [[after(far_mid_b, sum_last_a, both_last_a), far_end_b], [mid_b, last_end_b]], panels
+    )
+    both_far_a = add(where, after(sum_far_a, went_last_a, sum_far_b), came_last_a)
     went_far_a = middle(both_far_a)
-    (sum_last_b,) = ffn(where, [[after(mid_b, both_far_a, went_last_a), last_end_b]], panels)
     came_last_b = near(sum_last_b)
     head_other = swap_cores(after(head_weight, sum_last_b))
     code_other = swap_cores(after(codes, sum_last_b))
     came_near_b = near(after(sum_near_b, last_end_b))
-    both_near_a = add(where, sum_near_a, after(went_far_a, went_last_a, came_near_b), flops=AHEAD)
+    both_near_a = add(where, sum_near_a, after(went_far_a, came_near_b), flops=AHEAD)
     came_near_a = near(both_near_a)
-    both_far_b = add(where, after(sum_far_b, both_near_a), came_last_b, True)
+    both_far_b = add(where, after(sum_far_b, both_near_a), came_last_b, always=True)
     went_far_b = across(both_far_b)
     out_a, kept_a, sent_a = block_rows(
-        where, 0, False, sum_own_a, after(came_near_a, noise_both), went_last_a, tokens, gate, bias_out
+        where, 0, False, sum_own_a, after(came_near_a, noise_both, noise_core), went_last_a, tokens, gate, bias_out, ada_head
     )
     came_a = swap_twins(sent_a)
-    mixed_a = mix_twins(where, kept_a, came_a, ada_head, head_twin)
+    mixed_a = mix_twins(where, kept_a, came_a, ada_head)
     mix_near_a, mix_far_a = near(mixed_a), across(mixed_a)
     block_out, kept_b, sent_b = block_rows(
-        where, step, True, sum_own_b, after(came_near_b, mixed_a, head_other, code_other), went_far_b, tokens, gate, bias_out, (out_a,)
+        where, step, True, sum_own_b, after(came_near_b, mixed_a, head_other, code_other), went_far_b, tokens, gate, bias_out, ada_head, (out_a,)
     )
     came_b = after(swap_twins(sent_b), mix_far_a)
     mix_last_a = near(mix_far_a)
-    mixed_b = mix_twins(where, kept_b, came_b, ada_head, head_twin)
+    mixed_b = mix_twins(where, kept_b, came_b, ada_head)
     mix_near_b, mix_far_b = near(mixed_b), across(mixed_b)
     heads = (head_weight, head_other, biases, bias_other, codes, code_other)
     noises = (noise_own, noise_core, noise_twin, noise_both)

time: 234 us -> 224 us (0.957)
  waiting for transfers between devices: 81.5 us -> 66.7 us
  starting transfers between devices: 74.7 us -> 80.1 us
  Pallas kernels: 68.7 us -> 65.1 us
  local copies, waits for them, and re-layouts: 5.97 us -> 9.17 us
    ppermute x41 -> x40, waiting for transfers between devices: 81.5 us -> 66.7 us  [permute_devices(): return lax.ppermute(value, ('dp', 'mp'), pairs)]
    ppermute x41 -> x40, starting transfers between devices: 74.7 us -> 80.1 us  [permute_devices(): return lax.ppermute(value, ('dp', 'mp'), pairs)]
    pallas_call x20 -> x19, Pallas kernels: 68.7 us -> 65.1 us  [call(): pl.pallas_call(kernel, out_shape=outs, in_specs=[SCALARS] + (specs or [ON...]
    unnamed x36 -> x44, local copies, waits for them, and re-layouts: 5.38 us -> 8.59 us
  transfers between devices with their start and end apart: 41 -> 40, of which waited for: 18 -> 18; matrix products, arithmetic and copies ran while one was open for 1% -> 1% of each run, Pallas kernels for 27% -> 27%
where the time goes in v7:
time: 224 us; the launch traced here: 223 us
  starting transfers between devices  80.1 us (36%)
  waiting for transfers between devices  66.7 us (30%)
  Pallas kernels  65.1 us (29%)
  local copies, waits for them, and re-layouts  9.17 us (4%)
    ppermute x40, starting transfers between devices, permute_devices(): return lax.ppermute(value, ('dp', 'mp'), pairs)  80.1 us
    ppermute x40, waiting for transfers between devices, permute_devices(): return lax.ppermute(value, ('dp', 'mp'), pairs)  66.7 us
    pallas_call x19, Pallas kernels, call(): pl.pallas_call(kernel, out_shape=outs, in_specs=[SCALARS] + (specs or [ON...  65.1 us
    unnamed x44, local copies, waits for them, and re-layouts  8.59 us
  transfers between devices with their start and end apart: 40, of which 18 were waited for; matrix products, arithmetic and copies ran while one was open for 1% of the time, Pallas kernels for 27%

profile of v7, /device:TPU:13, one launch (start us, length us, event | category | flops | bytes accessed | tf_op | source)
XLA Modules:
  0.0 223.3 jit_solution(15494398451173317767)
XLA Ops:
  6.3 4.3 %collective-permute-start.5 = (bf16[128,2304]{1,0:T(8,128)(2,1)S(1)}, bf16[128,2304]{1,0:T(8,128)(2,1)S(1)}, u32[]{:S(2)}, u32[]{:S(2)}) collective-permute-start(bf16[128,2304]{1,0:T(8,128)(2,1)S(1)} %shard_map.158.refs_0_), channel_id=1, source_target_pairs={{0,0},{1,1},{2,4},{3,5},{4,2},{5,3},{6,6},{7,7},{8,8},{9,9},{10,12... | collective-permute-start | bytes 1769480 | tf_op jit(solution)/shard_map/ppermute | solution.py:36
  11.6 7.5 %collective-permute-done.3.refs_1_ = bf16[128,2304]{1,0:T(8,128)(2,1)S(1)} collective-permute-done((bf16[128,2304]{1,0:T(8,128)(2,1)S(1)}, bf16[128,2304]{1,0:T(8,128)(2,1)S(1)}, u32[]{:S(2)}, u32[]{:S(2)}) %collective-permute-start.3) | collective-permute-done | bytes 589856 | tf_op jit(solution)/shard_map/ppermute | solution.py:36
  19.1 3.2 %collective-permute-start.4 = (bf16[128,2304]{1,0:T(8,128)(2,1)S(1)}, bf16[128,2304]{1,0:T(8,128)(2,1)S(1)}, u32[]{:S(2)}, u32[]{:S(2)}) collective-permute-start(bf16[128,2304]{1,0:T(8,128)(2,1)S(1)} %collective-permute-done.3.refs_1_), channel_id=1, source_target_pairs={{0,0},{1,1},{2,4},{3,5},{4,2},{5,3},{6,6},{7,7},{8,8},{9,9},{10,12... | collective-permute-start | bytes 1769480 | tf_op jit(solution)/shard_map/ppermute | solution.py:36
  22.3 2.0 collective-permute-done.5.refs_0_
  24.3 2.1 collective-permute-start.6
  26.4 11.9 %shard_map.160 = (bf16[128,2304]{1,0:T(8,128)(2,1)S(1)}, bf16[128,2304]{1,0:T(8,128)(2,1)S(1)}) custom-call(s32[6]{0:T(128)S(1)} %stack.35.where_ref, bf16[128,2304]{1,0:T(8,128)(2,1)S(1)} %shard_map.158.refs_0_, bf16[128,2304]{1,0:T(8,128)(2,1)S(1)} %collective-permute-done.3.refs_1_, bf16[2304,1152]{1,0:T(8,128)(2,1)} %refs_4_.9, ...), custom_call_target="tpu_custom_call" | custom-call | tf_op jit(solution)/shard_map/pallas_call | solution.py:169
  39.1 3.1 %collective-permute-start.8 = (bf16[128,2304]{1,0:T(8,128)(2,1)S(1)}, bf16[128,2304]{1,0:T(8,128)(2,1)S(1)}, u32[]{:S(2)}, u32[]{:S(2)}) collective-permute-start(bf16[128,2304]{1,0:T(8,128)(2,1)S(1)} %shard_map.159.refs_0_), channel_id=1, source_target_pairs={{0,0},{1,1},{2,4},{3,5},{4,2},{5,3},{6,6},{7,7},{8,8},{9,9},{10,12... | collective-permute-start | bytes 1769480 | tf_op jit(solution)/shard_map/ppermute | solution.py:36
  42.3 1.3 collective-permute-start.12
  43.7 2.5 %copy-done = bf16[2304,1152]{1,0:T(8,128)(2,1)S(1)} copy-done((bf16[2304,1152]{1,0:T(8,128)(2,1)S(1)}, bf16[2304,1152]{1,0:T(8,128)(2,1)}, u32[]{:S(2)}) %copy-start) | copy-done | bytes 5308440
  46.2 2.5 %copy-done.2 = bf16[1152,2304]{1,0:T(8,128)(2,1)S(1)} copy-done((bf16[1152,2304]{1,0:T(8,128)(2,1)S(1)}, bf16[1152,2304]{1,0:T(8,128)(2,1)}, u32[]{:S(2)}) %copy-start.2) | copy-done | bytes 5308440
  49.3 7.6 %shard_map.161.a_ref = bf16[128,2304]{1,0:T(8,128)(2,1)S(1)} custom-call(s32[6]{0:T(128)S(1)} %copy-done.9, bf16[128,2304]{1,0:T(8,128)(2,1)S(1)} %collective-permute-done.4.refs_0_, bf16[128,2304]{1,0:T(8,128)(2,1)} %collective-permute-done.6.refs_1_, bf16[2304,1152]{1,0:T(8,128)(2,1)S(1)} %copy-done, ...), custom_call_target="tpu_custom_call" | custom-call | tf_op jit(solution)/shard_map/pallas_call | solution.py:169
  56.9 1.3 collective-permute-start.14
  58.3 2.8 %collective-permute-start.9 = (bf16[128,2304]{1,0:T(8,128)(2,1)S(1)}, bf16[128,2304]{1,0:T(8,128)(2,1)S(1)}, u32[]{:S(2)}, u32[]{:S(2)}) collective-permute-start(bf16[128,2304]{1,0:T(8,128)(2,1)S(1)} %collective-permute-done.7.refs_1_), channel_id=1, source_target_pairs={{0,0},{1,1},{2,4},{3,5},{4,2},{5,3},{6,6},{7,7},{8,8},{9,9},{10,12... | collective-permute-start | bytes 1769480 | tf_op jit(solution)/shard_map/ppermute | solution.py:36
  61.6 2.1 collective-permute-start.16
  63.8 10.1 %shard_map.162 = (bf16[128,2304]{1,0:T(8,128)(2,1)S(1)}, bf16[128,2304]{1,0:T(8,128)(2,1)S(1)}) custom-call(s32[6]{0:T(128)S(1)} %copy-done.10, bf16[128,2304]{1,0:T(8,128)(2,1)S(1)} %shard_map.159.refs_0_, bf16[128,2304]{1,0:T(8,128)(2,1)S(1)} %collective-permute-done.7.refs_1_, bf16[2304,1152]{1,0:T(8,128)(2,1)S(1)} %copy-done.1, ...), custom_call_target="tpu_custom_call" | custom-call | tf_op jit(solution)/shard_map/pallas_call | solution.py:169
  73.9 1.3 collective-permute-start.10
  75.2 7.3 %shard_map.163.a_ref = bf16[128,2304]{1,0:T(8,128)(2,1)S(1)} custom-call(s32[6]{0:T(128)S(1)} %copy-done.10, bf16[128,2304]{1,0:T(8,128)(2,1)S(1)} %collective-permute-done.5.refs_0_, bf16[128,2304]{1,0:T(8,128)(2,1)S(1)} %collective-permute-done.12.refs_1_, bf16[2304,1152]{1,0:T(8,128)(2,1)S(1)} %copy-done.1, ...), custom_call_target="tpu_custom_call" | custom-call | tf_op jit(solution)/shard_map/pallas_call | solution.py:169
  83.3 3.0 %collective-permute-start.15 = (bf16[128,2304]{1,0:T(8,128)(2,1)S(1)}, bf16[128,2304]{1,0:T(8,128)(2,1)S(1)}, u32[]{:S(2)}, u32[]{:S(2)}) collective-permute-start(bf16[128,2304]{1,0:T(8,128)(2,1)S(1)} %shard_map.164), channel_id=1, source_target_pairs={{0,0},{1,1},{2,4},{3,5},{4,2},{5,3},{6,6},{7,7},{8,8},{9,9},{10,12... | collective-permute-start | bytes 1769480 | tf_op jit(solution)/shard_map/ppermute | solution.py:36
  86.3 1.3 collective-permute-start.17
  87.7 2.2 collective-permute-start.11
  89.9 10.0 %shard_map.165 = (bf16[128,2304]{1,0:T(8,128)(2,1)S(1)}, bf16[128,2304]{1,0:T(8,128)(2,1)S(1)}) custom-call(s32[6]{0:T(128)S(1)} %copy-done.10, bf16[128,2304]{1,0:T(8,128)(2,1)S(1)} %collective-permute-done.9.refs_0_, bf16[128,2304]{1,0:T(8,128)(2,1)S(1)} %collective-permute-done.16.refs_1_, bf16[128,2304]{1,0:T(8,128)(2,1)S(1)} %collective-permute-done.8.refs_2_, ...), custom_call_target="tpu_custom_call" | custom-call | tf_op jit(solution)/shard_map/pallas_call | solution.py:169
  100.9 3.3 %collective-permute-start.18 = (bf16[128,2304]{1,0:T(8,128)(2,1)S(1)}, bf16[128,2304]{1,0:T(8,128)(2,1)S(1)}, u32[]{:S(2)}, u32[]{:S(2)}) collective-permute-start(bf16[128,2304]{1,0:T(8,128)(2,1)S(1)} %shard_map.166), channel_id=1, source_target_pairs={{0,0},{1,1},{2,4},{3,5},{4,2},{5,3},{6,6},{7,7},{8,8},{9,9},{10,12... | collective-permute-start | bytes 1769480 | tf_op jit(solution)/shard_map/ppermute | solution.py:36
  104.3 6.8 %collective-permute-start.23 = (bf16[2304,512]{1,0:T(8,128)(2,1)S(1)}, bf16[2304,512]{1,0:T(8,128)(2,1)S(1)}, u32[]{:S(2)}, u32[]{:S(2)}) collective-permute-start(bf16[2304,512]{1,0:T(8,128)(2,1)S(1)} %copy-done.6), channel_id=1, source_target_pairs={{0,1},{1,0},{2,3},{3,2},{4,5},{5,4},{6,7},{7,6},{8,9},{9,8},{10,11... | collective-permute-start | bytes 7077896 | tf_op jit(solution)/shard_map/ppermute | solution.py:36
  111.0 1.8 collective-permute-done.11.near_ref
  113.6 8.4 %collective-permute-start.20 = (f32[2,128,512]{2,1,0:T(8,128)S(1)}, f32[2,128,512]{2,1,0:T(8,128)S(1)}, u32[]{:S(2)}, u32[]{:S(2)}) collective-permute-start(f32[2,128,512]{2,1,0:T(8,128)S(1)} %bitcast.33), channel_id=1, source_target_pairs={{0,17},{1,16},{2,19},{3,18},{4,21},{5,20},{6,23},{7,22},{8,25},{9,... | collective-permute-start | bytes 1572872 | tf_op jit(solution)/shard_map/ppermute | solution.py:36
  122.1 3.4 %collective-permute-done.25.b_ref = bf16[128,2304]{1,0:T(8,128)(2,1)S(1)} collective-permute-done((bf16[128,2304]{1,0:T(8,128)(2,1)S(1)}, bf16[128,2304]{1,0:T(8,128)(2,1)S(1)}, u32[]{:S(2)}, u32[]{:S(2)}) %collective-permute-start.25) | collective-permute-done | bytes 589856 | tf_op jit(solution)/shard_map/ppermute | solution.py:36
  126.2 8.5 %collective-permute-done.20.noise_both = f32[2,128,512]{2,1,0:T(8,128)S(1)} collective-permute-done((f32[2,128,512]{2,1,0:T(8,128)S(1)}, f32[2,128,512]{2,1,0:T(8,128)S(1)}, u32[]{:S(2)}, u32[]{:S(2)}) %collective-permute-start.20) | collective-permute-done | bytes 524320 | tf_op jit(solution)/shard_map/ppermute | solution.py:36
  134.8 3.3 %collective-permute-done.19.near_ref = bf16[128,2304]{1,0:T(8,128)(2,1)S(1)} collective-permute-done((bf16[128,2304]{1,0:T(8,128)(2,1)S(1)}, bf16[128,2304]{1,0:T(8,128)(2,1)S(1)}, u32[]{:S(2)}, u32[]{:S(2)}) %collective-permute-start.19) | collective-permute-done | bytes 589856 | tf_op jit(solution)/shard_map/ppermute | solution.py:36
  138.1 1.5 shard_map.168
  139.6 1.3 collective-permute-start.22
  140.9 4.6 %collective-permute-done.22.came_ref = bf16[64,2304]{1,0:T(8,128)(2,1)S(1)} collective-permute-done((bf16[64,2304]{1,0:T(8,128)(2,1)S(1)}, bf16[64,2304]{1,0:T(8,128)(2,1)S(1)}, u32[]{:S(2)}, u32[]{:S(2)}) %collective-permute-start.22) | collective-permute-done | bytes 294944 | tf_op jit(solution)/shard_map/ppermute | solution.py:36
  146.6 9.0 %collective-permute-start.24 = (bf16[32,512]{1,0:T(8,128)(2,1)S(1)}, bf16[32,512]{1,0:T(8,128)(2,1)S(1)}, u32[]{:S(2)}, u32[]{:S(2)}) collective-permute-start(bf16[32,512]{1,0:T(8,128)(2,1)S(1)} %bitcast.27), channel_id=1, source_target_pairs={{0,1},{1,0},{2,3},{3,2},{4,5},{5,4},{6,7},{7,6},{8,9},{9,8},{10,11... | collective-permute-start | bytes 98312 | tf_op jit(solution)/shard_map/ppermute | solution.py:36
  156.5 2.4 %shard_map.171 = (bf16[256,2304]{1,0:T(8,128)(2,1)}, bf16[64,2304]{1,0:T(8,128)(2,1)S(1)}, bf16[64,2304]{1,0:T(8,128)(2,1)S(1)}) custom-call(s32[6]{0:T(128)S(1)} %copy-done.10, bf16[128,2304]{1,0:T(8,128)(2,1)S(1)} %get-tuple-element.61.own_ref, bf16[128,2304]{1,0:T(8,128)(2,1)S(1)} %collective-permute-done.11.near_ref, ...), custom_call_target="tpu_custom_call" | custom-call | tf_op jit(solution)/shard_map/pallas_call | solution.py:169
  161.0 4.8 %collective-permute-done.28.far_ref = bf16[64,2304]{1,0:T(8,128)(2,1)S(1)} collective-permute-done((bf16[64,2304]{1,0:T(8,128)(2,1)S(1)}, bf16[64,2304]{1,0:T(8,128)(2,1)S(1)}, u32[]{:S(2)}, u32[]{:S(2)}) %collective-permute-start.28) | collective-permute-done | bytes 294944 | tf_op jit(solution)/shard_map/ppermute | solution.py:36
  165.7 2.7 %collective-permute-start.30 = (bf16[64,2304]{1,0:T(8,128)(2,1)S(1)}, bf16[64,2304]{1,0:T(8,128)(2,1)S(1)}, u32[]{:S(2)}, u32[]{:S(2)}) collective-permute-start(bf16[64,2304]{1,0:T(8,128)(2,1)S(1)} %collective-permute-done.28.far_ref), channel_id=1, source_target_pairs={{0,2},{1,3},{2,0},{3,1},{4,6},{5,7},{6,4},{7,5},{8,10},{9,11},{10,... | collective-permute-start | bytes 884744 | tf_op jit(solution)/shard_map/ppermute | solution.py:36
  169.5 1.9 collective-permute-start.32
  172.4 12.6 %collective-permute-done.30.last_ref = bf16[64,2304]{1,0:T(8,128)(2,1)S(1)} collective-permute-done((bf16[64,2304]{1,0:T(8,128)(2,1)S(1)}, bf16[64,2304]{1,0:T(8,128)(2,1)S(1)}, u32[]{:S(2)}, u32[]{:S(2)}) %collective-permute-start.30) | collective-permute-done | bytes 294944 | tf_op jit(solution)/shard_map/ppermute | solution.py:36
  185.1 2.6 %shard_map.173 = f32[40,256]{1,0:T(8,128)S(1)} custom-call(s32[6]{0:T(128)S(1)} %copy-done.10, bf16[64,2304]{1,0:T(8,128)(2,1)S(1)} %shard_map.169.own_ref, bf16[64,2304]{1,0:T(8,128)(2,1)S(1)} %collective-permute-done.29.near_ref, bf16[64,2304]{1,0:T(8,128)(2,1)S(1)} %collective-permute-done.28.far_ref, ...), custom_call_target="tpu_custom_call" | custom-call | flops 40000000000 | tf_op jit(solution)/shard_map/pallas_call | solution.py:169
  188.3 1.6 collective-permute-start.33
  190.1 1.3 collective-permute-done.31.near_ref
  191.4 6.3 %collective-permute-done.33.last_ref = bf16[64,2304]{1,0:T(8,128)(2,1)S(1)} collective-permute-done((bf16[64,2304]{1,0:T(8,128)(2,1)S(1)}, bf16[64,2304]{1,0:T(8,128)(2,1)S(1)}, u32[]{:S(2)}, u32[]{:S(2)}) %collective-permute-start.33) | collective-permute-done | bytes 294944 | tf_op jit(solution)/shard_map/ppermute | solution.py:36
  197.7 2.6 %shard_map.174 = f32[40,256]{1,0:T(8,128)S(1)} custom-call(s32[6]{0:T(128)S(1)} %copy-done.10, bf16[64,2304]{1,0:T(8,128)(2,1)S(1)} %shard_map.172.own_ref, bf16[64,2304]{1,0:T(8,128)(2,1)S(1)} %collective-permute-done.31.near_ref, bf16[64,2304]{1,0:T(8,128)(2,1)S(1)} %collective-permute-done.32.far_ref, ...), custom_call_target="tpu_custom_call" | custom-call | tf_op jit(solution)/shard_map/pallas_call | solution.py:169
  200.5 2.2 collective-permute-start.34
  204.2 2.3 %collective-permute-done.35.refs_2_ = f32[40,128]{1,0:T(8,128)S(1)} collective-permute-done((f32[40,128]{1,0:T(8,128)S(1)}, f32[40,128]{1,0:T(8,128)S(1)}, u32[]{:S(2)}, u32[]{:S(2)}) %collective-permute-start.35) | collective-permute-done | bytes 20512 | tf_op jit(solution)/shard_map/ppermute | solution.py:36
  207.0 5.0 %collective-permute-start.37 = (f32[32,128]{1,0:T(8,128)S(1)}, f32[32,128]{1,0:T(8,128)S(1)}, u32[]{:S(2)}, u32[]{:S(2)}) collective-permute-start(f32[32,128]{1,0:T(8,128)S(1)} %shard_map.175), channel_id=1, source_target_pairs={{0,0},{1,2},{2,4},{3,6},{4,16},{5,18},{6,20},{7,22},{8,8},{9,10},{... | collective-permute-start | bytes 49160 | tf_op jit(solution)/shard_map/ppermute | solution.py:36
  212.0 2.7 %collective-permute-start.38 = (f32[32,128]{1,0:T(8,128)S(1)}, f32[32,128]{1,0:T(8,128)S(1)}, u32[]{:S(2)}, u32[]{:S(2)}) collective-permute-start(f32[32,128]{1,0:T(8,128)S(1)} %shard_map.175), channel_id=1, source_target_pairs={{0,1},{1,3},{2,5},{3,7},{4,17},{5,19},{6,21},{7,23},{8,9},{9,11},{... | collective-permute-start | bytes 49160 | tf_op jit(solution)/shard_map/ppermute | solution.py:36
  216.1 5.5 %collective-permute-done.39.halo_ref = f32[32,128]{1,0:T(8,128)S(1)} collective-permute-done((f32[32,128]{1,0:T(8,128)S(1)}, f32[32,128]{1,0:T(8,128)S(1)}, u32[]{:S(2)}, u32[]{:S(2)}) %collective-permute-start.39) | collective-permute-done | bytes 16416 | tf_op jit(solution)/shard_map/ppermute | solution.py:36
  221.6 1.7 shard_map.176
  (107 shorter events, 22.4 us)
Async XLA Ops:
  0.6 18.5 %collective-permute-start = (bf16[2304,1152]{1,0:T(8,128)(2,1)}, bf16[2304,1152]{1,0:T(8,128)(2,1)}, u32[]{:S(2)}, u32[]{:S(2)}) collective-permute-start(bf16[2304,1152]{1,0:T(8,128)(2,1)} %refs_4_.9), channel_id=1, source_target_pairs={{0,1},{1,0},{2,3},{3,2},{4,5},{5,4},{6,7},{7,6},{8,9},{9,8},{10,11... | collective-permute-start | bytes 15925256 | tf_op jit(solution)/shard_map/ppermute | solution.py:36
  1.4 17.7 %collective-permute-start.1 = (bf16[1152,2304]{1,0:T(8,128)(2,1)}, bf16[1152,2304]{1,0:T(8,128)(2,1)}, u32[]{:S(2)}, u32[]{:S(2)}) collective-permute-start(bf16[1152,2304]{1,0:T(8,128)(2,1)} %refs_6_.1), channel_id=1, source_target_pairs={{0,1},{1,0},{2,3},{3,2},{4,5},{5,4},{6,7},{7,6},{8,9},{9,8},{10,11... | collective-permute-start | bytes 15925256 | tf_op jit(solution)/shard_map/ppermute | solution.py:36
  3.6 34.7 %copy-start.8 = (s32[6]{0:T(128)}, s32[6]{0:T(128)S(1)}, u32[]{:S(2)}) copy-start(s32[6]{0:T(128)S(1)} %stack.35.where_ref) | copy-start | bytes 76
  4.6 14.5 %collective-permute-start.3 = (bf16[128,2304]{1,0:T(8,128)(2,1)S(1)}, bf16[128,2304]{1,0:T(8,128)(2,1)S(1)}, u32[]{:S(2)}, u32[]{:S(2)}) collective-permute-start(bf16[128,2304]{1,0:T(8,128)(2,1)S(1)} %shard_map.158.refs_0_), channel_id=1, source_target_pairs={{0,2},{1,3},{2,0},{3,1},{4,6},{5,7},{6,4},{7,5},{8,10},{9,11},{10,... | collective-permute-start | bytes 1769480 | tf_op jit(solution)/shard_map/ppermute | solution.py:36
  5.5 6.1 %collective-permute-start.2 = (f32[1,1664]{1,0:T(1,128)S(1)}, f32[1,1664]{1,0:T(1,128)S(1)}, u32[]{:S(2)}, u32[]{:S(2)}) collective-permute-start(f32[1,1664]{1,0:T(1,128)S(1)} %broadcast_in_dim.12.refs_6_.refs_8_.bias_a), channel_id=1, source_target_pairs={{0,1},{1,0},{2,3},{3,2},{4,5},{5,4},{6,7},{7,6},{8,9},{9,8},{10,11... | collective-permute-start | bytes 19976 | tf_op jit(solution)/shard_map/ppermute | solution.py:36
  6.3 18.0 %collective-permute-start.5 = (bf16[128,2304]{1,0:T(8,128)(2,1)S(1)}, bf16[128,2304]{1,0:T(8,128)(2,1)S(1)}, u32[]{:S(2)}, u32[]{:S(2)}) collective-permute-start(bf16[128,2304]{1,0:T(8,128)(2,1)S(1)} %shard_map.158.refs_0_), channel_id=1, source_target_pairs={{0,0},{1,1},{2,4},{3,5},{4,2},{5,3},{6,6},{7,7},{8,8},{9,9},{10,12... | collective-permute-start | bytes 1769480 | tf_op jit(solution)/shard_map/ppermute | solution.py:36
  19.1 20.0 %collective-permute-start.4 = (bf16[128,2304]{1,0:T(8,128)(2,1)S(1)}, bf16[128,2304]{1,0:T(8,128)(2,1)S(1)}, u32[]{:S(2)}, u32[]{:S(2)}) collective-permute-start(bf16[128,2304]{1,0:T(8,128)(2,1)S(1)} %collective-permute-done.3.refs_1_), channel_id=1, source_target_pairs={{0,0},{1,1},{2,4},{3,5},{4,2},{5,3},{6,6},{7,7},{8,8},{9,9},{10,12... | collective-permute-start | bytes 1769480 | tf_op jit(solution)/shard_map/ppermute | solution.py:36
  24.3 19.3 %collective-permute-start.6 = (bf16[128,2304]{1,0:T(8,128)(2,1)S(1)}, bf16[128,2304]{1,0:T(8,128)(2,1)}, u32[]{:S(2)}, u32[]{:S(2)}) collective-permute-start(bf16[128,2304]{1,0:T(8,128)(2,1)S(1)} %collective-permute-done.5.refs_0_), channel_id=1, source_target_pairs={{2,0},{3,1},{4,6},{5,7},{10,8},{11,9},{12,14},{13,15},{18,16},{19,... | collective-permute-start | bytes 1769480 | tf_op jit(solution)/shard_map/ppermute | solution.py:36
  26.4 31.8 %collective-permute-start.7 = (bf16[128,2304]{1,0:T(8,128)(2,1)S(1)}, bf16[128,2304]{1,0:T(8,128)(2,1)S(1)}, u32[]{:S(2)}, u32[]{:S(2)}) collective-permute-start(bf16[128,2304]{1,0:T(8,128)(2,1)S(1)} %shard_map.159.refs_0_), channel_id=1, source_target_pairs={{0,2},{1,3},{2,0},{3,1},{4,6},{5,7},{6,4},{7,5},{8,10},{9,11},{10,... | collective-permute-start | bytes 1769480 | tf_op jit(solution)/shard_map/ppermute | solution.py:36
  39.1 19.1 %collective-permute-start.8 = (bf16[128,2304]{1,0:T(8,128)(2,1)S(1)}, bf16[128,2304]{1,0:T(8,128)(2,1)S(1)}, u32[]{:S(2)}, u32[]{:S(2)}) collective-permute-start(bf16[128,2304]{1,0:T(8,128)(2,1)S(1)} %shard_map.159.refs_0_), channel_id=1, source_target_pairs={{0,0},{1,1},{2,4},{3,5},{4,2},{5,3},{6,6},{7,7},{8,8},{9,9},{10,12... | collective-permute-start | bytes 1769480 | tf_op jit(solution)/shard_map/ppermute | solution.py:36
  42.3 32.9 %collective-permute-start.12 = (bf16[128,2304]{1,0:T(8,128)(2,1)S(1)}, bf16[128,2304]{1,0:T(8,128)(2,1)S(1)}, u32[]{:S(2)}, u32[]{:S(2)}) collective-permute-start(bf16[128,2304]{1,0:T(8,128)(2,1)S(1)} %collective-permute-done.4.refs_0_), channel_id=1, source_target_pairs={{2,0},{3,1},{4,6},{5,7},{10,8},{11,9},{12,14},{13,15},{18,16},{19,... | collective-permute-start | bytes 1769480 | tf_op jit(solution)/shard_map/ppermute | solution.py:36
  56.9 25.6 %collective-permute-start.14 = (bf16[128,2304]{1,0:T(8,128)(2,1)S(1)}, bf16[128,2304]{1,0:T(8,128)(2,1)S(1)}, u32[]{:S(2)}, u32[]{:S(2)}) collective-permute-start(bf16[128,2304]{1,0:T(8,128)(2,1)S(1)} %shard_map.161.a_ref), channel_id=1, source_target_pairs={{0,2},{1,3},{6,4},{7,5},{8,10},{9,11},{14,12},{15,13},{16,18},{17,... | collective-permute-start | bytes 1769480 | tf_op jit(solution)/shard_map/ppermute | solution.py:36
  58.3 15.6 %collective-permute-start.9 = (bf16[128,2304]{1,0:T(8,128)(2,1)S(1)}, bf16[128,2304]{1,0:T(8,128)(2,1)S(1)}, u32[]{:S(2)}, u32[]{:S(2)}) collective-permute-start(bf16[128,2304]{1,0:T(8,128)(2,1)S(1)} %collective-permute-done.7.refs_1_), channel_id=1, source_target_pairs={{0,0},{1,1},{2,4},{3,5},{4,2},{5,3},{6,6},{7,7},{8,8},{9,9},{10,12... | collective-permute-start | bytes 1769480 | tf_op jit(solution)/shard_map/ppermute | solution.py:36
  61.3 13.9 %collective-permute-start.13 = (f32[2,128,512]{2,1,0:T(8,128)S(1)}, f32[2,128,512]{2,1,0:T(8,128)S(1)}, u32[]{:S(2)}, u32[]{:S(2)}) collective-permute-start(f32[2,128,512]{2,1,0:T(8,128)S(1)} %bitcast.34), channel_id=1, source_target_pairs={{0,16},{1,17},{2,18},{3,19},{4,20},{5,21},{6,22},{7,23},{8,24},{9,... | collective-permute-start | bytes 1572872 | tf_op jit(solution)/shard_map/ppermute | solution.py:36
  61.6 28.3 %collective-permute-start.16 = (bf16[128,2304]{1,0:T(8,128)(2,1)S(1)}, bf16[128,2304]{1,0:T(8,128)(2,1)S(1)}, u32[]{:S(2)}, u32[]{:S(2)}) collective-permute-start(bf16[128,2304]{1,0:T(8,128)(2,1)S(1)} %collective-permute-done.8.refs_2_), channel_id=1, source_target_pairs={{2,0},{3,1},{4,6},{5,7},{10,8},{11,9},{12,14},{13,15},{18,16},{19,... | collective-permute-start | bytes 1769480 | tf_op jit(solution)/shard_map/ppermute | solution.py:36
  73.9 13.9 %collective-permute-start.10 = (bf16[128,2304]{1,0:T(8,128)(2,1)S(1)}, bf16[128,2304]{1,0:T(8,128)(2,1)S(1)}, u32[]{:S(2)}, u32[]{:S(2)}) collective-permute-start(bf16[128,2304]{1,0:T(8,128)(2,1)S(1)} %collective-permute-done.9.refs_0_), channel_id=1, source_target_pairs={{2,0},{3,1},{4,6},{5,7},{10,8},{11,9},{12,14},{13,15},{18,16},{19,... | collective-permute-start | bytes 1769480 | tf_op jit(solution)/shard_map/ppermute | solution.py:36
  83.3 29.5 %copy-start.18 = (bf16[128,2304]{1,0:T(8,128)(2,1)S(1)}, bf16[128,2304]{1,0:T(8,128)(2,1)}, u32[]{:S(2)}) copy-start(bf16[128,2304]{1,0:T(8,128)(2,1)} %copy-done.17) | copy-start | bytes 1769476
  83.3 16.7 %collective-permute-start.15 = (bf16[128,2304]{1,0:T(8,128)(2,1)S(1)}, bf16[128,2304]{1,0:T(8,128)(2,1)S(1)}, u32[]{:S(2)}, u32[]{:S(2)}) collective-permute-start(bf16[128,2304]{1,0:T(8,128)(2,1)S(1)} %shard_map.164), channel_id=1, source_target_pairs={{0,0},{1,1},{2,4},{3,5},{4,2},{5,3},{6,6},{7,7},{8,8},{9,9},{10,12... | collective-permute-start | bytes 1769480 | tf_op jit(solution)/shard_map/ppermute | solution.py:36
  86.3 13.8 %collective-permute-start.17 = (bf16[128,2304]{1,0:T(8,128)(2,1)S(1)}, bf16[128,2304]{1,0:T(8,128)(2,1)S(1)}, u32[]{:S(2)}, u32[]{:S(2)}) collective-permute-start(bf16[128,2304]{1,0:T(8,128)(2,1)S(1)} %shard_map.163.a_ref), channel_id=1, source_target_pairs={{0,2},{1,3},{6,4},{7,5},{8,10},{9,11},{14,12},{15,13},{16,18},{17,... | collective-permute-start | bytes 1769480 | tf_op jit(solution)/shard_map/ppermute | solution.py:36
  87.7 25.0 %collective-permute-start.11 = (bf16[128,2304]{1,0:T(8,128)(2,1)S(1)}, bf16[128,2304]{1,0:T(8,128)(2,1)S(1)}, u32[]{:S(2)}, u32[]{:S(2)}) collective-permute-start(bf16[128,2304]{1,0:T(8,128)(2,1)S(1)} %get-tuple-element.64), channel_id=1, source_target_pairs={{0,2},{1,3},{2,0},{3,1},{4,6},{5,7},{6,4},{7,5},{8,10},{9,11},{10,... | collective-permute-start | bytes 1769480 | tf_op jit(solution)/shard_map/ppermute | solution.py:36
  100.9 11.9 %collective-permute-start.18 = (bf16[128,2304]{1,0:T(8,128)(2,1)S(1)}, bf16[128,2304]{1,0:T(8,128)(2,1)S(1)}, u32[]{:S(2)}, u32[]{:S(2)}) collective-permute-start(bf16[128,2304]{1,0:T(8,128)(2,1)S(1)} %shard_map.166), channel_id=1, source_target_pairs={{0,0},{1,1},{2,4},{3,5},{4,2},{5,3},{6,6},{7,7},{8,8},{9,9},{10,12... | collective-permute-start | bytes 1769480 | tf_op jit(solution)/shard_map/ppermute | solution.py:36
  104.1 33.9 %copy-start.7 = (f32[2,2,2304]{2,1,0:T(2,128)S(1)}, f32[2,2,2304]{2,1,0:T(2,128)}, u32[]{:S(2)}) copy-start(f32[2,2,2304]{2,1,0:T(2,128)} %ada_ref.11) | copy-start | bytes 110596
  104.2 33.9 %copy-start.14 = (f32[2,2304]{1,0:T(2,128)S(1)}, f32[2,2304]{1,0:T(2,128)}, u32[]{:S(2)}) copy-start(f32[2,2304]{1,0:T(2,128)} %gate_ref.3) | copy-start | bytes 55300
  104.2 21.3 %collective-permute-start.25 = (bf16[128,2304]{1,0:T(8,128)(2,1)S(1)}, bf16[128,2304]{1,0:T(8,128)(2,1)S(1)}, u32[]{:S(2)}, u32[]{:S(2)}) collective-permute-start(bf16[128,2304]{1,0:T(8,128)(2,1)S(1)} %get-tuple-element.77), channel_id=1, source_target_pairs={{0,2},{1,3},{2,0},{3,1},{4,6},{5,7},{6,4},{7,5},{8,10},{9,11},{10,... | collective-permute-start | bytes 1769480 | tf_op jit(solution)/shard_map/ppermute | solution.py:36
  104.3 52.2 %collective-permute-start.23 = (bf16[2304,512]{1,0:T(8,128)(2,1)S(1)}, bf16[2304,512]{1,0:T(8,128)(2,1)S(1)}, u32[]{:S(2)}, u32[]{:S(2)}) collective-permute-start(bf16[2304,512]{1,0:T(8,128)(2,1)S(1)} %copy-done.6), channel_id=1, source_target_pairs={{0,1},{1,0},{2,3},{3,2},{4,5},{5,4},{6,7},{7,6},{8,9},{9,8},{10,11... | collective-permute-start | bytes 7077896 | tf_op jit(solution)/shard_map/ppermute | solution.py:36
  113.5 24.5 %collective-permute-start.19 = (bf16[128,2304]{1,0:T(8,128)(2,1)S(1)}, bf16[128,2304]{1,0:T(8,128)(2,1)S(1)}, u32[]{:S(2)}, u32[]{:S(2)}) collective-permute-start(bf16[128,2304]{1,0:T(8,128)(2,1)S(1)} %shard_map.167), channel_id=1, source_target_pairs={{0,2},{1,3},{2,0},{3,1},{4,6},{5,7},{6,4},{7,5},{8,10},{9,11},{10,... | collective-permute-start | bytes 1769480 | tf_op jit(solution)/shard_map/ppermute | solution.py:36
  113.6 21.1 %collective-permute-start.20 = (f32[2,128,512]{2,1,0:T(8,128)S(1)}, f32[2,128,512]{2,1,0:T(8,128)S(1)}, u32[]{:S(2)}, u32[]{:S(2)}) collective-permute-start(f32[2,128,512]{2,1,0:T(8,128)S(1)} %bitcast.33), channel_id=1, source_target_pairs={{0,17},{1,16},{2,19},{3,18},{4,21},{5,20},{6,23},{7,22},{8,25},{9,... | collective-permute-start | bytes 1572872 | tf_op jit(solution)/shard_map/ppermute | solution.py:36
  122.0 12.7 %collective-permute-start.21 = (f32[2,128,512]{2,1,0:T(8,128)S(1)}, f32[2,128,512]{2,1,0:T(8,128)S(1)}, u32[]{:S(2)}, u32[]{:S(2)}) collective-permute-start(f32[2,128,512]{2,1,0:T(8,128)S(1)} %bitcast.32), channel_id=1, source_target_pairs={{0,1},{1,0},{2,3},{3,2},{4,5},{5,4},{6,7},{7,6},{8,9},{9,8},{10,11... | collective-permute-start | bytes 1572872 | tf_op jit(solution)/shard_map/ppermute | solution.py:36
  126.1 30.4 %collective-permute-start.26 = (bf16[128,2304]{1,0:T(8,128)(2,1)S(1)}, bf16[128,2304]{1,0:T(8,128)(2,1)S(1)}, u32[]{:S(2)}, u32[]{:S(2)}) collective-permute-start(bf16[128,2304]{1,0:T(8,128)(2,1)S(1)} %shard_map.170), channel_id=1, source_target_pairs={{0,4},{1,5},{2,6},{3,7},{4,0},{5,1},{6,2},{7,3},{8,12},{9,13},{10,... | collective-permute-start | bytes 1769480 | tf_op jit(solution)/shard_map/ppermute | solution.py:36
  139.6 5.9 %collective-permute-start.22 = (bf16[64,2304]{1,0:T(8,128)(2,1)S(1)}, bf16[64,2304]{1,0:T(8,128)(2,1)S(1)}, u32[]{:S(2)}, u32[]{:S(2)}) collective-permute-start(bf16[64,2304]{1,0:T(8,128)(2,1)S(1)} %get-tuple-element.76), channel_id=1, source_target_pairs={{0,16},{1,17},{2,18},{3,19},{4,20},{5,21},{6,22},{7,23},{8,24},{9,... | collective-permute-start | bytes 884744 | tf_op jit(solution)/shard_map/ppermute | solution.py:36
  146.5 19.2 %collective-permute-start.28 = (bf16[64,2304]{1,0:T(8,128)(2,1)S(1)}, bf16[64,2304]{1,0:T(8,128)(2,1)S(1)}, u32[]{:S(2)}, u32[]{:S(2)}) collective-permute-start(bf16[64,2304]{1,0:T(8,128)(2,1)S(1)} %shard_map.169.own_ref), channel_id=1, source_target_pairs={{0,4},{1,5},{2,6},{3,7},{4,0},{5,1},{6,2},{7,3},{8,12},{9,13},{10,... | collective-permute-start | bytes 884744 | tf_op jit(solution)/shard_map/ppermute | solution.py:36
  146.6 9.9 %collective-permute-start.24 = (bf16[32,512]{1,0:T(8,128)(2,1)S(1)}, bf16[32,512]{1,0:T(8,128)(2,1)S(1)}, u32[]{:S(2)}, u32[]{:S(2)}) collective-permute-start(bf16[32,512]{1,0:T(8,128)(2,1)S(1)} %bitcast.27), channel_id=1, source_target_pairs={{0,1},{1,0},{2,3},{3,2},{4,5},{5,4},{6,7},{7,6},{8,9},{9,8},{10,11... | collective-permute-start | bytes 98312 | tf_op jit(solution)/shard_map/ppermute | solution.py:36
  158.9 9.5 %collective-permute-start.27 = (bf16[64,2304]{1,0:T(8,128)(2,1)S(1)}, bf16[64,2304]{1,0:T(8,128)(2,1)S(1)}, u32[]{:S(2)}, u32[]{:S(2)}) collective-permute-start(bf16[64,2304]{1,0:T(8,128)(2,1)S(1)} %get-tuple-element.85), channel_id=1, source_target_pairs={{0,16},{1,17},{2,18},{3,19},{4,20},{5,21},{6,22},{7,23},{8,24},{9,... | collective-permute-start | bytes 884744 | tf_op jit(solution)/shard_map/ppermute | solution.py:36
  160.1 12.3 %collective-permute-start.29 = (bf16[64,2304]{1,0:T(8,128)(2,1)S(1)}, bf16[64,2304]{1,0:T(8,128)(2,1)S(1)}, u32[]{:S(2)}, u32[]{:S(2)}) collective-permute-start(bf16[64,2304]{1,0:T(8,128)(2,1)S(1)} %shard_map.169.own_ref), channel_id=1, source_target_pairs={{0,2},{1,3},{2,0},{3,1},{4,6},{5,7},{6,4},{7,5},{8,10},{9,11},{10,... | collective-permute-start | bytes 884744 | tf_op jit(solution)/shard_map/ppermute | solution.py:36
  165.7 19.3 %collective-permute-start.30 = (bf16[64,2304]{1,0:T(8,128)(2,1)S(1)}, bf16[64,2304]{1,0:T(8,128)(2,1)S(1)}, u32[]{:S(2)}, u32[]{:S(2)}) collective-permute-start(bf16[64,2304]{1,0:T(8,128)(2,1)S(1)} %collective-permute-done.28.far_ref), channel_id=1, source_target_pairs={{0,2},{1,3},{2,0},{3,1},{4,6},{5,7},{6,4},{7,5},{8,10},{9,11},{10,... | collective-permute-start | bytes 884744 | tf_op jit(solution)/shard_map/ppermute | solution.py:36
  169.4 22.0 %collective-permute-start.31 = (bf16[64,2304]{1,0:T(8,128)(2,1)S(1)}, bf16[64,2304]{1,0:T(8,128)(2,1)S(1)}, u32[]{:S(2)}, u32[]{:S(2)}) collective-permute-start(bf16[64,2304]{1,0:T(8,128)(2,1)S(1)} %shard_map.172.own_ref), channel_id=1, source_target_pairs={{0,2},{1,3},{2,0},{3,1},{4,6},{5,7},{6,4},{7,5},{8,10},{9,11},{10,... | collective-permute-start | bytes 884744 | tf_op jit(solution)/shard_map/ppermute | solution.py:36
  169.5 18.8 %collective-permute-start.32 = (bf16[64,2304]{1,0:T(8,128)(2,1)S(1)}, bf16[64,2304]{1,0:T(8,128)(2,1)S(1)}, u32[]{:S(2)}, u32[]{:S(2)}) collective-permute-start(bf16[64,2304]{1,0:T(8,128)(2,1)S(1)} %shard_map.172.own_ref), channel_id=1, source_target_pairs={{0,4},{1,5},{2,6},{3,7},{4,0},{5,1},{6,2},{7,3},{8,12},{9,13},{10,... | collective-permute-start | bytes 884744 | tf_op jit(solution)/shard_map/ppermute | solution.py:36
  188.3 9.4 %collective-permute-start.33 = (bf16[64,2304]{1,0:T(8,128)(2,1)S(1)}, bf16[64,2304]{1,0:T(8,128)(2,1)S(1)}, u32[]{:S(2)}, u32[]{:S(2)}) collective-permute-start(bf16[64,2304]{1,0:T(8,128)(2,1)S(1)} %collective-permute-done.32.far_ref), channel_id=1, source_target_pairs={{0,2},{1,3},{2,0},{3,1},{4,6},{5,7},{6,4},{7,5},{8,10},{9,11},{10,... | collective-permute-start | bytes 884744 | tf_op jit(solution)/shard_map/ppermute | solution.py:36
  190.0 26.0 %copy-start.21 = (f32[32]{0:T(128)S(1)}, f32[32]{0:T(128)}, u32[]{:S(2)}) copy-start(f32[32]{0:T(128)} %param.28) | copy-start | bytes 388
  190.0 31.5 %copy-start.11 = (s32[6]{0:T(128)S(1)}, s32[6]{0:T(128)}, u32[]{:S(2)}) copy-start(s32[6]{0:T(128)} %copy-done.8) | copy-start | bytes 76
  190.1 31.5 %copy-start.12 = (f32[32,32,3,3]{1,0,3,2:T(8,128)S(1)}, f32[32,32,3,3]{1,0,3,2:T(8,128)}, u32[]{:S(2)}) copy-start(f32[32,32,3,3]{1,0,3,2:T(8,128)} %param.27) | copy-start | bytes 110596
  190.1 31.5 %copy-start.16 = (f32[1,32,128]{2,1,0:T(8,128)S(1)}, f32[1,32,128]{2,1,0:T(8,128)}, u32[]{:S(2)}) copy-start(f32[1,32,128]{2,1,0:T(8,128)} %param.29) | copy-start | bytes 49156
  200.5 3.7 %collective-permute-start.34 = (f32[40,128]{1,0:T(8,128)S(1)}, f32[40,128]{1,0:T(8,128)S(1)}, u32[]{:S(2)}, u32[]{:S(2)}) collective-permute-start(f32[40,128]{1,0:T(8,128)S(1)} %pad_maximum_fusion.1), channel_id=1, source_target_pairs={{0,2},{1,3},{2,0},{3,1},{4,6},{5,7},{6,4},{7,5},{8,10},{9,11},{10,... | collective-permute-start | bytes 61448 | tf_op jit(solution)/shard_map/ppermute | solution.py:36
  202.8 3.6 %collective-permute-start.35 = (f32[40,128]{1,0:T(8,128)S(1)}, f32[40,128]{1,0:T(8,128)S(1)}, u32[]{:S(2)}, u32[]{:S(2)}) collective-permute-start(f32[40,128]{1,0:T(8,128)S(1)} %pad_maximum_fusion.2), channel_id=1, source_target_pairs={{0,4},{1,5},{2,6},{3,7},{4,0},{5,1},{6,2},{7,3},{8,12},{9,13},{10,... | collective-permute-start | bytes 61448 | tf_op jit(solution)/shard_map/ppermute | solution.py:36
  203.4 3.1 %collective-permute-start.36 = (f32[40,128]{1,0:T(8,128)S(1)}, f32[40,128]{1,0:T(8,128)S(1)}, u32[]{:S(2)}, u32[]{:S(2)}) collective-permute-start(f32[40,128]{1,0:T(8,128)S(1)} %pad_maximum_fusion.3), channel_id=1, source_target_pairs={{0,6},{1,7},{2,4},{3,5},{4,2},{5,3},{6,0},{7,1},{8,14},{9,15},{10,... | collective-permute-start | bytes 61448 | tf_op jit(solution)/shard_map/ppermute | solution.py:36
  207.0 9.1 %collective-permute-start.37 = (f32[32,128]{1,0:T(8,128)S(1)}, f32[32,128]{1,0:T(8,128)S(1)}, u32[]{:S(2)}, u32[]{:S(2)}) collective-permute-start(f32[32,128]{1,0:T(8,128)S(1)} %shard_map.175), channel_id=1, source_target_pairs={{0,0},{1,2},{2,4},{3,6},{4,16},{5,18},{6,20},{7,22},{8,8},{9,10},{... | collective-permute-start | bytes 49160 | tf_op jit(solution)/shard_map/ppermute | solution.py:36
  212.0 4.1 %collective-permute-start.38 = (f32[32,128]{1,0:T(8,128)S(1)}, f32[32,128]{1,0:T(8,128)S(1)}, u32[]{:S(2)}, u32[]{:S(2)}) collective-permute-start(f32[32,128]{1,0:T(8,128)S(1)} %shard_map.175), channel_id=1, source_target_pairs={{0,1},{1,3},{2,5},{3,7},{4,17},{5,19},{6,21},{7,23},{8,9},{9,11},{... | collective-permute-start | bytes 49160 | tf_op jit(solution)/shard_map/ppermute | solution.py:36
  214.7 6.8 %collective-permute-start.39 = (f32[32,128]{1,0:T(8,128)S(1)}, f32[32,128]{1,0:T(8,128)S(1)}, u32[]{:S(2)}, u32[]{:S(2)}) collective-permute-start(f32[32,128]{1,0:T(8,128)S(1)} %shard_map.175), channel_id=1, source_target_pairs={{1,1},{2,3},{3,5},{5,17},{6,19},{7,21},{9,9},{10,11},{11,13},{13,2... | collective-permute-start | bytes 49160 | tf_op jit(solution)/shard_map/ppermute | solution.py:36
  (14 other events, 144.1 us)

commit v8 on v7

--- a/solution.py
+++ b/solution.py
@@ -550,23 +550,24 @@
     came_far_a = inward(sum_far_a)
     near_b, mid_b = barrier((near_b, mid_b, sum_far_a))[:2]
     far_mid_b, far_end_b = middle(near_b), outward(mid_b)
-    sum_own_b, sum_near_b = ffn(where, [[after(own_b, sum_far_a)], [after(near_b, mid_b)]], panels)
-    (sum_last_a,) = ffn(where, [[mid_a, after(last_end_a, sum_near_b, noise_twin, far_mid_b)]], panels)
+    (sum_last_a,) = ffn(where, [[mid_a, after(last_end_a, near_b, mid_b)]], panels)
     came_last_a = inward(sum_last_a)
-    last_end_b = outward(after(far_mid_b, sum_near_b))
+    far_mid_b = after(far_mid_b, sum_last_a)
+    last_end_b = outward(far_mid_b)
+    both_last_a = add(where, after(sum_last_a, far_mid_b), came_far_a)
+    went_last_a = middle(both_last_a)
+    sum_own_b, sum_near_b = ffn(where, [[after(own_b, both_last_a, far_end_b)], [near_b]], panels)
     noise_both = swap_both(after(noise_both, noise_twin))
-    both_last_a = add(where, sum_last_a, came_far_a)
-    went_last_a = middle(both_last_a)
+    both_far_a = add(where, after(sum_far_a, went_last_a, sum_near_b), came_last_a)
+    went_far_a = middle(both_far_a)
     sum_far_b, sum_last_b = ffn(
-        where, [[after(far_mid_b, sum_last_a, both_last_a), far_end_b], [mid_b, last_end_b]], panels
-    )
-    both_far_a = add(where, after(sum_far_a, went_last_a, sum_far_b), came_last_a)
-    went_far_a = middle(both_far_a)
+        where, [[after(far_mid_b, both_far_a), far_end_b], [mid_b, last_end_b]], panels
+    )
     came_last_b = near(sum_last_b)
     head_other = swap_cores(after(head_weight, sum_last_b))
     code_other = swap_cores(after(codes, sum_last_b))
     came_near_b = near(after(sum_near_b, last_end_b))
-    both_near_a = add(where, sum_near_a, after(went_far_a, came_near_b), flops=AHEAD)
+    both_near_a = add(where, sum_near_a, after(went_far_a, came_near_b, noise_twin), flops=AHEAD)
     came_near_a = near(both_near_a)
     both_far_b = add(where, after(sum_far_b, both_near_a), came_last_b, always=True)
     went_far_b = across(both_far_b)

time: 224 us -> 240 us (1.071)
  local copies, waits for them, and re-layouts: 9.17 us -> 16.8 us
  waiting for transfers between devices: 66.7 us -> 71 us
    unnamed x44 -> x60, local copies, waits for them, and re-layouts: 8.59 us -> 16.2 us
    ppermute x40, waiting for transfers between devices: 66.7 us -> 71 us  [permute_devices(): return lax.ppermute(value, ('dp', 'mp'), pairs)]
  transfers between devices with their start and end apart: 40 -> 40, of which waited for: 18 -> 18; matrix products, arithmetic and copies ran while one was open for 1% -> 1% of each run, Pallas kernels for 27% -> 26%
where the time goes in v8:
time: 240 us; the launch traced here: 238 us
  starting transfers between devices  81.4 us (34%)
  waiting for transfers between devices  71 us (30%)
  Pallas kernels  67.2 us (28%)
  local copies, waits for them, and re-layouts  16.8 us (7%)
    ppermute x40, starting transfers between devices, permute_devices(): return lax.ppermute(value, ('dp', 'mp'), pairs)  81.4 us
    ppermute x40, waiting for transfers between devices, permute_devices(): return lax.ppermute(value, ('dp', 'mp'), pairs)  71 us
    pallas_call x19, Pallas kernels, call(): pl.pallas_call(kernel, out_shape=outs, in_specs=[SCALARS] + (specs or [ON...  67.2 us
    unnamed x60, local copies, waits for them, and re-layouts  16.2 us
  transfers between devices with their start and end apart: 40, of which 18 were waited for; matrix products, arithmetic and copies ran while one was open for 1% of the time, Pallas kernels for 26%

profile of v8, /device:TPU:13, one launch (start us, length us, event | category | flops | bytes accessed | tf_op | source)
XLA Modules:
  0.0 238.5 jit_solution(2916492934146487919)
XLA Ops:
  6.3 4.3 %collective-permute-start.4 = (bf16[128,2304]{1,0:T(8,128)(2,1)S(1)}, bf16[128,2304]{1,0:T(8,128)(2,1)S(1)}, u32[]{:S(2)}, u32[]{:S(2)}) collective-permute-start(bf16[128,2304]{1,0:T(8,128)(2,1)S(1)} %shard_map.158.refs_0_), channel_id=1, source_target_pairs={{0,0},{1,1},{2,4},{3,5},{4,2},{5,3},{6,6},{7,7},{8,8},{9,9},{10,12... | collective-permute-start | bytes 1769480 | tf_op jit(solution)/shard_map/ppermute | solution.py:36
  11.7 7.4 %collective-permute-done.3.refs_1_ = bf16[128,2304]{1,0:T(8,128)(2,1)S(1)} collective-permute-done((bf16[128,2304]{1,0:T(8,128)(2,1)S(1)}, bf16[128,2304]{1,0:T(8,128)(2,1)S(1)}, u32[]{:S(2)}, u32[]{:S(2)}) %collective-permute-start.3) | collective-permute-done | bytes 589856 | tf_op jit(solution)/shard_map/ppermute | solution.py:36
  19.1 3.2 %collective-permute-start.5 = (bf16[128,2304]{1,0:T(8,128)(2,1)S(1)}, bf16[128,2304]{1,0:T(8,128)(2,1)S(1)}, u32[]{:S(2)}, u32[]{:S(2)}) collective-permute-start(bf16[128,2304]{1,0:T(8,128)(2,1)S(1)} %collective-permute-done.3.refs_1_), channel_id=1, source_target_pairs={{0,0},{1,1},{2,4},{3,5},{4,2},{5,3},{6,6},{7,7},{8,8},{9,9},{10,12... | collective-permute-start | bytes 1769480 | tf_op jit(solution)/shard_map/ppermute | solution.py:36
  22.3 2.0 collective-permute-done.4.refs_0_
  25.7 11.9 %shard_map.160 = (bf16[128,2304]{1,0:T(8,128)(2,1)S(1)}, bf16[128,2304]{1,0:T(8,128)(2,1)S(1)}) custom-call(s32[6]{0:T(128)S(1)} %stack.35.where_ref, bf16[128,2304]{1,0:T(8,128)(2,1)S(1)} %shard_map.158.refs_0_, bf16[128,2304]{1,0:T(8,128)(2,1)S(1)} %collective-permute-done.3.refs_1_, bf16[2304,1152]{1,0:T(8,128)(2,1)} %refs_4_.9, ...), custom_call_target="tpu_custom_call" | custom-call | tf_op jit(solution)/shard_map/pallas_call | solution.py:169
  39.3 3.1 %collective-permute-start.8 = (bf16[128,2304]{1,0:T(8,128)(2,1)S(1)}, bf16[128,2304]{1,0:T(8,128)(2,1)S(1)}, u32[]{:S(2)}, u32[]{:S(2)}) collective-permute-start(bf16[128,2304]{1,0:T(8,128)(2,1)S(1)} %shard_map.159.refs_0_), channel_id=1, source_target_pairs={{0,0},{1,1},{2,4},{3,5},{4,2},{5,3},{6,6},{7,7},{8,8},{9,9},{10,12... | collective-permute-start | bytes 1769480 | tf_op jit(solution)/shard_map/ppermute | solution.py:36
  43.8 7.3 %shard_map.161.a_ref = bf16[128,2304]{1,0:T(8,128)(2,1)S(1)} custom-call(s32[6]{0:T(128)S(1)} %stack.35.where_ref, bf16[128,2304]{1,0:T(8,128)(2,1)S(1)} %collective-permute-done.5.refs_0_, bf16[128,2304]{1,0:T(8,128)(2,1)S(1)} %collective-permute-done.9.refs_1_, bf16[2304,1152]{1,0:T(8,128)(2,1)S(1)} %bitcast.25, ...), custom_call_target="tpu_custom_call" | custom-call | tf_op jit(solution)/shard_map/pallas_call | solution.py:169
  51.1 4.0 %collective-permute-done.8.refs_2_ = bf16[128,2304]{1,0:T(8,128)(2,1)S(1)} collective-permute-done((bf16[128,2304]{1,0:T(8,128)(2,1)S(1)}, bf16[128,2304]{1,0:T(8,128)(2,1)S(1)}, u32[]{:S(2)}, u32[]{:S(2)}) %collective-permute-start.8) | collective-permute-done | bytes 589856 | tf_op jit(solution)/shard_map/ppermute | solution.py:36
  55.2 2.7 %collective-permute-start.10 = (bf16[128,2304]{1,0:T(8,128)(2,1)S(1)}, bf16[128,2304]{1,0:T(8,128)(2,1)S(1)}, u32[]{:S(2)}, u32[]{:S(2)}) collective-permute-start(bf16[128,2304]{1,0:T(8,128)(2,1)S(1)} %collective-permute-done.7.refs_1_), channel_id=1, source_target_pairs={{0,0},{1,1},{2,4},{3,5},{4,2},{5,3},{6,6},{7,7},{8,8},{9,9},{10,12... | collective-permute-start | bytes 1769480 | tf_op jit(solution)/shard_map/ppermute | solution.py:36
  59.2 4.2 %collective-permute-start.12 = (bf16[128,2304]{1,0:T(8,128)(2,1)S(1)}, bf16[128,2304]{1,0:T(8,128)(2,1)S(1)}, u32[]{:S(2)}, u32[]{:S(2)}) collective-permute-start(bf16[128,2304]{1,0:T(8,128)(2,1)S(1)} %collective-permute-done.8.refs_2_), channel_id=1, source_target_pairs={{2,0},{3,1},{4,6},{5,7},{10,8},{11,9},{12,14},{13,15},{18,16},{19,... | collective-permute-start | bytes 1769480 | tf_op jit(solution)/shard_map/ppermute | solution.py:36
  64.1 7.3 %shard_map.162.a_ref = bf16[128,2304]{1,0:T(8,128)(2,1)S(1)} custom-call(s32[6]{0:T(128)S(1)} %copy-done.13, bf16[128,2304]{1,0:T(8,128)(2,1)S(1)} %collective-permute-done.4.refs_0_, bf16[128,2304]{1,0:T(8,128)(2,1)S(1)} %collective-permute-done.6.refs_1_, bf16[2304,1152]{1,0:T(8,128)(2,1)S(1)} %bitcast.25, ...), custom_call_target="tpu_custom_call" | custom-call | tf_op jit(solution)/shard_map/pallas_call | solution.py:169
  72.2 1.5 shard_map.163
  73.7 3.0 %collective-permute-start.15 = (bf16[128,2304]{1,0:T(8,128)(2,1)}, bf16[128,2304]{1,0:T(8,128)(2,1)}, u32[]{:S(2)}, u32[]{:S(2)}) collective-permute-start(bf16[128,2304]{1,0:T(8,128)(2,1)} %shard_map.163), channel_id=1, source_target_pairs={{0,0},{1,1},{2,4},{3,5},{4,2},{5,3},{6,6},{7,7},{8,8},{9,9},{10,12... | collective-permute-start | bytes 1769480 | tf_op jit(solution)/shard_map/ppermute | solution.py:36
  78.0 7.4 %collective-permute-start.13 = (bf16[128,2304]{1,0:T(8,128)(2,1)S(1)}, bf16[128,2304]{1,0:T(8,128)(2,1)}, u32[]{:S(2)}, u32[]{:S(2)}) collective-permute-start(bf16[128,2304]{1,0:T(8,128)(2,1)S(1)} %collective-permute-done.10.refs_0_), channel_id=1, source_target_pairs={{2,0},{3,1},{4,6},{5,7},{10,8},{11,9},{12,14},{13,15},{18,16},{19,... | collective-permute-start | bytes 1769480 | tf_op jit(solution)/shard_map/ppermute | solution.py:36
  85.5 2.5 %copy-done = bf16[2304,1152]{1,0:T(8,128)(2,1)S(1)} copy-done((bf16[2304,1152]{1,0:T(8,128)(2,1)S(1)}, bf16[2304,1152]{1,0:T(8,128)(2,1)}, u32[]{:S(2)}) %copy-start) | copy-done | bytes 5308440
  88.0 2.5 %copy-done.2 = bf16[1152,2304]{1,0:T(8,128)(2,1)S(1)} copy-done((bf16[1152,2304]{1,0:T(8,128)(2,1)S(1)}, bf16[1152,2304]{1,0:T(8,128)(2,1)}, u32[]{:S(2)}) %copy-start.2) | copy-done | bytes 5308440
  92.2 10.2 %shard_map.164 = (bf16[128,2304]{1,0:T(8,128)(2,1)S(1)}, bf16[128,2304]{1,0:T(8,128)(2,1)S(1)}) custom-call(s32[6]{0:T(128)S(1)} %copy-done.14, bf16[128,2304]{1,0:T(8,128)(2,1)S(1)} %shard_map.159.refs_0_, bf16[128,2304]{1,0:T(8,128)(2,1)S(1)} %copy-done.8, bf16[2304,1152]{1,0:T(8,128)(2,1)S(1)} %copy-done, ...), custom_call_target="tpu_custom_call" | custom-call | tf_op jit(solution)/shard_map/pallas_call | solution.py:169
  103.7 2.9 %collective-permute-start.17 = (bf16[128,2304]{1,0:T(8,128)(2,1)S(1)}, bf16[128,2304]{1,0:T(8,128)(2,1)S(1)}, u32[]{:S(2)}, u32[]{:S(2)}) collective-permute-start(bf16[128,2304]{1,0:T(8,128)(2,1)S(1)} %shard_map.165), channel_id=1, source_target_pairs={{0,0},{1,1},{2,4},{3,5},{4,2},{5,3},{6,6},{7,7},{8,8},{9,9},{10,12... | collective-permute-start | bytes 1769480 | tf_op jit(solution)/shard_map/ppermute | solution.py:36
  107.3 2.5 %copy-done.1 = bf16[2304,1152]{1,0:T(8,128)(2,1)S(1)} copy-done((bf16[2304,1152]{1,0:T(8,128)(2,1)S(1)}, bf16[2304,1152]{1,0:T(8,128)(2,1)}, u32[]{:S(2)}) %copy-start.1) | copy-done | bytes 5308440
  109.8 2.5 %copy-done.3 = bf16[1152,2304]{1,0:T(8,128)(2,1)S(1)} copy-done((bf16[1152,2304]{1,0:T(8,128)(2,1)S(1)}, bf16[1152,2304]{1,0:T(8,128)(2,1)}, u32[]{:S(2)}) %copy-start.3) | copy-done | bytes 5308440
  112.3 10.4 %shard_map.169 = (bf16[128,2304]{1,0:T(8,128)(2,1)S(1)}, bf16[128,2304]{1,0:T(8,128)(2,1)S(1)}) custom-call(s32[6]{0:T(128)S(1)} %copy-done.15, bf16[128,2304]{1,0:T(8,128)(2,1)S(1)} %collective-permute-done.10.refs_0_, bf16[128,2304]{1,0:T(8,128)(2,1)S(1)} %collective-permute-done.12.refs_1_, bf16[128,2304]{1,0:T(8,128)(2,1)S(1)} %collective-permute-done.8.refs_2_, ...), custom_call_target="tpu_custom_call" | custom-call | tf_op jit(solution)/shard_map/pallas_call | solution.py:169
  122.7 1.5 collective-permute-start.25
  124.2 4.0 %collective-permute-start.23 = (bf16[2304,512]{1,0:T(8,128)(2,1)S(1)}, bf16[2304,512]{1,0:T(8,128)(2,1)S(1)}, u32[]{:S(2)}, u32[]{:S(2)}) collective-permute-start(bf16[2304,512]{1,0:T(8,128)(2,1)S(1)} %copy-done.6), channel_id=1, source_target_pairs={{0,1},{1,0},{2,3},{3,2},{4,5},{5,4},{6,7},{7,6},{8,9},{9,8},{10,11... | collective-permute-start | bytes 7077896 | tf_op jit(solution)/shard_map/ppermute | solution.py:36
  130.8 3.4 %collective-permute-done.25.b_ref = bf16[128,2304]{1,0:T(8,128)(2,1)S(1)} collective-permute-done((bf16[128,2304]{1,0:T(8,128)(2,1)S(1)}, bf16[128,2304]{1,0:T(8,128)(2,1)S(1)}, u32[]{:S(2)}, u32[]{:S(2)}) %collective-permute-start.25) | collective-permute-done | bytes 589856 | tf_op jit(solution)/shard_map/ppermute | solution.py:36
  134.9 2.5 %collective-permute-start.26 = (bf16[128,2304]{1,0:T(8,128)(2,1)S(1)}, bf16[128,2304]{1,0:T(8,128)(2,1)S(1)}, u32[]{:S(2)}, u32[]{:S(2)}) collective-permute-start(bf16[128,2304]{1,0:T(8,128)(2,1)S(1)} %shard_map.170), channel_id=1, source_target_pairs={{0,4},{1,5},{2,6},{3,7},{4,0},{5,1},{6,2},{7,3},{8,12},{9,13},{10,... | collective-permute-start | bytes 1769480 | tf_op jit(solution)/shard_map/ppermute | solution.py:36
  137.4 5.6 %collective-permute-done.20.noise_both = f32[2,128,512]{2,1,0:T(8,128)S(1)} collective-permute-done((f32[2,128,512]{2,1,0:T(8,128)S(1)}, f32[2,128,512]{2,1,0:T(8,128)S(1)}, u32[]{:S(2)}, u32[]{:S(2)}) %collective-permute-start.20) | collective-permute-done | bytes 524320 | tf_op jit(solution)/shard_map/ppermute | solution.py:36
  143.0 9.0 %collective-permute-done.19.near_ref = bf16[128,2304]{1,0:T(8,128)(2,1)S(1)} collective-permute-done((bf16[128,2304]{1,0:T(8,128)(2,1)S(1)}, bf16[128,2304]{1,0:T(8,128)(2,1)S(1)}, u32[]{:S(2)}, u32[]{:S(2)}) %collective-permute-start.19) | collective-permute-done | bytes 589856 | tf_op jit(solution)/shard_map/ppermute | solution.py:36
  152.1 2.0 shard_map.167
  155.4 4.6 %collective-permute-done.22.came_ref = bf16[64,2304]{1,0:T(8,128)(2,1)S(1)} collective-permute-done((bf16[64,2304]{1,0:T(8,128)(2,1)S(1)}, bf16[64,2304]{1,0:T(8,128)(2,1)S(1)}, u32[]{:S(2)}, u32[]{:S(2)}) %collective-permute-start.22) | collective-permute-done | bytes 294944 | tf_op jit(solution)/shard_map/ppermute | solution.py:36
  161.0 4.4 %collective-permute-start.28 = (bf16[64,2304]{1,0:T(8,128)(2,1)S(1)}, bf16[64,2304]{1,0:T(8,128)(2,1)S(1)}, u32[]{:S(2)}, u32[]{:S(2)}) collective-permute-start(bf16[64,2304]{1,0:T(8,128)(2,1)S(1)} %shard_map.168.own_ref), channel_id=1, source_target_pairs={{0,4},{1,5},{2,6},{3,7},{4,0},{5,1},{6,2},{7,3},{8,12},{9,13},{10,... | collective-permute-start | bytes 884744 | tf_op jit(solution)/shard_map/ppermute | solution.py:36
  165.4 5.2 %collective-permute-start.24 = (bf16[32,512]{1,0:T(8,128)(2,1)S(1)}, bf16[32,512]{1,0:T(8,128)(2,1)S(1)}, u32[]{:S(2)}, u32[]{:S(2)}) collective-permute-start(bf16[32,512]{1,0:T(8,128)(2,1)S(1)} %bitcast.31), channel_id=1, source_target_pairs={{0,1},{1,0},{2,3},{3,2},{4,5},{5,4},{6,7},{7,6},{8,9},{9,8},{10,11... | collective-permute-start | bytes 98312 | tf_op jit(solution)/shard_map/ppermute | solution.py:36
  171.5 2.4 %shard_map.171 = (bf16[256,2304]{1,0:T(8,128)(2,1)}, bf16[64,2304]{1,0:T(8,128)(2,1)S(1)}, bf16[64,2304]{1,0:T(8,128)(2,1)S(1)}) custom-call(s32[6]{0:T(128)S(1)} %copy-done.15, bf16[128,2304]{1,0:T(8,128)(2,1)S(1)} %get-tuple-element.63.own_ref, bf16[128,2304]{1,0:T(8,128)(2,1)S(1)} %collective-permute-done.14.near_ref, ...), custom_call_target="tpu_custom_call" | custom-call | tf_op jit(solution)/shard_map/pallas_call | solution.py:169
  175.2 2.1 collective-permute-done.28.far_ref
  177.2 2.4 %collective-permute-start.30 = (bf16[64,2304]{1,0:T(8,128)(2,1)S(1)}, bf16[64,2304]{1,0:T(8,128)(2,1)S(1)}, u32[]{:S(2)}, u32[]{:S(2)}) collective-permute-start(bf16[64,2304]{1,0:T(8,128)(2,1)S(1)} %collective-permute-done.28.far_ref), channel_id=1, source_target_pairs={{0,2},{1,3},{2,0},{3,1},{4,6},{5,7},{6,4},{7,5},{8,10},{9,11},{10,... | collective-permute-start | bytes 884744 | tf_op jit(solution)/shard_map/ppermute | solution.py:36
  181.4 1.5 collective-permute-start.31
  182.9 5.9 %collective-permute-done.29.near_ref = bf16[64,2304]{1,0:T(8,128)(2,1)S(1)} collective-permute-done((bf16[64,2304]{1,0:T(8,128)(2,1)S(1)}, bf16[64,2304]{1,0:T(8,128)(2,1)S(1)}, u32[]{:S(2)}, u32[]{:S(2)}) %collective-permute-start.29) | collective-permute-done | bytes 294944 | tf_op jit(solution)/shard_map/ppermute | solution.py:36
  188.7 9.6 %collective-permute-done.30.last_ref = bf16[64,2304]{1,0:T(8,128)(2,1)S(1)} collective-permute-done((bf16[64,2304]{1,0:T(8,128)(2,1)S(1)}, bf16[64,2304]{1,0:T(8,128)(2,1)S(1)}, u32[]{:S(2)}, u32[]{:S(2)}) %collective-permute-start.30) | collective-permute-done | bytes 294944 | tf_op jit(solution)/shard_map/ppermute | solution.py:36
  198.3 2.6 %shard_map.173 = f32[40,256]{1,0:T(8,128)S(1)} custom-call(s32[6]{0:T(128)S(1)} %copy-done.15, bf16[64,2304]{1,0:T(8,128)(2,1)S(1)} %shard_map.168.own_ref, bf16[64,2304]{1,0:T(8,128)(2,1)S(1)} %collective-permute-done.29.near_ref, bf16[64,2304]{1,0:T(8,128)(2,1)S(1)} %collective-permute-done.28.far_ref, ...), custom_call_target="tpu_custom_call" | custom-call | flops 40000000000 | tf_op jit(solution)/shard_map/pallas_call | solution.py:169
  200.9 2.3 collective-permute-start.33
  203.3 1.4 collective-permute-done.31.near_ref
  204.7 6.3 %collective-permute-done.33.last_ref = bf16[64,2304]{1,0:T(8,128)(2,1)S(1)} collective-permute-done((bf16[64,2304]{1,0:T(8,128)(2,1)S(1)}, bf16[64,2304]{1,0:T(8,128)(2,1)S(1)}, u32[]{:S(2)}, u32[]{:S(2)}) %collective-permute-start.33) | collective-permute-done | bytes 294944 | tf_op jit(solution)/shard_map/ppermute | solution.py:36
  211.0 2.6 %shard_map.174 = f32[40,256]{1,0:T(8,128)S(1)} custom-call(s32[6]{0:T(128)S(1)} %copy-done.15, bf16[64,2304]{1,0:T(8,128)(2,1)S(1)} %shard_map.172.own_ref, bf16[64,2304]{1,0:T(8,128)(2,1)S(1)} %collective-permute-done.31.near_ref, bf16[64,2304]{1,0:T(8,128)(2,1)S(1)} %collective-permute-done.32.far_ref, ...), custom_call_target="tpu_custom_call" | custom-call | tf_op jit(solution)/shard_map/pallas_call | solution.py:169
  213.9 4.3 %collective-permute-start.35 = (f32[40,128]{1,0:T(8,128)S(1)}, f32[40,128]{1,0:T(8,128)S(1)}, u32[]{:S(2)}, u32[]{:S(2)}) collective-permute-start(f32[40,128]{1,0:T(8,128)S(1)} %pad_maximum_fusion.2), channel_id=1, source_target_pairs={{0,4},{1,5},{2,6},{3,7},{4,0},{5,1},{6,2},{7,3},{8,12},{9,13},{10,... | collective-permute-start | bytes 61448 | tf_op jit(solution)/shard_map/ppermute | solution.py:36
  219.5 1.4 collective-permute-done.34.refs_1_
  221.5 5.0 %collective-permute-start.37 = (f32[32,128]{1,0:T(8,128)S(1)}, f32[32,128]{1,0:T(8,128)S(1)}, u32[]{:S(2)}, u32[]{:S(2)}) collective-permute-start(f32[32,128]{1,0:T(8,128)S(1)} %shard_map.175), channel_id=1, source_target_pairs={{0,0},{1,2},{2,4},{3,6},{4,16},{5,18},{6,20},{7,22},{8,8},{9,10},{... | collective-permute-start | bytes 49160 | tf_op jit(solution)/shard_map/ppermute | solution.py:36
  226.5 3.5 %collective-permute-start.38 = (f32[32,128]{1,0:T(8,128)S(1)}, f32[32,128]{1,0:T(8,128)S(1)}, u32[]{:S(2)}, u32[]{:S(2)}) collective-permute-start(f32[32,128]{1,0:T(8,128)S(1)} %shard_map.175), channel_id=1, source_target_pairs={{0,1},{1,3},{2,5},{3,7},{4,17},{5,19},{6,21},{7,23},{8,9},{9,11},{... | collective-permute-start | bytes 49160 | tf_op jit(solution)/shard_map/ppermute | solution.py:36
  231.7 5.1 %collective-permute-done.39.halo_ref = f32[32,128]{1,0:T(8,128)S(1)} collective-permute-done((f32[32,128]{1,0:T(8,128)S(1)}, f32[32,128]{1,0:T(8,128)S(1)}, u32[]{:S(2)}, u32[]{:S(2)}) %collective-permute-start.39) | collective-permute-done | bytes 16416 | tf_op jit(solution)/shard_map/ppermute | solution.py:36
  236.8 1.7 shard_map.176
  (125 shorter events, 32.0 us)
Async XLA Ops:
  0.6 18.5 %collective-permute-start = (bf16[2304,1152]{1,0:T(8,128)(2,1)}, bf16[2304,1152]{1,0:T(8,128)(2,1)}, u32[]{:S(2)}, u32[]{:S(2)}) collective-permute-start(bf16[2304,1152]{1,0:T(8,128)(2,1)} %refs_4_.9), channel_id=1, source_target_pairs={{0,1},{1,0},{2,3},{3,2},{4,5},{5,4},{6,7},{7,6},{8,9},{9,8},{10,11... | collective-permute-start | bytes 15925256 | tf_op jit(solution)/shard_map/ppermute | solution.py:36
  1.4 17.7 %collective-permute-start.1 = (bf16[1152,2304]{1,0:T(8,128)(2,1)}, bf16[1152,2304]{1,0:T(8,128)(2,1)}, u32[]{:S(2)}, u32[]{:S(2)}) collective-permute-start(bf16[1152,2304]{1,0:T(8,128)(2,1)} %refs_6_.1), channel_id=1, source_target_pairs={{0,1},{1,0},{2,3},{3,2},{4,5},{5,4},{6,7},{7,6},{8,9},{9,8},{10,11... | collective-permute-start | bytes 15925256 | tf_op jit(solution)/shard_map/ppermute | solution.py:36
  3.6 40.2 %copy-start.12 = (s32[6]{0:T(128)}, s32[6]{0:T(128)S(1)}, u32[]{:S(2)}) copy-start(s32[6]{0:T(128)S(1)} %stack.35.where_ref) | copy-start | bytes 76
  4.6 14.5 %collective-permute-start.3 = (bf16[128,2304]{1,0:T(8,128)(2,1)S(1)}, bf16[128,2304]{1,0:T(8,128)(2,1)S(1)}, u32[]{:S(2)}, u32[]{:S(2)}) collective-permute-start(bf16[128,2304]{1,0:T(8,128)(2,1)S(1)} %shard_map.158.refs_0_), channel_id=1, source_target_pairs={{0,2},{1,3},{2,0},{3,1},{4,6},{5,7},{6,4},{7,5},{8,10},{9,11},{10,... | collective-permute-start | bytes 1769480 | tf_op jit(solution)/shard_map/ppermute | solution.py:36
  5.5 6.1 %collective-permute-start.2 = (f32[1,1664]{1,0:T(1,128)S(1)}, f32[1,1664]{1,0:T(1,128)S(1)}, u32[]{:S(2)}, u32[]{:S(2)}) collective-permute-start(f32[1,1664]{1,0:T(1,128)S(1)} %broadcast_in_dim.12.refs_6_.refs_8_.bias_a), channel_id=1, source_target_pairs={{0,1},{1,0},{2,3},{3,2},{4,5},{5,4},{6,7},{7,6},{8,9},{9,8},{10,11... | collective-permute-start | bytes 19976 | tf_op jit(solution)/shard_map/ppermute | solution.py:36
  6.3 18.0 %collective-permute-start.4 = (bf16[128,2304]{1,0:T(8,128)(2,1)S(1)}, bf16[128,2304]{1,0:T(8,128)(2,1)S(1)}, u32[]{:S(2)}, u32[]{:S(2)}) collective-permute-start(bf16[128,2304]{1,0:T(8,128)(2,1)S(1)} %shard_map.158.refs_0_), channel_id=1, source_target_pairs={{0,0},{1,1},{2,4},{3,5},{4,2},{5,3},{6,6},{7,7},{8,8},{9,9},{10,12... | collective-permute-start | bytes 1769480 | tf_op jit(solution)/shard_map/ppermute | solution.py:36
  10.6 33.1 %slice-start = ((s8[5308416]{0:T(1024)(128)(4,1)}), s8[4194304]{0:T(1024)(128)(4,1)S(1)}, s32[]{:S(2)}) async-start(s8[5308416]{0:T(1024)(128)(4,1)} %bitcast.24), calls=%async_computation | async-start | bytes 8388608
  10.6 33.1 %slice-start.2 = ((s8[5308416]{0:T(1024)(128)(4,1)}), s8[4194304]{0:T(1024)(128)(4,1)S(1)}, s32[]{:S(2)}) async-start(s8[5308416]{0:T(1024)(128)(4,1)} %bitcast.26), calls=%async_computation.2 | async-start | bytes 8388608
  11.6 32.2 %slice-start.1 = ((s8[5308416]{0:T(1024)(128)(4,1)}), s8[1114112]{0:T(1024)(128)(4,1)S(1)}, s32[]{:S(2)}) async-start(s8[5308416]{0:T(1024)(128)(4,1)} %bitcast.24), calls=%async_computation.1 | async-start | bytes 2228224
  11.6 32.1 %slice-start.3 = ((s8[5308416]{0:T(1024)(128)(4,1)}), s8[1114112]{0:T(1024)(128)(4,1)S(1)}, s32[]{:S(2)}) async-start(s8[5308416]{0:T(1024)(128)(4,1)} %bitcast.26), calls=%async_computation.3 | async-start | bytes 2228224
  19.1 20.1 %collective-permute-start.5 = (bf16[128,2304]{1,0:T(8,128)(2,1)S(1)}, bf16[128,2304]{1,0:T(8,128)(2,1)S(1)}, u32[]{:S(2)}, u32[]{:S(2)}) collective-permute-start(bf16[128,2304]{1,0:T(8,128)(2,1)S(1)} %collective-permute-done.3.refs_1_), channel_id=1, source_target_pairs={{0,0},{1,1},{2,4},{3,5},{4,2},{5,3},{6,6},{7,7},{8,8},{9,9},{10,12... | collective-permute-start | bytes 1769480 | tf_op jit(solution)/shard_map/ppermute | solution.py:36
  24.3 19.5 %collective-permute-start.9 = (bf16[128,2304]{1,0:T(8,128)(2,1)S(1)}, bf16[128,2304]{1,0:T(8,128)(2,1)S(1)}, u32[]{:S(2)}, u32[]{:S(2)}) collective-permute-start(bf16[128,2304]{1,0:T(8,128)(2,1)S(1)} %collective-permute-done.4.refs_0_), channel_id=1, source_target_pairs={{2,0},{3,1},{4,6},{5,7},{10,8},{11,9},{12,14},{13,15},{18,16},{19,... | collective-permute-start | bytes 1769480 | tf_op jit(solution)/shard_map/ppermute | solution.py:36
  25.6 25.5 %collective-permute-start.7 = (bf16[128,2304]{1,0:T(8,128)(2,1)S(1)}, bf16[128,2304]{1,0:T(8,128)(2,1)S(1)}, u32[]{:S(2)}, u32[]{:S(2)}) collective-permute-start(bf16[128,2304]{1,0:T(8,128)(2,1)S(1)} %shard_map.159.refs_0_), channel_id=1, source_target_pairs={{0,2},{1,3},{2,0},{3,1},{4,6},{5,7},{6,4},{7,5},{8,10},{9,11},{10,... | collective-permute-start | bytes 1769480 | tf_op jit(solution)/shard_map/ppermute | solution.py:36
  39.3 15.9 %collective-permute-start.8 = (bf16[128,2304]{1,0:T(8,128)(2,1)S(1)}, bf16[128,2304]{1,0:T(8,128)(2,1)S(1)}, u32[]{:S(2)}, u32[]{:S(2)}) collective-permute-start(bf16[128,2304]{1,0:T(8,128)(2,1)S(1)} %shard_map.159.refs_0_), channel_id=1, source_target_pairs={{0,0},{1,1},{2,4},{3,5},{4,2},{5,3},{6,6},{7,7},{8,8},{9,9},{10,12... | collective-permute-start | bytes 1769480 | tf_op jit(solution)/shard_map/ppermute | solution.py:36
  42.4 21.0 %collective-permute-start.6 = (bf16[128,2304]{1,0:T(8,128)(2,1)S(1)}, bf16[128,2304]{1,0:T(8,128)(2,1)S(1)}, u32[]{:S(2)}, u32[]{:S(2)}) collective-permute-start(bf16[128,2304]{1,0:T(8,128)(2,1)S(1)} %collective-permute-done.5.refs_0_), channel_id=1, source_target_pairs={{2,0},{3,1},{4,6},{5,7},{10,8},{11,9},{12,14},{13,15},{18,16},{19,... | collective-permute-start | bytes 1769480 | tf_op jit(solution)/shard_map/ppermute | solution.py:36
  55.2 16.2 %collective-permute-start.10 = (bf16[128,2304]{1,0:T(8,128)(2,1)S(1)}, bf16[128,2304]{1,0:T(8,128)(2,1)S(1)}, u32[]{:S(2)}, u32[]{:S(2)}) collective-permute-start(bf16[128,2304]{1,0:T(8,128)(2,1)S(1)} %collective-permute-done.7.refs_1_), channel_id=1, source_target_pairs={{0,0},{1,1},{2,4},{3,5},{4,2},{5,3},{6,6},{7,7},{8,8},{9,9},{10,12... | collective-permute-start | bytes 1769480 | tf_op jit(solution)/shard_map/ppermute | solution.py:36
  57.9 14.3 %collective-permute-start.11 = (bf16[128,2304]{1,0:T(8,128)(2,1)S(1)}, bf16[128,2304]{1,0:T(8,128)(2,1)S(1)}, u32[]{:S(2)}, u32[]{:S(2)}) collective-permute-start(bf16[128,2304]{1,0:T(8,128)(2,1)S(1)} %shard_map.161.a_ref), channel_id=1, source_target_pairs={{0,2},{1,3},{6,4},{7,5},{8,10},{9,11},{14,12},{15,13},{16,18},{17,... | collective-permute-start | bytes 1769480 | tf_op jit(solution)/shard_map/ppermute | solution.py:36
  59.2 26.3 %collective-permute-start.12 = (bf16[128,2304]{1,0:T(8,128)(2,1)S(1)}, bf16[128,2304]{1,0:T(8,128)(2,1)S(1)}, u32[]{:S(2)}, u32[]{:S(2)}) collective-permute-start(bf16[128,2304]{1,0:T(8,128)(2,1)S(1)} %collective-permute-done.8.refs_2_), channel_id=1, source_target_pairs={{2,0},{3,1},{4,6},{5,7},{10,8},{11,9},{12,14},{13,15},{18,16},{19,... | collective-permute-start | bytes 1769480 | tf_op jit(solution)/shard_map/ppermute | solution.py:36
  73.7 28.7 %collective-permute-start.15 = (bf16[128,2304]{1,0:T(8,128)(2,1)}, bf16[128,2304]{1,0:T(8,128)(2,1)}, u32[]{:S(2)}, u32[]{:S(2)}) collective-permute-start(bf16[128,2304]{1,0:T(8,128)(2,1)} %shard_map.163), channel_id=1, source_target_pairs={{0,0},{1,1},{2,4},{3,5},{4,2},{5,3},{6,6},{7,7},{8,8},{9,9},{10,12... | collective-permute-start | bytes 1769480 | tf_op jit(solution)/shard_map/ppermute | solution.py:36
  76.7 25.7 %collective-permute-start.16 = (bf16[128,2304]{1,0:T(8,128)(2,1)S(1)}, bf16[128,2304]{1,0:T(8,128)(2,1)}, u32[]{:S(2)}, u32[]{:S(2)}) collective-permute-start(bf16[128,2304]{1,0:T(8,128)(2,1)S(1)} %shard_map.162.a_ref), channel_id=1, source_target_pairs={{0,2},{1,3},{6,4},{7,5},{8,10},{9,11},{14,12},{15,13},{16,18},{17,... | collective-permute-start | bytes 1769480 | tf_op jit(solution)/shard_map/ppermute | solution.py:36
  78.0 28.6 %collective-permute-start.13 = (bf16[128,2304]{1,0:T(8,128)(2,1)S(1)}, bf16[128,2304]{1,0:T(8,128)(2,1)}, u32[]{:S(2)}, u32[]{:S(2)}) collective-permute-start(bf16[128,2304]{1,0:T(8,128)(2,1)S(1)} %collective-permute-done.10.refs_0_), channel_id=1, source_target_pairs={{2,0},{3,1},{4,6},{5,7},{10,8},{11,9},{12,14},{13,15},{18,16},{19,... | collective-permute-start | bytes 1769480 | tf_op jit(solution)/shard_map/ppermute | solution.py:36
  103.7 24.5 %collective-permute-start.17 = (bf16[128,2304]{1,0:T(8,128)(2,1)S(1)}, bf16[128,2304]{1,0:T(8,128)(2,1)S(1)}, u32[]{:S(2)}, u32[]{:S(2)}) collective-permute-start(bf16[128,2304]{1,0:T(8,128)(2,1)S(1)} %shard_map.165), channel_id=1, source_target_pairs={{0,0},{1,1},{2,4},{3,5},{4,2},{5,3},{6,6},{7,7},{8,8},{9,9},{10,12... | collective-permute-start | bytes 1769480 | tf_op jit(solution)/shard_map/ppermute | solution.py:36
  106.7 21.6 %collective-permute-start.14 = (bf16[128,2304]{1,0:T(8,128)(2,1)S(1)}, bf16[128,2304]{1,0:T(8,128)(2,1)S(1)}, u32[]{:S(2)}, u32[]{:S(2)}) collective-permute-start(bf16[128,2304]{1,0:T(8,128)(2,1)S(1)} %get-tuple-element.65), channel_id=1, source_target_pairs={{0,2},{1,3},{2,0},{3,1},{4,6},{5,7},{6,4},{7,5},{8,10},{9,11},{10,... | collective-permute-start | bytes 1769480 | tf_op jit(solution)/shard_map/ppermute | solution.py:36
  107.0 21.3 %collective-permute-start.18 = (f32[2,128,512]{2,1,0:T(8,128)S(1)}, f32[2,128,512]{2,1,0:T(8,128)S(1)}, u32[]{:S(2)}, u32[]{:S(2)}) collective-permute-start(f32[2,128,512]{2,1,0:T(8,128)S(1)} %bitcast.38), channel_id=1, source_target_pairs={{0,16},{1,17},{2,18},{3,19},{4,20},{5,21},{6,22},{7,23},{8,24},{9,... | collective-permute-start | bytes 1572872 | tf_op jit(solution)/shard_map/ppermute | solution.py:36
  122.7 11.4 %collective-permute-start.25 = (bf16[128,2304]{1,0:T(8,128)(2,1)S(1)}, bf16[128,2304]{1,0:T(8,128)(2,1)S(1)}, u32[]{:S(2)}, u32[]{:S(2)}) collective-permute-start(bf16[128,2304]{1,0:T(8,128)(2,1)S(1)} %get-tuple-element.76), channel_id=1, source_target_pairs={{0,2},{1,3},{2,0},{3,1},{4,6},{5,7},{6,4},{7,5},{8,10},{9,11},{10,... | collective-permute-start | bytes 1769480 | tf_op jit(solution)/shard_map/ppermute | solution.py:36
  124.2 47.3 %collective-permute-start.23 = (bf16[2304,512]{1,0:T(8,128)(2,1)S(1)}, bf16[2304,512]{1,0:T(8,128)(2,1)S(1)}, u32[]{:S(2)}, u32[]{:S(2)}) collective-permute-start(bf16[2304,512]{1,0:T(8,128)(2,1)S(1)} %copy-done.6), channel_id=1, source_target_pairs={{0,1},{1,0},{2,3},{3,2},{4,5},{5,4},{6,7},{7,6},{8,9},{9,8},{10,11... | collective-permute-start | bytes 7077896 | tf_op jit(solution)/shard_map/ppermute | solution.py:36
  129.0 23.0 %collective-permute-start.19 = (bf16[128,2304]{1,0:T(8,128)(2,1)S(1)}, bf16[128,2304]{1,0:T(8,128)(2,1)S(1)}, u32[]{:S(2)}, u32[]{:S(2)}) collective-permute-start(bf16[128,2304]{1,0:T(8,128)(2,1)S(1)} %shard_map.166), channel_id=1, source_target_pairs={{0,2},{1,3},{2,0},{3,1},{4,6},{5,7},{6,4},{7,5},{8,10},{9,11},{10,... | collective-permute-start | bytes 1769480 | tf_op jit(solution)/shard_map/ppermute | solution.py:36
  129.1 13.9 %collective-permute-start.20 = (f32[2,128,512]{2,1,0:T(8,128)S(1)}, f32[2,128,512]{2,1,0:T(8,128)S(1)}, u32[]{:S(2)}, u32[]{:S(2)}) collective-permute-start(f32[2,128,512]{2,1,0:T(8,128)S(1)} %bitcast.37), channel_id=1, source_target_pairs={{0,17},{1,16},{2,19},{3,18},{4,21},{5,20},{6,23},{7,22},{8,25},{9,... | collective-permute-start | bytes 1572872 | tf_op jit(solution)/shard_map/ppermute | solution.py:36
  130.3 12.7 %collective-permute-start.21 = (f32[2,128,512]{2,1,0:T(8,128)S(1)}, f32[2,128,512]{2,1,0:T(8,128)S(1)}, u32[]{:S(2)}, u32[]{:S(2)}) collective-permute-start(f32[2,128,512]{2,1,0:T(8,128)S(1)} %bitcast.36), channel_id=1, source_target_pairs={{0,1},{1,0},{2,3},{3,2},{4,5},{5,4},{6,7},{7,6},{8,9},{9,8},{10,11... | collective-permute-start | bytes 1572872 | tf_op jit(solution)/shard_map/ppermute | solution.py:36
  134.8 30.6 %copy-start.19 = (bf16[512,32]{0,1:T(8,128)(2,1)S(1)}, bf16[512,32]{0,1:T(8,128)(2,1)}, u32[]{:S(2)}) copy-start(bf16[512,32]{0,1:T(8,128)(2,1)} %param.26) | copy-start | bytes 98308
  134.9 36.7 %collective-permute-start.26 = (bf16[128,2304]{1,0:T(8,128)(2,1)S(1)}, bf16[128,2304]{1,0:T(8,128)(2,1)S(1)}, u32[]{:S(2)}, u32[]{:S(2)}) collective-permute-start(bf16[128,2304]{1,0:T(8,128)(2,1)S(1)} %shard_map.170), channel_id=1, source_target_pairs={{0,4},{1,5},{2,6},{3,7},{4,0},{5,1},{6,2},{7,3},{8,12},{9,13},{10,... | collective-permute-start | bytes 1769480 | tf_op jit(solution)/shard_map/ppermute | solution.py:36
  154.1 5.9 %collective-permute-start.22 = (bf16[64,2304]{1,0:T(8,128)(2,1)S(1)}, bf16[64,2304]{1,0:T(8,128)(2,1)S(1)}, u32[]{:S(2)}, u32[]{:S(2)}) collective-permute-start(bf16[64,2304]{1,0:T(8,128)(2,1)S(1)} %get-tuple-element.74), channel_id=1, source_target_pairs={{0,16},{1,17},{2,18},{3,19},{4,20},{5,21},{6,22},{7,23},{8,24},{9,... | collective-permute-start | bytes 884744 | tf_op jit(solution)/shard_map/ppermute | solution.py:36
  161.0 16.2 %collective-permute-start.28 = (bf16[64,2304]{1,0:T(8,128)(2,1)S(1)}, bf16[64,2304]{1,0:T(8,128)(2,1)S(1)}, u32[]{:S(2)}, u32[]{:S(2)}) collective-permute-start(bf16[64,2304]{1,0:T(8,128)(2,1)S(1)} %shard_map.168.own_ref), channel_id=1, source_target_pairs={{0,4},{1,5},{2,6},{3,7},{4,0},{5,1},{6,2},{7,3},{8,12},{9,13},{10,... | collective-permute-start | bytes 884744 | tf_op jit(solution)/shard_map/ppermute | solution.py:36
  165.4 6.1 %collective-permute-start.24 = (bf16[32,512]{1,0:T(8,128)(2,1)S(1)}, bf16[32,512]{1,0:T(8,128)(2,1)S(1)}, u32[]{:S(2)}, u32[]{:S(2)}) collective-permute-start(bf16[32,512]{1,0:T(8,128)(2,1)S(1)} %bitcast.31), channel_id=1, source_target_pairs={{0,1},{1,0},{2,3},{3,2},{4,5},{5,4},{6,7},{7,6},{8,9},{9,8},{10,11... | collective-permute-start | bytes 98312 | tf_op jit(solution)/shard_map/ppermute | solution.py:36
  173.9 5.7 %collective-permute-start.27 = (bf16[64,2304]{1,0:T(8,128)(2,1)S(1)}, bf16[64,2304]{1,0:T(8,128)(2,1)S(1)}, u32[]{:S(2)}, u32[]{:S(2)}) collective-permute-start(bf16[64,2304]{1,0:T(8,128)(2,1)S(1)} %get-tuple-element.85), channel_id=1, source_target_pairs={{0,16},{1,17},{2,18},{3,19},{4,20},{5,21},{6,22},{7,23},{8,24},{9,... | collective-permute-start | bytes 884744 | tf_op jit(solution)/shard_map/ppermute | solution.py:36
  175.2 13.6 %collective-permute-start.29 = (bf16[64,2304]{1,0:T(8,128)(2,1)S(1)}, bf16[64,2304]{1,0:T(8,128)(2,1)S(1)}, u32[]{:S(2)}, u32[]{:S(2)}) collective-permute-start(bf16[64,2304]{1,0:T(8,128)(2,1)S(1)} %shard_map.168.own_ref), channel_id=1, source_target_pairs={{0,2},{1,3},{2,0},{3,1},{4,6},{5,7},{6,4},{7,5},{8,10},{9,11},{10,... | collective-permute-start | bytes 884744 | tf_op jit(solution)/shard_map/ppermute | solution.py:36
  177.2 21.1 %collective-permute-start.30 = (bf16[64,2304]{1,0:T(8,128)(2,1)S(1)}, bf16[64,2304]{1,0:T(8,128)(2,1)S(1)}, u32[]{:S(2)}, u32[]{:S(2)}) collective-permute-start(bf16[64,2304]{1,0:T(8,128)(2,1)S(1)} %collective-permute-done.28.far_ref), channel_id=1, source_target_pairs={{0,2},{1,3},{2,0},{3,1},{4,6},{5,7},{6,4},{7,5},{8,10},{9,11},{10,... | collective-permute-start | bytes 884744 | tf_op jit(solution)/shard_map/ppermute | solution.py:36
  180.7 20.3 %collective-permute-start.32 = (bf16[64,2304]{1,0:T(8,128)(2,1)S(1)}, bf16[64,2304]{1,0:T(8,128)(2,1)S(1)}, u32[]{:S(2)}, u32[]{:S(2)}) collective-permute-start(bf16[64,2304]{1,0:T(8,128)(2,1)S(1)} %shard_map.172.own_ref), channel_id=1, source_target_pairs={{0,4},{1,5},{2,6},{3,7},{4,0},{5,1},{6,2},{7,3},{8,12},{9,13},{10,... | collective-permute-start | bytes 884744 | tf_op jit(solution)/shard_map/ppermute | solution.py:36
  181.4 23.3 %collective-permute-start.31 = (bf16[64,2304]{1,0:T(8,128)(2,1)S(1)}, bf16[64,2304]{1,0:T(8,128)(2,1)S(1)}, u32[]{:S(2)}, u32[]{:S(2)}) collective-permute-start(bf16[64,2304]{1,0:T(8,128)(2,1)S(1)} %shard_map.172.own_ref), channel_id=1, source_target_pairs={{0,2},{1,3},{2,0},{3,1},{4,6},{5,7},{6,4},{7,5},{8,10},{9,11},{10,... | collective-permute-start | bytes 884744 | tf_op jit(solution)/shard_map/ppermute | solution.py:36
  200.9 10.0 %collective-permute-start.33 = (bf16[64,2304]{1,0:T(8,128)(2,1)S(1)}, bf16[64,2304]{1,0:T(8,128)(2,1)S(1)}, u32[]{:S(2)}, u32[]{:S(2)}) collective-permute-start(bf16[64,2304]{1,0:T(8,128)(2,1)S(1)} %collective-permute-done.32.far_ref), channel_id=1, source_target_pairs={{0,2},{1,3},{2,0},{3,1},{4,6},{5,7},{6,4},{7,5},{8,10},{9,11},{10,... | collective-permute-start | bytes 884744 | tf_op jit(solution)/shard_map/ppermute | solution.py:36
  203.3 33.5 %copy-start.16 = (f32[32,32,3,3]{1,0,3,2:T(8,128)S(1)}, f32[32,32,3,3]{1,0,3,2:T(8,128)}, u32[]{:S(2)}) copy-start(f32[32,32,3,3]{1,0,3,2:T(8,128)} %param.27) | copy-start | bytes 110596
  203.3 33.5 %copy-start.20 = (f32[1,32,128]{2,1,0:T(8,128)S(1)}, f32[1,32,128]{2,1,0:T(8,128)}, u32[]{:S(2)}) copy-start(f32[1,32,128]{2,1,0:T(8,128)} %param.29) | copy-start | bytes 49156
  213.8 4.6 %collective-permute-start.36 = (f32[40,128]{1,0:T(8,128)S(1)}, f32[40,128]{1,0:T(8,128)S(1)}, u32[]{:S(2)}, u32[]{:S(2)}) collective-permute-start(f32[40,128]{1,0:T(8,128)S(1)} %pad_maximum_fusion.3), channel_id=1, source_target_pairs={{0,6},{1,7},{2,4},{3,5},{4,2},{5,3},{6,0},{7,1},{8,14},{9,15},{10,... | collective-permute-start | bytes 61448 | tf_op jit(solution)/shard_map/ppermute | solution.py:36
  213.9 5.6 %collective-permute-start.35 = (f32[40,128]{1,0:T(8,128)S(1)}, f32[40,128]{1,0:T(8,128)S(1)}, u32[]{:S(2)}, u32[]{:S(2)}) collective-permute-start(f32[40,128]{1,0:T(8,128)S(1)} %pad_maximum_fusion.2), channel_id=1, source_target_pairs={{0,4},{1,5},{2,6},{3,7},{4,0},{5,1},{6,2},{7,3},{8,12},{9,13},{10,... | collective-permute-start | bytes 61448 | tf_op jit(solution)/shard_map/ppermute | solution.py:36
  218.2 2.6 %collective-permute-start.34 = (f32[40,128]{1,0:T(8,128)S(1)}, f32[40,128]{1,0:T(8,128)S(1)}, u32[]{:S(2)}, u32[]{:S(2)}) collective-permute-start(f32[40,128]{1,0:T(8,128)S(1)} %pad_maximum_fusion.1), channel_id=1, source_target_pairs={{0,2},{1,3},{2,0},{3,1},{4,6},{5,7},{6,4},{7,5},{8,10},{9,11},{10,... | collective-permute-start | bytes 61448 | tf_op jit(solution)/shard_map/ppermute | solution.py:36
  221.5 9.9 %collective-permute-start.37 = (f32[32,128]{1,0:T(8,128)S(1)}, f32[32,128]{1,0:T(8,128)S(1)}, u32[]{:S(2)}, u32[]{:S(2)}) collective-permute-start(f32[32,128]{1,0:T(8,128)S(1)} %shard_map.175), channel_id=1, source_target_pairs={{0,0},{1,2},{2,4},{3,6},{4,16},{5,18},{6,20},{7,22},{8,8},{9,10},{... | collective-permute-start | bytes 49160 | tf_op jit(solution)/shard_map/ppermute | solution.py:36
  226.5 5.2 %collective-permute-start.38 = (f32[32,128]{1,0:T(8,128)S(1)}, f32[32,128]{1,0:T(8,128)S(1)}, u32[]{:S(2)}, u32[]{:S(2)}) collective-permute-start(f32[32,128]{1,0:T(8,128)S(1)} %shard_map.175), channel_id=1, source_target_pairs={{0,1},{1,3},{2,5},{3,7},{4,17},{5,19},{6,21},{7,23},{8,9},{9,11},{... | collective-permute-start | bytes 49160 | tf_op jit(solution)/shard_map/ppermute | solution.py:36
  229.9 6.8 %collective-permute-start.39 = (f32[32,128]{1,0:T(8,128)S(1)}, f32[32,128]{1,0:T(8,128)S(1)}, u32[]{:S(2)}, u32[]{:S(2)}) collective-permute-start(f32[32,128]{1,0:T(8,128)S(1)} %shard_map.175), channel_id=1, source_target_pairs={{1,1},{2,3},{3,5},{5,17},{6,19},{7,21},{9,9},{10,11},{11,13},{13,2... | collective-permute-start | bytes 49160 | tf_op jit(solution)/shard_map/ppermute | solution.py:36
  (22 other events, 236.1 us)

commit v9 on v8

--- a/solution.py
+++ b/solution.py
@@ -534,7 +534,11 @@
         noise_for(1 - core, upper),
         noise_for(1 - core, 1 - upper),
     )
-    up_other, down_other, bias_other, near_a, own_b = barrier((up_other, down_other, bias_other, near_a, own_b))
+    (
+        up_other, down_other, bias_other, near_a, own_b, noise_own, noise_twin, noise_core, noise_both
+    ) = barrier(
+        (up_other, down_other, bias_other, near_a, own_b, noise_own, noise_twin, noise_core, noise_both)
+    )
     panels = (up_weight, up_other, down_weight, down_other, biases, bias_other)
     far_mid_a = middle(near_a)
     near_b = near(after(own_b, near_a))

time: 240 us -> 216 us (0.900); the launches traced: 238 us -> 212 us
  local copies, waits for them, and re-layouts: 16.8 us -> 4.2 us
  waiting for transfers between devices: 71 us -> 60.9 us
    unnamed x60 -> x32, local copies, waits for them, and re-layouts: 16.2 us -> 2.12 us
    ppermute x40, waiting for transfers between devices: 71 us -> 60.9 us  [permute_devices(): return lax.ppermute(value, ('dp', 'mp'), pairs)]
  transfers between devices with their start and end apart: 40 -> 40, of which waited for: 18 -> 18; matrix products, arithmetic and copies ran while one was open for 1% -> 1% of each run, Pallas kernels for 26% -> 28%
where the time goes in v9:
time: 216 us; the launch traced here: 212 us
  starting transfers between devices  79.8 us (37%)
  Pallas kernels  64.9 us (30%)
  waiting for transfers between devices  60.9 us (28%)
  local copies, waits for them, and re-layouts  4.2 us (2%)
    ppermute x40, starting transfers between devices, permute_devices(): return lax.ppermute(value, ('dp', 'mp'), pairs)  79.8 us
    pallas_call x19, Pallas kernels, call(): pl.pallas_call(kernel, out_shape=outs, in_specs=[SCALARS] + (specs or [ON...  64.9 us
    ppermute x40, waiting for transfers between devices, permute_devices(): return lax.ppermute(value, ('dp', 'mp'), pairs)  60.9 us
  transfers between devices with their start and end apart: 40, of which 18 were waited for; matrix products, arithmetic and copies ran while one was open for 1% of the time, Pallas kernels for 28%

profile of v9, /device:TPU:13, one launch (start us, length us, event | category | flops | bytes accessed | tf_op | source)
XLA Modules:
  0.0 211.9 jit_solution(8473216132023611828)
XLA Ops:
  4.8 4.3 %collective-permute-start.4 = (bf16[128,2304]{1,0:T(8,128)(2,1)S(1)}, bf16[128,2304]{1,0:T(8,128)(2,1)S(1)}, u32[]{:S(2)}, u32[]{:S(2)}) collective-permute-start(bf16[128,2304]{1,0:T(8,128)(2,1)S(1)} %shard_map.158.refs_0_), channel_id=1, source_target_pairs={{0,0},{1,1},{2,4},{3,5},{4,2},{5,3},{6,6},{7,7},{8,8},{9,9},{10,12... | collective-permute-start | bytes 1769480 | tf_op jit(solution)/shard_map/ppermute | solution.py:36
  10.9 1.7 constant_dynamic-slice_fusion
  13.7 3.6 %collective-permute-done.2.refs_7_.refs_9_.bias_b = f32[1,1664]{1,0:T(1,128)S(1)} collective-permute-done((f32[1,1664]{1,0:T(1,128)S(1)}, f32[1,1664]{1,0:T(1,128)S(1)}, u32[]{:S(2)}, u32[]{:S(2)}) %collective-permute-start.2) | collective-permute-done | bytes 6688 | tf_op jit(solution)/shard_map/ppermute | solution.py:36
  17.4 1.8 collective-permute-done.3.refs_1_
  19.1 3.3 %collective-permute-start.5 = (bf16[128,2304]{1,0:T(8,128)(2,1)S(1)}, bf16[128,2304]{1,0:T(8,128)(2,1)S(1)}, u32[]{:S(2)}, u32[]{:S(2)}) collective-permute-start(bf16[128,2304]{1,0:T(8,128)(2,1)S(1)} %collective-permute-done.3.refs_1_), channel_id=1, source_target_pairs={{0,0},{1,1},{2,4},{3,5},{4,2},{5,3},{6,6},{7,7},{8,8},{9,9},{10,12... | collective-permute-start | bytes 1769480 | tf_op jit(solution)/shard_map/ppermute | solution.py:36
  22.5 1.3 collective-permute-start.9
  23.9 11.9 %shard_map.160 = (bf16[128,2304]{1,0:T(8,128)(2,1)S(1)}, bf16[128,2304]{1,0:T(8,128)(2,1)S(1)}) custom-call(s32[6]{0:T(128)S(1)} %stack.35.where_ref, bf16[128,2304]{1,0:T(8,128)(2,1)S(1)} %shard_map.158.refs_0_, bf16[128,2304]{1,0:T(8,128)(2,1)S(1)} %collective-permute-done.3.refs_1_, bf16[2304,1152]{1,0:T(8,128)(2,1)} %refs_4_.9, ...), custom_call_target="tpu_custom_call" | custom-call | tf_op jit(solution)/shard_map/pallas_call | solution.py:169
  35.8 2.7 %collective-permute-start.8 = (bf16[128,2304]{1,0:T(8,128)(2,1)S(1)}, bf16[128,2304]{1,0:T(8,128)(2,1)S(1)}, u32[]{:S(2)}, u32[]{:S(2)}) collective-permute-start(bf16[128,2304]{1,0:T(8,128)(2,1)S(1)} %shard_map.159.refs_0_), channel_id=1, source_target_pairs={{0,0},{1,1},{2,4},{3,5},{4,2},{5,3},{6,6},{7,7},{8,8},{9,9},{10,12... | collective-permute-start | bytes 1769480 | tf_op jit(solution)/shard_map/ppermute | solution.py:36
  38.5 1.4 collective-permute-start.6
  40.0 7.3 %shard_map.161.a_ref = bf16[128,2304]{1,0:T(8,128)(2,1)S(1)} custom-call(s32[6]{0:T(128)S(1)} %stack.35.where_ref, bf16[128,2304]{1,0:T(8,128)(2,1)S(1)} %collective-permute-done.5.refs_0_, bf16[128,2304]{1,0:T(8,128)(2,1)S(1)} %collective-permute-done.9.refs_1_, bf16[2304,1152]{1,0:T(8,128)(2,1)S(1)} %bitcast.25, ...), custom_call_target="tpu_custom_call" | custom-call | tf_op jit(solution)/shard_map/pallas_call | solution.py:169
  47.8 3.2 %collective-permute-done.8.refs_2_ = bf16[128,2304]{1,0:T(8,128)(2,1)S(1)} collective-permute-done((bf16[128,2304]{1,0:T(8,128)(2,1)S(1)}, bf16[128,2304]{1,0:T(8,128)(2,1)S(1)}, u32[]{:S(2)}, u32[]{:S(2)}) %collective-permute-start.8) | collective-permute-done | bytes 589856 | tf_op jit(solution)/shard_map/ppermute | solution.py:36
  51.0 2.6 %collective-permute-start.10 = (bf16[128,2304]{1,0:T(8,128)(2,1)S(1)}, bf16[128,2304]{1,0:T(8,128)(2,1)S(1)}, u32[]{:S(2)}, u32[]{:S(2)}) collective-permute-start(bf16[128,2304]{1,0:T(8,128)(2,1)S(1)} %collective-permute-done.7.refs_1_), channel_id=1, source_target_pairs={{0,0},{1,1},{2,4},{3,5},{4,2},{5,3},{6,6},{7,7},{8,8},{9,9},{10,12... | collective-permute-start | bytes 1769480 | tf_op jit(solution)/shard_map/ppermute | solution.py:36
  53.6 1.3 collective-permute-start.11
  54.9 4.2 %collective-permute-start.12 = (bf16[128,2304]{1,0:T(8,128)(2,1)S(1)}, bf16[128,2304]{1,0:T(8,128)(2,1)S(1)}, u32[]{:S(2)}, u32[]{:S(2)}) collective-permute-start(bf16[128,2304]{1,0:T(8,128)(2,1)S(1)} %collective-permute-done.8.refs_2_), channel_id=1, source_target_pairs={{2,0},{3,1},{4,6},{5,7},{10,8},{11,9},{12,14},{13,15},{18,16},{19,... | collective-permute-start | bytes 1769480 | tf_op jit(solution)/shard_map/ppermute | solution.py:36
  60.4 7.3 %shard_map.162.a_ref = bf16[128,2304]{1,0:T(8,128)(2,1)S(1)} custom-call(s32[6]{0:T(128)S(1)} %stack.35.where_ref, bf16[128,2304]{1,0:T(8,128)(2,1)S(1)} %collective-permute-done.4.refs_0_, bf16[128,2304]{1,0:T(8,128)(2,1)S(1)} %collective-permute-done.6.refs_1_, bf16[2304,1152]{1,0:T(8,128)(2,1)S(1)} %bitcast.25, ...), custom_call_target="tpu_custom_call" | custom-call | tf_op jit(solution)/shard_map/pallas_call | solution.py:169
  68.5 2.6 %collective-permute-start.15 = (bf16[128,2304]{1,0:T(8,128)(2,1)S(1)}, bf16[128,2304]{1,0:T(8,128)(2,1)S(1)}, u32[]{:S(2)}, u32[]{:S(2)}) collective-permute-start(bf16[128,2304]{1,0:T(8,128)(2,1)S(1)} %shard_map.163), channel_id=1, source_target_pairs={{0,0},{1,1},{2,4},{3,5},{4,2},{5,3},{6,6},{7,7},{8,8},{9,9},{10,12... | collective-permute-start | bytes 1769480 | tf_op jit(solution)/shard_map/ppermute | solution.py:36
  71.1 2.2 %collective-permute-start.13 = (bf16[128,2304]{1,0:T(8,128)(2,1)S(1)}, bf16[128,2304]{1,0:T(8,128)(2,1)S(1)}, u32[]{:S(2)}, u32[]{:S(2)}) collective-permute-start(bf16[128,2304]{1,0:T(8,128)(2,1)S(1)} %collective-permute-done.10.refs_0_), channel_id=1, source_target_pairs={{2,0},{3,1},{4,6},{5,7},{10,8},{11,9},{12,14},{13,15},{18,16},{19,... | collective-permute-start | bytes 1769480 | tf_op jit(solution)/shard_map/ppermute | solution.py:36
  73.3 1.3 collective-permute-start.16
  74.6 10.1 %shard_map.164 = (bf16[128,2304]{1,0:T(8,128)(2,1)S(1)}, bf16[128,2304]{1,0:T(8,128)(2,1)S(1)}) custom-call(s32[6]{0:T(128)S(1)} %stack.35.where_ref, bf16[128,2304]{1,0:T(8,128)(2,1)S(1)} %shard_map.159.refs_0_, bf16[128,2304]{1,0:T(8,128)(2,1)S(1)} %collective-permute-done.7.refs_1_, bf16[2304,1152]{1,0:T(8,128)(2,1)S(1)} %bitcast.25, ...), custom_call_target="tpu_custom_call" | custom-call | tf_op jit(solution)/shard_map/pallas_call | solution.py:169
  84.8 2.2 %collective-permute-start.14 = (bf16[128,2304]{1,0:T(8,128)(2,1)S(1)}, bf16[128,2304]{1,0:T(8,128)(2,1)S(1)}, u32[]{:S(2)}, u32[]{:S(2)}) collective-permute-start(bf16[128,2304]{1,0:T(8,128)(2,1)S(1)} %get-tuple-element.69), channel_id=1, source_target_pairs={{0,2},{1,3},{2,0},{3,1},{4,6},{5,7},{6,4},{7,5},{8,10},{9,11},{10,... | collective-permute-start | bytes 1769480 | tf_op jit(solution)/shard_map/ppermute | solution.py:36
  87.7 3.0 %collective-permute-start.17 = (bf16[128,2304]{1,0:T(8,128)(2,1)S(1)}, bf16[128,2304]{1,0:T(8,128)(2,1)S(1)}, u32[]{:S(2)}, u32[]{:S(2)}) collective-permute-start(bf16[128,2304]{1,0:T(8,128)(2,1)S(1)} %shard_map.165), channel_id=1, source_target_pairs={{0,0},{1,1},{2,4},{3,5},{4,2},{5,3},{6,6},{7,7},{8,8},{9,9},{10,12... | collective-permute-start | bytes 1769480 | tf_op jit(solution)/shard_map/ppermute | solution.py:36
  91.0 10.1 %shard_map.169 = (bf16[128,2304]{1,0:T(8,128)(2,1)S(1)}, bf16[128,2304]{1,0:T(8,128)(2,1)S(1)}) custom-call(s32[6]{0:T(128)S(1)} %stack.35.where_ref, bf16[128,2304]{1,0:T(8,128)(2,1)S(1)} %collective-permute-done.10.refs_0_, bf16[128,2304]{1,0:T(8,128)(2,1)S(1)} %collective-permute-done.12.refs_1_, bf16[128,2304]{1,0:T(8,128)(2,1)S(1)} %collective-permute-done.8.refs_2_, ...), custom_call_target="tpu_custom_call" | custom-call | tf_op jit(solution)/shard_map/pallas_call | solution.py:169
  101.2 6.9 %collective-permute-start.23 = (bf16[2304,512]{1,0:T(8,128)(2,1)S(1)}, bf16[2304,512]{1,0:T(8,128)(2,1)S(1)}, u32[]{:S(2)}, u32[]{:S(2)}) collective-permute-start(bf16[2304,512]{1,0:T(8,128)(2,1)S(1)} %copy-done.2), channel_id=1, source_target_pairs={{0,1},{1,0},{2,3},{3,2},{4,5},{5,4},{6,7},{7,6},{8,9},{9,8},{10,11... | collective-permute-start | bytes 7077896 | tf_op jit(solution)/shard_map/ppermute | solution.py:36
  108.8 1.7 collective-permute-start.19
  110.5 1.4 collective-permute-start.20
  113.5 11.2 %collective-permute-done.20.noise_both = f32[2,128,512]{2,1,0:T(8,128)S(1)} collective-permute-done((f32[2,128,512]{2,1,0:T(8,128)S(1)}, f32[2,128,512]{2,1,0:T(8,128)S(1)}, u32[]{:S(2)}, u32[]{:S(2)}) %collective-permute-start.20) | collective-permute-done | bytes 524320 | tf_op jit(solution)/shard_map/ppermute | solution.py:36
  124.7 5.4 %collective-permute-done.19.near_ref = bf16[128,2304]{1,0:T(8,128)(2,1)S(1)} collective-permute-done((bf16[128,2304]{1,0:T(8,128)(2,1)S(1)}, bf16[128,2304]{1,0:T(8,128)(2,1)S(1)}, u32[]{:S(2)}, u32[]{:S(2)}) %collective-permute-start.19) | collective-permute-done | bytes 589856 | tf_op jit(solution)/shard_map/ppermute | solution.py:36
  130.1 1.5 shard_map.167
  131.6 1.3 collective-permute-start.22
  132.9 4.6 %collective-permute-done.22.came_ref = bf16[64,2304]{1,0:T(8,128)(2,1)S(1)} collective-permute-done((bf16[64,2304]{1,0:T(8,128)(2,1)S(1)}, bf16[64,2304]{1,0:T(8,128)(2,1)S(1)}, u32[]{:S(2)}, u32[]{:S(2)}) %collective-permute-start.22) | collective-permute-done | bytes 294944 | tf_op jit(solution)/shard_map/ppermute | solution.py:36
  138.5 2.7 %collective-permute-start.28 = (bf16[64,2304]{1,0:T(8,128)(2,1)S(1)}, bf16[64,2304]{1,0:T(8,128)(2,1)S(1)}, u32[]{:S(2)}, u32[]{:S(2)}) collective-permute-start(bf16[64,2304]{1,0:T(8,128)(2,1)S(1)} %shard_map.168.own_ref), channel_id=1, source_target_pairs={{0,4},{1,5},{2,6},{3,7},{4,0},{5,1},{6,2},{7,3},{8,12},{9,13},{10,... | collective-permute-start | bytes 884744 | tf_op jit(solution)/shard_map/ppermute | solution.py:36
  141.2 8.0 %collective-permute-start.24 = (bf16[32,512]{1,0:T(8,128)(2,1)S(1)}, bf16[32,512]{1,0:T(8,128)(2,1)S(1)}, u32[]{:S(2)}, u32[]{:S(2)}) collective-permute-start(bf16[32,512]{1,0:T(8,128)(2,1)S(1)} %bitcast.31), channel_id=1, source_target_pairs={{0,1},{1,0},{2,3},{3,2},{4,5},{5,4},{6,7},{7,6},{8,9},{9,8},{10,11... | collective-permute-start | bytes 98312 | tf_op jit(solution)/shard_map/ppermute | solution.py:36
  150.1 2.4 %shard_map.171 = (bf16[256,2304]{1,0:T(8,128)(2,1)}, bf16[64,2304]{1,0:T(8,128)(2,1)S(1)}, bf16[64,2304]{1,0:T(8,128)(2,1)S(1)}) custom-call(s32[6]{0:T(128)S(1)} %stack.35.where_ref, bf16[128,2304]{1,0:T(8,128)(2,1)S(1)} %get-tuple-element.67.own_ref, bf16[128,2304]{1,0:T(8,128)(2,1)S(1)} %collective-permute-done.14.near_ref, ...), custom_call_target="tpu_custom_call" | custom-call | tf_op jit(solution)/shard_map/pallas_call | solution.py:169
  154.5 2.7 %collective-permute-start.30 = (bf16[64,2304]{1,0:T(8,128)(2,1)S(1)}, bf16[64,2304]{1,0:T(8,128)(2,1)S(1)}, u32[]{:S(2)}, u32[]{:S(2)}) collective-permute-start(bf16[64,2304]{1,0:T(8,128)(2,1)S(1)} %collective-permute-done.28.far_ref), channel_id=1, source_target_pairs={{0,2},{1,3},{2,0},{3,1},{4,6},{5,7},{6,4},{7,5},{8,10},{9,11},{10,... | collective-permute-start | bytes 884744 | tf_op jit(solution)/shard_map/ppermute | solution.py:36
  159.2 1.8 collective-permute-start.31
  161.0 4.5 %collective-permute-done.29.near_ref = bf16[64,2304]{1,0:T(8,128)(2,1)S(1)} collective-permute-done((bf16[64,2304]{1,0:T(8,128)(2,1)S(1)}, bf16[64,2304]{1,0:T(8,128)(2,1)S(1)}, u32[]{:S(2)}, u32[]{:S(2)}) %collective-permute-start.29) | collective-permute-done | bytes 294944 | tf_op jit(solution)/shard_map/ppermute | solution.py:36
  165.5 9.7 %collective-permute-done.30.last_ref = bf16[64,2304]{1,0:T(8,128)(2,1)S(1)} collective-permute-done((bf16[64,2304]{1,0:T(8,128)(2,1)S(1)}, bf16[64,2304]{1,0:T(8,128)(2,1)S(1)}, u32[]{:S(2)}, u32[]{:S(2)}) %collective-permute-start.30) | collective-permute-done | bytes 294944 | tf_op jit(solution)/shard_map/ppermute | solution.py:36
  175.3 2.6 %shard_map.173 = f32[40,256]{1,0:T(8,128)S(1)} custom-call(s32[6]{0:T(128)S(1)} %stack.35.where_ref, bf16[64,2304]{1,0:T(8,128)(2,1)S(1)} %shard_map.168.own_ref, bf16[64,2304]{1,0:T(8,128)(2,1)S(1)} %collective-permute-done.29.near_ref, bf16[64,2304]{1,0:T(8,128)(2,1)S(1)} %collective-permute-done.28.far_ref, ...), custom_call_target="tpu_custom_call" | custom-call | flops 40000000000 | tf_op jit(solution)/shard_map/pallas_call | solution.py:169
  177.9 2.3 %collective-permute-start.33 = (bf16[64,2304]{1,0:T(8,128)(2,1)S(1)}, bf16[64,2304]{1,0:T(8,128)(2,1)S(1)}, u32[]{:S(2)}, u32[]{:S(2)}) collective-permute-start(bf16[64,2304]{1,0:T(8,128)(2,1)S(1)} %collective-permute-done.32.far_ref), channel_id=1, source_target_pairs={{0,2},{1,3},{2,0},{3,1},{4,6},{5,7},{6,4},{7,5},{8,10},{9,11},{10,... | collective-permute-start | bytes 884744 | tf_op jit(solution)/shard_map/ppermute | solution.py:36
  180.3 1.3 collective-permute-done.31.near_ref
  181.6 6.3 %collective-permute-done.33.last_ref = bf16[64,2304]{1,0:T(8,128)(2,1)S(1)} collective-permute-done((bf16[64,2304]{1,0:T(8,128)(2,1)S(1)}, bf16[64,2304]{1,0:T(8,128)(2,1)S(1)}, u32[]{:S(2)}, u32[]{:S(2)}) %collective-permute-start.33) | collective-permute-done | bytes 294944 | tf_op jit(solution)/shard_map/ppermute | solution.py:36
  187.9 2.6 %shard_map.174 = f32[40,256]{1,0:T(8,128)S(1)} custom-call(s32[6]{0:T(128)S(1)} %stack.35.where_ref, bf16[64,2304]{1,0:T(8,128)(2,1)S(1)} %shard_map.172.own_ref, bf16[64,2304]{1,0:T(8,128)(2,1)S(1)} %collective-permute-done.31.near_ref, bf16[64,2304]{1,0:T(8,128)(2,1)S(1)} %collective-permute-done.32.far_ref, ...), custom_call_target="tpu_custom_call" | custom-call | tf_op jit(solution)/shard_map/pallas_call | solution.py:169
  190.7 2.6 %collective-permute-start.35 = (f32[40,128]{1,0:T(8,128)S(1)}, f32[40,128]{1,0:T(8,128)S(1)}, u32[]{:S(2)}, u32[]{:S(2)}) collective-permute-start(f32[40,128]{1,0:T(8,128)S(1)} %pad_maximum_fusion.2), channel_id=1, source_target_pairs={{0,4},{1,5},{2,6},{3,7},{4,0},{5,1},{6,2},{7,3},{8,12},{9,13},{10,... | collective-permute-start | bytes 61448 | tf_op jit(solution)/shard_map/ppermute | solution.py:36
  197.5 1.3 collective-permute-start.39
  198.8 6.7 %collective-permute-start.38 = (f32[32,128]{1,0:T(8,128)S(1)}, f32[32,128]{1,0:T(8,128)S(1)}, u32[]{:S(2)}, u32[]{:S(2)}) collective-permute-start(f32[32,128]{1,0:T(8,128)S(1)} %shard_map.175), channel_id=1, source_target_pairs={{0,1},{1,3},{2,5},{3,7},{4,17},{5,19},{6,21},{7,23},{8,9},{9,11},{... | collective-permute-start | bytes 49160 | tf_op jit(solution)/shard_map/ppermute | solution.py:36
  205.5 1.9 collective-permute-start.37
  207.5 2.7 %collective-permute-done.37.first_ref = f32[32,128]{1,0:T(8,128)S(1)} collective-permute-done((f32[32,128]{1,0:T(8,128)S(1)}, f32[32,128]{1,0:T(8,128)S(1)}, u32[]{:S(2)}, u32[]{:S(2)}) %collective-permute-start.37) | collective-permute-done | bytes 16416 | tf_op jit(solution)/shard_map/ppermute | solution.py:36
  210.2 1.7 shard_map.176
  (97 shorter events, 23.3 us)
Async XLA Ops:
  0.6 18.5 %collective-permute-start = (bf16[2304,1152]{1,0:T(8,128)(2,1)}, bf16[2304,1152]{1,0:T(8,128)(2,1)}, u32[]{:S(2)}, u32[]{:S(2)}) collective-permute-start(bf16[2304,1152]{1,0:T(8,128)(2,1)} %refs_4_.9), channel_id=1, source_target_pairs={{0,1},{1,0},{2,3},{3,2},{4,5},{5,4},{6,7},{7,6},{8,9},{9,8},{10,11... | collective-permute-start | bytes 15925256 | tf_op jit(solution)/shard_map/ppermute | solution.py:36
  1.4 17.8 %collective-permute-start.1 = (bf16[1152,2304]{1,0:T(8,128)(2,1)}, bf16[1152,2304]{1,0:T(8,128)(2,1)}, u32[]{:S(2)}, u32[]{:S(2)}) collective-permute-start(bf16[1152,2304]{1,0:T(8,128)(2,1)} %refs_6_.1), channel_id=1, source_target_pairs={{0,1},{1,0},{2,3},{3,2},{4,5},{5,4},{6,7},{7,6},{8,9},{9,8},{10,11... | collective-permute-start | bytes 15925256 | tf_op jit(solution)/shard_map/ppermute | solution.py:36
  4.6 14.5 %collective-permute-start.3 = (bf16[128,2304]{1,0:T(8,128)(2,1)S(1)}, bf16[128,2304]{1,0:T(8,128)(2,1)S(1)}, u32[]{:S(2)}, u32[]{:S(2)}) collective-permute-start(bf16[128,2304]{1,0:T(8,128)(2,1)S(1)} %shard_map.158.refs_0_), channel_id=1, source_target_pairs={{0,2},{1,3},{2,0},{3,1},{4,6},{5,7},{6,4},{7,5},{8,10},{9,11},{10,... | collective-permute-start | bytes 1769480 | tf_op jit(solution)/shard_map/ppermute | solution.py:36
  4.8 17.7 %collective-permute-start.4 = (bf16[128,2304]{1,0:T(8,128)(2,1)S(1)}, bf16[128,2304]{1,0:T(8,128)(2,1)S(1)}, u32[]{:S(2)}, u32[]{:S(2)}) collective-permute-start(bf16[128,2304]{1,0:T(8,128)(2,1)S(1)} %shard_map.158.refs_0_), channel_id=1, source_target_pairs={{0,0},{1,1},{2,4},{3,5},{4,2},{5,3},{6,6},{7,7},{8,8},{9,9},{10,12... | collective-permute-start | bytes 1769480 | tf_op jit(solution)/shard_map/ppermute | solution.py:36
  9.9 7.5 %collective-permute-start.2 = (f32[1,1664]{1,0:T(1,128)S(1)}, f32[1,1664]{1,0:T(1,128)S(1)}, u32[]{:S(2)}, u32[]{:S(2)}) collective-permute-start(f32[1,1664]{1,0:T(1,128)S(1)} %broadcast_in_dim.12.refs_6_.refs_8_.bias_a), channel_id=1, source_target_pairs={{0,1},{1,0},{2,3},{3,2},{4,5},{5,4},{6,7},{7,6},{8,9},{9,8},{10,11... | collective-permute-start | bytes 19976 | tf_op jit(solution)/shard_map/ppermute | solution.py:36
  12.7 27.2 %slice-start = ((s8[5308416]{0:T(1024)(128)(4,1)}), s8[4194304]{0:T(1024)(128)(4,1)S(1)}, s32[]{:S(2)}) async-start(s8[5308416]{0:T(1024)(128)(4,1)} %bitcast.24), calls=%async_computation | async-start | bytes 8388608
  12.7 27.2 %slice-start.2 = ((s8[5308416]{0:T(1024)(128)(4,1)}), s8[4194304]{0:T(1024)(128)(4,1)S(1)}, s32[]{:S(2)}) async-start(s8[5308416]{0:T(1024)(128)(4,1)} %bitcast.26), calls=%async_computation.2 | async-start | bytes 8388608
  19.1 16.7 %collective-permute-start.5 = (bf16[128,2304]{1,0:T(8,128)(2,1)S(1)}, bf16[128,2304]{1,0:T(8,128)(2,1)S(1)}, u32[]{:S(2)}, u32[]{:S(2)}) collective-permute-start(bf16[128,2304]{1,0:T(8,128)(2,1)S(1)} %collective-permute-done.3.refs_1_), channel_id=1, source_target_pairs={{0,0},{1,1},{2,4},{3,5},{4,2},{5,3},{6,6},{7,7},{8,8},{9,9},{10,12... | collective-permute-start | bytes 1769480 | tf_op jit(solution)/shard_map/ppermute | solution.py:36
  22.5 17.4 %collective-permute-start.9 = (bf16[128,2304]{1,0:T(8,128)(2,1)S(1)}, bf16[128,2304]{1,0:T(8,128)(2,1)S(1)}, u32[]{:S(2)}, u32[]{:S(2)}) collective-permute-start(bf16[128,2304]{1,0:T(8,128)(2,1)S(1)} %collective-permute-done.4.refs_0_), channel_id=1, source_target_pairs={{2,0},{3,1},{4,6},{5,7},{10,8},{11,9},{12,14},{13,15},{18,16},{19,... | collective-permute-start | bytes 1769480 | tf_op jit(solution)/shard_map/ppermute | solution.py:36
  23.8 23.9 %collective-permute-start.7 = (bf16[128,2304]{1,0:T(8,128)(2,1)S(1)}, bf16[128,2304]{1,0:T(8,128)(2,1)S(1)}, u32[]{:S(2)}, u32[]{:S(2)}) collective-permute-start(bf16[128,2304]{1,0:T(8,128)(2,1)S(1)} %shard_map.159.refs_0_), channel_id=1, source_target_pairs={{0,2},{1,3},{2,0},{3,1},{4,6},{5,7},{6,4},{7,5},{8,10},{9,11},{10,... | collective-permute-start | bytes 1769480 | tf_op jit(solution)/shard_map/ppermute | solution.py:36
  35.8 15.2 %collective-permute-start.8 = (bf16[128,2304]{1,0:T(8,128)(2,1)S(1)}, bf16[128,2304]{1,0:T(8,128)(2,1)S(1)}, u32[]{:S(2)}, u32[]{:S(2)}) collective-permute-start(bf16[128,2304]{1,0:T(8,128)(2,1)S(1)} %shard_map.159.refs_0_), channel_id=1, source_target_pairs={{0,0},{1,1},{2,4},{3,5},{4,2},{5,3},{6,6},{7,7},{8,8},{9,9},{10,12... | collective-permute-start | bytes 1769480 | tf_op jit(solution)/shard_map/ppermute | solution.py:36
  38.5 21.9 %collective-permute-start.6 = (bf16[128,2304]{1,0:T(8,128)(2,1)S(1)}, bf16[128,2304]{1,0:T(8,128)(2,1)S(1)}, u32[]{:S(2)}, u32[]{:S(2)}) collective-permute-start(bf16[128,2304]{1,0:T(8,128)(2,1)S(1)} %collective-permute-done.5.refs_0_), channel_id=1, source_target_pairs={{2,0},{3,1},{4,6},{5,7},{10,8},{11,9},{12,14},{13,15},{18,16},{19,... | collective-permute-start | bytes 1769480 | tf_op jit(solution)/shard_map/ppermute | solution.py:36
  51.0 16.7 %collective-permute-start.10 = (bf16[128,2304]{1,0:T(8,128)(2,1)S(1)}, bf16[128,2304]{1,0:T(8,128)(2,1)S(1)}, u32[]{:S(2)}, u32[]{:S(2)}) collective-permute-start(bf16[128,2304]{1,0:T(8,128)(2,1)S(1)} %collective-permute-done.7.refs_1_), channel_id=1, source_target_pairs={{0,0},{1,1},{2,4},{3,5},{4,2},{5,3},{6,6},{7,7},{8,8},{9,9},{10,12... | collective-permute-start | bytes 1769480 | tf_op jit(solution)/shard_map/ppermute | solution.py:36
  53.6 14.2 %collective-permute-start.11 = (bf16[128,2304]{1,0:T(8,128)(2,1)S(1)}, bf16[128,2304]{1,0:T(8,128)(2,1)S(1)}, u32[]{:S(2)}, u32[]{:S(2)}) collective-permute-start(bf16[128,2304]{1,0:T(8,128)(2,1)S(1)} %shard_map.161.a_ref), channel_id=1, source_target_pairs={{0,2},{1,3},{6,4},{7,5},{8,10},{9,11},{14,12},{15,13},{16,18},{17,... | collective-permute-start | bytes 1769480 | tf_op jit(solution)/shard_map/ppermute | solution.py:36
  54.9 19.7 %collective-permute-start.12 = (bf16[128,2304]{1,0:T(8,128)(2,1)S(1)}, bf16[128,2304]{1,0:T(8,128)(2,1)S(1)}, u32[]{:S(2)}, u32[]{:S(2)}) collective-permute-start(bf16[128,2304]{1,0:T(8,128)(2,1)S(1)} %collective-permute-done.8.refs_2_), channel_id=1, source_target_pairs={{2,0},{3,1},{4,6},{5,7},{10,8},{11,9},{12,14},{13,15},{18,16},{19,... | collective-permute-start | bytes 1769480 | tf_op jit(solution)/shard_map/ppermute | solution.py:36
  68.5 16.3 %collective-permute-start.15 = (bf16[128,2304]{1,0:T(8,128)(2,1)S(1)}, bf16[128,2304]{1,0:T(8,128)(2,1)S(1)}, u32[]{:S(2)}, u32[]{:S(2)}) collective-permute-start(bf16[128,2304]{1,0:T(8,128)(2,1)S(1)} %shard_map.163), channel_id=1, source_target_pairs={{0,0},{1,1},{2,4},{3,5},{4,2},{5,3},{6,6},{7,7},{8,8},{9,9},{10,12... | collective-permute-start | bytes 1769480 | tf_op jit(solution)/shard_map/ppermute | solution.py:36
  71.1 13.7 %collective-permute-start.13 = (bf16[128,2304]{1,0:T(8,128)(2,1)S(1)}, bf16[128,2304]{1,0:T(8,128)(2,1)S(1)}, u32[]{:S(2)}, u32[]{:S(2)}) collective-permute-start(bf16[128,2304]{1,0:T(8,128)(2,1)S(1)} %collective-permute-done.10.refs_0_), channel_id=1, source_target_pairs={{2,0},{3,1},{4,6},{5,7},{10,8},{11,9},{12,14},{13,15},{18,16},{19,... | collective-permute-start | bytes 1769480 | tf_op jit(solution)/shard_map/ppermute | solution.py:36
  73.3 13.6 %collective-permute-start.16 = (bf16[128,2304]{1,0:T(8,128)(2,1)S(1)}, bf16[128,2304]{1,0:T(8,128)(2,1)S(1)}, u32[]{:S(2)}, u32[]{:S(2)}) collective-permute-start(bf16[128,2304]{1,0:T(8,128)(2,1)S(1)} %shard_map.162.a_ref), channel_id=1, source_target_pairs={{0,2},{1,3},{6,4},{7,5},{8,10},{9,11},{14,12},{15,13},{16,18},{17,... | collective-permute-start | bytes 1769480 | tf_op jit(solution)/shard_map/ppermute | solution.py:36
  84.8 23.3 %collective-permute-start.14 = (bf16[128,2304]{1,0:T(8,128)(2,1)S(1)}, bf16[128,2304]{1,0:T(8,128)(2,1)S(1)}, u32[]{:S(2)}, u32[]{:S(2)}) collective-permute-start(bf16[128,2304]{1,0:T(8,128)(2,1)S(1)} %get-tuple-element.69), channel_id=1, source_target_pairs={{0,2},{1,3},{2,0},{3,1},{4,6},{5,7},{6,4},{7,5},{8,10},{9,11},{10,... | collective-permute-start | bytes 1769480 | tf_op jit(solution)/shard_map/ppermute | solution.py:36
  87.7 20.4 %collective-permute-start.17 = (bf16[128,2304]{1,0:T(8,128)(2,1)S(1)}, bf16[128,2304]{1,0:T(8,128)(2,1)S(1)}, u32[]{:S(2)}, u32[]{:S(2)}) collective-permute-start(bf16[128,2304]{1,0:T(8,128)(2,1)S(1)} %shard_map.165), channel_id=1, source_target_pairs={{0,0},{1,1},{2,4},{3,5},{4,2},{5,3},{6,6},{7,7},{8,8},{9,9},{10,12... | collective-permute-start | bytes 1769480 | tf_op jit(solution)/shard_map/ppermute | solution.py:36
  90.7 17.4 %collective-permute-start.18 = (f32[2,128,512]{2,1,0:T(8,128)S(1)}, f32[2,128,512]{2,1,0:T(8,128)S(1)}, u32[]{:S(2)}, u32[]{:S(2)}) collective-permute-start(f32[2,128,512]{2,1,0:T(8,128)S(1)} %bitcast.38), channel_id=1, source_target_pairs={{0,16},{1,17},{2,18},{3,19},{4,20},{5,21},{6,22},{7,23},{8,24},{9,... | collective-permute-start | bytes 1572872 | tf_op jit(solution)/shard_map/ppermute | solution.py:36
  101.1 29.0 %copy-start.3 = (f32[2,2,2304]{2,1,0:T(2,128)S(1)}, f32[2,2,2304]{2,1,0:T(2,128)}, u32[]{:S(2)}) copy-start(f32[2,2,2304]{2,1,0:T(2,128)} %ada_ref.11) | copy-start | bytes 110596
  101.1 29.0 %copy-start.7 = (f32[2,2304]{1,0:T(2,128)S(1)}, f32[2,2304]{1,0:T(2,128)}, u32[]{:S(2)}) copy-start(f32[2,2304]{1,0:T(2,128)} %gate_ref.3) | copy-start | bytes 55300
  101.1 11.1 %collective-permute-start.25 = (bf16[128,2304]{1,0:T(8,128)(2,1)S(1)}, bf16[128,2304]{1,0:T(8,128)(2,1)S(1)}, u32[]{:S(2)}, u32[]{:S(2)}) collective-permute-start(bf16[128,2304]{1,0:T(8,128)(2,1)S(1)} %get-tuple-element.83), channel_id=1, source_target_pairs={{0,2},{1,3},{2,0},{3,1},{4,6},{5,7},{6,4},{7,5},{8,10},{9,11},{10,... | collective-permute-start | bytes 1769480 | tf_op jit(solution)/shard_map/ppermute | solution.py:36
  101.2 48.9 %collective-permute-start.23 = (bf16[2304,512]{1,0:T(8,128)(2,1)S(1)}, bf16[2304,512]{1,0:T(8,128)(2,1)S(1)}, u32[]{:S(2)}, u32[]{:S(2)}) collective-permute-start(bf16[2304,512]{1,0:T(8,128)(2,1)S(1)} %copy-done.2), channel_id=1, source_target_pairs={{0,1},{1,0},{2,3},{3,2},{4,5},{5,4},{6,7},{7,6},{8,9},{9,8},{10,11... | collective-permute-start | bytes 7077896 | tf_op jit(solution)/shard_map/ppermute | solution.py:36
  108.8 21.3 %collective-permute-start.19 = (bf16[128,2304]{1,0:T(8,128)(2,1)S(1)}, bf16[128,2304]{1,0:T(8,128)(2,1)S(1)}, u32[]{:S(2)}, u32[]{:S(2)}) collective-permute-start(bf16[128,2304]{1,0:T(8,128)(2,1)S(1)} %shard_map.166), channel_id=1, source_target_pairs={{0,2},{1,3},{2,0},{3,1},{4,6},{5,7},{6,4},{7,5},{8,10},{9,11},{10,... | collective-permute-start | bytes 1769480 | tf_op jit(solution)/shard_map/ppermute | solution.py:36
  110.5 14.1 %collective-permute-start.20 = (f32[2,128,512]{2,1,0:T(8,128)S(1)}, f32[2,128,512]{2,1,0:T(8,128)S(1)}, u32[]{:S(2)}, u32[]{:S(2)}) collective-permute-start(f32[2,128,512]{2,1,0:T(8,128)S(1)} %bitcast.37), channel_id=1, source_target_pairs={{0,17},{1,16},{2,19},{3,18},{4,21},{5,20},{6,23},{7,22},{8,25},{9,... | collective-permute-start | bytes 1572872 | tf_op jit(solution)/shard_map/ppermute | solution.py:36
  112.0 12.7 %collective-permute-start.21 = (f32[2,128,512]{2,1,0:T(8,128)S(1)}, f32[2,128,512]{2,1,0:T(8,128)S(1)}, u32[]{:S(2)}, u32[]{:S(2)}) collective-permute-start(f32[2,128,512]{2,1,0:T(8,128)S(1)} %bitcast.36), channel_id=1, source_target_pairs={{0,1},{1,0},{2,3},{3,2},{4,5},{5,4},{6,7},{7,6},{8,9},{9,8},{10,11... | collective-permute-start | bytes 1572872 | tf_op jit(solution)/shard_map/ppermute | solution.py:36
  112.9 28.4 %copy-start.8 = (bf16[512,32]{0,1:T(8,128)(2,1)S(1)}, bf16[512,32]{0,1:T(8,128)(2,1)}, u32[]{:S(2)}) copy-start(bf16[512,32]{0,1:T(8,128)(2,1)} %param.26) | copy-start | bytes 98308
  112.9 37.2 %collective-permute-start.26 = (bf16[128,2304]{1,0:T(8,128)(2,1)S(1)}, bf16[128,2304]{1,0:T(8,128)(2,1)S(1)}, u32[]{:S(2)}, u32[]{:S(2)}) collective-permute-start(bf16[128,2304]{1,0:T(8,128)(2,1)S(1)} %shard_map.170), channel_id=1, source_target_pairs={{0,4},{1,5},{2,6},{3,7},{4,0},{5,1},{6,2},{7,3},{8,12},{9,13},{10,... | collective-permute-start | bytes 1769480 | tf_op jit(solution)/shard_map/ppermute | solution.py:36
  131.6 5.9 %collective-permute-start.22 = (bf16[64,2304]{1,0:T(8,128)(2,1)S(1)}, bf16[64,2304]{1,0:T(8,128)(2,1)S(1)}, u32[]{:S(2)}, u32[]{:S(2)}) collective-permute-start(bf16[64,2304]{1,0:T(8,128)(2,1)S(1)} %get-tuple-element.81), channel_id=1, source_target_pairs={{0,16},{1,17},{2,18},{3,19},{4,20},{5,21},{6,22},{7,23},{8,24},{9,... | collective-permute-start | bytes 884744 | tf_op jit(solution)/shard_map/ppermute | solution.py:36
  138.5 16.0 %collective-permute-start.28 = (bf16[64,2304]{1,0:T(8,128)(2,1)S(1)}, bf16[64,2304]{1,0:T(8,128)(2,1)S(1)}, u32[]{:S(2)}, u32[]{:S(2)}) collective-permute-start(bf16[64,2304]{1,0:T(8,128)(2,1)S(1)} %shard_map.168.own_ref), channel_id=1, source_target_pairs={{0,4},{1,5},{2,6},{3,7},{4,0},{5,1},{6,2},{7,3},{8,12},{9,13},{10,... | collective-permute-start | bytes 884744 | tf_op jit(solution)/shard_map/ppermute | solution.py:36
  141.2 8.8 %collective-permute-start.24 = (bf16[32,512]{1,0:T(8,128)(2,1)S(1)}, bf16[32,512]{1,0:T(8,128)(2,1)S(1)}, u32[]{:S(2)}, u32[]{:S(2)}) collective-permute-start(bf16[32,512]{1,0:T(8,128)(2,1)S(1)} %bitcast.31), channel_id=1, source_target_pairs={{0,1},{1,0},{2,3},{3,2},{4,5},{5,4},{6,7},{7,6},{8,9},{9,8},{10,11... | collective-permute-start | bytes 98312 | tf_op jit(solution)/shard_map/ppermute | solution.py:36
  152.5 5.6 %collective-permute-start.27 = (bf16[64,2304]{1,0:T(8,128)(2,1)S(1)}, bf16[64,2304]{1,0:T(8,128)(2,1)S(1)}, u32[]{:S(2)}, u32[]{:S(2)}) collective-permute-start(bf16[64,2304]{1,0:T(8,128)(2,1)S(1)} %get-tuple-element.92), channel_id=1, source_target_pairs={{0,16},{1,17},{2,18},{3,19},{4,20},{5,21},{6,22},{7,23},{8,24},{9,... | collective-permute-start | bytes 884744 | tf_op jit(solution)/shard_map/ppermute | solution.py:36
  153.7 11.8 %collective-permute-start.29 = (bf16[64,2304]{1,0:T(8,128)(2,1)S(1)}, bf16[64,2304]{1,0:T(8,128)(2,1)S(1)}, u32[]{:S(2)}, u32[]{:S(2)}) collective-permute-start(bf16[64,2304]{1,0:T(8,128)(2,1)S(1)} %shard_map.168.own_ref), channel_id=1, source_target_pairs={{0,2},{1,3},{2,0},{3,1},{4,6},{5,7},{6,4},{7,5},{8,10},{9,11},{10,... | collective-permute-start | bytes 884744 | tf_op jit(solution)/shard_map/ppermute | solution.py:36
  154.5 20.7 %collective-permute-start.30 = (bf16[64,2304]{1,0:T(8,128)(2,1)S(1)}, bf16[64,2304]{1,0:T(8,128)(2,1)S(1)}, u32[]{:S(2)}, u32[]{:S(2)}) collective-permute-start(bf16[64,2304]{1,0:T(8,128)(2,1)S(1)} %collective-permute-done.28.far_ref), channel_id=1, source_target_pairs={{0,2},{1,3},{2,0},{3,1},{4,6},{5,7},{6,4},{7,5},{8,10},{9,11},{10,... | collective-permute-start | bytes 884744 | tf_op jit(solution)/shard_map/ppermute | solution.py:36
  159.0 18.9 %collective-permute-start.32 = (bf16[64,2304]{1,0:T(8,128)(2,1)S(1)}, bf16[64,2304]{1,0:T(8,128)(2,1)S(1)}, u32[]{:S(2)}, u32[]{:S(2)}) collective-permute-start(bf16[64,2304]{1,0:T(8,128)(2,1)S(1)} %shard_map.172.own_ref), channel_id=1, source_target_pairs={{0,4},{1,5},{2,6},{3,7},{4,0},{5,1},{6,2},{7,3},{8,12},{9,13},{10,... | collective-permute-start | bytes 884744 | tf_op jit(solution)/shard_map/ppermute | solution.py:36
  159.2 22.4 %collective-permute-start.31 = (bf16[64,2304]{1,0:T(8,128)(2,1)S(1)}, bf16[64,2304]{1,0:T(8,128)(2,1)S(1)}, u32[]{:S(2)}, u32[]{:S(2)}) collective-permute-start(bf16[64,2304]{1,0:T(8,128)(2,1)S(1)} %shard_map.172.own_ref), channel_id=1, source_target_pairs={{0,2},{1,3},{2,0},{3,1},{4,6},{5,7},{6,4},{7,5},{8,10},{9,11},{10,... | collective-permute-start | bytes 884744 | tf_op jit(solution)/shard_map/ppermute | solution.py:36
  177.9 10.0 %collective-permute-start.33 = (bf16[64,2304]{1,0:T(8,128)(2,1)S(1)}, bf16[64,2304]{1,0:T(8,128)(2,1)S(1)}, u32[]{:S(2)}, u32[]{:S(2)}) collective-permute-start(bf16[64,2304]{1,0:T(8,128)(2,1)S(1)} %collective-permute-done.32.far_ref), channel_id=1, source_target_pairs={{0,2},{1,3},{2,0},{3,1},{4,6},{5,7},{6,4},{7,5},{8,10},{9,11},{10,... | collective-permute-start | bytes 884744 | tf_op jit(solution)/shard_map/ppermute | solution.py:36
  180.2 27.2 %copy-start.11 = (f32[32]{0:T(128)S(1)}, f32[32]{0:T(128)}, u32[]{:S(2)}) copy-start(f32[32]{0:T(128)} %param.28) | copy-start | bytes 388
  180.2 30.0 %copy-start.4 = (f32[32,32,3,3]{1,0,3,2:T(8,128)S(1)}, f32[32,32,3,3]{1,0,3,2:T(8,128)}, u32[]{:S(2)}) copy-start(f32[32,32,3,3]{1,0,3,2:T(8,128)} %param.27) | copy-start | bytes 110596
  180.2 30.0 %copy-start.9 = (f32[1,32,128]{2,1,0:T(8,128)S(1)}, f32[1,32,128]{2,1,0:T(8,128)}, u32[]{:S(2)}) copy-start(f32[1,32,128]{2,1,0:T(8,128)} %param.29) | copy-start | bytes 49156
  190.7 4.1 %collective-permute-start.35 = (f32[40,128]{1,0:T(8,128)S(1)}, f32[40,128]{1,0:T(8,128)S(1)}, u32[]{:S(2)}, u32[]{:S(2)}) collective-permute-start(f32[40,128]{1,0:T(8,128)S(1)} %pad_maximum_fusion.2), channel_id=1, source_target_pairs={{0,4},{1,5},{2,6},{3,7},{4,0},{5,1},{6,2},{7,3},{8,12},{9,13},{10,... | collective-permute-start | bytes 61448 | tf_op jit(solution)/shard_map/ppermute | solution.py:36
  193.4 2.6 %collective-permute-start.36 = (f32[40,128]{1,0:T(8,128)S(1)}, f32[40,128]{1,0:T(8,128)S(1)}, u32[]{:S(2)}, u32[]{:S(2)}) collective-permute-start(f32[40,128]{1,0:T(8,128)S(1)} %pad_maximum_fusion.3), channel_id=1, source_target_pairs={{0,6},{1,7},{2,4},{3,5},{4,2},{5,3},{6,0},{7,1},{8,14},{9,15},{10,... | collective-permute-start | bytes 61448 | tf_op jit(solution)/shard_map/ppermute | solution.py:36
  194.2 2.6 %collective-permute-start.34 = (f32[40,128]{1,0:T(8,128)S(1)}, f32[40,128]{1,0:T(8,128)S(1)}, u32[]{:S(2)}, u32[]{:S(2)}) collective-permute-start(f32[40,128]{1,0:T(8,128)S(1)} %pad_maximum_fusion.1), channel_id=1, source_target_pairs={{0,2},{1,3},{2,0},{3,1},{4,6},{5,7},{6,4},{7,5},{8,10},{9,11},{10,... | collective-permute-start | bytes 61448 | tf_op jit(solution)/shard_map/ppermute | solution.py:36
  197.5 10.0 %collective-permute-start.39 = (f32[32,128]{1,0:T(8,128)S(1)}, f32[32,128]{1,0:T(8,128)S(1)}, u32[]{:S(2)}, u32[]{:S(2)}) collective-permute-start(f32[32,128]{1,0:T(8,128)S(1)} %shard_map.175), channel_id=1, source_target_pairs={{1,1},{2,3},{3,5},{5,17},{6,19},{7,21},{9,9},{10,11},{11,13},{13,2... | collective-permute-start | bytes 49160 | tf_op jit(solution)/shard_map/ppermute | solution.py:36
  198.8 8.7 %collective-permute-start.38 = (f32[32,128]{1,0:T(8,128)S(1)}, f32[32,128]{1,0:T(8,128)S(1)}, u32[]{:S(2)}, u32[]{:S(2)}) collective-permute-start(f32[32,128]{1,0:T(8,128)S(1)} %shard_map.175), channel_id=1, source_target_pairs={{0,1},{1,3},{2,5},{3,7},{4,17},{5,19},{6,21},{7,23},{8,9},{9,11},{... | collective-permute-start | bytes 49160 | tf_op jit(solution)/shard_map/ppermute | solution.py:36
  205.5 4.8 %collective-permute-start.37 = (f32[32,128]{1,0:T(8,128)S(1)}, f32[32,128]{1,0:T(8,128)S(1)}, u32[]{:S(2)}, u32[]{:S(2)}) collective-permute-start(f32[32,128]{1,0:T(8,128)S(1)} %shard_map.175), channel_id=1, source_target_pairs={{0,0},{1,2},{2,4},{3,6},{4,16},{5,18},{6,20},{7,22},{8,8},{9,10},{... | collective-permute-start | bytes 49160 | tf_op jit(solution)/shard_map/ppermute | solution.py:36
  (8 other events, 85.8 us)

commit v10 on v9

--- a/solution.py
+++ b/solution.py
@@ -162,7 +162,7 @@
 ON_CHIP = pl.BlockSpec(memory_space=pltpu.VMEM)
 VMEM_LIMIT = 16 * 1024 * 1024
 AHEAD = 40_000_000_000
-MID, UPPER, IMAGE, ODD, SAME, CORE = range(6)
+MID, UPPER, IMAGE, ODD, SAME, CORE, FIRST, LAST = range(8)
 
 
 def call(kernel, where, args, outs, scratch=(), flops=0, specs=None, limit=VMEM_LIMIT):
@@ -422,8 +422,10 @@
         jnp.where(lane < half, lower, shift(higher, half)),
         jnp.where(lane < half, shift(lower, half), higher),
     )
-    above = jnp.where(early, shift(halo, SIDE), shift(higher, SIDE - half))
-    below = jnp.where(early, shift(lower, half - SIDE), shift(halo, -SIDE))
+    before = jnp.where(where_ref[FIRST] == 1, 0.0, shift(halo, SIDE))
+    behind = jnp.where(where_ref[LAST] == 1, 0.0, shift(halo, -SIDE))
+    above = jnp.where(early, before, shift(higher, SIDE - half))
+    below = jnp.where(early, shift(lower, half - SIDE), behind)
     rows = (
         jnp.where(lane < SIDE, above, shift(centre, SIDE)),
         centre,
@@ -473,6 +475,8 @@
             z_index % 2,
             z_index // 2 == upper,
             core,
+            z_index == 0,
+            z_index == mp // 2 - 1,
         ]
     ).astype(jnp.int32)
 
@@ -572,9 +576,9 @@
     code_other = swap_cores(after(codes, sum_last_b))
     came_near_b = near(after(sum_near_b, last_end_b))
     both_near_a = add(where, sum_near_a, after(went_far_a, came_near_b, noise_twin), flops=AHEAD)
-    came_near_a = near(both_near_a)
     both_far_b = add(where, after(sum_far_b, both_near_a), came_last_b, always=True)
     went_far_b = across(both_far_b)
+    came_near_a = near(after(both_near_a, both_far_b))
     out_a, kept_a, sent_a = block_rows(
         where, 0, False, sum_own_a, after(came_near_a, noise_both, noise_core), went_last_a, tokens, gate, bias_out, ada_head
     )
@@ -610,9 +614,7 @@
     def to_halo(d, m):
         y, x = d // half_dp, d % half_dp
         z, c = m // 2, m % 2
-        block = 2 * (z % 2) + c + (1 if y == 1 else -1)
-        if block < 0 or block > 3:
-            return None
+        block = (2 * (z % 2) + c + (1 if y == 1 else -1)) % 4
         return ((z // 2) * half_dp + x, 2 * block + (0 if y == 1 else 1))
 
     first = permute_devices(soft, dp, mp, lambda d, m: to_cells(d, m, lambda y: y))

time: 216 us -> 220 us (1.019); the launches traced: 212 us -> 220 us
  waiting for transfers between devices: 60.9 us -> 68.6 us
    ppermute x40, waiting for transfers between devices: 60.9 us -> 68.6 us  [permute_devices(): return lax.ppermute(value, ('dp', 'mp'), pairs)]
  transfers between devices with their start and end apart: 40 -> 40, of which waited for: 18 -> 18; matrix products, arithmetic and copies ran while one was open for 1% -> 1% of each run, Pallas kernels for 28% -> 27%
where the time goes in v10:
time: 220 us
  starting transfers between devices  79.9 us (36%)
  waiting for transfers between devices  68.6 us (31%)
  Pallas kernels  64.9 us (30%)
  local copies, waits for them, and re-layouts  4.2 us (2%)
    ppermute x40, starting transfers between devices, permute_devices(): return lax.ppermute(value, ('dp', 'mp'), pairs)  79.9 us
    ppermute x40, waiting for transfers between devices, permute_devices(): return lax.ppermute(value, ('dp', 'mp'), pairs)  68.6 us
    pallas_call x19, Pallas kernels, call(): pl.pallas_call(kernel, out_shape=outs, in_specs=[SCALARS] + (specs or [ON...  64.9 us
  transfers between devices with their start and end apart: 40, of which 18 were waited for; matrix products, arithmetic and copies ran while one was open for 1% of the time, Pallas kernels for 27%

profile of v10, /device:TPU:13, one launch (start us, length us, event | category | flops | bytes accessed | tf_op | source)
XLA Modules:
  0.0 219.8 jit_solution(433253054223361966)
XLA Ops:
  4.8 4.3 %collective-permute-start.4 = (bf16[128,2304]{1,0:T(8,128)(2,1)S(1)}, bf16[128,2304]{1,0:T(8,128)(2,1)S(1)}, u32[]{:S(2)}, u32[]{:S(2)}) collective-permute-start(bf16[128,2304]{1,0:T(8,128)(2,1)S(1)} %shard_map.158.refs_0_), channel_id=1, source_target_pairs={{0,0},{1,1},{2,4},{3,5},{4,2},{5,3},{6,6},{7,7},{8,8},{9,9},{10,12... | collective-permute-start | bytes 1769480 | tf_op jit(solution)/shard_map/ppermute | solution.py:36
  10.9 1.7 constant_dynamic-slice_fusion
  13.7 3.6 %collective-permute-done.2.refs_7_.refs_9_.bias_b = f32[1,1664]{1,0:T(1,128)S(1)} collective-permute-done((f32[1,1664]{1,0:T(1,128)S(1)}, f32[1,1664]{1,0:T(1,128)S(1)}, u32[]{:S(2)}, u32[]{:S(2)}) %collective-permute-start.2) | collective-permute-done | bytes 6688 | tf_op jit(solution)/shard_map/ppermute | solution.py:36
  17.4 1.8 collective-permute-done.3.refs_1_
  19.2 3.3 %collective-permute-start.5 = (bf16[128,2304]{1,0:T(8,128)(2,1)S(1)}, bf16[128,2304]{1,0:T(8,128)(2,1)S(1)}, u32[]{:S(2)}, u32[]{:S(2)}) collective-permute-start(bf16[128,2304]{1,0:T(8,128)(2,1)S(1)} %collective-permute-done.3.refs_1_), channel_id=1, source_target_pairs={{0,0},{1,1},{2,4},{3,5},{4,2},{5,3},{6,6},{7,7},{8,8},{9,9},{10,12... | collective-permute-start | bytes 1769480 | tf_op jit(solution)/shard_map/ppermute | solution.py:36
  22.5 1.3 collective-permute-start.9
  23.9 11.9 %shard_map.160 = (bf16[128,2304]{1,0:T(8,128)(2,1)S(1)}, bf16[128,2304]{1,0:T(8,128)(2,1)S(1)}) custom-call(s32[8]{0:T(128)S(1)} %stack.51.where_ref, bf16[128,2304]{1,0:T(8,128)(2,1)S(1)} %shard_map.158.refs_0_, bf16[128,2304]{1,0:T(8,128)(2,1)S(1)} %collective-permute-done.3.refs_1_, bf16[2304,1152]{1,0:T(8,128)(2,1)} %refs_4_.9, ...), custom_call_target="tpu_custom_call" | custom-call | tf_op jit(solution)/shard_map/pallas_call | solution.py:169
  35.8 2.7 %collective-permute-start.8 = (bf16[128,2304]{1,0:T(8,128)(2,1)S(1)}, bf16[128,2304]{1,0:T(8,128)(2,1)S(1)}, u32[]{:S(2)}, u32[]{:S(2)}) collective-permute-start(bf16[128,2304]{1,0:T(8,128)(2,1)S(1)} %shard_map.159.refs_0_), channel_id=1, source_target_pairs={{0,0},{1,1},{2,4},{3,5},{4,2},{5,3},{6,6},{7,7},{8,8},{9,9},{10,12... | collective-permute-start | bytes 1769480 | tf_op jit(solution)/shard_map/ppermute | solution.py:36
  38.5 1.4 collective-permute-start.6
  40.0 7.3 %shard_map.161.a_ref = bf16[128,2304]{1,0:T(8,128)(2,1)S(1)} custom-call(s32[8]{0:T(128)S(1)} %stack.51.where_ref, bf16[128,2304]{1,0:T(8,128)(2,1)S(1)} %collective-permute-done.5.refs_0_, bf16[128,2304]{1,0:T(8,128)(2,1)S(1)} %collective-permute-done.9.refs_1_, bf16[2304,1152]{1,0:T(8,128)(2,1)S(1)} %bitcast.27, ...), custom_call_target="tpu_custom_call" | custom-call | tf_op jit(solution)/shard_map/pallas_call | solution.py:169
  47.8 3.2 %collective-permute-done.8.refs_2_ = bf16[128,2304]{1,0:T(8,128)(2,1)S(1)} collective-permute-done((bf16[128,2304]{1,0:T(8,128)(2,1)S(1)}, bf16[128,2304]{1,0:T(8,128)(2,1)S(1)}, u32[]{:S(2)}, u32[]{:S(2)}) %collective-permute-start.8) | collective-permute-done | bytes 589856 | tf_op jit(solution)/shard_map/ppermute | solution.py:36
  51.0 2.6 %collective-permute-start.10 = (bf16[128,2304]{1,0:T(8,128)(2,1)S(1)}, bf16[128,2304]{1,0:T(8,128)(2,1)S(1)}, u32[]{:S(2)}, u32[]{:S(2)}) collective-permute-start(bf16[128,2304]{1,0:T(8,128)(2,1)S(1)} %collective-permute-done.7.refs_1_), channel_id=1, source_target_pairs={{0,0},{1,1},{2,4},{3,5},{4,2},{5,3},{6,6},{7,7},{8,8},{9,9},{10,12... | collective-permute-start | bytes 1769480 | tf_op jit(solution)/shard_map/ppermute | solution.py:36
  54.9 4.2 %collective-permute-start.12 = (bf16[128,2304]{1,0:T(8,128)(2,1)S(1)}, bf16[128,2304]{1,0:T(8,128)(2,1)S(1)}, u32[]{:S(2)}, u32[]{:S(2)}) collective-permute-start(bf16[128,2304]{1,0:T(8,128)(2,1)S(1)} %collective-permute-done.8.refs_2_), channel_id=1, source_target_pairs={{2,0},{3,1},{4,6},{5,7},{10,8},{11,9},{12,14},{13,15},{18,16},{19,... | collective-permute-start | bytes 1769480 | tf_op jit(solution)/shard_map/ppermute | solution.py:36
  59.1 1.3 collective-permute-done.6.refs_1_
  60.4 7.3 %shard_map.162.a_ref = bf16[128,2304]{1,0:T(8,128)(2,1)S(1)} custom-call(s32[8]{0:T(128)S(1)} %stack.51.where_ref, bf16[128,2304]{1,0:T(8,128)(2,1)S(1)} %collective-permute-done.4.refs_0_, bf16[128,2304]{1,0:T(8,128)(2,1)S(1)} %collective-permute-done.6.refs_1_, bf16[2304,1152]{1,0:T(8,128)(2,1)S(1)} %bitcast.27, ...), custom_call_target="tpu_custom_call" | custom-call | tf_op jit(solution)/shard_map/pallas_call | solution.py:169
  68.5 2.6 %collective-permute-start.15 = (bf16[128,2304]{1,0:T(8,128)(2,1)S(1)}, bf16[128,2304]{1,0:T(8,128)(2,1)S(1)}, u32[]{:S(2)}, u32[]{:S(2)}) collective-permute-start(bf16[128,2304]{1,0:T(8,128)(2,1)S(1)} %shard_map.163), channel_id=1, source_target_pairs={{0,0},{1,1},{2,4},{3,5},{4,2},{5,3},{6,6},{7,7},{8,8},{9,9},{10,12... | collective-permute-start | bytes 1769480 | tf_op jit(solution)/shard_map/ppermute | solution.py:36
  72.4 4.1 %collective-permute-start.13 = (bf16[128,2304]{1,0:T(8,128)(2,1)S(1)}, bf16[128,2304]{1,0:T(8,128)(2,1)S(1)}, u32[]{:S(2)}, u32[]{:S(2)}) collective-permute-start(bf16[128,2304]{1,0:T(8,128)(2,1)S(1)} %collective-permute-done.10.refs_0_), channel_id=1, source_target_pairs={{2,0},{3,1},{4,6},{5,7},{10,8},{11,9},{12,14},{13,15},{18,16},{19,... | collective-permute-start | bytes 1769480 | tf_op jit(solution)/shard_map/ppermute | solution.py:36
  76.5 10.1 %shard_map.164 = (bf16[128,2304]{1,0:T(8,128)(2,1)S(1)}, bf16[128,2304]{1,0:T(8,128)(2,1)S(1)}) custom-call(s32[8]{0:T(128)S(1)} %stack.51.where_ref, bf16[128,2304]{1,0:T(8,128)(2,1)S(1)} %shard_map.159.refs_0_, bf16[128,2304]{1,0:T(8,128)(2,1)S(1)} %collective-permute-done.7.refs_1_, bf16[2304,1152]{1,0:T(8,128)(2,1)S(1)} %bitcast.27, ...), custom_call_target="tpu_custom_call" | custom-call | tf_op jit(solution)/shard_map/pallas_call | solution.py:169
  87.4 3.0 %collective-permute-start.17 = (bf16[128,2304]{1,0:T(8,128)(2,1)S(1)}, bf16[128,2304]{1,0:T(8,128)(2,1)S(1)}, u32[]{:S(2)}, u32[]{:S(2)}) collective-permute-start(bf16[128,2304]{1,0:T(8,128)(2,1)S(1)} %shard_map.165), channel_id=1, source_target_pairs={{0,0},{1,1},{2,4},{3,5},{4,2},{5,3},{6,6},{7,7},{8,8},{9,9},{10,12... | collective-permute-start | bytes 1769480 | tf_op jit(solution)/shard_map/ppermute | solution.py:36
  90.8 10.1 %shard_map.167 = (bf16[128,2304]{1,0:T(8,128)(2,1)S(1)}, bf16[128,2304]{1,0:T(8,128)(2,1)S(1)}) custom-call(s32[8]{0:T(128)S(1)} %stack.51.where_ref, bf16[128,2304]{1,0:T(8,128)(2,1)S(1)} %collective-permute-done.10.refs_0_, bf16[128,2304]{1,0:T(8,128)(2,1)S(1)} %collective-permute-done.12.refs_1_, bf16[128,2304]{1,0:T(8,128)(2,1)S(1)} %collective-permute-done.8.refs_2_, ...), custom_call_target="tpu_custom_call" | custom-call | tf_op jit(solution)/shard_map/pallas_call | solution.py:169
  100.9 1.4 collective-permute-start.19
  102.3 5.9 %collective-permute-start.24 = (bf16[2304,512]{1,0:T(8,128)(2,1)S(1)}, bf16[2304,512]{1,0:T(8,128)(2,1)S(1)}, u32[]{:S(2)}, u32[]{:S(2)}) collective-permute-start(bf16[2304,512]{1,0:T(8,128)(2,1)S(1)} %copy-done.2), channel_id=1, source_target_pairs={{0,1},{1,0},{2,3},{3,2},{4,5},{5,4},{6,7},{7,6},{8,9},{9,8},{10,11... | collective-permute-start | bytes 7077896 | tf_op jit(solution)/shard_map/ppermute | solution.py:36
  109.0 5.7 %collective-permute-done.19.b_ref = bf16[128,2304]{1,0:T(8,128)(2,1)S(1)} collective-permute-done((bf16[128,2304]{1,0:T(8,128)(2,1)S(1)}, bf16[128,2304]{1,0:T(8,128)(2,1)S(1)}, u32[]{:S(2)}, u32[]{:S(2)}) %collective-permute-start.19) | collective-permute-done | bytes 589856 | tf_op jit(solution)/shard_map/ppermute | solution.py:36
  115.5 6.2 %collective-permute-start.21 = (f32[2,128,512]{2,1,0:T(8,128)S(1)}, f32[2,128,512]{2,1,0:T(8,128)S(1)}, u32[]{:S(2)}, u32[]{:S(2)}) collective-permute-start(f32[2,128,512]{2,1,0:T(8,128)S(1)} %bitcast.39), channel_id=1, source_target_pairs={{0,17},{1,16},{2,19},{3,18},{4,21},{5,20},{6,23},{7,22},{8,25},{9,... | collective-permute-start | bytes 1572872 | tf_op jit(solution)/shard_map/ppermute | solution.py:36
  121.7 1.5 collective-permute-start.26
  123.2 10.7 %collective-permute-done.21.noise_both = f32[2,128,512]{2,1,0:T(8,128)S(1)} collective-permute-done((f32[2,128,512]{2,1,0:T(8,128)S(1)}, f32[2,128,512]{2,1,0:T(8,128)S(1)}, u32[]{:S(2)}, u32[]{:S(2)}) %collective-permute-start.21) | collective-permute-done | bytes 524320 | tf_op jit(solution)/shard_map/ppermute | solution.py:36
  133.9 1.5 shard_map.169
  135.5 6.4 %collective-permute-done.23.came_ref = bf16[64,2304]{1,0:T(8,128)(2,1)S(1)} collective-permute-done((bf16[64,2304]{1,0:T(8,128)(2,1)S(1)}, bf16[64,2304]{1,0:T(8,128)(2,1)S(1)}, u32[]{:S(2)}, u32[]{:S(2)}) %collective-permute-start.23) | collective-permute-done | bytes 294944 | tf_op jit(solution)/shard_map/ppermute | solution.py:36
  142.9 1.8 collective-permute-start.28
  144.7 3.6 %collective-permute-start.25 = (bf16[32,512]{1,0:T(8,128)(2,1)S(1)}, bf16[32,512]{1,0:T(8,128)(2,1)S(1)}, u32[]{:S(2)}, u32[]{:S(2)}) collective-permute-start(bf16[32,512]{1,0:T(8,128)(2,1)S(1)} %bitcast.33), channel_id=1, source_target_pairs={{0,1},{1,0},{2,3},{3,2},{4,5},{5,4},{6,7},{7,6},{8,9},{9,8},{10,11... | collective-permute-start | bytes 98312 | tf_op jit(solution)/shard_map/ppermute | solution.py:36
  149.1 5.3 %collective-permute-done.26.far_ref = bf16[128,2304]{1,0:T(8,128)(2,1)S(1)} collective-permute-done((bf16[128,2304]{1,0:T(8,128)(2,1)S(1)}, bf16[128,2304]{1,0:T(8,128)(2,1)S(1)}, u32[]{:S(2)}, u32[]{:S(2)}) %collective-permute-start.26) | collective-permute-done | bytes 589856 | tf_op jit(solution)/shard_map/ppermute | solution.py:36
  154.4 2.4 %shard_map.171 = (bf16[256,2304]{1,0:T(8,128)(2,1)}, bf16[64,2304]{1,0:T(8,128)(2,1)S(1)}, bf16[64,2304]{1,0:T(8,128)(2,1)S(1)}) custom-call(s32[8]{0:T(128)S(1)} %stack.51.where_ref, bf16[128,2304]{1,0:T(8,128)(2,1)S(1)} %get-tuple-element.68.own_ref, bf16[128,2304]{1,0:T(8,128)(2,1)S(1)} %collective-permute-done.14.near_ref, ...), custom_call_target="tpu_custom_call" | custom-call | tf_op jit(solution)/shard_map/pallas_call | solution.py:169
  157.1 2.6 %collective-permute-start.29 = (bf16[64,2304]{1,0:T(8,128)(2,1)S(1)}, bf16[64,2304]{1,0:T(8,128)(2,1)S(1)}, u32[]{:S(2)}, u32[]{:S(2)}) collective-permute-start(bf16[64,2304]{1,0:T(8,128)(2,1)S(1)} %shard_map.170.own_ref), channel_id=1, source_target_pairs={{0,2},{1,3},{2,0},{3,1},{4,6},{5,7},{6,4},{7,5},{8,10},{9,11},{10,... | collective-permute-start | bytes 884744 | tf_op jit(solution)/shard_map/ppermute | solution.py:36
  160.7 2.6 %collective-permute-start.30 = (bf16[64,2304]{1,0:T(8,128)(2,1)S(1)}, bf16[64,2304]{1,0:T(8,128)(2,1)S(1)}, u32[]{:S(2)}, u32[]{:S(2)}) collective-permute-start(bf16[64,2304]{1,0:T(8,128)(2,1)S(1)} %collective-permute-done.28.far_ref), channel_id=1, source_target_pairs={{0,2},{1,3},{2,0},{3,1},{4,6},{5,7},{6,4},{7,5},{8,10},{9,11},{10,... | collective-permute-start | bytes 884744 | tf_op jit(solution)/shard_map/ppermute | solution.py:36
  164.3 2.9 %collective-permute-start.32 = (bf16[64,2304]{1,0:T(8,128)(2,1)S(1)}, bf16[64,2304]{1,0:T(8,128)(2,1)S(1)}, u32[]{:S(2)}, u32[]{:S(2)}) collective-permute-start(bf16[64,2304]{1,0:T(8,128)(2,1)S(1)} %shard_map.172.own_ref), channel_id=1, source_target_pairs={{0,4},{1,5},{2,6},{3,7},{4,0},{5,1},{6,2},{7,3},{8,12},{9,13},{10,... | collective-permute-start | bytes 884744 | tf_op jit(solution)/shard_map/ppermute | solution.py:36
  167.4 12.5 %collective-permute-done.30.last_ref = bf16[64,2304]{1,0:T(8,128)(2,1)S(1)} collective-permute-done((bf16[64,2304]{1,0:T(8,128)(2,1)S(1)}, bf16[64,2304]{1,0:T(8,128)(2,1)S(1)}, u32[]{:S(2)}, u32[]{:S(2)}) %collective-permute-start.30) | collective-permute-done | bytes 294944 | tf_op jit(solution)/shard_map/ppermute | solution.py:36
  179.9 2.6 %shard_map.173 = f32[40,256]{1,0:T(8,128)S(1)} custom-call(s32[8]{0:T(128)S(1)} %stack.51.where_ref, bf16[64,2304]{1,0:T(8,128)(2,1)S(1)} %shard_map.170.own_ref, bf16[64,2304]{1,0:T(8,128)(2,1)S(1)} %collective-permute-done.29.near_ref, bf16[64,2304]{1,0:T(8,128)(2,1)S(1)} %collective-permute-done.28.far_ref, ...), custom_call_target="tpu_custom_call" | custom-call | flops 40000000000 | tf_op jit(solution)/shard_map/pallas_call | solution.py:169
  182.5 2.4 %collective-permute-start.33 = (bf16[64,2304]{1,0:T(8,128)(2,1)S(1)}, bf16[64,2304]{1,0:T(8,128)(2,1)S(1)}, u32[]{:S(2)}, u32[]{:S(2)}) collective-permute-start(bf16[64,2304]{1,0:T(8,128)(2,1)S(1)} %collective-permute-done.32.far_ref), channel_id=1, source_target_pairs={{0,2},{1,3},{2,0},{3,1},{4,6},{5,7},{6,4},{7,5},{8,10},{9,11},{10,... | collective-permute-start | bytes 884744 | tf_op jit(solution)/shard_map/ppermute | solution.py:36
  185.0 1.3 collective-permute-done.31.near_ref
  186.3 6.3 %collective-permute-done.33.last_ref = bf16[64,2304]{1,0:T(8,128)(2,1)S(1)} collective-permute-done((bf16[64,2304]{1,0:T(8,128)(2,1)S(1)}, bf16[64,2304]{1,0:T(8,128)(2,1)S(1)}, u32[]{:S(2)}, u32[]{:S(2)}) %collective-permute-start.33) | collective-permute-done | bytes 294944 | tf_op jit(solution)/shard_map/ppermute | solution.py:36
  192.6 2.6 %shard_map.174 = f32[40,256]{1,0:T(8,128)S(1)} custom-call(s32[8]{0:T(128)S(1)} %stack.51.where_ref, bf16[64,2304]{1,0:T(8,128)(2,1)S(1)} %shard_map.172.own_ref, bf16[64,2304]{1,0:T(8,128)(2,1)S(1)} %collective-permute-done.31.near_ref, bf16[64,2304]{1,0:T(8,128)(2,1)S(1)} %collective-permute-done.32.far_ref, ...), custom_call_target="tpu_custom_call" | custom-call | tf_op jit(solution)/shard_map/pallas_call | solution.py:169
  196.3 3.5 %collective-permute-start.35 = (f32[40,128]{1,0:T(8,128)S(1)}, f32[40,128]{1,0:T(8,128)S(1)}, u32[]{:S(2)}, u32[]{:S(2)}) collective-permute-start(f32[40,128]{1,0:T(8,128)S(1)} %pad_maximum_fusion.2), channel_id=1, source_target_pairs={{0,4},{1,5},{2,6},{3,7},{4,0},{5,1},{6,2},{7,3},{8,12},{9,13},{10,... | collective-permute-start | bytes 61448 | tf_op jit(solution)/shard_map/ppermute | solution.py:36
  201.1 1.9 collective-permute-done.34.refs_1_
  203.6 1.9 collective-permute-start.37
  205.5 5.7 %collective-permute-start.38 = (f32[32,128]{1,0:T(8,128)S(1)}, f32[32,128]{1,0:T(8,128)S(1)}, u32[]{:S(2)}, u32[]{:S(2)}) collective-permute-start(f32[32,128]{1,0:T(8,128)S(1)} %shard_map.175), channel_id=1, source_target_pairs={{0,1},{1,3},{2,5},{3,7},{4,17},{5,19},{6,21},{7,23},{8,9},{9,11},{... | collective-permute-start | bytes 49160 | tf_op jit(solution)/shard_map/ppermute | solution.py:36
  211.2 1.9 collective-permute-start.39
  213.3 4.8 %collective-permute-done.39.halo_ref = f32[32,128]{1,0:T(8,128)S(1)} collective-permute-done((f32[32,128]{1,0:T(8,128)S(1)}, f32[32,128]{1,0:T(8,128)S(1)}, u32[]{:S(2)}, u32[]{:S(2)}) %collective-permute-start.39) | collective-permute-done | bytes 16416 | tf_op jit(solution)/shard_map/ppermute | solution.py:36
  218.1 1.7 shard_map.176
  (97 shorter events, 21.0 us)
Async XLA Ops:
  0.6 18.5 %collective-permute-start = (bf16[2304,1152]{1,0:T(8,128)(2,1)}, bf16[2304,1152]{1,0:T(8,128)(2,1)}, u32[]{:S(2)}, u32[]{:S(2)}) collective-permute-start(bf16[2304,1152]{1,0:T(8,128)(2,1)} %refs_4_.9), channel_id=1, source_target_pairs={{0,1},{1,0},{2,3},{3,2},{4,5},{5,4},{6,7},{7,6},{8,9},{9,8},{10,11... | collective-permute-start | bytes 15925256 | tf_op jit(solution)/shard_map/ppermute | solution.py:36
  1.4 17.8 %collective-permute-start.1 = (bf16[1152,2304]{1,0:T(8,128)(2,1)}, bf16[1152,2304]{1,0:T(8,128)(2,1)}, u32[]{:S(2)}, u32[]{:S(2)}) collective-permute-start(bf16[1152,2304]{1,0:T(8,128)(2,1)} %refs_6_.1), channel_id=1, source_target_pairs={{0,1},{1,0},{2,3},{3,2},{4,5},{5,4},{6,7},{7,6},{8,9},{9,8},{10,11... | collective-permute-start | bytes 15925256 | tf_op jit(solution)/shard_map/ppermute | solution.py:36
  4.6 14.5 %collective-permute-start.3 = (bf16[128,2304]{1,0:T(8,128)(2,1)S(1)}, bf16[128,2304]{1,0:T(8,128)(2,1)S(1)}, u32[]{:S(2)}, u32[]{:S(2)}) collective-permute-start(bf16[128,2304]{1,0:T(8,128)(2,1)S(1)} %shard_map.158.refs_0_), channel_id=1, source_target_pairs={{0,2},{1,3},{2,0},{3,1},{4,6},{5,7},{6,4},{7,5},{8,10},{9,11},{10,... | collective-permute-start | bytes 1769480 | tf_op jit(solution)/shard_map/ppermute | solution.py:36
  4.8 17.7 %collective-permute-start.4 = (bf16[128,2304]{1,0:T(8,128)(2,1)S(1)}, bf16[128,2304]{1,0:T(8,128)(2,1)S(1)}, u32[]{:S(2)}, u32[]{:S(2)}) collective-permute-start(bf16[128,2304]{1,0:T(8,128)(2,1)S(1)} %shard_map.158.refs_0_), channel_id=1, source_target_pairs={{0,0},{1,1},{2,4},{3,5},{4,2},{5,3},{6,6},{7,7},{8,8},{9,9},{10,12... | collective-permute-start | bytes 1769480 | tf_op jit(solution)/shard_map/ppermute | solution.py:36
  9.9 7.5 %collective-permute-start.2 = (f32[1,1664]{1,0:T(1,128)S(1)}, f32[1,1664]{1,0:T(1,128)S(1)}, u32[]{:S(2)}, u32[]{:S(2)}) collective-permute-start(f32[1,1664]{1,0:T(1,128)S(1)} %broadcast_in_dim.12.refs_6_.refs_8_.bias_a), channel_id=1, source_target_pairs={{0,1},{1,0},{2,3},{3,2},{4,5},{5,4},{6,7},{7,6},{8,9},{9,8},{10,11... | collective-permute-start | bytes 19976 | tf_op jit(solution)/shard_map/ppermute | solution.py:36
  12.7 27.2 %slice-start = ((s8[5308416]{0:T(1024)(128)(4,1)}), s8[4194304]{0:T(1024)(128)(4,1)S(1)}, s32[]{:S(2)}) async-start(s8[5308416]{0:T(1024)(128)(4,1)} %bitcast.26), calls=%async_computation | async-start | bytes 8388608
  12.7 27.2 %slice-start.2 = ((s8[5308416]{0:T(1024)(128)(4,1)}), s8[4194304]{0:T(1024)(128)(4,1)S(1)}, s32[]{:S(2)}) async-start(s8[5308416]{0:T(1024)(128)(4,1)} %bitcast.28), calls=%async_computation.2 | async-start | bytes 8388608
  19.2 16.7 %collective-permute-start.5 = (bf16[128,2304]{1,0:T(8,128)(2,1)S(1)}, bf16[128,2304]{1,0:T(8,128)(2,1)S(1)}, u32[]{:S(2)}, u32[]{:S(2)}) collective-permute-start(bf16[128,2304]{1,0:T(8,128)(2,1)S(1)} %collective-permute-done.3.refs_1_), channel_id=1, source_target_pairs={{0,0},{1,1},{2,4},{3,5},{4,2},{5,3},{6,6},{7,7},{8,8},{9,9},{10,12... | collective-permute-start | bytes 1769480 | tf_op jit(solution)/shard_map/ppermute | solution.py:36
  22.5 17.4 %collective-permute-start.9 = (bf16[128,2304]{1,0:T(8,128)(2,1)S(1)}, bf16[128,2304]{1,0:T(8,128)(2,1)S(1)}, u32[]{:S(2)}, u32[]{:S(2)}) collective-permute-start(bf16[128,2304]{1,0:T(8,128)(2,1)S(1)} %collective-permute-done.4.refs_0_), channel_id=1, source_target_pairs={{2,0},{3,1},{4,6},{5,7},{10,8},{11,9},{12,14},{13,15},{18,16},{19,... | collective-permute-start | bytes 1769480 | tf_op jit(solution)/shard_map/ppermute | solution.py:36
  23.8 23.9 %collective-permute-start.7 = (bf16[128,2304]{1,0:T(8,128)(2,1)S(1)}, bf16[128,2304]{1,0:T(8,128)(2,1)S(1)}, u32[]{:S(2)}, u32[]{:S(2)}) collective-permute-start(bf16[128,2304]{1,0:T(8,128)(2,1)S(1)} %shard_map.159.refs_0_), channel_id=1, source_target_pairs={{0,2},{1,3},{2,0},{3,1},{4,6},{5,7},{6,4},{7,5},{8,10},{9,11},{10,... | collective-permute-start | bytes 1769480 | tf_op jit(solution)/shard_map/ppermute | solution.py:36
  35.8 15.2 %collective-permute-start.8 = (bf16[128,2304]{1,0:T(8,128)(2,1)S(1)}, bf16[128,2304]{1,0:T(8,128)(2,1)S(1)}, u32[]{:S(2)}, u32[]{:S(2)}) collective-permute-start(bf16[128,2304]{1,0:T(8,128)(2,1)S(1)} %shard_map.159.refs_0_), channel_id=1, source_target_pairs={{0,0},{1,1},{2,4},{3,5},{4,2},{5,3},{6,6},{7,7},{8,8},{9,9},{10,12... | collective-permute-start | bytes 1769480 | tf_op jit(solution)/shard_map/ppermute | solution.py:36
  38.5 21.9 %collective-permute-start.6 = (bf16[128,2304]{1,0:T(8,128)(2,1)S(1)}, bf16[128,2304]{1,0:T(8,128)(2,1)S(1)}, u32[]{:S(2)}, u32[]{:S(2)}) collective-permute-start(bf16[128,2304]{1,0:T(8,128)(2,1)S(1)} %collective-permute-done.5.refs_0_), channel_id=1, source_target_pairs={{2,0},{3,1},{4,6},{5,7},{10,8},{11,9},{12,14},{13,15},{18,16},{19,... | collective-permute-start | bytes 1769480 | tf_op jit(solution)/shard_map/ppermute | solution.py:36
  51.0 16.7 %collective-permute-start.10 = (bf16[128,2304]{1,0:T(8,128)(2,1)S(1)}, bf16[128,2304]{1,0:T(8,128)(2,1)S(1)}, u32[]{:S(2)}, u32[]{:S(2)}) collective-permute-start(bf16[128,2304]{1,0:T(8,128)(2,1)S(1)} %collective-permute-done.7.refs_1_), channel_id=1, source_target_pairs={{0,0},{1,1},{2,4},{3,5},{4,2},{5,3},{6,6},{7,7},{8,8},{9,9},{10,12... | collective-permute-start | bytes 1769480 | tf_op jit(solution)/shard_map/ppermute | solution.py:36
  53.6 14.2 %collective-permute-start.11 = (bf16[128,2304]{1,0:T(8,128)(2,1)S(1)}, bf16[128,2304]{1,0:T(8,128)(2,1)S(1)}, u32[]{:S(2)}, u32[]{:S(2)}) collective-permute-start(bf16[128,2304]{1,0:T(8,128)(2,1)S(1)} %shard_map.161.a_ref), channel_id=1, source_target_pairs={{0,2},{1,3},{6,4},{7,5},{8,10},{9,11},{14,12},{15,13},{16,18},{17,... | collective-permute-start | bytes 1769480 | tf_op jit(solution)/shard_map/ppermute | solution.py:36
  54.9 21.6 %collective-permute-start.12 = (bf16[128,2304]{1,0:T(8,128)(2,1)S(1)}, bf16[128,2304]{1,0:T(8,128)(2,1)S(1)}, u32[]{:S(2)}, u32[]{:S(2)}) collective-permute-start(bf16[128,2304]{1,0:T(8,128)(2,1)S(1)} %collective-permute-done.8.refs_2_), channel_id=1, source_target_pairs={{2,0},{3,1},{4,6},{5,7},{10,8},{11,9},{12,14},{13,15},{18,16},{19,... | collective-permute-start | bytes 1769480 | tf_op jit(solution)/shard_map/ppermute | solution.py:36
  68.5 18.1 %collective-permute-start.15 = (bf16[128,2304]{1,0:T(8,128)(2,1)S(1)}, bf16[128,2304]{1,0:T(8,128)(2,1)S(1)}, u32[]{:S(2)}, u32[]{:S(2)}) collective-permute-start(bf16[128,2304]{1,0:T(8,128)(2,1)S(1)} %shard_map.163), channel_id=1, source_target_pairs={{0,0},{1,1},{2,4},{3,5},{4,2},{5,3},{6,6},{7,7},{8,8},{9,9},{10,12... | collective-permute-start | bytes 1769480 | tf_op jit(solution)/shard_map/ppermute | solution.py:36
  71.1 15.5 %collective-permute-start.16 = (bf16[128,2304]{1,0:T(8,128)(2,1)S(1)}, bf16[128,2304]{1,0:T(8,128)(2,1)S(1)}, u32[]{:S(2)}, u32[]{:S(2)}) collective-permute-start(bf16[128,2304]{1,0:T(8,128)(2,1)S(1)} %shard_map.162.a_ref), channel_id=1, source_target_pairs={{0,2},{1,3},{6,4},{7,5},{8,10},{9,11},{14,12},{15,13},{16,18},{17,... | collective-permute-start | bytes 1769480 | tf_op jit(solution)/shard_map/ppermute | solution.py:36
  72.4 18.0 %collective-permute-start.13 = (bf16[128,2304]{1,0:T(8,128)(2,1)S(1)}, bf16[128,2304]{1,0:T(8,128)(2,1)S(1)}, u32[]{:S(2)}, u32[]{:S(2)}) collective-permute-start(bf16[128,2304]{1,0:T(8,128)(2,1)S(1)} %collective-permute-done.10.refs_0_), channel_id=1, source_target_pairs={{2,0},{3,1},{4,6},{5,7},{10,8},{11,9},{12,14},{13,15},{18,16},{19,... | collective-permute-start | bytes 1769480 | tf_op jit(solution)/shard_map/ppermute | solution.py:36
  87.4 20.9 %collective-permute-start.17 = (bf16[128,2304]{1,0:T(8,128)(2,1)S(1)}, bf16[128,2304]{1,0:T(8,128)(2,1)S(1)}, u32[]{:S(2)}, u32[]{:S(2)}) collective-permute-start(bf16[128,2304]{1,0:T(8,128)(2,1)S(1)} %shard_map.165), channel_id=1, source_target_pairs={{0,0},{1,1},{2,4},{3,5},{4,2},{5,3},{6,6},{7,7},{8,8},{9,9},{10,12... | collective-permute-start | bytes 1769480 | tf_op jit(solution)/shard_map/ppermute | solution.py:36
  90.4 17.9 %collective-permute-start.14 = (bf16[128,2304]{1,0:T(8,128)(2,1)S(1)}, bf16[128,2304]{1,0:T(8,128)(2,1)S(1)}, u32[]{:S(2)}, u32[]{:S(2)}) collective-permute-start(bf16[128,2304]{1,0:T(8,128)(2,1)S(1)} %get-tuple-element.70), channel_id=1, source_target_pairs={{0,2},{1,3},{2,0},{3,1},{4,6},{5,7},{6,4},{7,5},{8,10},{9,11},{10,... | collective-permute-start | bytes 1769480 | tf_op jit(solution)/shard_map/ppermute | solution.py:36
  90.5 17.8 %collective-permute-start.18 = (f32[2,128,512]{2,1,0:T(8,128)S(1)}, f32[2,128,512]{2,1,0:T(8,128)S(1)}, u32[]{:S(2)}, u32[]{:S(2)}) collective-permute-start(f32[2,128,512]{2,1,0:T(8,128)S(1)} %bitcast.40), channel_id=1, source_target_pairs={{0,16},{1,17},{2,18},{3,19},{4,20},{5,21},{6,22},{7,23},{8,24},{9,... | collective-permute-start | bytes 1572872 | tf_op jit(solution)/shard_map/ppermute | solution.py:36
  100.8 33.1 %copy-start.3 = (f32[2,2,2304]{2,1,0:T(2,128)S(1)}, f32[2,2,2304]{2,1,0:T(2,128)}, u32[]{:S(2)}) copy-start(f32[2,2,2304]{2,1,0:T(2,128)} %ada_ref.11) | copy-start | bytes 110596
  100.9 33.1 %copy-start.7 = (f32[2,2304]{1,0:T(2,128)S(1)}, f32[2,2304]{1,0:T(2,128)}, u32[]{:S(2)}) copy-start(f32[2,2304]{1,0:T(2,128)} %gate_ref.3) | copy-start | bytes 55300
  100.9 13.8 %collective-permute-start.19 = (bf16[128,2304]{1,0:T(8,128)(2,1)S(1)}, bf16[128,2304]{1,0:T(8,128)(2,1)S(1)}, u32[]{:S(2)}, u32[]{:S(2)}) collective-permute-start(bf16[128,2304]{1,0:T(8,128)(2,1)S(1)} %get-tuple-element.79), channel_id=1, source_target_pairs={{0,2},{1,3},{2,0},{3,1},{4,6},{5,7},{6,4},{7,5},{8,10},{9,11},{10,... | collective-permute-start | bytes 1769480 | tf_op jit(solution)/shard_map/ppermute | solution.py:36
  102.3 46.8 %collective-permute-start.24 = (bf16[2304,512]{1,0:T(8,128)(2,1)S(1)}, bf16[2304,512]{1,0:T(8,128)(2,1)S(1)}, u32[]{:S(2)}, u32[]{:S(2)}) collective-permute-start(bf16[2304,512]{1,0:T(8,128)(2,1)S(1)} %copy-done.2), channel_id=1, source_target_pairs={{0,1},{1,0},{2,3},{3,2},{4,5},{5,4},{6,7},{7,6},{8,9},{9,8},{10,11... | collective-permute-start | bytes 7077896 | tf_op jit(solution)/shard_map/ppermute | solution.py:36
  115.4 29.3 %copy-start.8 = (bf16[512,32]{0,1:T(8,128)(2,1)S(1)}, bf16[512,32]{0,1:T(8,128)(2,1)}, u32[]{:S(2)}) copy-start(bf16[512,32]{0,1:T(8,128)(2,1)} %param.26) | copy-start | bytes 98308
  115.4 18.5 %collective-permute-start.20 = (bf16[128,2304]{1,0:T(8,128)(2,1)S(1)}, bf16[128,2304]{1,0:T(8,128)(2,1)S(1)}, u32[]{:S(2)}, u32[]{:S(2)}) collective-permute-start(bf16[128,2304]{1,0:T(8,128)(2,1)S(1)} %shard_map.166), channel_id=1, source_target_pairs={{0,2},{1,3},{2,0},{3,1},{4,6},{5,7},{6,4},{7,5},{8,10},{9,11},{10,... | collective-permute-start | bytes 1769480 | tf_op jit(solution)/shard_map/ppermute | solution.py:36
  115.5 18.4 %collective-permute-start.21 = (f32[2,128,512]{2,1,0:T(8,128)S(1)}, f32[2,128,512]{2,1,0:T(8,128)S(1)}, u32[]{:S(2)}, u32[]{:S(2)}) collective-permute-start(f32[2,128,512]{2,1,0:T(8,128)S(1)} %bitcast.39), channel_id=1, source_target_pairs={{0,17},{1,16},{2,19},{3,18},{4,21},{5,20},{6,23},{7,22},{8,25},{9,... | collective-permute-start | bytes 1572872 | tf_op jit(solution)/shard_map/ppermute | solution.py:36
  121.7 12.2 %collective-permute-start.22 = (f32[2,128,512]{2,1,0:T(8,128)S(1)}, f32[2,128,512]{2,1,0:T(8,128)S(1)}, u32[]{:S(2)}, u32[]{:S(2)}) collective-permute-start(f32[2,128,512]{2,1,0:T(8,128)S(1)} %bitcast.38), channel_id=1, source_target_pairs={{0,1},{1,0},{2,3},{3,2},{4,5},{5,4},{6,7},{7,6},{8,9},{9,8},{10,11... | collective-permute-start | bytes 1572872 | tf_op jit(solution)/shard_map/ppermute | solution.py:36
  121.7 32.7 %collective-permute-start.26 = (bf16[128,2304]{1,0:T(8,128)(2,1)S(1)}, bf16[128,2304]{1,0:T(8,128)(2,1)S(1)}, u32[]{:S(2)}, u32[]{:S(2)}) collective-permute-start(bf16[128,2304]{1,0:T(8,128)(2,1)S(1)} %shard_map.168), channel_id=1, source_target_pairs={{0,4},{1,5},{2,6},{3,7},{4,0},{5,1},{6,2},{7,3},{8,12},{9,13},{10,... | collective-permute-start | bytes 1769480 | tf_op jit(solution)/shard_map/ppermute | solution.py:36
  135.4 6.4 %collective-permute-start.23 = (bf16[64,2304]{1,0:T(8,128)(2,1)S(1)}, bf16[64,2304]{1,0:T(8,128)(2,1)S(1)}, u32[]{:S(2)}, u32[]{:S(2)}) collective-permute-start(bf16[64,2304]{1,0:T(8,128)(2,1)S(1)} %get-tuple-element.87), channel_id=1, source_target_pairs={{0,16},{1,17},{2,18},{3,19},{4,20},{5,21},{6,22},{7,23},{8,24},{9,... | collective-permute-start | bytes 884744 | tf_op jit(solution)/shard_map/ppermute | solution.py:36
  142.9 17.8 %collective-permute-start.28 = (bf16[64,2304]{1,0:T(8,128)(2,1)S(1)}, bf16[64,2304]{1,0:T(8,128)(2,1)S(1)}, u32[]{:S(2)}, u32[]{:S(2)}) collective-permute-start(bf16[64,2304]{1,0:T(8,128)(2,1)S(1)} %shard_map.170.own_ref), channel_id=1, source_target_pairs={{0,4},{1,5},{2,6},{3,7},{4,0},{5,1},{6,2},{7,3},{8,12},{9,13},{10,... | collective-permute-start | bytes 884744 | tf_op jit(solution)/shard_map/ppermute | solution.py:36
  144.7 4.5 %collective-permute-start.25 = (bf16[32,512]{1,0:T(8,128)(2,1)S(1)}, bf16[32,512]{1,0:T(8,128)(2,1)S(1)}, u32[]{:S(2)}, u32[]{:S(2)}) collective-permute-start(bf16[32,512]{1,0:T(8,128)(2,1)S(1)} %bitcast.33), channel_id=1, source_target_pairs={{0,1},{1,0},{2,3},{3,2},{4,5},{5,4},{6,7},{7,6},{8,9},{9,8},{10,11... | collective-permute-start | bytes 98312 | tf_op jit(solution)/shard_map/ppermute | solution.py:36
  156.8 6.5 %collective-permute-start.27 = (bf16[64,2304]{1,0:T(8,128)(2,1)S(1)}, bf16[64,2304]{1,0:T(8,128)(2,1)S(1)}, u32[]{:S(2)}, u32[]{:S(2)}) collective-permute-start(bf16[64,2304]{1,0:T(8,128)(2,1)S(1)} %get-tuple-element.94), channel_id=1, source_target_pairs={{0,16},{1,17},{2,18},{3,19},{4,20},{5,21},{6,22},{7,23},{8,24},{9,... | collective-permute-start | bytes 884744 | tf_op jit(solution)/shard_map/ppermute | solution.py:36
  157.1 10.3 %collective-permute-start.29 = (bf16[64,2304]{1,0:T(8,128)(2,1)S(1)}, bf16[64,2304]{1,0:T(8,128)(2,1)S(1)}, u32[]{:S(2)}, u32[]{:S(2)}) collective-permute-start(bf16[64,2304]{1,0:T(8,128)(2,1)S(1)} %shard_map.170.own_ref), channel_id=1, source_target_pairs={{0,2},{1,3},{2,0},{3,1},{4,6},{5,7},{6,4},{7,5},{8,10},{9,11},{10,... | collective-permute-start | bytes 884744 | tf_op jit(solution)/shard_map/ppermute | solution.py:36
  160.7 19.1 %collective-permute-start.30 = (bf16[64,2304]{1,0:T(8,128)(2,1)S(1)}, bf16[64,2304]{1,0:T(8,128)(2,1)S(1)}, u32[]{:S(2)}, u32[]{:S(2)}) collective-permute-start(bf16[64,2304]{1,0:T(8,128)(2,1)S(1)} %collective-permute-done.28.far_ref), channel_id=1, source_target_pairs={{0,2},{1,3},{2,0},{3,1},{4,6},{5,7},{6,4},{7,5},{8,10},{9,11},{10,... | collective-permute-start | bytes 884744 | tf_op jit(solution)/shard_map/ppermute | solution.py:36
  164.3 18.2 %collective-permute-start.32 = (bf16[64,2304]{1,0:T(8,128)(2,1)S(1)}, bf16[64,2304]{1,0:T(8,128)(2,1)S(1)}, u32[]{:S(2)}, u32[]{:S(2)}) collective-permute-start(bf16[64,2304]{1,0:T(8,128)(2,1)S(1)} %shard_map.172.own_ref), channel_id=1, source_target_pairs={{0,4},{1,5},{2,6},{3,7},{4,0},{5,1},{6,2},{7,3},{8,12},{9,13},{10,... | collective-permute-start | bytes 884744 | tf_op jit(solution)/shard_map/ppermute | solution.py:36
  167.1 19.2 %collective-permute-start.31 = (bf16[64,2304]{1,0:T(8,128)(2,1)S(1)}, bf16[64,2304]{1,0:T(8,128)(2,1)S(1)}, u32[]{:S(2)}, u32[]{:S(2)}) collective-permute-start(bf16[64,2304]{1,0:T(8,128)(2,1)S(1)} %shard_map.172.own_ref), channel_id=1, source_target_pairs={{0,2},{1,3},{2,0},{3,1},{4,6},{5,7},{6,4},{7,5},{8,10},{9,11},{10,... | collective-permute-start | bytes 884744 | tf_op jit(solution)/shard_map/ppermute | solution.py:36
  182.5 10.1 %collective-permute-start.33 = (bf16[64,2304]{1,0:T(8,128)(2,1)S(1)}, bf16[64,2304]{1,0:T(8,128)(2,1)S(1)}, u32[]{:S(2)}, u32[]{:S(2)}) collective-permute-start(bf16[64,2304]{1,0:T(8,128)(2,1)S(1)} %collective-permute-done.32.far_ref), channel_id=1, source_target_pairs={{0,2},{1,3},{2,0},{3,1},{4,6},{5,7},{6,4},{7,5},{8,10},{9,11},{10,... | collective-permute-start | bytes 884744 | tf_op jit(solution)/shard_map/ppermute | solution.py:36
  185.0 28.2 %copy-start.11 = (f32[32]{0:T(128)S(1)}, f32[32]{0:T(128)}, u32[]{:S(2)}) copy-start(f32[32]{0:T(128)} %param.28) | copy-start | bytes 388
  185.0 33.1 %copy-start.4 = (f32[32,32,3,3]{1,0,3,2:T(8,128)S(1)}, f32[32,32,3,3]{1,0,3,2:T(8,128)}, u32[]{:S(2)}) copy-start(f32[32,32,3,3]{1,0,3,2:T(8,128)} %param.27) | copy-start | bytes 110596
  185.0 33.1 %copy-start.9 = (f32[1,32,128]{2,1,0:T(8,128)S(1)}, f32[1,32,128]{2,1,0:T(8,128)}, u32[]{:S(2)}) copy-start(f32[1,32,128]{2,1,0:T(8,128)} %param.29) | copy-start | bytes 49156
  195.4 4.6 %collective-permute-start.36 = (f32[40,128]{1,0:T(8,128)S(1)}, f32[40,128]{1,0:T(8,128)S(1)}, u32[]{:S(2)}, u32[]{:S(2)}) collective-permute-start(f32[40,128]{1,0:T(8,128)S(1)} %pad_maximum_fusion.3), channel_id=1, source_target_pairs={{0,6},{1,7},{2,4},{3,5},{4,2},{5,3},{6,0},{7,1},{8,14},{9,15},{10,... | collective-permute-start | bytes 61448 | tf_op jit(solution)/shard_map/ppermute | solution.py:36
  196.3 4.8 %collective-permute-start.35 = (f32[40,128]{1,0:T(8,128)S(1)}, f32[40,128]{1,0:T(8,128)S(1)}, u32[]{:S(2)}, u32[]{:S(2)}) collective-permute-start(f32[40,128]{1,0:T(8,128)S(1)} %pad_maximum_fusion.2), channel_id=1, source_target_pairs={{0,4},{1,5},{2,6},{3,7},{4,0},{5,1},{6,2},{7,3},{8,12},{9,13},{10,... | collective-permute-start | bytes 61448 | tf_op jit(solution)/shard_map/ppermute | solution.py:36
  199.9 3.1 %collective-permute-start.34 = (f32[40,128]{1,0:T(8,128)S(1)}, f32[40,128]{1,0:T(8,128)S(1)}, u32[]{:S(2)}, u32[]{:S(2)}) collective-permute-start(f32[40,128]{1,0:T(8,128)S(1)} %pad_maximum_fusion.1), channel_id=1, source_target_pairs={{0,2},{1,3},{2,0},{3,1},{4,6},{5,7},{6,4},{7,5},{8,10},{9,11},{10,... | collective-permute-start | bytes 61448 | tf_op jit(solution)/shard_map/ppermute | solution.py:36
  203.6 9.7 %collective-permute-start.37 = (f32[32,128]{1,0:T(8,128)S(1)}, f32[32,128]{1,0:T(8,128)S(1)}, u32[]{:S(2)}, u32[]{:S(2)}) collective-permute-start(f32[32,128]{1,0:T(8,128)S(1)} %shard_map.175), channel_id=1, source_target_pairs={{0,0},{1,2},{2,4},{3,6},{4,16},{5,18},{6,20},{7,22},{8,8},{9,10},{... | collective-permute-start | bytes 49160 | tf_op jit(solution)/shard_map/ppermute | solution.py:36
  205.5 7.7 %collective-permute-start.38 = (f32[32,128]{1,0:T(8,128)S(1)}, f32[32,128]{1,0:T(8,128)S(1)}, u32[]{:S(2)}, u32[]{:S(2)}) collective-permute-start(f32[32,128]{1,0:T(8,128)S(1)} %shard_map.175), channel_id=1, source_target_pairs={{0,1},{1,3},{2,5},{3,7},{4,17},{5,19},{6,21},{7,23},{8,9},{9,11},{... | collective-permute-start | bytes 49160 | tf_op jit(solution)/shard_map/ppermute | solution.py:36
  211.2 6.8 %collective-permute-start.39 = (f32[32,128]{1,0:T(8,128)S(1)}, f32[32,128]{1,0:T(8,128)S(1)}, u32[]{:S(2)}, u32[]{:S(2)}) collective-permute-start(f32[32,128]{1,0:T(8,128)S(1)} %shard_map.175), channel_id=1, source_target_pairs={{0,7},{1,1},{2,3},{3,5},{4,23},{5,17},{6,19},{7,21},{8,15},{9,9},{... | collective-permute-start | bytes 49160 | tf_op jit(solution)/shard_map/ppermute | solution.py:36
  (8 other events, 97.3 us)

commit v11 on v9

--- a/solution.py
+++ b/solution.py
@@ -267,7 +267,7 @@
     in_place = pl.BlockSpec(memory_space=pltpu.HBM)
     specs = [in_place if fetch and i in (0, 2) else ON_CHIP for i in range(len(panels))]
     return call(
-        functools.partial(ffn_kernel, groups, 256, fetch),
+        functools.partial(ffn_kernel, groups, 768, fetch),
         where,
         (*parts, *panels),
         [shape_of((rows, width))] * len(slots),

time: 216 us -> 216 us (level)
  transfers between devices with their start and end apart: 40 -> 40, of which waited for: 18 -> 17; matrix products, arithmetic and copies ran while one was open for 1% -> 1% of each run, Pallas kernels for 28% -> 29%
where the time goes in v11:
time: 216 us; the launch traced here: 212 us
  starting transfers between devices  79.1 us (37%)
  Pallas kernels  66.4 us (31%)
  waiting for transfers between devices  60.4 us (28%)
  local copies, waits for them, and re-layouts  4.2 us (2%)
    ppermute x40, starting transfers between devices, permute_devices(): return lax.ppermute(value, ('dp', 'mp'), pairs)  79.1 us
    pallas_call x19, Pallas kernels, call(): pl.pallas_call(kernel, out_shape=outs, in_specs=[SCALARS] + (specs or [ON...  66.4 us
    ppermute x40, waiting for transfers between devices, permute_devices(): return lax.ppermute(value, ('dp', 'mp'), pairs)  60.4 us
  transfers between devices with their start and end apart: 40, of which 17 were waited for; matrix products, arithmetic and copies ran while one was open for 1% of the time, Pallas kernels for 29%

profile of v11, /device:TPU:13, one launch (start us, length us, event | category | flops | bytes accessed | tf_op | source)
XLA Modules:
  0.0 212.3 jit_solution(1394536359955346016)
XLA Ops:
  4.8 4.3 %collective-permute-start.4 = (bf16[128,2304]{1,0:T(8,128)(2,1)S(1)}, bf16[128,2304]{1,0:T(8,128)(2,1)S(1)}, u32[]{:S(2)}, u32[]{:S(2)}) collective-permute-start(bf16[128,2304]{1,0:T(8,128)(2,1)S(1)} %shard_map.158.refs_0_), channel_id=1, source_target_pairs={{0,0},{1,1},{2,4},{3,5},{4,2},{5,3},{6,6},{7,7},{8,8},{9,9},{10,12... | collective-permute-start | bytes 1769480 | tf_op jit(solution)/shard_map/ppermute | solution.py:36
  10.9 1.7 constant_dynamic-slice_fusion
  13.7 3.6 %collective-permute-done.2.refs_7_.refs_9_.bias_b = f32[1,1664]{1,0:T(1,128)S(1)} collective-permute-done((f32[1,1664]{1,0:T(1,128)S(1)}, f32[1,1664]{1,0:T(1,128)S(1)}, u32[]{:S(2)}, u32[]{:S(2)}) %collective-permute-start.2) | collective-permute-done | bytes 6688 | tf_op jit(solution)/shard_map/ppermute | solution.py:36
  17.4 1.8 collective-permute-done.3.refs_1_
  19.1 3.3 %collective-permute-start.5 = (bf16[128,2304]{1,0:T(8,128)(2,1)S(1)}, bf16[128,2304]{1,0:T(8,128)(2,1)S(1)}, u32[]{:S(2)}, u32[]{:S(2)}) collective-permute-start(bf16[128,2304]{1,0:T(8,128)(2,1)S(1)} %collective-permute-done.3.refs_1_), channel_id=1, source_target_pairs={{0,0},{1,1},{2,4},{3,5},{4,2},{5,3},{6,6},{7,7},{8,8},{9,9},{10,12... | collective-permute-start | bytes 1769480 | tf_op jit(solution)/shard_map/ppermute | solution.py:36
  22.5 1.3 collective-permute-start.9
  23.9 13.3 %shard_map.160 = (bf16[128,2304]{1,0:T(8,128)(2,1)S(1)}, bf16[128,2304]{1,0:T(8,128)(2,1)S(1)}) custom-call(s32[6]{0:T(128)S(1)} %stack.35.where_ref, bf16[128,2304]{1,0:T(8,128)(2,1)S(1)} %shard_map.158.refs_0_, bf16[128,2304]{1,0:T(8,128)(2,1)S(1)} %collective-permute-done.3.refs_1_, bf16[2304,1152]{1,0:T(8,128)(2,1)} %refs_4_.9, ...), custom_call_target="tpu_custom_call" | custom-call | tf_op jit(solution)/shard_map/pallas_call | solution.py:169
  37.2 2.7 %collective-permute-start.8 = (bf16[128,2304]{1,0:T(8,128)(2,1)S(1)}, bf16[128,2304]{1,0:T(8,128)(2,1)S(1)}, u32[]{:S(2)}, u32[]{:S(2)}) collective-permute-start(bf16[128,2304]{1,0:T(8,128)(2,1)S(1)} %shard_map.159.refs_0_), channel_id=1, source_target_pairs={{0,0},{1,1},{2,4},{3,5},{4,2},{5,3},{6,6},{7,7},{8,8},{9,9},{10,12... | collective-permute-start | bytes 1769480 | tf_op jit(solution)/shard_map/ppermute | solution.py:36
  39.9 1.4 collective-permute-start.6
  41.4 7.3 %shard_map.161.a_ref = bf16[128,2304]{1,0:T(8,128)(2,1)S(1)} custom-call(s32[6]{0:T(128)S(1)} %stack.35.where_ref, bf16[128,2304]{1,0:T(8,128)(2,1)S(1)} %collective-permute-done.5.refs_0_, bf16[128,2304]{1,0:T(8,128)(2,1)S(1)} %collective-permute-done.9.refs_1_, bf16[2304,1152]{1,0:T(8,128)(2,1)S(1)} %bitcast.25, ...), custom_call_target="tpu_custom_call" | custom-call | tf_op jit(solution)/shard_map/pallas_call | solution.py:169
  48.7 3.7 %collective-permute-done.8.refs_2_ = bf16[128,2304]{1,0:T(8,128)(2,1)S(1)} collective-permute-done((bf16[128,2304]{1,0:T(8,128)(2,1)S(1)}, bf16[128,2304]{1,0:T(8,128)(2,1)S(1)}, u32[]{:S(2)}, u32[]{:S(2)}) %collective-permute-start.8) | collective-permute-done | bytes 589856 | tf_op jit(solution)/shard_map/ppermute | solution.py:36
  52.4 2.6 %collective-permute-start.10 = (bf16[128,2304]{1,0:T(8,128)(2,1)S(1)}, bf16[128,2304]{1,0:T(8,128)(2,1)S(1)}, u32[]{:S(2)}, u32[]{:S(2)}) collective-permute-start(bf16[128,2304]{1,0:T(8,128)(2,1)S(1)} %collective-permute-done.7.refs_1_), channel_id=1, source_target_pairs={{0,0},{1,1},{2,4},{3,5},{4,2},{5,3},{6,6},{7,7},{8,8},{9,9},{10,12... | collective-permute-start | bytes 1769480 | tf_op jit(solution)/shard_map/ppermute | solution.py:36
  55.0 1.3 collective-permute-start.11
  56.3 4.2 %collective-permute-start.12 = (bf16[128,2304]{1,0:T(8,128)(2,1)S(1)}, bf16[128,2304]{1,0:T(8,128)(2,1)S(1)}, u32[]{:S(2)}, u32[]{:S(2)}) collective-permute-start(bf16[128,2304]{1,0:T(8,128)(2,1)S(1)} %collective-permute-done.8.refs_2_), channel_id=1, source_target_pairs={{2,0},{3,1},{4,6},{5,7},{10,8},{11,9},{12,14},{13,15},{18,16},{19,... | collective-permute-start | bytes 1769480 | tf_op jit(solution)/shard_map/ppermute | solution.py:36
  60.6 7.3 %shard_map.162.a_ref = bf16[128,2304]{1,0:T(8,128)(2,1)S(1)} custom-call(s32[6]{0:T(128)S(1)} %stack.35.where_ref, bf16[128,2304]{1,0:T(8,128)(2,1)S(1)} %collective-permute-done.4.refs_0_, bf16[128,2304]{1,0:T(8,128)(2,1)S(1)} %collective-permute-done.6.refs_1_, bf16[2304,1152]{1,0:T(8,128)(2,1)S(1)} %bitcast.25, ...), custom_call_target="tpu_custom_call" | custom-call | tf_op jit(solution)/shard_map/pallas_call | solution.py:169
  69.7 2.7 %collective-permute-start.15 = (bf16[128,2304]{1,0:T(8,128)(2,1)S(1)}, bf16[128,2304]{1,0:T(8,128)(2,1)S(1)}, u32[]{:S(2)}, u32[]{:S(2)}) collective-permute-start(bf16[128,2304]{1,0:T(8,128)(2,1)S(1)} %shard_map.163), channel_id=1, source_target_pairs={{0,0},{1,1},{2,4},{3,5},{4,2},{5,3},{6,6},{7,7},{8,8},{9,9},{10,12... | collective-permute-start | bytes 1769480 | tf_op jit(solution)/shard_map/ppermute | solution.py:36
  72.4 1.3 collective-permute-start.13
  73.7 1.3 collective-permute-start.16
  75.0 10.1 %shard_map.164 = (bf16[128,2304]{1,0:T(8,128)(2,1)S(1)}, bf16[128,2304]{1,0:T(8,128)(2,1)S(1)}) custom-call(s32[6]{0:T(128)S(1)} %stack.35.where_ref, bf16[128,2304]{1,0:T(8,128)(2,1)S(1)} %shard_map.159.refs_0_, bf16[128,2304]{1,0:T(8,128)(2,1)S(1)} %collective-permute-done.7.refs_1_, bf16[2304,1152]{1,0:T(8,128)(2,1)S(1)} %bitcast.25, ...), custom_call_target="tpu_custom_call" | custom-call | tf_op jit(solution)/shard_map/pallas_call | solution.py:169
  85.2 2.2 %collective-permute-start.14 = (bf16[128,2304]{1,0:T(8,128)(2,1)S(1)}, bf16[128,2304]{1,0:T(8,128)(2,1)S(1)}, u32[]{:S(2)}, u32[]{:S(2)}) collective-permute-start(bf16[128,2304]{1,0:T(8,128)(2,1)S(1)} %get-tuple-element.69), channel_id=1, source_target_pairs={{0,2},{1,3},{2,0},{3,1},{4,6},{5,7},{6,4},{7,5},{8,10},{9,11},{10,... | collective-permute-start | bytes 1769480 | tf_op jit(solution)/shard_map/ppermute | solution.py:36
  88.1 2.9 %collective-permute-start.17 = (bf16[128,2304]{1,0:T(8,128)(2,1)S(1)}, bf16[128,2304]{1,0:T(8,128)(2,1)S(1)}, u32[]{:S(2)}, u32[]{:S(2)}) collective-permute-start(bf16[128,2304]{1,0:T(8,128)(2,1)S(1)} %shard_map.165), channel_id=1, source_target_pairs={{0,0},{1,1},{2,4},{3,5},{4,2},{5,3},{6,6},{7,7},{8,8},{9,9},{10,12... | collective-permute-start | bytes 1769480 | tf_op jit(solution)/shard_map/ppermute | solution.py:36
  91.3 10.1 %shard_map.169 = (bf16[128,2304]{1,0:T(8,128)(2,1)S(1)}, bf16[128,2304]{1,0:T(8,128)(2,1)S(1)}) custom-call(s32[6]{0:T(128)S(1)} %stack.35.where_ref, bf16[128,2304]{1,0:T(8,128)(2,1)S(1)} %collective-permute-done.10.refs_0_, bf16[128,2304]{1,0:T(8,128)(2,1)S(1)} %collective-permute-done.12.refs_1_, bf16[128,2304]{1,0:T(8,128)(2,1)S(1)} %collective-permute-done.8.refs_2_, ...), custom_call_target="tpu_custom_call" | custom-call | tf_op jit(solution)/shard_map/pallas_call | solution.py:169
  101.5 6.9 %collective-permute-start.23 = (bf16[2304,512]{1,0:T(8,128)(2,1)S(1)}, bf16[2304,512]{1,0:T(8,128)(2,1)S(1)}, u32[]{:S(2)}, u32[]{:S(2)}) collective-permute-start(bf16[2304,512]{1,0:T(8,128)(2,1)S(1)} %copy-done.2), channel_id=1, source_target_pairs={{0,1},{1,0},{2,3},{3,2},{4,5},{5,4},{6,7},{7,6},{8,9},{9,8},{10,11... | collective-permute-start | bytes 7077896 | tf_op jit(solution)/shard_map/ppermute | solution.py:36
  109.1 1.7 collective-permute-start.19
  110.8 1.4 collective-permute-start.20
  113.9 11.1 %collective-permute-done.20.noise_both = f32[2,128,512]{2,1,0:T(8,128)S(1)} collective-permute-done((f32[2,128,512]{2,1,0:T(8,128)S(1)}, f32[2,128,512]{2,1,0:T(8,128)S(1)}, u32[]{:S(2)}, u32[]{:S(2)}) %collective-permute-start.20) | collective-permute-done | bytes 524320 | tf_op jit(solution)/shard_map/ppermute | solution.py:36
  125.0 5.4 %collective-permute-done.19.near_ref = bf16[128,2304]{1,0:T(8,128)(2,1)S(1)} collective-permute-done((bf16[128,2304]{1,0:T(8,128)(2,1)S(1)}, bf16[128,2304]{1,0:T(8,128)(2,1)S(1)}, u32[]{:S(2)}, u32[]{:S(2)}) %collective-permute-start.19) | collective-permute-done | bytes 589856 | tf_op jit(solution)/shard_map/ppermute | solution.py:36
  130.4 1.5 shard_map.167
  131.9 1.3 collective-permute-start.22
  133.2 4.6 %collective-permute-done.22.came_ref = bf16[64,2304]{1,0:T(8,128)(2,1)S(1)} collective-permute-done((bf16[64,2304]{1,0:T(8,128)(2,1)S(1)}, bf16[64,2304]{1,0:T(8,128)(2,1)S(1)}, u32[]{:S(2)}, u32[]{:S(2)}) %collective-permute-start.22) | collective-permute-done | bytes 294944 | tf_op jit(solution)/shard_map/ppermute | solution.py:36
  138.8 2.8 %collective-permute-start.28 = (bf16[64,2304]{1,0:T(8,128)(2,1)S(1)}, bf16[64,2304]{1,0:T(8,128)(2,1)S(1)}, u32[]{:S(2)}, u32[]{:S(2)}) collective-permute-start(bf16[64,2304]{1,0:T(8,128)(2,1)S(1)} %shard_map.168.own_ref), channel_id=1, source_target_pairs={{0,4},{1,5},{2,6},{3,7},{4,0},{5,1},{6,2},{7,3},{8,12},{9,13},{10,... | collective-permute-start | bytes 884744 | tf_op jit(solution)/shard_map/ppermute | solution.py:36
  141.6 7.9 %collective-permute-start.24 = (bf16[32,512]{1,0:T(8,128)(2,1)S(1)}, bf16[32,512]{1,0:T(8,128)(2,1)S(1)}, u32[]{:S(2)}, u32[]{:S(2)}) collective-permute-start(bf16[32,512]{1,0:T(8,128)(2,1)S(1)} %bitcast.31), channel_id=1, source_target_pairs={{0,1},{1,0},{2,3},{3,2},{4,5},{5,4},{6,7},{7,6},{8,9},{9,8},{10,11... | collective-permute-start | bytes 98312 | tf_op jit(solution)/shard_map/ppermute | solution.py:36
  150.4 2.4 %shard_map.171 = (bf16[256,2304]{1,0:T(8,128)(2,1)}, bf16[64,2304]{1,0:T(8,128)(2,1)S(1)}, bf16[64,2304]{1,0:T(8,128)(2,1)S(1)}) custom-call(s32[6]{0:T(128)S(1)} %stack.35.where_ref, bf16[128,2304]{1,0:T(8,128)(2,1)S(1)} %get-tuple-element.67.own_ref, bf16[128,2304]{1,0:T(8,128)(2,1)S(1)} %collective-permute-done.14.near_ref, ...), custom_call_target="tpu_custom_call" | custom-call | tf_op jit(solution)/shard_map/pallas_call | solution.py:169
  154.8 2.7 %collective-permute-start.30 = (bf16[64,2304]{1,0:T(8,128)(2,1)S(1)}, bf16[64,2304]{1,0:T(8,128)(2,1)S(1)}, u32[]{:S(2)}, u32[]{:S(2)}) collective-permute-start(bf16[64,2304]{1,0:T(8,128)(2,1)S(1)} %collective-permute-done.28.far_ref), channel_id=1, source_target_pairs={{0,2},{1,3},{2,0},{3,1},{4,6},{5,7},{6,4},{7,5},{8,10},{9,11},{10,... | collective-permute-start | bytes 884744 | tf_op jit(solution)/shard_map/ppermute | solution.py:36
  159.5 1.8 collective-permute-start.31
  161.4 4.5 %collective-permute-done.29.near_ref = bf16[64,2304]{1,0:T(8,128)(2,1)S(1)} collective-permute-done((bf16[64,2304]{1,0:T(8,128)(2,1)S(1)}, bf16[64,2304]{1,0:T(8,128)(2,1)S(1)}, u32[]{:S(2)}, u32[]{:S(2)}) %collective-permute-start.29) | collective-permute-done | bytes 294944 | tf_op jit(solution)/shard_map/ppermute | solution.py:36
  165.9 9.7 %collective-permute-done.30.last_ref = bf16[64,2304]{1,0:T(8,128)(2,1)S(1)} collective-permute-done((bf16[64,2304]{1,0:T(8,128)(2,1)S(1)}, bf16[64,2304]{1,0:T(8,128)(2,1)S(1)}, u32[]{:S(2)}, u32[]{:S(2)}) %collective-permute-start.30) | collective-permute-done | bytes 294944 | tf_op jit(solution)/shard_map/ppermute | solution.py:36
  175.6 2.6 %shard_map.173 = f32[40,256]{1,0:T(8,128)S(1)} custom-call(s32[6]{0:T(128)S(1)} %stack.35.where_ref, bf16[64,2304]{1,0:T(8,128)(2,1)S(1)} %shard_map.168.own_ref, bf16[64,2304]{1,0:T(8,128)(2,1)S(1)} %collective-permute-done.29.near_ref, bf16[64,2304]{1,0:T(8,128)(2,1)S(1)} %collective-permute-done.28.far_ref, ...), custom_call_target="tpu_custom_call" | custom-call | flops 40000000000 | tf_op jit(solution)/shard_map/pallas_call | solution.py:169
  178.2 2.3 %collective-permute-start.33 = (bf16[64,2304]{1,0:T(8,128)(2,1)S(1)}, bf16[64,2304]{1,0:T(8,128)(2,1)S(1)}, u32[]{:S(2)}, u32[]{:S(2)}) collective-permute-start(bf16[64,2304]{1,0:T(8,128)(2,1)S(1)} %collective-permute-done.32.far_ref), channel_id=1, source_target_pairs={{0,2},{1,3},{2,0},{3,1},{4,6},{5,7},{6,4},{7,5},{8,10},{9,11},{10,... | collective-permute-start | bytes 884744 | tf_op jit(solution)/shard_map/ppermute | solution.py:36
  180.6 1.3 collective-permute-done.31.near_ref
  181.9 6.3 %collective-permute-done.33.last_ref = bf16[64,2304]{1,0:T(8,128)(2,1)S(1)} collective-permute-done((bf16[64,2304]{1,0:T(8,128)(2,1)S(1)}, bf16[64,2304]{1,0:T(8,128)(2,1)S(1)}, u32[]{:S(2)}, u32[]{:S(2)}) %collective-permute-start.33) | collective-permute-done | bytes 294944 | tf_op jit(solution)/shard_map/ppermute | solution.py:36
  188.2 2.6 %shard_map.174 = f32[40,256]{1,0:T(8,128)S(1)} custom-call(s32[6]{0:T(128)S(1)} %stack.35.where_ref, bf16[64,2304]{1,0:T(8,128)(2,1)S(1)} %shard_map.172.own_ref, bf16[64,2304]{1,0:T(8,128)(2,1)S(1)} %collective-permute-done.31.near_ref, bf16[64,2304]{1,0:T(8,128)(2,1)S(1)} %collective-permute-done.32.far_ref, ...), custom_call_target="tpu_custom_call" | custom-call | tf_op jit(solution)/shard_map/pallas_call | solution.py:169
  191.0 2.7 %collective-permute-start.35 = (f32[40,128]{1,0:T(8,128)S(1)}, f32[40,128]{1,0:T(8,128)S(1)}, u32[]{:S(2)}, u32[]{:S(2)}) collective-permute-start(f32[40,128]{1,0:T(8,128)S(1)} %pad_maximum_fusion.2), channel_id=1, source_target_pairs={{0,4},{1,5},{2,6},{3,7},{4,0},{5,1},{6,2},{7,3},{8,12},{9,13},{10,... | collective-permute-start | bytes 61448 | tf_op jit(solution)/shard_map/ppermute | solution.py:36
  197.8 1.3 collective-permute-start.39
  199.1 6.7 %collective-permute-start.38 = (f32[32,128]{1,0:T(8,128)S(1)}, f32[32,128]{1,0:T(8,128)S(1)}, u32[]{:S(2)}, u32[]{:S(2)}) collective-permute-start(f32[32,128]{1,0:T(8,128)S(1)} %shard_map.175), channel_id=1, source_target_pairs={{0,1},{1,3},{2,5},{3,7},{4,17},{5,19},{6,21},{7,23},{8,9},{9,11},{... | collective-permute-start | bytes 49160 | tf_op jit(solution)/shard_map/ppermute | solution.py:36
  205.8 1.9 collective-permute-start.37
  207.9 2.7 %collective-permute-done.37.first_ref = f32[32,128]{1,0:T(8,128)S(1)} collective-permute-done((f32[32,128]{1,0:T(8,128)S(1)}, f32[32,128]{1,0:T(8,128)S(1)}, u32[]{:S(2)}, u32[]{:S(2)}) %collective-permute-start.37) | collective-permute-done | bytes 16416 | tf_op jit(solution)/shard_map/ppermute | solution.py:36
  210.6 1.7 shard_map.176
  (97 shorter events, 22.5 us)
Async XLA Ops:
  0.6 18.5 %collective-permute-start = (bf16[2304,1152]{1,0:T(8,128)(2,1)}, bf16[2304,1152]{1,0:T(8,128)(2,1)}, u32[]{:S(2)}, u32[]{:S(2)}) collective-permute-start(bf16[2304,1152]{1,0:T(8,128)(2,1)} %refs_4_.9), channel_id=1, source_target_pairs={{0,1},{1,0},{2,3},{3,2},{4,5},{5,4},{6,7},{7,6},{8,9},{9,8},{10,11... | collective-permute-start | bytes 15925256 | tf_op jit(solution)/shard_map/ppermute | solution.py:36
  1.4 17.8 %collective-permute-start.1 = (bf16[1152,2304]{1,0:T(8,128)(2,1)}, bf16[1152,2304]{1,0:T(8,128)(2,1)}, u32[]{:S(2)}, u32[]{:S(2)}) collective-permute-start(bf16[1152,2304]{1,0:T(8,128)(2,1)} %refs_6_.1), channel_id=1, source_target_pairs={{0,1},{1,0},{2,3},{3,2},{4,5},{5,4},{6,7},{7,6},{8,9},{9,8},{10,11... | collective-permute-start | bytes 15925256 | tf_op jit(solution)/shard_map/ppermute | solution.py:36
  4.6 14.5 %collective-permute-start.3 = (bf16[128,2304]{1,0:T(8,128)(2,1)S(1)}, bf16[128,2304]{1,0:T(8,128)(2,1)S(1)}, u32[]{:S(2)}, u32[]{:S(2)}) collective-permute-start(bf16[128,2304]{1,0:T(8,128)(2,1)S(1)} %shard_map.158.refs_0_), channel_id=1, source_target_pairs={{0,2},{1,3},{2,0},{3,1},{4,6},{5,7},{6,4},{7,5},{8,10},{9,11},{10,... | collective-permute-start | bytes 1769480 | tf_op jit(solution)/shard_map/ppermute | solution.py:36
  4.8 17.7 %collective-permute-start.4 = (bf16[128,2304]{1,0:T(8,128)(2,1)S(1)}, bf16[128,2304]{1,0:T(8,128)(2,1)S(1)}, u32[]{:S(2)}, u32[]{:S(2)}) collective-permute-start(bf16[128,2304]{1,0:T(8,128)(2,1)S(1)} %shard_map.158.refs_0_), channel_id=1, source_target_pairs={{0,0},{1,1},{2,4},{3,5},{4,2},{5,3},{6,6},{7,7},{8,8},{9,9},{10,12... | collective-permute-start | bytes 1769480 | tf_op jit(solution)/shard_map/ppermute | solution.py:36
  9.9 7.5 %collective-permute-start.2 = (f32[1,1664]{1,0:T(1,128)S(1)}, f32[1,1664]{1,0:T(1,128)S(1)}, u32[]{:S(2)}, u32[]{:S(2)}) collective-permute-start(f32[1,1664]{1,0:T(1,128)S(1)} %broadcast_in_dim.12.refs_6_.refs_8_.bias_a), channel_id=1, source_target_pairs={{0,1},{1,0},{2,3},{3,2},{4,5},{5,4},{6,7},{7,6},{8,9},{9,8},{10,11... | collective-permute-start | bytes 19976 | tf_op jit(solution)/shard_map/ppermute | solution.py:36
  12.7 28.7 %slice-start = ((s8[5308416]{0:T(1024)(128)(4,1)}), s8[4194304]{0:T(1024)(128)(4,1)S(1)}, s32[]{:S(2)}) async-start(s8[5308416]{0:T(1024)(128)(4,1)} %bitcast.24), calls=%async_computation | async-start | bytes 8388608
  12.7 28.7 %slice-start.2 = ((s8[5308416]{0:T(1024)(128)(4,1)}), s8[4194304]{0:T(1024)(128)(4,1)S(1)}, s32[]{:S(2)}) async-start(s8[5308416]{0:T(1024)(128)(4,1)} %bitcast.26), calls=%async_computation.2 | async-start | bytes 8388608
  19.1 18.1 %collective-permute-start.5 = (bf16[128,2304]{1,0:T(8,128)(2,1)S(1)}, bf16[128,2304]{1,0:T(8,128)(2,1)S(1)}, u32[]{:S(2)}, u32[]{:S(2)}) collective-permute-start(bf16[128,2304]{1,0:T(8,128)(2,1)S(1)} %collective-permute-done.3.refs_1_), channel_id=1, source_target_pairs={{0,0},{1,1},{2,4},{3,5},{4,2},{5,3},{6,6},{7,7},{8,8},{9,9},{10,12... | collective-permute-start | bytes 1769480 | tf_op jit(solution)/shard_map/ppermute | solution.py:36
  22.5 18.8 %collective-permute-start.9 = (bf16[128,2304]{1,0:T(8,128)(2,1)S(1)}, bf16[128,2304]{1,0:T(8,128)(2,1)S(1)}, u32[]{:S(2)}, u32[]{:S(2)}) collective-permute-start(bf16[128,2304]{1,0:T(8,128)(2,1)S(1)} %collective-permute-done.4.refs_0_), channel_id=1, source_target_pairs={{2,0},{3,1},{4,6},{5,7},{10,8},{11,9},{12,14},{13,15},{18,16},{19,... | collective-permute-start | bytes 1769480 | tf_op jit(solution)/shard_map/ppermute | solution.py:36
  23.8 24.9 %collective-permute-start.7 = (bf16[128,2304]{1,0:T(8,128)(2,1)S(1)}, bf16[128,2304]{1,0:T(8,128)(2,1)S(1)}, u32[]{:S(2)}, u32[]{:S(2)}) collective-permute-start(bf16[128,2304]{1,0:T(8,128)(2,1)S(1)} %shard_map.159.refs_0_), channel_id=1, source_target_pairs={{0,2},{1,3},{2,0},{3,1},{4,6},{5,7},{6,4},{7,5},{8,10},{9,11},{10,... | collective-permute-start | bytes 1769480 | tf_op jit(solution)/shard_map/ppermute | solution.py:36
  37.2 15.2 %collective-permute-start.8 = (bf16[128,2304]{1,0:T(8,128)(2,1)S(1)}, bf16[128,2304]{1,0:T(8,128)(2,1)S(1)}, u32[]{:S(2)}, u32[]{:S(2)}) collective-permute-start(bf16[128,2304]{1,0:T(8,128)(2,1)S(1)} %shard_map.159.refs_0_), channel_id=1, source_target_pairs={{0,0},{1,1},{2,4},{3,5},{4,2},{5,3},{6,6},{7,7},{8,8},{9,9},{10,12... | collective-permute-start | bytes 1769480 | tf_op jit(solution)/shard_map/ppermute | solution.py:36
  39.9 20.7 %collective-permute-start.6 = (bf16[128,2304]{1,0:T(8,128)(2,1)S(1)}, bf16[128,2304]{1,0:T(8,128)(2,1)S(1)}, u32[]{:S(2)}, u32[]{:S(2)}) collective-permute-start(bf16[128,2304]{1,0:T(8,128)(2,1)S(1)} %collective-permute-done.5.refs_0_), channel_id=1, source_target_pairs={{2,0},{3,1},{4,6},{5,7},{10,8},{11,9},{12,14},{13,15},{18,16},{19,... | collective-permute-start | bytes 1769480 | tf_op jit(solution)/shard_map/ppermute | solution.py:36
  52.4 15.5 %collective-permute-start.10 = (bf16[128,2304]{1,0:T(8,128)(2,1)S(1)}, bf16[128,2304]{1,0:T(8,128)(2,1)S(1)}, u32[]{:S(2)}, u32[]{:S(2)}) collective-permute-start(bf16[128,2304]{1,0:T(8,128)(2,1)S(1)} %collective-permute-done.7.refs_1_), channel_id=1, source_target_pairs={{0,0},{1,1},{2,4},{3,5},{4,2},{5,3},{6,6},{7,7},{8,8},{9,9},{10,12... | collective-permute-start | bytes 1769480 | tf_op jit(solution)/shard_map/ppermute | solution.py:36
  55.0 13.9 %collective-permute-start.11 = (bf16[128,2304]{1,0:T(8,128)(2,1)S(1)}, bf16[128,2304]{1,0:T(8,128)(2,1)S(1)}, u32[]{:S(2)}, u32[]{:S(2)}) collective-permute-start(bf16[128,2304]{1,0:T(8,128)(2,1)S(1)} %shard_map.161.a_ref), channel_id=1, source_target_pairs={{0,2},{1,3},{6,4},{7,5},{8,10},{9,11},{14,12},{15,13},{16,18},{17,... | collective-permute-start | bytes 1769480 | tf_op jit(solution)/shard_map/ppermute | solution.py:36
  56.3 18.7 %collective-permute-start.12 = (bf16[128,2304]{1,0:T(8,128)(2,1)S(1)}, bf16[128,2304]{1,0:T(8,128)(2,1)S(1)}, u32[]{:S(2)}, u32[]{:S(2)}) collective-permute-start(bf16[128,2304]{1,0:T(8,128)(2,1)S(1)} %collective-permute-done.8.refs_2_), channel_id=1, source_target_pairs={{2,0},{3,1},{4,6},{5,7},{10,8},{11,9},{12,14},{13,15},{18,16},{19,... | collective-permute-start | bytes 1769480 | tf_op jit(solution)/shard_map/ppermute | solution.py:36
  69.7 15.5 %collective-permute-start.15 = (bf16[128,2304]{1,0:T(8,128)(2,1)S(1)}, bf16[128,2304]{1,0:T(8,128)(2,1)S(1)}, u32[]{:S(2)}, u32[]{:S(2)}) collective-permute-start(bf16[128,2304]{1,0:T(8,128)(2,1)S(1)} %shard_map.163), channel_id=1, source_target_pairs={{0,0},{1,1},{2,4},{3,5},{4,2},{5,3},{6,6},{7,7},{8,8},{9,9},{10,12... | collective-permute-start | bytes 1769480 | tf_op jit(solution)/shard_map/ppermute | solution.py:36
  72.4 12.8 %collective-permute-start.13 = (bf16[128,2304]{1,0:T(8,128)(2,1)S(1)}, bf16[128,2304]{1,0:T(8,128)(2,1)S(1)}, u32[]{:S(2)}, u32[]{:S(2)}) collective-permute-start(bf16[128,2304]{1,0:T(8,128)(2,1)S(1)} %collective-permute-done.10.refs_0_), channel_id=1, source_target_pairs={{2,0},{3,1},{4,6},{5,7},{10,8},{11,9},{12,14},{13,15},{18,16},{19,... | collective-permute-start | bytes 1769480 | tf_op jit(solution)/shard_map/ppermute | solution.py:36
  73.7 13.7 %collective-permute-start.16 = (bf16[128,2304]{1,0:T(8,128)(2,1)S(1)}, bf16[128,2304]{1,0:T(8,128)(2,1)S(1)}, u32[]{:S(2)}, u32[]{:S(2)}) collective-permute-start(bf16[128,2304]{1,0:T(8,128)(2,1)S(1)} %shard_map.162.a_ref), channel_id=1, source_target_pairs={{0,2},{1,3},{6,4},{7,5},{8,10},{9,11},{14,12},{15,13},{16,18},{17,... | collective-permute-start | bytes 1769480 | tf_op jit(solution)/shard_map/ppermute | solution.py:36
  85.2 23.2 %collective-permute-start.14 = (bf16[128,2304]{1,0:T(8,128)(2,1)S(1)}, bf16[128,2304]{1,0:T(8,128)(2,1)S(1)}, u32[]{:S(2)}, u32[]{:S(2)}) collective-permute-start(bf16[128,2304]{1,0:T(8,128)(2,1)S(1)} %get-tuple-element.69), channel_id=1, source_target_pairs={{0,2},{1,3},{2,0},{3,1},{4,6},{5,7},{6,4},{7,5},{8,10},{9,11},{10,... | collective-permute-start | bytes 1769480 | tf_op jit(solution)/shard_map/ppermute | solution.py:36
  88.1 20.3 %collective-permute-start.17 = (bf16[128,2304]{1,0:T(8,128)(2,1)S(1)}, bf16[128,2304]{1,0:T(8,128)(2,1)S(1)}, u32[]{:S(2)}, u32[]{:S(2)}) collective-permute-start(bf16[128,2304]{1,0:T(8,128)(2,1)S(1)} %shard_map.165), channel_id=1, source_target_pairs={{0,0},{1,1},{2,4},{3,5},{4,2},{5,3},{6,6},{7,7},{8,8},{9,9},{10,12... | collective-permute-start | bytes 1769480 | tf_op jit(solution)/shard_map/ppermute | solution.py:36
  91.1 17.3 %collective-permute-start.18 = (f32[2,128,512]{2,1,0:T(8,128)S(1)}, f32[2,128,512]{2,1,0:T(8,128)S(1)}, u32[]{:S(2)}, u32[]{:S(2)}) collective-permute-start(f32[2,128,512]{2,1,0:T(8,128)S(1)} %bitcast.38), channel_id=1, source_target_pairs={{0,16},{1,17},{2,18},{3,19},{4,20},{5,21},{6,22},{7,23},{8,24},{9,... | collective-permute-start | bytes 1572872 | tf_op jit(solution)/shard_map/ppermute | solution.py:36
  101.4 29.0 %copy-start.3 = (f32[2,2,2304]{2,1,0:T(2,128)S(1)}, f32[2,2,2304]{2,1,0:T(2,128)}, u32[]{:S(2)}) copy-start(f32[2,2,2304]{2,1,0:T(2,128)} %ada_ref.11) | copy-start | bytes 110596
  101.4 29.0 %copy-start.7 = (f32[2,2304]{1,0:T(2,128)S(1)}, f32[2,2304]{1,0:T(2,128)}, u32[]{:S(2)}) copy-start(f32[2,2304]{1,0:T(2,128)} %gate_ref.3) | copy-start | bytes 55300
  101.4 11.1 %collective-permute-start.25 = (bf16[128,2304]{1,0:T(8,128)(2,1)S(1)}, bf16[128,2304]{1,0:T(8,128)(2,1)S(1)}, u32[]{:S(2)}, u32[]{:S(2)}) collective-permute-start(bf16[128,2304]{1,0:T(8,128)(2,1)S(1)} %get-tuple-element.83), channel_id=1, source_target_pairs={{0,2},{1,3},{2,0},{3,1},{4,6},{5,7},{6,4},{7,5},{8,10},{9,11},{10,... | collective-permute-start | bytes 1769480 | tf_op jit(solution)/shard_map/ppermute | solution.py:36
  101.5 48.9 %collective-permute-start.23 = (bf16[2304,512]{1,0:T(8,128)(2,1)S(1)}, bf16[2304,512]{1,0:T(8,128)(2,1)S(1)}, u32[]{:S(2)}, u32[]{:S(2)}) collective-permute-start(bf16[2304,512]{1,0:T(8,128)(2,1)S(1)} %copy-done.2), channel_id=1, source_target_pairs={{0,1},{1,0},{2,3},{3,2},{4,5},{5,4},{6,7},{7,6},{8,9},{9,8},{10,11... | collective-permute-start | bytes 7077896 | tf_op jit(solution)/shard_map/ppermute | solution.py:36
  109.1 21.3 %collective-permute-start.19 = (bf16[128,2304]{1,0:T(8,128)(2,1)S(1)}, bf16[128,2304]{1,0:T(8,128)(2,1)S(1)}, u32[]{:S(2)}, u32[]{:S(2)}) collective-permute-start(bf16[128,2304]{1,0:T(8,128)(2,1)S(1)} %shard_map.166), channel_id=1, source_target_pairs={{0,2},{1,3},{2,0},{3,1},{4,6},{5,7},{6,4},{7,5},{8,10},{9,11},{10,... | collective-permute-start | bytes 1769480 | tf_op jit(solution)/shard_map/ppermute | solution.py:36
  110.8 14.1 %collective-permute-start.20 = (f32[2,128,512]{2,1,0:T(8,128)S(1)}, f32[2,128,512]{2,1,0:T(8,128)S(1)}, u32[]{:S(2)}, u32[]{:S(2)}) collective-permute-start(f32[2,128,512]{2,1,0:T(8,128)S(1)} %bitcast.37), channel_id=1, source_target_pairs={{0,17},{1,16},{2,19},{3,18},{4,21},{5,20},{6,23},{7,22},{8,25},{9,... | collective-permute-start | bytes 1572872 | tf_op jit(solution)/shard_map/ppermute | solution.py:36
  112.3 12.7 %collective-permute-start.21 = (f32[2,128,512]{2,1,0:T(8,128)S(1)}, f32[2,128,512]{2,1,0:T(8,128)S(1)}, u32[]{:S(2)}, u32[]{:S(2)}) collective-permute-start(f32[2,128,512]{2,1,0:T(8,128)S(1)} %bitcast.36), channel_id=1, source_target_pairs={{0,1},{1,0},{2,3},{3,2},{4,5},{5,4},{6,7},{7,6},{8,9},{9,8},{10,11... | collective-permute-start | bytes 1572872 | tf_op jit(solution)/shard_map/ppermute | solution.py:36
  113.2 28.4 %copy-start.8 = (bf16[512,32]{0,1:T(8,128)(2,1)S(1)}, bf16[512,32]{0,1:T(8,128)(2,1)}, u32[]{:S(2)}) copy-start(bf16[512,32]{0,1:T(8,128)(2,1)} %param.26) | copy-start | bytes 98308
  113.2 37.2 %collective-permute-start.26 = (bf16[128,2304]{1,0:T(8,128)(2,1)S(1)}, bf16[128,2304]{1,0:T(8,128)(2,1)S(1)}, u32[]{:S(2)}, u32[]{:S(2)}) collective-permute-start(bf16[128,2304]{1,0:T(8,128)(2,1)S(1)} %shard_map.170), channel_id=1, source_target_pairs={{0,4},{1,5},{2,6},{3,7},{4,0},{5,1},{6,2},{7,3},{8,12},{9,13},{10,... | collective-permute-start | bytes 1769480 | tf_op jit(solution)/shard_map/ppermute | solution.py:36
  131.9 5.9 %collective-permute-start.22 = (bf16[64,2304]{1,0:T(8,128)(2,1)S(1)}, bf16[64,2304]{1,0:T(8,128)(2,1)S(1)}, u32[]{:S(2)}, u32[]{:S(2)}) collective-permute-start(bf16[64,2304]{1,0:T(8,128)(2,1)S(1)} %get-tuple-element.81), channel_id=1, source_target_pairs={{0,16},{1,17},{2,18},{3,19},{4,20},{5,21},{6,22},{7,23},{8,24},{9,... | collective-permute-start | bytes 884744 | tf_op jit(solution)/shard_map/ppermute | solution.py:36
  138.8 16.0 %collective-permute-start.28 = (bf16[64,2304]{1,0:T(8,128)(2,1)S(1)}, bf16[64,2304]{1,0:T(8,128)(2,1)S(1)}, u32[]{:S(2)}, u32[]{:S(2)}) collective-permute-start(bf16[64,2304]{1,0:T(8,128)(2,1)S(1)} %shard_map.168.own_ref), channel_id=1, source_target_pairs={{0,4},{1,5},{2,6},{3,7},{4,0},{5,1},{6,2},{7,3},{8,12},{9,13},{10,... | collective-permute-start | bytes 884744 | tf_op jit(solution)/shard_map/ppermute | solution.py:36
  141.6 8.8 %collective-permute-start.24 = (bf16[32,512]{1,0:T(8,128)(2,1)S(1)}, bf16[32,512]{1,0:T(8,128)(2,1)S(1)}, u32[]{:S(2)}, u32[]{:S(2)}) collective-permute-start(bf16[32,512]{1,0:T(8,128)(2,1)S(1)} %bitcast.31), channel_id=1, source_target_pairs={{0,1},{1,0},{2,3},{3,2},{4,5},{5,4},{6,7},{7,6},{8,9},{9,8},{10,11... | collective-permute-start | bytes 98312 | tf_op jit(solution)/shard_map/ppermute | solution.py:36
  152.8 5.6 %collective-permute-start.27 = (bf16[64,2304]{1,0:T(8,128)(2,1)S(1)}, bf16[64,2304]{1,0:T(8,128)(2,1)S(1)}, u32[]{:S(2)}, u32[]{:S(2)}) collective-permute-start(bf16[64,2304]{1,0:T(8,128)(2,1)S(1)} %get-tuple-element.92), channel_id=1, source_target_pairs={{0,16},{1,17},{2,18},{3,19},{4,20},{5,21},{6,22},{7,23},{8,24},{9,... | collective-permute-start | bytes 884744 | tf_op jit(solution)/shard_map/ppermute | solution.py:36
  154.1 11.8 %collective-permute-start.29 = (bf16[64,2304]{1,0:T(8,128)(2,1)S(1)}, bf16[64,2304]{1,0:T(8,128)(2,1)S(1)}, u32[]{:S(2)}, u32[]{:S(2)}) collective-permute-start(bf16[64,2304]{1,0:T(8,128)(2,1)S(1)} %shard_map.168.own_ref), channel_id=1, source_target_pairs={{0,2},{1,3},{2,0},{3,1},{4,6},{5,7},{6,4},{7,5},{8,10},{9,11},{10,... | collective-permute-start | bytes 884744 | tf_op jit(solution)/shard_map/ppermute | solution.py:36
  154.8 20.7 %collective-permute-start.30 = (bf16[64,2304]{1,0:T(8,128)(2,1)S(1)}, bf16[64,2304]{1,0:T(8,128)(2,1)S(1)}, u32[]{:S(2)}, u32[]{:S(2)}) collective-permute-start(bf16[64,2304]{1,0:T(8,128)(2,1)S(1)} %collective-permute-done.28.far_ref), channel_id=1, source_target_pairs={{0,2},{1,3},{2,0},{3,1},{4,6},{5,7},{6,4},{7,5},{8,10},{9,11},{10,... | collective-permute-start | bytes 884744 | tf_op jit(solution)/shard_map/ppermute | solution.py:36
  159.4 18.8 %collective-permute-start.32 = (bf16[64,2304]{1,0:T(8,128)(2,1)S(1)}, bf16[64,2304]{1,0:T(8,128)(2,1)S(1)}, u32[]{:S(2)}, u32[]{:S(2)}) collective-permute-start(bf16[64,2304]{1,0:T(8,128)(2,1)S(1)} %shard_map.172.own_ref), channel_id=1, source_target_pairs={{0,4},{1,5},{2,6},{3,7},{4,0},{5,1},{6,2},{7,3},{8,12},{9,13},{10,... | collective-permute-start | bytes 884744 | tf_op jit(solution)/shard_map/ppermute | solution.py:36
  159.5 22.3 %collective-permute-start.31 = (bf16[64,2304]{1,0:T(8,128)(2,1)S(1)}, bf16[64,2304]{1,0:T(8,128)(2,1)S(1)}, u32[]{:S(2)}, u32[]{:S(2)}) collective-permute-start(bf16[64,2304]{1,0:T(8,128)(2,1)S(1)} %shard_map.172.own_ref), channel_id=1, source_target_pairs={{0,2},{1,3},{2,0},{3,1},{4,6},{5,7},{6,4},{7,5},{8,10},{9,11},{10,... | collective-permute-start | bytes 884744 | tf_op jit(solution)/shard_map/ppermute | solution.py:36
  178.2 10.0 %collective-permute-start.33 = (bf16[64,2304]{1,0:T(8,128)(2,1)S(1)}, bf16[64,2304]{1,0:T(8,128)(2,1)S(1)}, u32[]{:S(2)}, u32[]{:S(2)}) collective-permute-start(bf16[64,2304]{1,0:T(8,128)(2,1)S(1)} %collective-permute-done.32.far_ref), channel_id=1, source_target_pairs={{0,2},{1,3},{2,0},{3,1},{4,6},{5,7},{6,4},{7,5},{8,10},{9,11},{10,... | collective-permute-start | bytes 884744 | tf_op jit(solution)/shard_map/ppermute | solution.py:36
  180.6 27.2 %copy-start.11 = (f32[32]{0:T(128)S(1)}, f32[32]{0:T(128)}, u32[]{:S(2)}) copy-start(f32[32]{0:T(128)} %param.28) | copy-start | bytes 388
  180.6 30.0 %copy-start.4 = (f32[32,32,3,3]{1,0,3,2:T(8,128)S(1)}, f32[32,32,3,3]{1,0,3,2:T(8,128)}, u32[]{:S(2)}) copy-start(f32[32,32,3,3]{1,0,3,2:T(8,128)} %param.27) | copy-start | bytes 110596
  180.6 30.0 %copy-start.9 = (f32[1,32,128]{2,1,0:T(8,128)S(1)}, f32[1,32,128]{2,1,0:T(8,128)}, u32[]{:S(2)}) copy-start(f32[1,32,128]{2,1,0:T(8,128)} %param.29) | copy-start | bytes 49156
  191.0 4.1 %collective-permute-start.35 = (f32[40,128]{1,0:T(8,128)S(1)}, f32[40,128]{1,0:T(8,128)S(1)}, u32[]{:S(2)}, u32[]{:S(2)}) collective-permute-start(f32[40,128]{1,0:T(8,128)S(1)} %pad_maximum_fusion.2), channel_id=1, source_target_pairs={{0,4},{1,5},{2,6},{3,7},{4,0},{5,1},{6,2},{7,3},{8,12},{9,13},{10,... | collective-permute-start | bytes 61448 | tf_op jit(solution)/shard_map/ppermute | solution.py:36
  193.8 2.6 %collective-permute-start.36 = (f32[40,128]{1,0:T(8,128)S(1)}, f32[40,128]{1,0:T(8,128)S(1)}, u32[]{:S(2)}, u32[]{:S(2)}) collective-permute-start(f32[40,128]{1,0:T(8,128)S(1)} %pad_maximum_fusion.3), channel_id=1, source_target_pairs={{0,6},{1,7},{2,4},{3,5},{4,2},{5,3},{6,0},{7,1},{8,14},{9,15},{10,... | collective-permute-start | bytes 61448 | tf_op jit(solution)/shard_map/ppermute | solution.py:36
  194.6 2.6 %collective-permute-start.34 = (f32[40,128]{1,0:T(8,128)S(1)}, f32[40,128]{1,0:T(8,128)S(1)}, u32[]{:S(2)}, u32[]{:S(2)}) collective-permute-start(f32[40,128]{1,0:T(8,128)S(1)} %pad_maximum_fusion.1), channel_id=1, source_target_pairs={{0,2},{1,3},{2,0},{3,1},{4,6},{5,7},{6,4},{7,5},{8,10},{9,11},{10,... | collective-permute-start | bytes 61448 | tf_op jit(solution)/shard_map/ppermute | solution.py:36
  197.8 10.1 %collective-permute-start.39 = (f32[32,128]{1,0:T(8,128)S(1)}, f32[32,128]{1,0:T(8,128)S(1)}, u32[]{:S(2)}, u32[]{:S(2)}) collective-permute-start(f32[32,128]{1,0:T(8,128)S(1)} %shard_map.175), channel_id=1, source_target_pairs={{1,1},{2,3},{3,5},{5,17},{6,19},{7,21},{9,9},{10,11},{11,13},{13,2... | collective-permute-start | bytes 49160 | tf_op jit(solution)/shard_map/ppermute | solution.py:36
  199.1 8.8 %collective-permute-start.38 = (f32[32,128]{1,0:T(8,128)S(1)}, f32[32,128]{1,0:T(8,128)S(1)}, u32[]{:S(2)}, u32[]{:S(2)}) collective-permute-start(f32[32,128]{1,0:T(8,128)S(1)} %shard_map.175), channel_id=1, source_target_pairs={{0,1},{1,3},{2,5},{3,7},{4,17},{5,19},{6,21},{7,23},{8,9},{9,11},{... | collective-permute-start | bytes 49160 | tf_op jit(solution)/shard_map/ppermute | solution.py:36
  205.8 4.8 %collective-permute-start.37 = (f32[32,128]{1,0:T(8,128)S(1)}, f32[32,128]{1,0:T(8,128)S(1)}, u32[]{:S(2)}, u32[]{:S(2)}) collective-permute-start(f32[32,128]{1,0:T(8,128)S(1)} %shard_map.175), channel_id=1, source_target_pairs={{0,0},{1,2},{2,4},{3,6},{4,16},{5,18},{6,20},{7,22},{8,8},{9,10},{... | collective-permute-start | bytes 49160 | tf_op jit(solution)/shard_map/ppermute | solution.py:36
  (8 other events, 88.6 us)

commit v12 on v9

--- a/solution.py
+++ b/solution.py
@@ -585,7 +585,7 @@
         where, step, True, sum_own_b, after(came_near_b, mixed_a, head_other, code_other), went_far_b, tokens, gate, bias_out, ada_head, (out_a,)
     )
     came_b = after(swap_twins(sent_b), mix_far_a)
-    mix_last_a = near(mix_far_a)
+    mix_last_a = near(after(mix_far_a, mix_near_a))
     mixed_b = mix_twins(where, kept_b, came_b, ada_head)
     mix_near_b, mix_far_b = near(mixed_b), across(mixed_b)
     heads = (head_weight, head_other, biases, bias_other, codes, code_other)

time: 216 us -> 210 us (0.972)
  waiting for transfers between devices: 60.9 us -> 54.5 us
    ppermute x40, waiting for transfers between devices: 60.9 us -> 54.5 us  [permute_devices(): return lax.ppermute(value, ('dp', 'mp'), pairs)]
  transfers between devices with their start and end apart: 40 -> 40, of which waited for: 18 -> 17; matrix products, arithmetic and copies ran while one was open for 1% -> 1% of each run, Pallas kernels for 28% -> 29%
where the time goes in v12:
time: 210 us; the launch traced here: 207 us
  starting transfers between devices  81.4 us (39%)
  Pallas kernels  64.9 us (31%)
  waiting for transfers between devices  54.5 us (26%)
  local copies, waits for them, and re-layouts  4.2 us (2%)
    ppermute x40, starting transfers between devices, permute_devices(): return lax.ppermute(value, ('dp', 'mp'), pairs)  81.4 us
    pallas_call x19, Pallas kernels, call(): pl.pallas_call(kernel, out_shape=outs, in_specs=[SCALARS] + (specs or [ON...  64.9 us
    ppermute x40, waiting for transfers between devices, permute_devices(): return lax.ppermute(value, ('dp', 'mp'), pairs)  54.5 us
  transfers between devices with their start and end apart: 40, of which 17 were waited for; matrix products, arithmetic and copies ran while one was open for 1% of the time, Pallas kernels for 29%

profile of v12, /device:TPU:13, one launch (start us, length us, event | category | flops | bytes accessed | tf_op | source)
XLA Modules:
  0.0 207.1 jit_solution(16815297938356719130)
XLA Ops:
  4.8 4.3 %collective-permute-start.4 = (bf16[128,2304]{1,0:T(8,128)(2,1)S(1)}, bf16[128,2304]{1,0:T(8,128)(2,1)S(1)}, u32[]{:S(2)}, u32[]{:S(2)}) collective-permute-start(bf16[128,2304]{1,0:T(8,128)(2,1)S(1)} %shard_map.158.refs_0_), channel_id=1, source_target_pairs={{0,0},{1,1},{2,4},{3,5},{4,2},{5,3},{6,6},{7,7},{8,8},{9,9},{10,12... | collective-permute-start | bytes 1769480 | tf_op jit(solution)/shard_map/ppermute | solution.py:36
  10.9 1.7 constant_dynamic-slice_fusion
  13.7 3.6 %collective-permute-done.2.refs_7_.refs_9_.bias_b = f32[1,1664]{1,0:T(1,128)S(1)} collective-permute-done((f32[1,1664]{1,0:T(1,128)S(1)}, f32[1,1664]{1,0:T(1,128)S(1)}, u32[]{:S(2)}, u32[]{:S(2)}) %collective-permute-start.2) | collective-permute-done | bytes 6688 | tf_op jit(solution)/shard_map/ppermute | solution.py:36
  17.4 1.8 collective-permute-done.3.refs_1_
  19.1 3.3 %collective-permute-start.5 = (bf16[128,2304]{1,0:T(8,128)(2,1)S(1)}, bf16[128,2304]{1,0:T(8,128)(2,1)S(1)}, u32[]{:S(2)}, u32[]{:S(2)}) collective-permute-start(bf16[128,2304]{1,0:T(8,128)(2,1)S(1)} %collective-permute-done.3.refs_1_), channel_id=1, source_target_pairs={{0,0},{1,1},{2,4},{3,5},{4,2},{5,3},{6,6},{7,7},{8,8},{9,9},{10,12... | collective-permute-start | bytes 1769480 | tf_op jit(solution)/shard_map/ppermute | solution.py:36
  22.5 1.3 collective-permute-start.9
  23.9 11.9 %shard_map.160 = (bf16[128,2304]{1,0:T(8,128)(2,1)S(1)}, bf16[128,2304]{1,0:T(8,128)(2,1)S(1)}) custom-call(s32[6]{0:T(128)S(1)} %stack.35.where_ref, bf16[128,2304]{1,0:T(8,128)(2,1)S(1)} %shard_map.158.refs_0_, bf16[128,2304]{1,0:T(8,128)(2,1)S(1)} %collective-permute-done.3.refs_1_, bf16[2304,1152]{1,0:T(8,128)(2,1)} %refs_4_.9, ...), custom_call_target="tpu_custom_call" | custom-call | tf_op jit(solution)/shard_map/pallas_call | solution.py:169
  35.8 2.7 %collective-permute-start.8 = (bf16[128,2304]{1,0:T(8,128)(2,1)S(1)}, bf16[128,2304]{1,0:T(8,128)(2,1)S(1)}, u32[]{:S(2)}, u32[]{:S(2)}) collective-permute-start(bf16[128,2304]{1,0:T(8,128)(2,1)S(1)} %shard_map.159.refs_0_), channel_id=1, source_target_pairs={{0,0},{1,1},{2,4},{3,5},{4,2},{5,3},{6,6},{7,7},{8,8},{9,9},{10,12... | collective-permute-start | bytes 1769480 | tf_op jit(solution)/shard_map/ppermute | solution.py:36
  38.5 1.4 collective-permute-start.6
  40.0 7.3 %shard_map.161.a_ref = bf16[128,2304]{1,0:T(8,128)(2,1)S(1)} custom-call(s32[6]{0:T(128)S(1)} %stack.35.where_ref, bf16[128,2304]{1,0:T(8,128)(2,1)S(1)} %collective-permute-done.5.refs_0_, bf16[128,2304]{1,0:T(8,128)(2,1)S(1)} %collective-permute-done.9.refs_1_, bf16[2304,1152]{1,0:T(8,128)(2,1)S(1)} %bitcast.25, ...), custom_call_target="tpu_custom_call" | custom-call | tf_op jit(solution)/shard_map/pallas_call | solution.py:169
  47.8 3.2 %collective-permute-done.8.refs_2_ = bf16[128,2304]{1,0:T(8,128)(2,1)S(1)} collective-permute-done((bf16[128,2304]{1,0:T(8,128)(2,1)S(1)}, bf16[128,2304]{1,0:T(8,128)(2,1)S(1)}, u32[]{:S(2)}, u32[]{:S(2)}) %collective-permute-start.8) | collective-permute-done | bytes 589856 | tf_op jit(solution)/shard_map/ppermute | solution.py:36
  51.0 2.6 %collective-permute-start.10 = (bf16[128,2304]{1,0:T(8,128)(2,1)S(1)}, bf16[128,2304]{1,0:T(8,128)(2,1)S(1)}, u32[]{:S(2)}, u32[]{:S(2)}) collective-permute-start(bf16[128,2304]{1,0:T(8,128)(2,1)S(1)} %collective-permute-done.7.refs_1_), channel_id=1, source_target_pairs={{0,0},{1,1},{2,4},{3,5},{4,2},{5,3},{6,6},{7,7},{8,8},{9,9},{10,12... | collective-permute-start | bytes 1769480 | tf_op jit(solution)/shard_map/ppermute | solution.py:36
  53.6 1.3 collective-permute-start.11
  54.9 4.2 %collective-permute-start.12 = (bf16[128,2304]{1,0:T(8,128)(2,1)S(1)}, bf16[128,2304]{1,0:T(8,128)(2,1)S(1)}, u32[]{:S(2)}, u32[]{:S(2)}) collective-permute-start(bf16[128,2304]{1,0:T(8,128)(2,1)S(1)} %collective-permute-done.8.refs_2_), channel_id=1, source_target_pairs={{2,0},{3,1},{4,6},{5,7},{10,8},{11,9},{12,14},{13,15},{18,16},{19,... | collective-permute-start | bytes 1769480 | tf_op jit(solution)/shard_map/ppermute | solution.py:36
  60.4 7.3 %shard_map.162.a_ref = bf16[128,2304]{1,0:T(8,128)(2,1)S(1)} custom-call(s32[6]{0:T(128)S(1)} %stack.35.where_ref, bf16[128,2304]{1,0:T(8,128)(2,1)S(1)} %collective-permute-done.4.refs_0_, bf16[128,2304]{1,0:T(8,128)(2,1)S(1)} %collective-permute-done.6.refs_1_, bf16[2304,1152]{1,0:T(8,128)(2,1)S(1)} %bitcast.25, ...), custom_call_target="tpu_custom_call" | custom-call | tf_op jit(solution)/shard_map/pallas_call | solution.py:169
  68.5 2.6 %collective-permute-start.15 = (bf16[128,2304]{1,0:T(8,128)(2,1)S(1)}, bf16[128,2304]{1,0:T(8,128)(2,1)S(1)}, u32[]{:S(2)}, u32[]{:S(2)}) collective-permute-start(bf16[128,2304]{1,0:T(8,128)(2,1)S(1)} %shard_map.163), channel_id=1, source_target_pairs={{0,0},{1,1},{2,4},{3,5},{4,2},{5,3},{6,6},{7,7},{8,8},{9,9},{10,12... | collective-permute-start | bytes 1769480 | tf_op jit(solution)/shard_map/ppermute | solution.py:36
  71.1 2.2 %collective-permute-start.13 = (bf16[128,2304]{1,0:T(8,128)(2,1)S(1)}, bf16[128,2304]{1,0:T(8,128)(2,1)S(1)}, u32[]{:S(2)}, u32[]{:S(2)}) collective-permute-start(bf16[128,2304]{1,0:T(8,128)(2,1)S(1)} %collective-permute-done.10.refs_0_), channel_id=1, source_target_pairs={{2,0},{3,1},{4,6},{5,7},{10,8},{11,9},{12,14},{13,15},{18,16},{19,... | collective-permute-start | bytes 1769480 | tf_op jit(solution)/shard_map/ppermute | solution.py:36
  73.3 1.3 collective-permute-start.16
  74.6 10.1 %shard_map.164 = (bf16[128,2304]{1,0:T(8,128)(2,1)S(1)}, bf16[128,2304]{1,0:T(8,128)(2,1)S(1)}) custom-call(s32[6]{0:T(128)S(1)} %stack.35.where_ref, bf16[128,2304]{1,0:T(8,128)(2,1)S(1)} %shard_map.159.refs_0_, bf16[128,2304]{1,0:T(8,128)(2,1)S(1)} %collective-permute-done.7.refs_1_, bf16[2304,1152]{1,0:T(8,128)(2,1)S(1)} %bitcast.25, ...), custom_call_target="tpu_custom_call" | custom-call | tf_op jit(solution)/shard_map/pallas_call | solution.py:169
  84.8 2.2 %collective-permute-start.14 = (bf16[128,2304]{1,0:T(8,128)(2,1)S(1)}, bf16[128,2304]{1,0:T(8,128)(2,1)S(1)}, u32[]{:S(2)}, u32[]{:S(2)}) collective-permute-start(bf16[128,2304]{1,0:T(8,128)(2,1)S(1)} %get-tuple-element.70), channel_id=1, source_target_pairs={{0,2},{1,3},{2,0},{3,1},{4,6},{5,7},{6,4},{7,5},{8,10},{9,11},{10,... | collective-permute-start | bytes 1769480 | tf_op jit(solution)/shard_map/ppermute | solution.py:36
  87.7 3.0 %collective-permute-start.17 = (bf16[128,2304]{1,0:T(8,128)(2,1)S(1)}, bf16[128,2304]{1,0:T(8,128)(2,1)S(1)}, u32[]{:S(2)}, u32[]{:S(2)}) collective-permute-start(bf16[128,2304]{1,0:T(8,128)(2,1)S(1)} %shard_map.165), channel_id=1, source_target_pairs={{0,0},{1,1},{2,4},{3,5},{4,2},{5,3},{6,6},{7,7},{8,8},{9,9},{10,12... | collective-permute-start | bytes 1769480 | tf_op jit(solution)/shard_map/ppermute | solution.py:36
  91.0 10.1 %shard_map.169 = (bf16[128,2304]{1,0:T(8,128)(2,1)S(1)}, bf16[128,2304]{1,0:T(8,128)(2,1)S(1)}) custom-call(s32[6]{0:T(128)S(1)} %stack.35.where_ref, bf16[128,2304]{1,0:T(8,128)(2,1)S(1)} %collective-permute-done.10.refs_0_, bf16[128,2304]{1,0:T(8,128)(2,1)S(1)} %collective-permute-done.12.refs_1_, bf16[128,2304]{1,0:T(8,128)(2,1)S(1)} %collective-permute-done.8.refs_2_, ...), custom_call_target="tpu_custom_call" | custom-call | tf_op jit(solution)/shard_map/pallas_call | solution.py:169
  101.2 6.9 %collective-permute-start.23 = (bf16[2304,512]{1,0:T(8,128)(2,1)S(1)}, bf16[2304,512]{1,0:T(8,128)(2,1)S(1)}, u32[]{:S(2)}, u32[]{:S(2)}) collective-permute-start(bf16[2304,512]{1,0:T(8,128)(2,1)S(1)} %copy-done.2), channel_id=1, source_target_pairs={{0,1},{1,0},{2,3},{3,2},{4,5},{5,4},{6,7},{7,6},{8,9},{9,8},{10,11... | collective-permute-start | bytes 7077896 | tf_op jit(solution)/shard_map/ppermute | solution.py:36
  108.8 1.7 collective-permute-start.19
  110.5 1.4 collective-permute-start.20
  113.5 11.2 %collective-permute-done.20.noise_both = f32[2,128,512]{2,1,0:T(8,128)S(1)} collective-permute-done((f32[2,128,512]{2,1,0:T(8,128)S(1)}, f32[2,128,512]{2,1,0:T(8,128)S(1)}, u32[]{:S(2)}, u32[]{:S(2)}) %collective-permute-start.20) | collective-permute-done | bytes 524320 | tf_op jit(solution)/shard_map/ppermute | solution.py:36
  124.7 5.4 %collective-permute-done.19.near_ref = bf16[128,2304]{1,0:T(8,128)(2,1)S(1)} collective-permute-done((bf16[128,2304]{1,0:T(8,128)(2,1)S(1)}, bf16[128,2304]{1,0:T(8,128)(2,1)S(1)}, u32[]{:S(2)}, u32[]{:S(2)}) %collective-permute-start.19) | collective-permute-done | bytes 589856 | tf_op jit(solution)/shard_map/ppermute | solution.py:36
  130.1 1.5 shard_map.167
  131.6 1.3 collective-permute-start.22
  132.9 4.6 %collective-permute-done.22.came_ref = bf16[64,2304]{1,0:T(8,128)(2,1)S(1)} collective-permute-done((bf16[64,2304]{1,0:T(8,128)(2,1)S(1)}, bf16[64,2304]{1,0:T(8,128)(2,1)S(1)}, u32[]{:S(2)}, u32[]{:S(2)}) %collective-permute-start.22) | collective-permute-done | bytes 294944 | tf_op jit(solution)/shard_map/ppermute | solution.py:36
  138.5 2.3 %collective-permute-start.29 = (bf16[64,2304]{1,0:T(8,128)(2,1)S(1)}, bf16[64,2304]{1,0:T(8,128)(2,1)S(1)}, u32[]{:S(2)}, u32[]{:S(2)}) collective-permute-start(bf16[64,2304]{1,0:T(8,128)(2,1)S(1)} %shard_map.168.own_ref), channel_id=1, source_target_pairs={{0,2},{1,3},{2,0},{3,1},{4,6},{5,7},{6,4},{7,5},{8,10},{9,11},{10,... | collective-permute-start | bytes 884744 | tf_op jit(solution)/shard_map/ppermute | solution.py:36
  141.3 8.0 %collective-permute-start.24 = (bf16[32,512]{1,0:T(8,128)(2,1)S(1)}, bf16[32,512]{1,0:T(8,128)(2,1)S(1)}, u32[]{:S(2)}, u32[]{:S(2)}) collective-permute-start(bf16[32,512]{1,0:T(8,128)(2,1)S(1)} %bitcast.31), channel_id=1, source_target_pairs={{0,1},{1,0},{2,3},{3,2},{4,5},{5,4},{6,7},{7,6},{8,9},{9,8},{10,11... | collective-permute-start | bytes 98312 | tf_op jit(solution)/shard_map/ppermute | solution.py:36
  150.1 2.4 %shard_map.171 = (bf16[256,2304]{1,0:T(8,128)(2,1)}, bf16[64,2304]{1,0:T(8,128)(2,1)S(1)}, bf16[64,2304]{1,0:T(8,128)(2,1)S(1)}) custom-call(s32[6]{0:T(128)S(1)} %stack.35.where_ref, bf16[128,2304]{1,0:T(8,128)(2,1)S(1)} %get-tuple-element.68.own_ref, bf16[128,2304]{1,0:T(8,128)(2,1)S(1)} %collective-permute-done.14.near_ref, ...), custom_call_target="tpu_custom_call" | custom-call | tf_op jit(solution)/shard_map/pallas_call | solution.py:169
  153.8 1.7 collective-permute-start.30
  155.5 3.3 %collective-permute-done.27.came_ref = bf16[64,2304]{1,0:T(8,128)(2,1)S(1)} collective-permute-done((bf16[64,2304]{1,0:T(8,128)(2,1)S(1)}, bf16[64,2304]{1,0:T(8,128)(2,1)S(1)}, u32[]{:S(2)}, u32[]{:S(2)}) %collective-permute-start.27) | collective-permute-done | bytes 294944 | tf_op jit(solution)/shard_map/ppermute | solution.py:36
  159.8 1.8 collective-permute-start.32
  162.0 2.6 %shard_map.173 = f32[40,256]{1,0:T(8,128)S(1)} custom-call(s32[6]{0:T(128)S(1)} %stack.35.where_ref, bf16[64,2304]{1,0:T(8,128)(2,1)S(1)} %shard_map.168.own_ref, bf16[64,2304]{1,0:T(8,128)(2,1)S(1)} %collective-permute-done.29.near_ref, bf16[64,2304]{1,0:T(8,128)(2,1)S(1)} %collective-permute-done.28.far_ref, ...), custom_call_target="tpu_custom_call" | custom-call | flops 40000000000 | tf_op jit(solution)/shard_map/pallas_call | solution.py:169
  164.6 5.1 %collective-permute-done.32.far_ref = bf16[64,2304]{1,0:T(8,128)(2,1)S(1)} collective-permute-done((bf16[64,2304]{1,0:T(8,128)(2,1)S(1)}, bf16[64,2304]{1,0:T(8,128)(2,1)S(1)}, u32[]{:S(2)}, u32[]{:S(2)}) %collective-permute-start.32) | collective-permute-done | bytes 294944 | tf_op jit(solution)/shard_map/ppermute | solution.py:36
  169.8 3.0 %collective-permute-start.33 = (bf16[64,2304]{1,0:T(8,128)(2,1)S(1)}, bf16[64,2304]{1,0:T(8,128)(2,1)S(1)}, u32[]{:S(2)}, u32[]{:S(2)}) collective-permute-start(bf16[64,2304]{1,0:T(8,128)(2,1)S(1)} %collective-permute-done.32.far_ref), channel_id=1, source_target_pairs={{0,2},{1,3},{2,0},{3,1},{4,6},{5,7},{6,4},{7,5},{8,10},{9,11},{10,... | collective-permute-start | bytes 884744 | tf_op jit(solution)/shard_map/ppermute | solution.py:36
  172.8 2.8 %collective-permute-done.31.near_ref = bf16[64,2304]{1,0:T(8,128)(2,1)S(1)} collective-permute-done((bf16[64,2304]{1,0:T(8,128)(2,1)S(1)}, bf16[64,2304]{1,0:T(8,128)(2,1)S(1)}, u32[]{:S(2)}, u32[]{:S(2)}) %collective-permute-start.31) | collective-permute-done | bytes 294944 | tf_op jit(solution)/shard_map/ppermute | solution.py:36
  175.6 6.3 %collective-permute-done.33.last_ref = bf16[64,2304]{1,0:T(8,128)(2,1)S(1)} collective-permute-done((bf16[64,2304]{1,0:T(8,128)(2,1)S(1)}, bf16[64,2304]{1,0:T(8,128)(2,1)S(1)}, u32[]{:S(2)}, u32[]{:S(2)}) %collective-permute-start.33) | collective-permute-done | bytes 294944 | tf_op jit(solution)/shard_map/ppermute | solution.py:36
  181.9 2.6 %shard_map.174 = f32[40,256]{1,0:T(8,128)S(1)} custom-call(s32[6]{0:T(128)S(1)} %stack.35.where_ref, bf16[64,2304]{1,0:T(8,128)(2,1)S(1)} %shard_map.172.own_ref, bf16[64,2304]{1,0:T(8,128)(2,1)S(1)} %collective-permute-done.31.near_ref, bf16[64,2304]{1,0:T(8,128)(2,1)S(1)} %collective-permute-done.32.far_ref, ...), custom_call_target="tpu_custom_call" | custom-call | tf_op jit(solution)/shard_map/pallas_call | solution.py:169
  184.7 1.7 collective-permute-start.35
  190.5 1.3 collective-permute-start.39
  191.8 8.8 %collective-permute-start.38 = (f32[32,128]{1,0:T(8,128)S(1)}, f32[32,128]{1,0:T(8,128)S(1)}, u32[]{:S(2)}, u32[]{:S(2)}) collective-permute-start(f32[32,128]{1,0:T(8,128)S(1)} %shard_map.175), channel_id=1, source_target_pairs={{0,1},{1,3},{2,5},{3,7},{4,17},{5,19},{6,21},{7,23},{8,9},{9,11},{... | collective-permute-start | bytes 49160 | tf_op jit(solution)/shard_map/ppermute | solution.py:36
  200.7 1.9 collective-permute-start.37
  202.7 2.7 %collective-permute-done.37.first_ref = f32[32,128]{1,0:T(8,128)S(1)} collective-permute-done((f32[32,128]{1,0:T(8,128)S(1)}, f32[32,128]{1,0:T(8,128)S(1)}, u32[]{:S(2)}, u32[]{:S(2)}) %collective-permute-start.37) | collective-permute-done | bytes 16416 | tf_op jit(solution)/shard_map/ppermute | solution.py:36
  205.4 1.7 shard_map.176
  (97 shorter events, 22.3 us)
Async XLA Ops:
  0.6 18.5 %collective-permute-start = (bf16[2304,1152]{1,0:T(8,128)(2,1)}, bf16[2304,1152]{1,0:T(8,128)(2,1)}, u32[]{:S(2)}, u32[]{:S(2)}) collective-permute-start(bf16[2304,1152]{1,0:T(8,128)(2,1)} %refs_4_.9), channel_id=1, source_target_pairs={{0,1},{1,0},{2,3},{3,2},{4,5},{5,4},{6,7},{7,6},{8,9},{9,8},{10,11... | collective-permute-start | bytes 15925256 | tf_op jit(solution)/shard_map/ppermute | solution.py:36
  1.4 17.8 %collective-permute-start.1 = (bf16[1152,2304]{1,0:T(8,128)(2,1)}, bf16[1152,2304]{1,0:T(8,128)(2,1)}, u32[]{:S(2)}, u32[]{:S(2)}) collective-permute-start(bf16[1152,2304]{1,0:T(8,128)(2,1)} %refs_6_.1), channel_id=1, source_target_pairs={{0,1},{1,0},{2,3},{3,2},{4,5},{5,4},{6,7},{7,6},{8,9},{9,8},{10,11... | collective-permute-start | bytes 15925256 | tf_op jit(solution)/shard_map/ppermute | solution.py:36
  4.6 14.5 %collective-permute-start.3 = (bf16[128,2304]{1,0:T(8,128)(2,1)S(1)}, bf16[128,2304]{1,0:T(8,128)(2,1)S(1)}, u32[]{:S(2)}, u32[]{:S(2)}) collective-permute-start(bf16[128,2304]{1,0:T(8,128)(2,1)S(1)} %shard_map.158.refs_0_), channel_id=1, source_target_pairs={{0,2},{1,3},{2,0},{3,1},{4,6},{5,7},{6,4},{7,5},{8,10},{9,11},{10,... | collective-permute-start | bytes 1769480 | tf_op jit(solution)/shard_map/ppermute | solution.py:36
  4.8 17.7 %collective-permute-start.4 = (bf16[128,2304]{1,0:T(8,128)(2,1)S(1)}, bf16[128,2304]{1,0:T(8,128)(2,1)S(1)}, u32[]{:S(2)}, u32[]{:S(2)}) collective-permute-start(bf16[128,2304]{1,0:T(8,128)(2,1)S(1)} %shard_map.158.refs_0_), channel_id=1, source_target_pairs={{0,0},{1,1},{2,4},{3,5},{4,2},{5,3},{6,6},{7,7},{8,8},{9,9},{10,12... | collective-permute-start | bytes 1769480 | tf_op jit(solution)/shard_map/ppermute | solution.py:36
  9.9 7.5 %collective-permute-start.2 = (f32[1,1664]{1,0:T(1,128)S(1)}, f32[1,1664]{1,0:T(1,128)S(1)}, u32[]{:S(2)}, u32[]{:S(2)}) collective-permute-start(f32[1,1664]{1,0:T(1,128)S(1)} %broadcast_in_dim.12.refs_6_.refs_8_.bias_a), channel_id=1, source_target_pairs={{0,1},{1,0},{2,3},{3,2},{4,5},{5,4},{6,7},{7,6},{8,9},{9,8},{10,11... | collective-permute-start | bytes 19976 | tf_op jit(solution)/shard_map/ppermute | solution.py:36
  12.7 27.2 %slice-start = ((s8[5308416]{0:T(1024)(128)(4,1)}), s8[4194304]{0:T(1024)(128)(4,1)S(1)}, s32[]{:S(2)}) async-start(s8[5308416]{0:T(1024)(128)(4,1)} %bitcast.24), calls=%async_computation | async-start | bytes 8388608
  12.7 27.2 %slice-start.2 = ((s8[5308416]{0:T(1024)(128)(4,1)}), s8[4194304]{0:T(1024)(128)(4,1)S(1)}, s32[]{:S(2)}) async-start(s8[5308416]{0:T(1024)(128)(4,1)} %bitcast.26), calls=%async_computation.2 | async-start | bytes 8388608
  19.1 16.7 %collective-permute-start.5 = (bf16[128,2304]{1,0:T(8,128)(2,1)S(1)}, bf16[128,2304]{1,0:T(8,128)(2,1)S(1)}, u32[]{:S(2)}, u32[]{:S(2)}) collective-permute-start(bf16[128,2304]{1,0:T(8,128)(2,1)S(1)} %collective-permute-done.3.refs_1_), channel_id=1, source_target_pairs={{0,0},{1,1},{2,4},{3,5},{4,2},{5,3},{6,6},{7,7},{8,8},{9,9},{10,12... | collective-permute-start | bytes 1769480 | tf_op jit(solution)/shard_map/ppermute | solution.py:36
  22.5 17.4 %collective-permute-start.9 = (bf16[128,2304]{1,0:T(8,128)(2,1)S(1)}, bf16[128,2304]{1,0:T(8,128)(2,1)S(1)}, u32[]{:S(2)}, u32[]{:S(2)}) collective-permute-start(bf16[128,2304]{1,0:T(8,128)(2,1)S(1)} %collective-permute-done.4.refs_0_), channel_id=1, source_target_pairs={{2,0},{3,1},{4,6},{5,7},{10,8},{11,9},{12,14},{13,15},{18,16},{19,... | collective-permute-start | bytes 1769480 | tf_op jit(solution)/shard_map/ppermute | solution.py:36
  23.8 23.9 %collective-permute-start.7 = (bf16[128,2304]{1,0:T(8,128)(2,1)S(1)}, bf16[128,2304]{1,0:T(8,128)(2,1)S(1)}, u32[]{:S(2)}, u32[]{:S(2)}) collective-permute-start(bf16[128,2304]{1,0:T(8,128)(2,1)S(1)} %shard_map.159.refs_0_), channel_id=1, source_target_pairs={{0,2},{1,3},{2,0},{3,1},{4,6},{5,7},{6,4},{7,5},{8,10},{9,11},{10,... | collective-permute-start | bytes 1769480 | tf_op jit(solution)/shard_map/ppermute | solution.py:36
  35.8 15.2 %collective-permute-start.8 = (bf16[128,2304]{1,0:T(8,128)(2,1)S(1)}, bf16[128,2304]{1,0:T(8,128)(2,1)S(1)}, u32[]{:S(2)}, u32[]{:S(2)}) collective-permute-start(bf16[128,2304]{1,0:T(8,128)(2,1)S(1)} %shard_map.159.refs_0_), channel_id=1, source_target_pairs={{0,0},{1,1},{2,4},{3,5},{4,2},{5,3},{6,6},{7,7},{8,8},{9,9},{10,12... | collective-permute-start | bytes 1769480 | tf_op jit(solution)/shard_map/ppermute | solution.py:36
  38.5 21.9 %collective-permute-start.6 = (bf16[128,2304]{1,0:T(8,128)(2,1)S(1)}, bf16[128,2304]{1,0:T(8,128)(2,1)S(1)}, u32[]{:S(2)}, u32[]{:S(2)}) collective-permute-start(bf16[128,2304]{1,0:T(8,128)(2,1)S(1)} %collective-permute-done.5.refs_0_), channel_id=1, source_target_pairs={{2,0},{3,1},{4,6},{5,7},{10,8},{11,9},{12,14},{13,15},{18,16},{19,... | collective-permute-start | bytes 1769480 | tf_op jit(solution)/shard_map/ppermute | solution.py:36
  51.0 16.7 %collective-permute-start.10 = (bf16[128,2304]{1,0:T(8,128)(2,1)S(1)}, bf16[128,2304]{1,0:T(8,128)(2,1)S(1)}, u32[]{:S(2)}, u32[]{:S(2)}) collective-permute-start(bf16[128,2304]{1,0:T(8,128)(2,1)S(1)} %collective-permute-done.7.refs_1_), channel_id=1, source_target_pairs={{0,0},{1,1},{2,4},{3,5},{4,2},{5,3},{6,6},{7,7},{8,8},{9,9},{10,12... | collective-permute-start | bytes 1769480 | tf_op jit(solution)/shard_map/ppermute | solution.py:36
  53.6 14.2 %collective-permute-start.11 = (bf16[128,2304]{1,0:T(8,128)(2,1)S(1)}, bf16[128,2304]{1,0:T(8,128)(2,1)S(1)}, u32[]{:S(2)}, u32[]{:S(2)}) collective-permute-start(bf16[128,2304]{1,0:T(8,128)(2,1)S(1)} %shard_map.161.a_ref), channel_id=1, source_target_pairs={{0,2},{1,3},{6,4},{7,5},{8,10},{9,11},{14,12},{15,13},{16,18},{17,... | collective-permute-start | bytes 1769480 | tf_op jit(solution)/shard_map/ppermute | solution.py:36
  54.9 19.7 %collective-permute-start.12 = (bf16[128,2304]{1,0:T(8,128)(2,1)S(1)}, bf16[128,2304]{1,0:T(8,128)(2,1)S(1)}, u32[]{:S(2)}, u32[]{:S(2)}) collective-permute-start(bf16[128,2304]{1,0:T(8,128)(2,1)S(1)} %collective-permute-done.8.refs_2_), channel_id=1, source_target_pairs={{2,0},{3,1},{4,6},{5,7},{10,8},{11,9},{12,14},{13,15},{18,16},{19,... | collective-permute-start | bytes 1769480 | tf_op jit(solution)/shard_map/ppermute | solution.py:36
  68.5 16.3 %collective-permute-start.15 = (bf16[128,2304]{1,0:T(8,128)(2,1)S(1)}, bf16[128,2304]{1,0:T(8,128)(2,1)S(1)}, u32[]{:S(2)}, u32[]{:S(2)}) collective-permute-start(bf16[128,2304]{1,0:T(8,128)(2,1)S(1)} %shard_map.163), channel_id=1, source_target_pairs={{0,0},{1,1},{2,4},{3,5},{4,2},{5,3},{6,6},{7,7},{8,8},{9,9},{10,12... | collective-permute-start | bytes 1769480 | tf_op jit(solution)/shard_map/ppermute | solution.py:36
  71.1 13.7 %collective-permute-start.13 = (bf16[128,2304]{1,0:T(8,128)(2,1)S(1)}, bf16[128,2304]{1,0:T(8,128)(2,1)S(1)}, u32[]{:S(2)}, u32[]{:S(2)}) collective-permute-start(bf16[128,2304]{1,0:T(8,128)(2,1)S(1)} %collective-permute-done.10.refs_0_), channel_id=1, source_target_pairs={{2,0},{3,1},{4,6},{5,7},{10,8},{11,9},{12,14},{13,15},{18,16},{19,... | collective-permute-start | bytes 1769480 | tf_op jit(solution)/shard_map/ppermute | solution.py:36
  73.3 13.6 %collective-permute-start.16 = (bf16[128,2304]{1,0:T(8,128)(2,1)S(1)}, bf16[128,2304]{1,0:T(8,128)(2,1)S(1)}, u32[]{:S(2)}, u32[]{:S(2)}) collective-permute-start(bf16[128,2304]{1,0:T(8,128)(2,1)S(1)} %shard_map.162.a_ref), channel_id=1, source_target_pairs={{0,2},{1,3},{6,4},{7,5},{8,10},{9,11},{14,12},{15,13},{16,18},{17,... | collective-permute-start | bytes 1769480 | tf_op jit(solution)/shard_map/ppermute | solution.py:36
  84.8 23.3 %collective-permute-start.14 = (bf16[128,2304]{1,0:T(8,128)(2,1)S(1)}, bf16[128,2304]{1,0:T(8,128)(2,1)S(1)}, u32[]{:S(2)}, u32[]{:S(2)}) collective-permute-start(bf16[128,2304]{1,0:T(8,128)(2,1)S(1)} %get-tuple-element.70), channel_id=1, source_target_pairs={{0,2},{1,3},{2,0},{3,1},{4,6},{5,7},{6,4},{7,5},{8,10},{9,11},{10,... | collective-permute-start | bytes 1769480 | tf_op jit(solution)/shard_map/ppermute | solution.py:36
  87.7 20.4 %collective-permute-start.17 = (bf16[128,2304]{1,0:T(8,128)(2,1)S(1)}, bf16[128,2304]{1,0:T(8,128)(2,1)S(1)}, u32[]{:S(2)}, u32[]{:S(2)}) collective-permute-start(bf16[128,2304]{1,0:T(8,128)(2,1)S(1)} %shard_map.165), channel_id=1, source_target_pairs={{0,0},{1,1},{2,4},{3,5},{4,2},{5,3},{6,6},{7,7},{8,8},{9,9},{10,12... | collective-permute-start | bytes 1769480 | tf_op jit(solution)/shard_map/ppermute | solution.py:36
  90.7 17.4 %collective-permute-start.18 = (f32[2,128,512]{2,1,0:T(8,128)S(1)}, f32[2,128,512]{2,1,0:T(8,128)S(1)}, u32[]{:S(2)}, u32[]{:S(2)}) collective-permute-start(f32[2,128,512]{2,1,0:T(8,128)S(1)} %bitcast.38), channel_id=1, source_target_pairs={{0,16},{1,17},{2,18},{3,19},{4,20},{5,21},{6,22},{7,23},{8,24},{9,... | collective-permute-start | bytes 1572872 | tf_op jit(solution)/shard_map/ppermute | solution.py:36
  101.1 29.0 %copy-start.3 = (f32[2,2,2304]{2,1,0:T(2,128)S(1)}, f32[2,2,2304]{2,1,0:T(2,128)}, u32[]{:S(2)}) copy-start(f32[2,2,2304]{2,1,0:T(2,128)} %ada_ref.11) | copy-start | bytes 110596
  101.1 29.0 %copy-start.7 = (f32[2,2304]{1,0:T(2,128)S(1)}, f32[2,2304]{1,0:T(2,128)}, u32[]{:S(2)}) copy-start(f32[2,2304]{1,0:T(2,128)} %gate_ref.3) | copy-start | bytes 55300
  101.1 11.1 %collective-permute-start.25 = (bf16[128,2304]{1,0:T(8,128)(2,1)S(1)}, bf16[128,2304]{1,0:T(8,128)(2,1)S(1)}, u32[]{:S(2)}, u32[]{:S(2)}) collective-permute-start(bf16[128,2304]{1,0:T(8,128)(2,1)S(1)} %get-tuple-element.84), channel_id=1, source_target_pairs={{0,2},{1,3},{2,0},{3,1},{4,6},{5,7},{6,4},{7,5},{8,10},{9,11},{10,... | collective-permute-start | bytes 1769480 | tf_op jit(solution)/shard_map/ppermute | solution.py:36
  101.2 49.0 %collective-permute-start.23 = (bf16[2304,512]{1,0:T(8,128)(2,1)S(1)}, bf16[2304,512]{1,0:T(8,128)(2,1)S(1)}, u32[]{:S(2)}, u32[]{:S(2)}) collective-permute-start(bf16[2304,512]{1,0:T(8,128)(2,1)S(1)} %copy-done.2), channel_id=1, source_target_pairs={{0,1},{1,0},{2,3},{3,2},{4,5},{5,4},{6,7},{7,6},{8,9},{9,8},{10,11... | collective-permute-start | bytes 7077896 | tf_op jit(solution)/shard_map/ppermute | solution.py:36
  108.8 21.3 %collective-permute-start.19 = (bf16[128,2304]{1,0:T(8,128)(2,1)S(1)}, bf16[128,2304]{1,0:T(8,128)(2,1)S(1)}, u32[]{:S(2)}, u32[]{:S(2)}) collective-permute-start(bf16[128,2304]{1,0:T(8,128)(2,1)S(1)} %shard_map.166), channel_id=1, source_target_pairs={{0,2},{1,3},{2,0},{3,1},{4,6},{5,7},{6,4},{7,5},{8,10},{9,11},{10,... | collective-permute-start | bytes 1769480 | tf_op jit(solution)/shard_map/ppermute | solution.py:36
  110.5 14.1 %collective-permute-start.20 = (f32[2,128,512]{2,1,0:T(8,128)S(1)}, f32[2,128,512]{2,1,0:T(8,128)S(1)}, u32[]{:S(2)}, u32[]{:S(2)}) collective-permute-start(f32[2,128,512]{2,1,0:T(8,128)S(1)} %bitcast.37), channel_id=1, source_target_pairs={{0,17},{1,16},{2,19},{3,18},{4,21},{5,20},{6,23},{7,22},{8,25},{9,... | collective-permute-start | bytes 1572872 | tf_op jit(solution)/shard_map/ppermute | solution.py:36
  112.0 12.7 %collective-permute-start.21 = (f32[2,128,512]{2,1,0:T(8,128)S(1)}, f32[2,128,512]{2,1,0:T(8,128)S(1)}, u32[]{:S(2)}, u32[]{:S(2)}) collective-permute-start(f32[2,128,512]{2,1,0:T(8,128)S(1)} %bitcast.36), channel_id=1, source_target_pairs={{0,1},{1,0},{2,3},{3,2},{4,5},{5,4},{6,7},{7,6},{8,9},{9,8},{10,11... | collective-permute-start | bytes 1572872 | tf_op jit(solution)/shard_map/ppermute | solution.py:36
  112.9 28.4 %copy-start.8 = (bf16[512,32]{0,1:T(8,128)(2,1)S(1)}, bf16[512,32]{0,1:T(8,128)(2,1)}, u32[]{:S(2)}) copy-start(bf16[512,32]{0,1:T(8,128)(2,1)} %param.26) | copy-start | bytes 98308
  112.9 37.3 %collective-permute-start.26 = (bf16[128,2304]{1,0:T(8,128)(2,1)S(1)}, bf16[128,2304]{1,0:T(8,128)(2,1)S(1)}, u32[]{:S(2)}, u32[]{:S(2)}) collective-permute-start(bf16[128,2304]{1,0:T(8,128)(2,1)S(1)} %shard_map.170), channel_id=1, source_target_pairs={{0,4},{1,5},{2,6},{3,7},{4,0},{5,1},{6,2},{7,3},{8,12},{9,13},{10,... | collective-permute-start | bytes 1769480 | tf_op jit(solution)/shard_map/ppermute | solution.py:36
  131.6 5.9 %collective-permute-start.22 = (bf16[64,2304]{1,0:T(8,128)(2,1)S(1)}, bf16[64,2304]{1,0:T(8,128)(2,1)S(1)}, u32[]{:S(2)}, u32[]{:S(2)}) collective-permute-start(bf16[64,2304]{1,0:T(8,128)(2,1)S(1)} %get-tuple-element.82), channel_id=1, source_target_pairs={{0,16},{1,17},{2,18},{3,19},{4,20},{5,21},{6,22},{7,23},{8,24},{9,... | collective-permute-start | bytes 884744 | tf_op jit(solution)/shard_map/ppermute | solution.py:36
  138.5 15.3 %collective-permute-start.29 = (bf16[64,2304]{1,0:T(8,128)(2,1)S(1)}, bf16[64,2304]{1,0:T(8,128)(2,1)S(1)}, u32[]{:S(2)}, u32[]{:S(2)}) collective-permute-start(bf16[64,2304]{1,0:T(8,128)(2,1)S(1)} %shard_map.168.own_ref), channel_id=1, source_target_pairs={{0,2},{1,3},{2,0},{3,1},{4,6},{5,7},{6,4},{7,5},{8,10},{9,11},{10,... | collective-permute-start | bytes 884744 | tf_op jit(solution)/shard_map/ppermute | solution.py:36
  140.8 13.0 %collective-permute-start.28 = (bf16[64,2304]{1,0:T(8,128)(2,1)S(1)}, bf16[64,2304]{1,0:T(8,128)(2,1)S(1)}, u32[]{:S(2)}, u32[]{:S(2)}) collective-permute-start(bf16[64,2304]{1,0:T(8,128)(2,1)S(1)} %shard_map.168.own_ref), channel_id=1, source_target_pairs={{0,4},{1,5},{2,6},{3,7},{4,0},{5,1},{6,2},{7,3},{8,12},{9,13},{10,... | collective-permute-start | bytes 884744 | tf_op jit(solution)/shard_map/ppermute | solution.py:36
  141.3 8.8 %collective-permute-start.24 = (bf16[32,512]{1,0:T(8,128)(2,1)S(1)}, bf16[32,512]{1,0:T(8,128)(2,1)S(1)}, u32[]{:S(2)}, u32[]{:S(2)}) collective-permute-start(bf16[32,512]{1,0:T(8,128)(2,1)S(1)} %bitcast.31), channel_id=1, source_target_pairs={{0,1},{1,0},{2,3},{3,2},{4,5},{5,4},{6,7},{7,6},{8,9},{9,8},{10,11... | collective-permute-start | bytes 98312 | tf_op jit(solution)/shard_map/ppermute | solution.py:36
  152.6 6.2 %collective-permute-start.27 = (bf16[64,2304]{1,0:T(8,128)(2,1)S(1)}, bf16[64,2304]{1,0:T(8,128)(2,1)S(1)}, u32[]{:S(2)}, u32[]{:S(2)}) collective-permute-start(bf16[64,2304]{1,0:T(8,128)(2,1)S(1)} %get-tuple-element.93), channel_id=1, source_target_pairs={{0,16},{1,17},{2,18},{3,19},{4,20},{5,21},{6,22},{7,23},{8,24},{9,... | collective-permute-start | bytes 884744 | tf_op jit(solution)/shard_map/ppermute | solution.py:36
  153.8 8.2 %collective-permute-start.30 = (bf16[64,2304]{1,0:T(8,128)(2,1)S(1)}, bf16[64,2304]{1,0:T(8,128)(2,1)S(1)}, u32[]{:S(2)}, u32[]{:S(2)}) collective-permute-start(bf16[64,2304]{1,0:T(8,128)(2,1)S(1)} %collective-permute-done.28.far_ref), channel_id=1, source_target_pairs={{0,2},{1,3},{2,0},{3,1},{4,6},{5,7},{6,4},{7,5},{8,10},{9,11},{10,... | collective-permute-start | bytes 884744 | tf_op jit(solution)/shard_map/ppermute | solution.py:36
  159.8 10.0 %collective-permute-start.32 = (bf16[64,2304]{1,0:T(8,128)(2,1)S(1)}, bf16[64,2304]{1,0:T(8,128)(2,1)S(1)}, u32[]{:S(2)}, u32[]{:S(2)}) collective-permute-start(bf16[64,2304]{1,0:T(8,128)(2,1)S(1)} %shard_map.172.own_ref), channel_id=1, source_target_pairs={{0,4},{1,5},{2,6},{3,7},{4,0},{5,1},{6,2},{7,3},{8,12},{9,13},{10,... | collective-permute-start | bytes 884744 | tf_op jit(solution)/shard_map/ppermute | solution.py:36
  161.6 14.0 %collective-permute-start.31 = (bf16[64,2304]{1,0:T(8,128)(2,1)S(1)}, bf16[64,2304]{1,0:T(8,128)(2,1)S(1)}, u32[]{:S(2)}, u32[]{:S(2)}) collective-permute-start(bf16[64,2304]{1,0:T(8,128)(2,1)S(1)} %shard_map.172.own_ref), channel_id=1, source_target_pairs={{0,2},{1,3},{2,0},{3,1},{4,6},{5,7},{6,4},{7,5},{8,10},{9,11},{10,... | collective-permute-start | bytes 884744 | tf_op jit(solution)/shard_map/ppermute | solution.py:36
  169.8 12.2 %collective-permute-start.33 = (bf16[64,2304]{1,0:T(8,128)(2,1)S(1)}, bf16[64,2304]{1,0:T(8,128)(2,1)S(1)}, u32[]{:S(2)}, u32[]{:S(2)}) collective-permute-start(bf16[64,2304]{1,0:T(8,128)(2,1)S(1)} %collective-permute-done.32.far_ref), channel_id=1, source_target_pairs={{0,2},{1,3},{2,0},{3,1},{4,6},{5,7},{6,4},{7,5},{8,10},{9,11},{10,... | collective-permute-start | bytes 884744 | tf_op jit(solution)/shard_map/ppermute | solution.py:36
  172.8 29.8 %copy-start.11 = (f32[32]{0:T(128)S(1)}, f32[32]{0:T(128)}, u32[]{:S(2)}) copy-start(f32[32]{0:T(128)} %param.28) | copy-start | bytes 388
  172.8 32.6 %copy-start.4 = (f32[32,32,3,3]{1,0,3,2:T(8,128)S(1)}, f32[32,32,3,3]{1,0,3,2:T(8,128)}, u32[]{:S(2)}) copy-start(f32[32,32,3,3]{1,0,3,2:T(8,128)} %param.27) | copy-start | bytes 110596
  172.8 32.6 %copy-start.9 = (f32[1,32,128]{2,1,0:T(8,128)S(1)}, f32[1,32,128]{2,1,0:T(8,128)}, u32[]{:S(2)}) copy-start(f32[1,32,128]{2,1,0:T(8,128)} %param.29) | copy-start | bytes 49156
  184.7 3.8 %collective-permute-start.35 = (f32[40,128]{1,0:T(8,128)S(1)}, f32[40,128]{1,0:T(8,128)S(1)}, u32[]{:S(2)}, u32[]{:S(2)}) collective-permute-start(f32[40,128]{1,0:T(8,128)S(1)} %pad_maximum_fusion.2), channel_id=1, source_target_pairs={{0,4},{1,5},{2,6},{3,7},{4,0},{5,1},{6,2},{7,3},{8,12},{9,13},{10,... | collective-permute-start | bytes 61448 | tf_op jit(solution)/shard_map/ppermute | solution.py:36
  186.5 2.6 %collective-permute-start.36 = (f32[40,128]{1,0:T(8,128)S(1)}, f32[40,128]{1,0:T(8,128)S(1)}, u32[]{:S(2)}, u32[]{:S(2)}) collective-permute-start(f32[40,128]{1,0:T(8,128)S(1)} %pad_maximum_fusion.3), channel_id=1, source_target_pairs={{0,6},{1,7},{2,4},{3,5},{4,2},{5,3},{6,0},{7,1},{8,14},{9,15},{10,... | collective-permute-start | bytes 61448 | tf_op jit(solution)/shard_map/ppermute | solution.py:36
  187.3 2.6 %collective-permute-start.34 = (f32[40,128]{1,0:T(8,128)S(1)}, f32[40,128]{1,0:T(8,128)S(1)}, u32[]{:S(2)}, u32[]{:S(2)}) collective-permute-start(f32[40,128]{1,0:T(8,128)S(1)} %pad_maximum_fusion.1), channel_id=1, source_target_pairs={{0,2},{1,3},{2,0},{3,1},{4,6},{5,7},{6,4},{7,5},{8,10},{9,11},{10,... | collective-permute-start | bytes 61448 | tf_op jit(solution)/shard_map/ppermute | solution.py:36
  190.5 12.1 %collective-permute-start.39 = (f32[32,128]{1,0:T(8,128)S(1)}, f32[32,128]{1,0:T(8,128)S(1)}, u32[]{:S(2)}, u32[]{:S(2)}) collective-permute-start(f32[32,128]{1,0:T(8,128)S(1)} %shard_map.175), channel_id=1, source_target_pairs={{1,1},{2,3},{3,5},{5,17},{6,19},{7,21},{9,9},{10,11},{11,13},{13,2... | collective-permute-start | bytes 49160 | tf_op jit(solution)/shard_map/ppermute | solution.py:36
  191.8 10.9 %collective-permute-start.38 = (f32[32,128]{1,0:T(8,128)S(1)}, f32[32,128]{1,0:T(8,128)S(1)}, u32[]{:S(2)}, u32[]{:S(2)}) collective-permute-start(f32[32,128]{1,0:T(8,128)S(1)} %shard_map.175), channel_id=1, source_target_pairs={{0,1},{1,3},{2,5},{3,7},{4,17},{5,19},{6,21},{7,23},{8,9},{9,11},{... | collective-permute-start | bytes 49160 | tf_op jit(solution)/shard_map/ppermute | solution.py:36
  200.7 4.8 %collective-permute-start.37 = (f32[32,128]{1,0:T(8,128)S(1)}, f32[32,128]{1,0:T(8,128)S(1)}, u32[]{:S(2)}, u32[]{:S(2)}) collective-permute-start(f32[32,128]{1,0:T(8,128)S(1)} %shard_map.175), channel_id=1, source_target_pairs={{0,0},{1,2},{2,4},{3,6},{4,16},{5,18},{6,20},{7,22},{8,8},{9,10},{... | collective-permute-start | bytes 49160 | tf_op jit(solution)/shard_map/ppermute | solution.py:36
  (8 other events, 84.5 us)
